TPU v7x, 32 devices: a whole 2x2x4 slice. The times are simulated.
32 devices in a mesh: section: 4 (over y, x), row: 8 (over z, core).
Axes of the slice: x: 2, y: 2, z: 4, core: 2. Of those that a mesh axis runs over, the one named last changes fastest.
Arguments:
- tokens: int32 [4, 16, 128], P(None, 'row'), may hold values from 0 to 32
- embed: bfloat16 [33, 768], replicated, may hold values from -6 to 6
- ln_gain: float32 [4, 768], P('section'), may hold values from 0.5 to 1.5
- w_qkv: bfloat16 [4, 768, 2304], P('section'), may hold values from -0.21875 to 0.21875
- w_out: bfloat16 [4, 768, 768], P('section'), may hold values from -0.21875 to 0.21875
- out_grad: bfloat16 [4, 16, 128, 768], P(None, 'row'), may hold values from -0.01977539 to 0.01977539
Outputs:
- grad_qkv: float32 [4, 768, 2304], P('section', 'row')
- grad_out: float32 [4, 768, 768], P('section', 'row')
- grad_gain: float32 [4, 768], P('section', 'row')
All inputs are finite; a program needn't handle non-finite values.
Results may differ from a plain program's by a relative error of at most 0.04.
Values may be sent and summed in bfloat16 or wider, within the bound.
No kernel may reach another device: no remote copies, remote signals or barrier semaphores. Data moves between devices by JAX's collectives and lax.ppermute only.
A program may use at most 192 MiB of HBM per device.

v0:
```python
import math

import jax
import jax.numpy as jnp
from jax import lax
from jax.sharding import PartitionSpec as P

HEADS = 12
HEAD_DIM = 64
MICRO = 4


def shifted(value, axis, steps):
    count = lax.axis_size(axis)
    initial, last = (max(0, -steps), min(count, count - steps))
    return lax.ppermute(value, axis, [(source, source + steps) for source in range(initial, last)])


def norm_rows(x, gain):
    centred = x - jnp.mean(x, axis=-1, keepdims=True)
    spread = jnp.mean(centred * centred, axis=-1, keepdims=True)
    return (centred * lax.rsqrt(spread + 1e-05) * gain).astype(jnp.bfloat16)


def split_heads(qkv):
    parts = qkv.reshape(qkv.shape[0], qkv.shape[1], 3, HEADS, HEAD_DIM)
    return (parts[:, :, 0], parts[:, :, 1], parts[:, :, 2])


def project_rows(normed, wqkv):
    nrows, seq, width = normed.shape
    qkv = jnp.dot(normed.reshape(-1, width), wqkv, preferred_element_type=jnp.float32).astype(
        jnp.bfloat16
    )
    return qkv.reshape(nrows, seq, 3 * width)


def one_hot_table(tok_rows, vocab):
    flat = tok_rows.reshape(-1)
    return (jnp.arange(vocab, dtype=jnp.int32)[:, None] == flat[None, :]).astype(jnp.bfloat16)


def embed_rows(tok_rows, embed):
    table = one_hot_table(tok_rows, embed.shape[0])
    picked = lax.dot_general(
        table, embed, (((0,), (0,)), ((), ())), preferred_element_type=jnp.float32
    )
    return picked.reshape(tok_rows.shape[0], tok_rows.shape[1], embed.shape[1])


def layer_forward(x, gain, wqkv, wout, scale):
    nrows, seq, width = x.shape
    qkv = project_rows(norm_rows(x, gain), wqkv)
    query, keys, values = split_heads(qkv)
    share = lax.psum_scatter(
        scale * jnp.einsum("rihd,rjhd->ihj", query, keys, preferred_element_type=jnp.float32),
        "row",
        scatter_dimension=0,
        tiled=True,
    )
    own_probs = jax.nn.softmax(share, axis=-1).astype(jnp.bfloat16)
    probs = lax.all_gather(own_probs, "row", axis=0, tiled=True)
    mixed = jnp.einsum("ihj,rjhd->rihd", probs, values, preferred_element_type=jnp.float32).astype(
        jnp.bfloat16
    )
    mixed = mixed.reshape(-1, width)
    output = x + jnp.dot(mixed, wout, preferred_element_type=jnp.float32).reshape(nrows, seq, width)
    return (output, probs, qkv)


def soft_back(probs, d_probs):
    prob_f = probs.astype(jnp.float32)
    return (prob_f * (d_probs - jnp.sum(d_probs * prob_f, axis=-1, keepdims=True))).astype(
        jnp.bfloat16
    )


def layer_backward(x, gain, wqkv, wout, probs, qkv, upstream, scale):
    nrows, seq, width = x.shape
    normed, norm_back = jax.vjp(norm_rows, x, gain)
    query, keys, values = split_heads(qkv)
    mixed = jnp.einsum("ihj,rjhd->rihd", probs, values, preferred_element_type=jnp.float32).astype(
        jnp.bfloat16
    )
    flat_up = upstream.astype(jnp.bfloat16).reshape(-1, width)
    g_out = lax.dot_general(
        mixed.reshape(-1, width),
        flat_up,
        (((0,), (0,)), ((), ())),
        preferred_element_type=jnp.float32,
    )
    d_mixed = lax.dot_general(
        flat_up, wout, (((1,), (1,)), ((), ())), preferred_element_type=jnp.float32
    ).astype(jnp.bfloat16)
    d_mixed = d_mixed.reshape(nrows, seq, HEADS, HEAD_DIM)
    share_rows = seq // lax.axis_size("row")
    d_share = lax.psum_scatter(
        jnp.einsum("rihd,rjhd->ihj", d_mixed, values, preferred_element_type=jnp.float32),
        "row",
        scatter_dimension=0,
        tiled=True,
    )
    own_probs = lax.dynamic_slice_in_dim(probs, lax.axis_index("row") * share_rows, share_rows, 0)
    d_logits = lax.all_gather(soft_back(own_probs, d_share), "row", axis=0, tiled=True)
    d_values = jnp.einsum(
        "ihj,rihd->rjhd", probs, d_mixed, preferred_element_type=jnp.float32
    ).astype(jnp.bfloat16)
    d_query = (
        scale * jnp.einsum("ihj,rjhd->rihd", d_logits, keys, preferred_element_type=jnp.float32)
    ).astype(jnp.bfloat16)
    d_keys = (
        scale * jnp.einsum("ihj,rihd->rjhd", d_logits, query, preferred_element_type=jnp.float32)
    ).astype(jnp.bfloat16)
    d_qkv = jnp.stack([d_query, d_keys, d_values], axis=2).reshape(-1, 3 * width)
    g_qkv = lax.dot_general(
        normed.reshape(-1, width),
        d_qkv,
        (((0,), (0,)), ((), ())),
        preferred_element_type=jnp.float32,
    )
    d_normed = lax.dot_general(
        d_qkv, wqkv, (((1,), (1,)), ((), ())), preferred_element_type=jnp.float32
    ).astype(jnp.bfloat16)
    d_input, g_gain = norm_back(d_normed.reshape(nrows, seq, width))
    d_x = upstream + d_input
    return (d_x, g_qkv, g_out, g_gain)


def store_slot(buffer, value, index, valid):
    previous = lax.dynamic_index_in_dim(buffer, index, 0, keepdims=False)
    return lax.dynamic_update_index_in_dim(buffer, jnp.where(valid, value, previous), index, 0)


def local(tokens, embed, ln_gain, w_qkv, w_out, out_grad):
    n_section = lax.axis_size("section")
    n_row = lax.axis_size("row")
    section = lax.axis_index("section")
    rows_here = tokens.shape[1]
    seq = tokens.shape[2]
    width = embed.shape[1]
    scale = HEAD_DIM ** (-0.5) / math.sqrt(rows_here * n_row)
    gain = ln_gain[0]
    wqkv = w_qkv[0]
    wout = w_out[0]
    turns = MICRO + n_section - 1
    inputs_kept = jnp.zeros((MICRO, rows_here, seq, width), jnp.float32)
    probs_kept = jnp.zeros((MICRO, seq, HEADS, seq), jnp.bfloat16)
    qkv_kept = jnp.zeros((MICRO, rows_here, seq, 3 * width), jnp.bfloat16)
    incoming = jnp.zeros((rows_here, seq, width), jnp.float32)
    for turn in range(turns):
        micro = turn - section
        valid = (micro >= 0) & (micro < MICRO)
        index = jnp.clip(micro, 0, MICRO - 1)
        tok_now = lax.dynamic_index_in_dim(tokens, index, 0, keepdims=False)
        layer_in = jnp.where(section == 0, embed_rows(tok_now, embed), incoming)
        layer_out, probs, qkv = layer_forward(layer_in, gain, wqkv, wout, scale)
        inputs_kept = store_slot(inputs_kept, layer_in, index, valid)
        probs_kept = store_slot(probs_kept, probs, index, valid)
        qkv_kept = store_slot(qkv_kept, qkv, index, valid)
        if turn + 1 < turns:
            incoming = shifted(layer_out, "section", 1)
    acc_qkv = jnp.zeros((width, 3 * width), jnp.float32)
    acc_out = jnp.zeros((width, width), jnp.float32)
    acc_gain = jnp.zeros((width,), jnp.float32)
    returning = jnp.zeros((rows_here, seq, width), jnp.float32)
    for turn in range(turns):
        micro = turn - (n_section - 1 - section)
        valid = (micro >= 0) & (micro < MICRO)
        index = jnp.clip(micro, 0, MICRO - 1)
        arriving = lax.dynamic_index_in_dim(out_grad, index, 0, keepdims=False).astype(jnp.float32)
        upstream = jnp.where(section == n_section - 1, arriving, returning)
        layer_in = lax.dynamic_index_in_dim(inputs_kept, index, 0, keepdims=False)
        probs = lax.dynamic_index_in_dim(probs_kept, index, 0, keepdims=False)
        qkv = lax.dynamic_index_in_dim(qkv_kept, index, 0, keepdims=False)
        d_x, g_qkv, g_out, g_gain = layer_backward(
            layer_in, gain, wqkv, wout, probs, qkv, upstream, scale
        )
        acc_qkv = acc_qkv + jnp.where(valid, g_qkv, 0.0)
        acc_out = acc_out + jnp.where(valid, g_out, 0.0)
        acc_gain = acc_gain + jnp.where(valid, g_gain, 0.0)
        if turn + 1 < turns:
            returning = shifted(d_x, "section", -1)
    grad_qkv, grad_out, grad_gain = (
        lax.psum_scatter(acc_qkv[None], "row", scatter_dimension=1, tiled=True),
        lax.psum_scatter(acc_out[None], "row", scatter_dimension=1, tiled=True),
        lax.psum_scatter(acc_gain[None], "row", scatter_dimension=1, tiled=True),
    )
    return (grad_qkv, grad_out, grad_gain)


def solution(mesh):
    in_specs = (
        P(None, "row", None),
        P(),
        P("section", None),
        P("section", None, None),
        P("section", None, None),
        P(None, "row", None, None),
    )
    out_specs = (P("section", "row", None), P("section", "row", None), P("section", "row"))
    return jax.shard_map(local, mesh=mesh, in_specs=in_specs, out_specs=out_specs, check_vma=False)
```

profile of v0, /device:TPU:0, one launch (start us, length us, event | category | flops | bytes accessed | tf_op | source)
XLA Modules:
  0.0 1312.5 jit_solution(17656316970041154780)
XLA Ops:
  30.6 35.2 %reduce-scatter.20.cloned.1.call-done = f32[16,12,128]{2,1,0:T(8,128)} async-done(((f32[128,12,128]{2,1,0:T(8,128)}), f32[16,12,128]{2,1,0:T(8,128)}) %reduce-scatter.20.cloned.1.call-update) | async-done | bytes 98320 | tf_op jit(solution)/shard_map/reduce_scatter | solution.py:55
  67.2 14.5 %all_gather.42 = bf16[128,12,128]{2,0,1:T(8,128)(2,1)S(1)} all-gather(bf16[16,12,128]{2,0,1:T(8,128)(2,1)S(1)} %copy.197), channel_id=1, replica_groups=mesh['section'=4,'row'=8] {'row'}, dimensions={0}, use_global_device_ids=true | all-gather | bytes 442368 | tf_op jit(solution)/shard_map/all_gather | solution.py:62
  87.7 16.9 %collective-permute-done = f32[2,128,768]{2,1,0:T(8,128)S(1)} collective-permute-done((f32[2,128,768]{2,1,0:T(8,128)S(1)}, f32[2,128,768]{2,1,0:T(8,128)S(1)}, u32[]{:S(2)}, u32[]{:S(2)}) %collective-permute-start) | collective-permute-done | bytes 786464 | tf_op jit(solution)/shard_map/ppermute | solution.py:16
  120.6 31.5 %reduce-scatter.22.cloned.1.call-done = f32[16,12,128]{2,1,0:T(8,128)} async-done(((f32[128,12,128]{2,1,0:T(8,128)}), f32[16,12,128]{2,1,0:T(8,128)}) %reduce-scatter.22.cloned.1.call-update) | async-done | bytes 98320 | tf_op jit(solution)/shard_map/reduce_scatter | solution.py:55
  153.5 14.5 %all_gather.43 = bf16[128,12,128]{2,0,1:T(8,128)(2,1)S(1)} all-gather(bf16[16,12,128]{2,0,1:T(8,128)(2,1)S(1)} %copy.205), channel_id=1, replica_groups=mesh['section'=4,'row'=8] {'row'}, dimensions={0}, use_global_device_ids=true | all-gather | bytes 442368 | tf_op jit(solution)/shard_map/all_gather | solution.py:62
  170.2 4.1 collective-permute-start.1
  174.6 16.9 %collective-permute-done.1 = f32[2,128,768]{2,1,0:T(8,128)S(1)} collective-permute-done((f32[2,128,768]{2,1,0:T(8,128)S(1)}, f32[2,128,768]{2,1,0:T(8,128)S(1)}, u32[]{:S(2)}, u32[]{:S(2)}) %collective-permute-start.1) | collective-permute-done | bytes 786464 | tf_op jit(solution)/shard_map/ppermute | solution.py:16
  215.7 23.6 %reduce-scatter.24.cloned.1.call-done = f32[16,12,128]{2,1,0:T(8,128)} async-done(((f32[128,12,128]{2,1,0:T(8,128)}), f32[16,12,128]{2,1,0:T(8,128)}) %reduce-scatter.24.cloned.1.call-update) | async-done | bytes 98320 | tf_op jit(solution)/shard_map/reduce_scatter | solution.py:55
  240.8 14.5 %all_gather.44 = bf16[128,12,128]{2,0,1:T(8,128)(2,1)S(1)} all-gather(bf16[16,12,128]{2,0,1:T(8,128)(2,1)S(1)} %copy.213), channel_id=1, replica_groups=mesh['section'=4,'row'=8] {'row'}, dimensions={0}, use_global_device_ids=true | all-gather | bytes 442368 | tf_op jit(solution)/shard_map/all_gather | solution.py:62
  258.3 4.5 collective-permute-start.2
  309.4 18.6 %reduce-scatter.26.cloned.1.call-done = f32[16,12,128]{2,1,0:T(8,128)} async-done(((f32[128,12,128]{2,1,0:T(8,128)}), f32[16,12,128]{2,1,0:T(8,128)}) %reduce-scatter.26.cloned.1.call-update) | async-done | bytes 98320 | tf_op jit(solution)/shard_map/reduce_scatter | solution.py:55
  329.5 14.5 %all_gather.45 = bf16[128,12,128]{2,0,1:T(8,128)(2,1)S(1)} all-gather(bf16[16,12,128]{2,0,1:T(8,128)(2,1)S(1)} %copy.221), channel_id=1, replica_groups=mesh['section'=4,'row'=8] {'row'}, dimensions={0}, use_global_device_ids=true | all-gather | bytes 442368 | tf_op jit(solution)/shard_map/all_gather | solution.py:62
  347.0 4.7 collective-permute-start.3
  358.2 10.1 collective-permute-done.3
  398.8 18.3 %reduce-scatter.28.cloned.1.call-done = f32[16,12,128]{2,1,0:T(8,128)} async-done(((f32[128,12,128]{2,1,0:T(8,128)}), f32[16,12,128]{2,1,0:T(8,128)}) %reduce-scatter.28.cloned.1.call-update) | async-done | bytes 98320 | tf_op jit(solution)/shard_map/reduce_scatter | solution.py:55
  418.6 14.5 %all_gather.46 = bf16[128,12,128]{2,0,1:T(8,128)(2,1)S(1)} all-gather(bf16[16,12,128]{2,0,1:T(8,128)(2,1)S(1)} %copy.229), channel_id=1, replica_groups=mesh['section'=4,'row'=8] {'row'}, dimensions={0}, use_global_device_ids=true | all-gather | bytes 442368 | tf_op jit(solution)/shard_map/all_gather | solution.py:62
  436.1 4.5 collective-permute-start.4
  450.0 7.3 collective-permute-done.4
  484.2 22.0 %reduce-scatter.30.cloned.1.call-done = f32[16,12,128]{2,1,0:T(8,128)} async-done(((f32[128,12,128]{2,1,0:T(8,128)}), f32[16,12,128]{2,1,0:T(8,128)}) %reduce-scatter.30.cloned.1.call-update) | async-done | bytes 98320 | tf_op jit(solution)/shard_map/reduce_scatter | solution.py:55
  507.8 14.5 %all_gather.47 = bf16[128,12,128]{2,0,1:T(8,128)(2,1)S(1)} all-gather(bf16[16,12,128]{2,0,1:T(8,128)(2,1)S(1)} %copy.237), channel_id=1, replica_groups=mesh['section'=4,'row'=8] {'row'}, dimensions={0}, use_global_device_ids=true | all-gather | bytes 442368 | tf_op jit(solution)/shard_map/all_gather | solution.py:62
  533.7 11.4 collective-permute-done.5
  564.9 6.7 constant_dynamic-slice_fusion.17
  584.1 5.5 fusion.426
  595.5 14.8 %all_gather.48 = bf16[128,12,128]{2,0,1:T(8,128)(2,1)S(1)} all-gather(bf16[16,12,128]{2,0,1:T(8,128)(2,1)S(1)} %copy.252), channel_id=1, replica_groups=mesh['section'=4,'row'=8] {'row'}, dimensions={0}, use_global_device_ids=true | all-gather | bytes 442368 | tf_op jit(solution)/shard_map/all_gather | solution.py:62
  614.2 13.0 reduce-scatter.34.cloned.1.call-done
  628.5 14.6 %all_gather.49 = bf16[128,12,128]{2,0,1:T(8,128)(2,1)S(1)} all-gather(bf16[16,12,128]{2,0,1:T(8,128)(2,1)S(1)} %fusion.203), channel_id=1, replica_groups=mesh['section'=4,'row'=8] {'row'}, dimensions={0}, use_global_device_ids=true | all-gather | bytes 442368 | tf_op jit(solution)/shard_map/all_gather | solution.py:104
  651.8 19.5 %collective-permute-done.6 = f32[2,128,768]{2,1,0:T(8,128)S(1)} collective-permute-done((f32[2,128,768]{2,1,0:T(8,128)S(1)}, f32[2,128,768]{2,1,0:T(8,128)S(1)}, u32[]{:S(2)}, u32[]{:S(2)}) %collective-permute-start.6) | collective-permute-done | bytes 786464 | tf_op jit(solution)/shard_map/ppermute | solution.py:16
  687.6 26.4 %reduce-scatter.36.cloned.1.call-done = f32[16,12,128]{2,1,0:T(8,128)} async-done(((f32[128,12,128]{2,1,0:T(8,128)}), f32[16,12,128]{2,1,0:T(8,128)}) %reduce-scatter.36.cloned.1.call-update) | async-done | bytes 98320 | tf_op jit(solution)/shard_map/reduce_scatter | solution.py:97
  715.2 14.5 %all_gather.50 = bf16[128,12,128]{2,0,1:T(8,128)(2,1)S(1)} all-gather(bf16[16,12,128]{2,0,1:T(8,128)(2,1)S(1)} %fusion.202), channel_id=1, replica_groups=mesh['section'=4,'row'=8] {'row'}, dimensions={0}, use_global_device_ids=true | all-gather | bytes 442368 | tf_op jit(solution)/shard_map/all_gather | solution.py:104
  738.9 19.0 %collective-permute-done.7 = f32[2,128,768]{2,1,0:T(8,128)S(1)} collective-permute-done((f32[2,128,768]{2,1,0:T(8,128)S(1)}, f32[2,128,768]{2,1,0:T(8,128)S(1)}, u32[]{:S(2)}, u32[]{:S(2)}) %collective-permute-start.7) | collective-permute-done | bytes 786464 | tf_op jit(solution)/shard_map/ppermute | solution.py:16
  775.5 24.7 %reduce-scatter.38.cloned.1.call-done = f32[16,12,128]{2,1,0:T(8,128)} async-done(((f32[128,12,128]{2,1,0:T(8,128)}), f32[16,12,128]{2,1,0:T(8,128)}) %reduce-scatter.38.cloned.1.call-update) | async-done | bytes 98320 | tf_op jit(solution)/shard_map/reduce_scatter | solution.py:97
  801.4 14.5 %all_gather.51 = bf16[128,12,128]{2,0,1:T(8,128)(2,1)S(1)} all-gather(bf16[16,12,128]{2,0,1:T(8,128)(2,1)S(1)} %fusion.201), channel_id=1, replica_groups=mesh['section'=4,'row'=8] {'row'}, dimensions={0}, use_global_device_ids=true | all-gather | bytes 442368 | tf_op jit(solution)/shard_map/all_gather | solution.py:104
  824.8 19.3 %collective-permute-done.8 = f32[2,128,768]{2,1,0:T(8,128)S(1)} collective-permute-done((f32[2,128,768]{2,1,0:T(8,128)S(1)}, f32[2,128,768]{2,1,0:T(8,128)S(1)}, u32[]{:S(2)}, u32[]{:S(2)}) %collective-permute-start.8) | collective-permute-done | bytes 786464 | tf_op jit(solution)/shard_map/ppermute | solution.py:16
  861.5 24.6 %reduce-scatter.40.cloned.1.call-done = f32[16,12,128]{2,1,0:T(8,128)} async-done(((f32[128,12,128]{2,1,0:T(8,128)}), f32[16,12,128]{2,1,0:T(8,128)}) %reduce-scatter.40.cloned.1.call-update) | async-done | bytes 98320 | tf_op jit(solution)/shard_map/reduce_scatter | solution.py:97
  887.3 14.9 %all_gather.52 = bf16[128,12,128]{2,0,1:T(8,128)(2,1)S(1)} all-gather(bf16[16,12,128]{2,0,1:T(8,128)(2,1)S(1)} %fusion.200), channel_id=1, replica_groups=mesh['section'=4,'row'=8] {'row'}, dimensions={0}, use_global_device_ids=true | all-gather | bytes 442368 | tf_op jit(solution)/shard_map/all_gather | solution.py:104
  911.1 19.3 %collective-permute-done.9 = f32[2,128,768]{2,1,0:T(8,128)S(1)} collective-permute-done((f32[2,128,768]{2,1,0:T(8,128)S(1)}, f32[2,128,768]{2,1,0:T(8,128)S(1)}, u32[]{:S(2)}, u32[]{:S(2)}) %collective-permute-start.9) | collective-permute-done | bytes 786464 | tf_op jit(solution)/shard_map/ppermute | solution.py:16
  951.6 21.3 %reduce-scatter.42.cloned.1.call-done = f32[16,12,128]{2,1,0:T(8,128)} async-done(((f32[128,12,128]{2,1,0:T(8,128)}), f32[16,12,128]{2,1,0:T(8,128)}) %reduce-scatter.42.cloned.1.call-update) | async-done | bytes 98320 | tf_op jit(solution)/shard_map/reduce_scatter | solution.py:97
  974.1 14.5 %all_gather.53 = bf16[128,12,128]{2,0,1:T(8,128)(2,1)S(1)} all-gather(bf16[16,12,128]{2,0,1:T(8,128)(2,1)S(1)} %fusion.199), channel_id=1, replica_groups=mesh['section'=4,'row'=8] {'row'}, dimensions={0}, use_global_device_ids=true | all-gather | bytes 442368 | tf_op jit(solution)/shard_map/all_gather | solution.py:104
  1000.0 17.2 %collective-permute-done.10 = f32[2,128,768]{2,1,0:T(8,128)S(1)} collective-permute-done((f32[2,128,768]{2,1,0:T(8,128)S(1)}, f32[2,128,768]{2,1,0:T(8,128)S(1)}, u32[]{:S(2)}, u32[]{:S(2)}) %collective-permute-start.10) | collective-permute-done | bytes 786464 | tf_op jit(solution)/shard_map/ppermute | solution.py:16
  1039.1 20.2 %reduce-scatter.44.cloned.1.call-done = f32[16,12,128]{2,1,0:T(8,128)} async-done(((f32[128,12,128]{2,1,0:T(8,128)}), f32[16,12,128]{2,1,0:T(8,128)}) %reduce-scatter.44.cloned.1.call-update) | async-done | bytes 98320 | tf_op jit(solution)/shard_map/reduce_scatter | solution.py:97
  1060.6 14.5 %all_gather.54 = bf16[128,12,128]{2,0,1:T(8,128)(2,1)S(1)} all-gather(bf16[16,12,128]{2,0,1:T(8,128)(2,1)S(1)} %fusion.198), channel_id=1, replica_groups=mesh['section'=4,'row'=8] {'row'}, dimensions={0}, use_global_device_ids=true | all-gather | bytes 442368 | tf_op jit(solution)/shard_map/all_gather | solution.py:104
  1118.7 18.2 %reduce-scatter.46.cloned.1.call-done = f32[16,12,128]{2,1,0:T(8,128)} async-done(((f32[128,12,128]{2,1,0:T(8,128)}), f32[16,12,128]{2,1,0:T(8,128)}) %reduce-scatter.46.cloned.1.call-update) | async-done | bytes 98320 | tf_op jit(solution)/shard_map/reduce_scatter | solution.py:97
  1138.2 14.5 %all_gather.55 = bf16[128,12,128]{2,0,1:T(8,128)(2,1)S(1)} all-gather(bf16[16,12,128]{2,0,1:T(8,128)(2,1)S(1)} %fusion.197), channel_id=1, replica_groups=mesh['section'=4,'row'=8] {'row'}, dimensions={0}, use_global_device_ids=true | all-gather | bytes 442368 | tf_op jit(solution)/shard_map/all_gather | solution.py:104
  1159.8 5.8 add_bitcast_fusion.1
  1165.7 5.5 fusion.154
  1191.5 12.7 add_bitcast_fusion
  1205.6 20.4 %reduce-scatter.50.cloned.1.call-done = f32[1,96,768]{2,1,0:T(8,128)} async-done(((f32[1,768,768]{2,1,0:T(8,128)}), f32[1,96,768]{2,1,0:T(8,128)}) %reduce-scatter.50.cloned.1.call-update) | async-done | bytes 294928 | tf_op jit(solution)/shard_map/reduce_scatter | solution.py:185
  1226.0 79.5 %reduce-scatter.48.cloned.1.call-done = f32[1,96,2304]{2,1,0:T(8,128)} async-done(((f32[1,768,2304]{2,1,0:T(8,128)}), f32[1,96,2304]{2,1,0:T(8,128)}) %reduce-scatter.48.cloned.1.call-update) | async-done | bytes 884752 | tf_op jit(solution)/shard_map/reduce_scatter | solution.py:184
  (795 shorter events, 483.6 us)
Async XLA Ops:
  7.2 58.5 %reduce-scatter.20.cloned.1.call-start = ((), (), s32[]{:S(2)}) async-start(), calls=%async_computation.17 | async-start | bytes 1179648 | tf_op jit(solution)/shard_map/reduce_scatter | solution.py:55
  30.5 121.6 %reduce-scatter.22.cloned.1.call-start = ((), (), s32[]{:S(2)}) async-start(), calls=%async_computation.18 | async-start | bytes 1179648 | tf_op jit(solution)/shard_map/reduce_scatter | solution.py:55
  65.7 17.5 %copy-start.47 = (f32[256,768]{1,0:T(8,128)S(1)}, f32[256,768]{1,0:T(8,128)}, u32[]{:S(2)}) copy-start(f32[256,768]{1,0:T(8,128)} %get-tuple-element.138) | copy-start | bytes 2359300
  83.8 20.8 %collective-permute-start = (f32[2,128,768]{2,1,0:T(8,128)S(1)}, f32[2,128,768]{2,1,0:T(8,128)S(1)}, u32[]{:S(2)}, u32[]{:S(2)}) collective-permute-start(f32[2,128,768]{2,1,0:T(8,128)S(1)} %convolution_add_fusion.5), channel_id=1, source_target_pairs={{0,8},{8,16},{16,24},{1,9},{9,17},{17,25},{2,10},{10,18},{18,26},{... | collective-permute-start | bytes 2359304 | tf_op jit(solution)/shard_map/ppermute | solution.py:16
  120.5 118.8 %reduce-scatter.24.cloned.1.call-start = ((), (), s32[]{:S(2)}) async-start(), calls=%async_computation.19 | async-start | bytes 1179648 | tf_op jit(solution)/shard_map/reduce_scatter | solution.py:55
  152.1 17.5 %copy-start.29 = (f32[2,128,768]{2,1,0:T(8,128)S(1)}, f32[2,128,768]{2,1,0:T(8,128)}, u32[]{:S(2)}) copy-start(f32[2,128,768]{2,1,0:T(8,128)} %copy-done.28) | copy-start | bytes 2359300
  170.2 21.3 %collective-permute-start.1 = (f32[2,128,768]{2,1,0:T(8,128)S(1)}, f32[2,128,768]{2,1,0:T(8,128)S(1)}, u32[]{:S(2)}, u32[]{:S(2)}) collective-permute-start(f32[2,128,768]{2,1,0:T(8,128)S(1)} %convolution_add_fusion.4), channel_id=1, source_target_pairs={{0,8},{8,16},{16,24},{1,9},{9,17},{17,25},{2,10},{10,18},{18,26},{... | collective-permute-start | bytes 2359304 | tf_op jit(solution)/shard_map/ppermute | solution.py:16
  207.5 120.6 %reduce-scatter.26.cloned.1.call-start = ((), (), s32[]{:S(2)}) async-start(), calls=%async_computation.20 | async-start | bytes 1179648 | tf_op jit(solution)/shard_map/reduce_scatter | solution.py:55
  239.4 17.5 %copy-start.4 = (bf16[1,768,768]{2,1,0:T(8,128)(2,1)S(1)}, bf16[1,768,768]{2,1,0:T(8,128)(2,1)}, u32[]{:S(2)}) copy-start(bf16[1,768,768]{2,1,0:T(8,128)(2,1)} %param.10) | copy-start | bytes 3538948
  239.4 17.5 %copy-start.31 = (f32[2,128,768]{2,1,0:T(8,128)S(1)}, f32[2,128,768]{2,1,0:T(8,128)}, u32[]{:S(2)}) copy-start(f32[2,128,768]{2,1,0:T(8,128)} %copy-done.30) | copy-start | bytes 2359300
  258.3 21.1 %collective-permute-start.2 = (f32[2,128,768]{2,1,0:T(8,128)}, f32[2,128,768]{2,1,0:T(8,128)}, u32[]{:S(2)}, u32[]{:S(2)}) collective-permute-start(f32[2,128,768]{2,1,0:T(8,128)} %convolution_add_fusion.3), channel_id=1, source_target_pairs={{0,8},{8,16},{16,24},{1,9},{9,17},{17,25},{2,10},{10,18},{18,26},{... | collective-permute-start | bytes 2359304 | tf_op jit(solution)/shard_map/ppermute | solution.py:16
  295.3 121.8 %reduce-scatter.28.cloned.1.call-start = ((), (), s32[]{:S(2)}) async-start(), calls=%async_computation.21 | async-start | bytes 1179648 | tf_op jit(solution)/shard_map/reduce_scatter | solution.py:55
  328.1 17.5 %copy-start.5 = (bf16[1,768,768]{2,1,0:T(8,128)(2,1)S(1)}, bf16[1,768,768]{2,1,0:T(8,128)(2,1)}, u32[]{:S(2)}) copy-start(bf16[1,768,768]{2,1,0:T(8,128)(2,1)} %param.10) | copy-start | bytes 3538948
  328.1 17.5 %copy-start.34 = (f32[2,128,768]{2,1,0:T(8,128)S(1)}, f32[2,128,768]{2,1,0:T(8,128)}, u32[]{:S(2)}) copy-start(f32[2,128,768]{2,1,0:T(8,128)} %copy-done.33) | copy-start | bytes 2359300
  347.0 21.2 %collective-permute-start.3 = (f32[2,128,768]{2,1,0:T(8,128)}, f32[2,128,768]{2,1,0:T(8,128)}, u32[]{:S(2)}, u32[]{:S(2)}) collective-permute-start(f32[2,128,768]{2,1,0:T(8,128)} %convolution_add_fusion.2), channel_id=1, source_target_pairs={{0,8},{8,16},{16,24},{1,9},{9,17},{17,25},{2,10},{10,18},{18,26},{... | collective-permute-start | bytes 2359304 | tf_op jit(solution)/shard_map/ppermute | solution.py:16
  384.3 121.9 %reduce-scatter.30.cloned.1.call-start = ((), (), s32[]{:S(2)}) async-start(), calls=%async_computation.22 | async-start | bytes 1179648 | tf_op jit(solution)/shard_map/reduce_scatter | solution.py:55
  417.1 17.5 %copy-start.6 = (bf16[1,768,768]{2,1,0:T(8,128)(2,1)S(1)}, bf16[1,768,768]{2,1,0:T(8,128)(2,1)}, u32[]{:S(2)}) copy-start(bf16[1,768,768]{2,1,0:T(8,128)(2,1)} %param.10) | copy-start | bytes 3538948
  417.1 17.5 %copy-start.36 = (f32[2,128,768]{2,1,0:T(8,128)S(1)}, f32[2,128,768]{2,1,0:T(8,128)}, u32[]{:S(2)}) copy-start(f32[2,128,768]{2,1,0:T(8,128)} %copy-done.35) | copy-start | bytes 2359300
  436.1 21.2 %collective-permute-start.4 = (f32[2,128,768]{2,1,0:T(8,128)}, f32[2,128,768]{2,1,0:T(8,128)}, u32[]{:S(2)}, u32[]{:S(2)}) collective-permute-start(f32[2,128,768]{2,1,0:T(8,128)} %convolution_add_fusion.1), channel_id=1, source_target_pairs={{0,8},{8,16},{16,24},{1,9},{9,17},{17,25},{2,10},{10,18},{18,26},{... | collective-permute-start | bytes 2359304 | tf_op jit(solution)/shard_map/ppermute | solution.py:16
  473.4 120.8 %reduce-scatter.32.cloned.1.call-start = ((), (), s32[]{:S(2)}) async-start(), calls=%async_computation.23 | async-start | bytes 1179648 | tf_op jit(solution)/shard_map/reduce_scatter | solution.py:55
  524.2 20.9 %collective-permute-start.5 = (f32[2,128,768]{2,1,0:T(8,128)S(1)}, f32[2,128,768]{2,1,0:T(8,128)S(1)}, u32[]{:S(2)}, u32[]{:S(2)}) collective-permute-start(f32[2,128,768]{2,1,0:T(8,128)S(1)} %convolution_add_fusion), channel_id=1, source_target_pairs={{0,8},{8,16},{16,24},{1,9},{9,17},{17,25},{2,10},{10,18},{18,26},{... | collective-permute-start | bytes 2359304 | tf_op jit(solution)/shard_map/ppermute | solution.py:16
  562.2 65.0 %reduce-scatter.34.cloned.1.call-start = ((), (), s32[]{:S(2)}) async-start(), calls=%async_computation.24 | async-start | bytes 1179648 | tf_op jit(solution)/shard_map/reduce_scatter | solution.py:97
  589.6 124.4 %reduce-scatter.36.cloned.1.call-start = ((), (), s32[]{:S(2)}) async-start(), calls=%async_computation.25 | async-start | bytes 1179648 | tf_op jit(solution)/shard_map/reduce_scatter | solution.py:97
  591.6 57.5 %copy-start.161 = (f32[2,128]{1,0:T(2,128)}, f32[2,128]{1,0:T(2,128)S(1)}, u32[]{:S(2)}) copy-start(f32[2,128]{1,0:T(2,128)S(1)} %fusion.416) | copy-start | bytes 3076
  594.2 18.0 %copy-start.79 = (bf16[2,128,12,64]{1,0,3,2:T(2,128)(2,1)S(1)}, bf16[2,128,12,64]{1,0,3,2:T(2,128)(2,1)}, u32[]{:S(2)}) copy-start(bf16[2,128,12,64]{1,0,3,2:T(2,128)(2,1)} %reshape.1020) | copy-start | bytes 1179652
  627.2 17.5 %copy-start.138 = (bf16[2,128,1,12,64]{1,4,0,3,2:T(8,128)(2,1)S(1)}, bf16[2,128,1,12,64]{1,4,0,3,2:T(8,128)(2,1)}, u32[]{:S(2)}) copy-start(bf16[2,128,1,12,64]{1,4,0,3,2:T(8,128)(2,1)} %fusion.108) | copy-start | bytes 1179652
  649.5 21.8 %collective-permute-start.6 = (f32[2,128,768]{2,1,0:T(8,128)S(1)}, f32[2,128,768]{2,1,0:T(8,128)S(1)}, u32[]{:S(2)}, u32[]{:S(2)}) collective-permute-start(f32[2,128,768]{2,1,0:T(8,128)S(1)} %fusion.219), channel_id=1, source_target_pairs={{8,0},{16,8},{24,16},{9,1},{17,9},{25,17},{10,2},{18,10},{26,18},{... | collective-permute-start | bytes 2359304 | tf_op jit(solution)/shard_map/ppermute | solution.py:16
  650.8 22.2 %copy-start.8 = (bf16[1,768,768]{2,1,0:T(8,128)(2,1)S(1)}, bf16[1,768,768]{2,1,0:T(8,128)(2,1)}, u32[]{:S(2)}) copy-start(bf16[1,768,768]{2,1,0:T(8,128)(2,1)} %param.10) | copy-start | bytes 3538948
  682.9 117.3 %reduce-scatter.38.cloned.1.call-start = ((), (), s32[]{:S(2)}) async-start(), calls=%async_computation.26 | async-start | bytes 1179648 | tf_op jit(solution)/shard_map/reduce_scatter | solution.py:97
  736.2 21.7 %collective-permute-start.7 = (f32[2,128,768]{2,1,0:T(8,128)S(1)}, f32[2,128,768]{2,1,0:T(8,128)S(1)}, u32[]{:S(2)}, u32[]{:S(2)}) collective-permute-start(f32[2,128,768]{2,1,0:T(8,128)S(1)} %fusion.222), channel_id=1, source_target_pairs={{8,0},{16,8},{24,16},{9,1},{17,9},{25,17},{10,2},{18,10},{26,18},{... | collective-permute-start | bytes 2359304 | tf_op jit(solution)/shard_map/ppermute | solution.py:16
  737.7 21.8 %copy-start.9 = (bf16[1,768,768]{2,1,0:T(8,128)(2,1)S(1)}, bf16[1,768,768]{2,1,0:T(8,128)(2,1)}, u32[]{:S(2)}) copy-start(bf16[1,768,768]{2,1,0:T(8,128)(2,1)} %param.10) | copy-start | bytes 3538948
  769.5 116.6 %reduce-scatter.40.cloned.1.call-start = ((), (), s32[]{:S(2)}) async-start(), calls=%async_computation.27 | async-start | bytes 1179648 | tf_op jit(solution)/shard_map/reduce_scatter | solution.py:97
  770.8 51.0 %copy-start.155 = (f32[2,128]{1,0:T(2,128)}, f32[2,128]{1,0:T(2,128)S(1)}, u32[]{:S(2)}) copy-start(f32[2,128]{1,0:T(2,128)S(1)} %get-tuple-element.128) | copy-start | bytes 3076
  822.4 21.7 %collective-permute-start.8 = (f32[2,128,768]{2,1,0:T(8,128)S(1)}, f32[2,128,768]{2,1,0:T(8,128)S(1)}, u32[]{:S(2)}, u32[]{:S(2)}) collective-permute-start(f32[2,128,768]{2,1,0:T(8,128)S(1)} %fusion.225), channel_id=1, source_target_pairs={{8,0},{16,8},{24,16},{9,1},{17,9},{25,17},{10,2},{18,10},{26,18},{... | collective-permute-start | bytes 2359304 | tf_op jit(solution)/shard_map/ppermute | solution.py:16
  823.7 22.0 %copy-start.10 = (bf16[1,768,768]{2,1,0:T(8,128)(2,1)S(1)}, bf16[1,768,768]{2,1,0:T(8,128)(2,1)}, u32[]{:S(2)}) copy-start(bf16[1,768,768]{2,1,0:T(8,128)(2,1)} %param.10) | copy-start | bytes 3538948
  855.7 117.2 %reduce-scatter.42.cloned.1.call-start = ((), (), s32[]{:S(2)}) async-start(), calls=%async_computation.28 | async-start | bytes 1179648 | tf_op jit(solution)/shard_map/reduce_scatter | solution.py:97
  856.9 51.2 %copy-start.157 = (f32[2,128]{1,0:T(2,128)}, f32[2,128]{1,0:T(2,128)S(1)}, u32[]{:S(2)}) copy-start(f32[2,128]{1,0:T(2,128)S(1)} %get-tuple-element.124) | copy-start | bytes 3076
  886.1 17.8 %copy-start.141 = (bf16[2,128,1,12,64]{1,4,0,3,2:T(8,128)(2,1)S(1)}, bf16[2,128,1,12,64]{1,4,0,3,2:T(8,128)(2,1)}, u32[]{:S(2)}) copy-start(bf16[2,128,1,12,64]{1,4,0,3,2:T(8,128)(2,1)} %fusion.111) | copy-start | bytes 1179652
  908.7 21.7 %collective-permute-start.9 = (f32[2,128,768]{2,1,0:T(8,128)S(1)}, f32[2,128,768]{2,1,0:T(8,128)S(1)}, u32[]{:S(2)}, u32[]{:S(2)}) collective-permute-start(f32[2,128,768]{2,1,0:T(8,128)S(1)} %fusion.228), channel_id=1, source_target_pairs={{8,0},{16,8},{24,16},{9,1},{17,9},{25,17},{10,2},{18,10},{26,18},{... | collective-permute-start | bytes 2359304 | tf_op jit(solution)/shard_map/ppermute | solution.py:16
  910.0 22.0 %copy-start.11 = (bf16[1,768,768]{2,1,0:T(8,128)(2,1)S(1)}, bf16[1,768,768]{2,1,0:T(8,128)(2,1)}, u32[]{:S(2)}) copy-start(bf16[1,768,768]{2,1,0:T(8,128)(2,1)} %param.10) | copy-start | bytes 3538948
  942.0 117.3 %reduce-scatter.44.cloned.1.call-start = ((), (), s32[]{:S(2)}) async-start(), calls=%async_computation.29 | async-start | bytes 1179648 | tf_op jit(solution)/shard_map/reduce_scatter | solution.py:97
  995.2 22.0 %collective-permute-start.10 = (f32[2,128,768]{2,1,0:T(8,128)S(1)}, f32[2,128,768]{2,1,0:T(8,128)S(1)}, u32[]{:S(2)}, u32[]{:S(2)}) collective-permute-start(f32[2,128,768]{2,1,0:T(8,128)S(1)} %fusion.231), channel_id=1, source_target_pairs={{8,0},{16,8},{24,16},{9,1},{17,9},{25,17},{10,2},{18,10},{26,18},{... | collective-permute-start | bytes 2359304 | tf_op jit(solution)/shard_map/ppermute | solution.py:16
  1000.0 18.9 %copy-start.12 = (bf16[1,768,768]{2,1,0:T(8,128)(2,1)S(1)}, bf16[1,768,768]{2,1,0:T(8,128)(2,1)}, u32[]{:S(2)}) copy-start(bf16[1,768,768]{2,1,0:T(8,128)(2,1)} %param.10) | copy-start | bytes 3538948
  1028.7 108.2 %reduce-scatter.46.cloned.1.call-start = ((), (), s32[]{:S(2)}) async-start(), calls=%async_computation.30 | async-start | bytes 1179648 | tf_op jit(solution)/shard_map/reduce_scatter | solution.py:97
  1081.6 13.4 %collective-permute-start.11 = (bf16[2,128,768]{2,1,0:T(8,128)(2,1)S(1)}, bf16[2,128,768]{2,1,0:T(8,128)(2,1)S(1)}, u32[]{:S(2)}, u32[]{:S(2)}) collective-permute-start(bf16[2,128,768]{2,1,0:T(8,128)(2,1)S(1)} %fusion.234), channel_id=1, source_target_pairs={{8,0},{16,8},{24,16},{9,1},{17,9},{25,17},{10,2},{18,10},{26,18},{... | collective-permute-start | bytes 1179656 | tf_op jit(solution)/shard_map/ppermute | solution.py:16
  1105.8 98.4 %reduce-scatter.52.cloned.1.call-start = ((), (), s32[]{:S(2)}) async-start(), calls=%async_computation.33 | async-start | bytes 442368
  1159.5 66.5 %reduce-scatter.50.cloned.1.call-start = ((), (), s32[]{:S(2)}) async-start(), calls=%async_computation.32 | async-start | bytes 2654208 | tf_op jit(solution)/shard_map/reduce_scatter | solution.py:185
  1165.7 139.9 %reduce-scatter.48.cloned.1.call-start = ((), (), s32[]{:S(2)}) async-start(), calls=%async_computation.31 | async-start | bytes 7962624 | tf_op jit(solution)/shard_map/reduce_scatter | solution.py:184
  (180 other events, 731.0 us)
Sparse Core Ops, SparseCore 0:
  30.6 35.0 reduce-scatter.19
  120.7 31.3 reduce-scatter.21
  207.6 31.6 reduce-scatter.23
  295.4 32.5 reduce-scatter.25
  384.5 32.6 reduce-scatter.27
  473.5 32.7 reduce-scatter.29
  562.3 31.7 reduce-scatter.31
  596.4 30.7 reduce-scatter.33
  683.0 30.8 reduce-scatter.35
  769.6 30.5 reduce-scatter.37
  855.8 30.2 reduce-scatter.39
  942.1 30.7 reduce-scatter.41
  1028.8 30.4 reduce-scatter.43
  1105.9 30.9 reduce-scatter.45
  1159.6 29.0 reduce-scatter.51
  1191.6 34.3 reduce-scatter.49
  1228.9 76.6 reduce-scatter.47
where the time goes:
time: 1330 us; the launch traced here: 1310 us
  waiting for transfers between devices  561 us (42%)
  local copies, waits for them, and re-layouts  221 us (17%)
  blocking collectives  203 us (15%)
  matrix products  174 us (13%)
  other arithmetic  99.8 us (8%)
  starting transfers between devices  35.1 us (3%)
  between operations  17.2 us (1%)
    ppermute x12, waiting for transfers between devices, shifted(): lax.ppermute(value, axis, [(source, source + steps) for source in range(i...  161 us
    reduce_scatter x7, waiting for transfers between devices, layer_forward(): lax.psum_scatter(scale * jnp.einsum('rihd,rjhd->ihj', query, keys, prefer...  152 us
    reduce_scatter x7, waiting for transfers between devices, layer_backward(): lax.psum_scatter(jnp.einsum('rihd,rjhd->ihj', d_mixed, values, preferred_...  148 us
    all_gather x7, blocking collectives, layer_backward(): lax.all_gather(soft_back(own_probs, d_share), 'row', axis=0, tiled=True)  102 us
    all_gather x7, blocking collectives, layer_forward(): probs = lax.all_gather(own_probs, 'row', axis=0, tiled=True)  102 us
    reduce_scatter x1, waiting for transfers between devices, local(): lax.psum_scatter(acc_qkv[None], 'row', scatter_dimension=1, tiled=True)  79.5 us
    dot_general x7, matrix products, layer_backward(): lax.dot_general(normed.reshape(-1, width), d_qkv, (((0,), (0,)), ((), ())...  38.4 us
    dynamic_update_slice x19, other arithmetic, store_slot(): lax.dynamic_update_index_in_dim(buffer, jnp.where(valid, value, previous)...  34.2 us
  transfers between devices with their start and end apart: 29, of which 28 were waited for; matrix products, arithmetic and copies ran while one was open for 17% of the time, Pallas kernels for 0%

commit v1 on v0

v1 whole, which is shorter than its diff:
```python
import functools
import math

import jax
import jax.numpy as jnp
from jax import lax
from jax.experimental import pallas as pl
from jax.experimental.pallas import tpu as pltpu
from jax.sharding import PartitionSpec as P

HEADS = 12
HEAD_DIM = 64
PACK = 128 // HEAD_DIM
F32 = jnp.float32
BF16 = jnp.bfloat16
VMEM_LIMIT = 48 * 1024 * 1024
NT = (((1,), (1,)), ((), ()))
TN = (((0,), (0,)), ((), ()))


def mm(a, b):
    return jnp.dot(a, b, preferred_element_type=F32)


def mm_nt(a, b):
    return lax.dot_general(a, b, NT, preferred_element_type=F32)


def lane_masks(lanes):
    place = lax.broadcasted_iota(jnp.int32, (1, lanes), 1) % (PACK * HEAD_DIM) // HEAD_DIM
    return [(place == n).astype(F32).astype(BF16) for n in range(PACK)]


def rows_to_lanes(ref, seq, first):
    width = PACK * HEAD_DIM
    count = ref.shape[0] // seq
    return jnp.concatenate(
        [ref[r * seq : (r + 1) * seq, first : first + width] for r in range(count)], axis=1
    )


def heads_to_rows(cat, masks):
    return jnp.concatenate([cat * mask for mask in masks], axis=0)


def lanes_to_rows(ref, seq, first, value):
    width = PACK * HEAD_DIM
    for r in range(ref.shape[0] // seq):
        ref[r * seq : (r + 1) * seq, first : first + width] = value[:, r * width : (r + 1) * width]


class Weights:
    def __init__(self, choice, member, own, pieces, columns, dst, sems):
        self.choice, self.member, self.own, self.pieces = choice, member, own, pieces
        self.columns, self.dst, self.sems = columns, dst, sems

    def each(self, act):
        @pl.when(self.choice == 0)
        def _():
            act(pltpu.make_async_copy(self.own.at[0], self.dst, self.sems.at[0]))

        for offset, group in self.pieces.items():

            @pl.when(self.choice == offset)
            def _(group=group):
                seen = 0
                for ref in group:
                    rows = ref.shape[1]
                    for n in range(ref.shape[0]):
                        start = pl.multiple_of((self.member ^ seen) * rows, rows)
                        act(
                            pltpu.make_async_copy(
                                ref.at[n, :, self.columns],
                                self.dst.at[pl.ds(start, rows)],
                                self.sems.at[seen],
                            )
                        )
                        seen += 1

    def start(self):
        self.each(lambda copy: copy.start())

    def wait(self):
        self.each(lambda copy: copy.wait())


def take_pieces(it, layout):
    return {offset: [next(it) for _ in range(count)] for offset, count in layout}


def softmax_heads(la, lb, scale, keep):
    seq = la.shape[0]
    for h in range(HEADS):
        at = slice(h * seq, (h + 1) * seq)
        logits = (la[:, at] + lb[:, at]) * scale
        e = jnp.exp(logits - jnp.max(logits, axis=-1, keepdims=True))
        keep(h, e / jnp.sum(e, axis=-1, keepdims=True))


def norm_parts(x):
    centred = x - jnp.mean(x, axis=-1, keepdims=True)
    spread = jnp.mean(centred * centred, axis=-1, keepdims=True)
    rstd = lax.rsqrt(spread + 1e-05)
    return centred * rstd, rstd


def pair_scores(ref_a, first_a, ref_b, first_b, out, out_rows, seq, masks, begin):
    width = PACK * HEAD_DIM
    for p in range(HEADS // PACK):
        a = rows_to_lanes(ref_a, seq, first_a + p * width)
        b = heads_to_rows(rows_to_lanes(ref_b, seq, first_b + p * width), masks)
        at = slice(p * PACK * seq, (p + 1) * PACK * seq)
        part = mm_nt(a, b)

        @pl.when(begin)
        def _():
            out[out_rows, at] = part

        @pl.when(jnp.logical_not(begin))
        def _():
            out[out_rows, at] += part


def pair_mix(weights, ref_b, first_b, out, first_out, scale, seq, masks):
    width = PACK * HEAD_DIM
    for p in range(HEADS // PACK):
        b = heads_to_rows(rows_to_lanes(ref_b, seq, first_b + p * width), masks)
        value = mm(weights[:, p * PACK * seq : (p + 1) * PACK * seq], b)
        if scale is not None:
            value = value * scale
        lanes_to_rows(out, seq, first_out + p * width, value.astype(BF16))


def forward_kernel(has_prev, has_top, layout, scale, seq, width, info, *refs):
    it = iter(refs)
    if has_prev:
        la, lb, v_prev = next(it), next(it), next(it)
    x_in, gain = next(it), next(it)
    top = next(it) if has_top else None
    own_q, own_o = next(it), next(it)
    pieces = take_pieces(it, layout)
    if has_prev:
        probs_out, mixed_out, x_out = next(it), next(it), next(it)
    h_out, qkv_out, score_out = next(it), next(it), next(it)
    if has_top:
        dmix_out = next(it)
    wq, sem_q = next(it), next(it)
    if has_prev:
        wo, sem_o = next(it), next(it)
    if has_top:
        wt, sem_t = next(it), next(it)
    step = pl.program_id(0)
    masks = lane_masks(PACK * HEAD_DIM * (x_in.shape[0] // seq))
    qcols, ocols = slice(0, 3 * width), slice(3 * width, 4 * width)

    @pl.when(step == 0)
    def _():
        jobs = []
        if has_prev:
            jobs.append(Weights(info[1], info[2], own_o, pieces, ocols, wo, sem_o))
        jobs.append(Weights(info[0], info[2], own_q, pieces, qcols, wq, sem_q))
        if has_top:
            jobs.append(Weights(info[0], info[2], own_o, pieces, ocols, wt, sem_t))
        for job in jobs:
            job.start()
        if has_prev:

            def keep(h, value):
                probs_out[:, h * seq : (h + 1) * seq] = value.astype(BF16)

            softmax_heads(la, lb, scale, keep)
        for job in jobs:
            job.wait()

    if has_prev:
        pair_mix(probs_out, v_prev, 0, mixed_out, 0, None, seq, masks)
        x = x_in[...] + mm(mixed_out[...], wo[...])
        x_out[...] = x
    else:
        x = x_in[...]
    hat, _ = norm_parts(x)
    h = (hat * gain[...]).astype(BF16)
    h_out[...] = h
    for t in range(3):
        at = slice(t * width, (t + 1) * width)
        qkv_out[:, at] = mm(h, wq[:, at]).astype(BF16)
    begin = step == 0
    pair_scores(qkv_out, 0, qkv_out, width, score_out, slice(0, seq), seq, masks, begin)
    if has_top:
        dmix_out[...] = mm_nt(top[...], wt[...]).astype(BF16)
        pair_scores(
            dmix_out, 0, qkv_out, 2 * width, score_out, slice(seq, 2 * seq), seq, masks, begin
        )


def backward_kernel(is_top, is_last, layout, scale, seq, width, info, *refs):
    it = iter(refs)
    sa, sb = next(it), next(it)
    if not is_top:
        probs = next(it)
    qkv, dmix, x_in, gain = next(it), next(it), next(it), next(it)
    if not is_last:
        dy, v_prev = next(it), next(it)
    own_q, own_o = next(it), next(it)
    pieces = take_pieces(it, layout)
    dqkv_out, gain_out = next(it), next(it)
    if is_top:
        mixed_out = next(it)
    if not is_last:
        dy_out, dyb_out, dmix_out, score_out = next(it), next(it), next(it), next(it)
    dl, dlt, pt = next(it), next(it), next(it)
    if is_top:
        probs = next(it)
    wq, sem_q = next(it), next(it)
    if not is_last:
        wo, sem_o = next(it), next(it)
    step = pl.program_id(0)
    masks = lane_masks(PACK * HEAD_DIM * (x_in.shape[0] // seq))
    qcols, ocols = slice(0, 3 * width), slice(3 * width, 4 * width)

    @pl.when(step == 0)
    def _():
        jobs = [Weights(info[0], info[2], own_q, pieces, qcols, wq, sem_q)]
        if not is_last:
            jobs.append(Weights(info[1], info[2], own_o, pieces, ocols, wo, sem_o))
        for job in jobs:
            job.start()
        if is_top:

            def keep(h, value):
                probs[:, h * seq : (h + 1) * seq] = value.astype(BF16)

            softmax_heads(sa.at[0:seq], sb.at[0:seq], scale, keep)
        first = seq if is_top else 0
        for h in range(HEADS):
            at = slice(h * seq, (h + 1) * seq)
            prob = probs[:, at].astype(F32)
            d_prob = sa[first : first + seq, at] + sb[first : first + seq, at]
            d_logit = prob * (d_prob - jnp.sum(d_prob * prob, axis=-1, keepdims=True))
            dl[:, at] = d_logit.astype(BF16)
            dlt[:, at] = jnp.transpose(d_logit).astype(BF16)
            pt[:, at] = jnp.transpose(prob).astype(BF16)
        for job in jobs:
            job.wait()

    if is_top:
        pair_mix(probs, qkv, 2 * width, mixed_out, 0, None, seq, masks)
    pair_mix(dl, qkv, width, dqkv_out, 0, scale, seq, masks)
    pair_mix(dlt, qkv, 0, dqkv_out, width, scale, seq, masks)
    pair_mix(pt, dmix, 0, dqkv_out, 2 * width, None, seq, masks)
    d_h = mm_nt(dqkv_out[...], wq[...]).astype(BF16).astype(F32)
    hat, rstd = norm_parts(x_in[...])
    part = jnp.sum(d_h * hat, axis=0, keepdims=True)

    @pl.when(step == 0)
    def _():
        gain_out[...] = part

    @pl.when(step > 0)
    def _():
        gain_out[...] += part

    if not is_last:
        d_hat = d_h * gain[...]
        mean_d = jnp.mean(d_hat, axis=-1, keepdims=True)
        mean_dh = jnp.mean(d_hat * hat, axis=-1, keepdims=True)
        d_x = dy[...].astype(F32) + rstd * (d_hat - mean_d - hat * mean_dh)
        dy_out[...] = d_x
        dyb_out[...] = d_x.astype(BF16)
        dmix_out[...] = mm_nt(dyb_out[...], wo[...]).astype(BF16)
        pair_scores(dmix_out, 0, v_prev, 0, score_out, slice(0, seq), seq, masks, step == 0)


class Chain:
    def __init__(self, section, member, n_group, own, gathered, seq, width, rows, scale):
        self.section, self.member, self.n_group = section, member, n_group
        self.own, self.seq, self.width, self.rows = own, seq, width, rows
        self.scale = scale
        self.layout = tuple((offset, len(group)) for offset, group in gathered.items())
        self.weights = [own[0], own[1]] + [a for group in gathered.values() for a in group]
        per_step = 4 if rows % 4 == 0 else (2 if rows % 2 == 0 else 1)
        self.chunk = per_step * seq
        self.steps = rows // per_step

    def info(self, now, other):
        return jnp.stack(
            [self.section ^ now, self.section ^ other, self.member]
        ).astype(jnp.int32)

    def whole(self, rows, lanes):
        return pl.BlockSpec((rows, lanes), lambda i, s: (0, 0))

    def tile(self, lanes, column=0):
        return pl.BlockSpec((self.chunk, lanes), lambda i, s: (i, column))

    def call(self, body, name, info, ins, in_specs, outs, out_specs, scratch, flops):
        size = sum(math.prod(o.shape) * o.dtype.itemsize for o in outs)
        size += sum(math.prod(a.shape) * a.dtype.itemsize for a in ins)
        any_spec = pl.BlockSpec(memory_space=pl.ANY)
        return pl.pallas_call(
            body,
            name=name,
            out_shape=outs,
            grid_spec=pltpu.PrefetchScalarGridSpec(
                num_scalar_prefetch=1,
                grid=(self.steps,),
                in_specs=in_specs + [any_spec] * len(self.weights),
                out_specs=out_specs,
                scratch_shapes=scratch,
            ),
            compiler_params=pltpu.CompilerParams(
                dimension_semantics=("arbitrary",), vmem_limit_bytes=VMEM_LIMIT
            ),
            cost_estimate=pl.CostEstimate(flops=flops, bytes_accessed=size, transcendentals=0),
        )(info, *ins, *self.weights)

    def wq_scratch(self):
        return [
            pltpu.VMEM((self.width, 3 * self.width), BF16),
            pltpu.SemaphoreType.DMA((self.n_group,)),
        ]

    def wo_scratch(self):
        return [
            pltpu.VMEM((self.width, self.width), BF16),
            pltpu.SemaphoreType.DMA((self.n_group,)),
        ]

    def forward(self, layer, x, gain, prev, top):
        seq, width = self.seq, self.width
        n = self.rows * seq
        hw = HEADS * seq
        ins, in_specs, outs, out_specs = [], [], [], []
        if prev is not None:
            ins += [prev[0], prev[1], prev[2]]
            in_specs += [self.whole(seq, hw), self.whole(seq, hw), self.tile(width, 2)]
            outs += [
                jax.ShapeDtypeStruct((seq, hw), BF16),
                jax.ShapeDtypeStruct((n, width), BF16),
                jax.ShapeDtypeStruct((n, width), F32),
            ]
            out_specs += [self.whole(seq, hw), self.tile(width), self.tile(width)]
        ins += [x, gain]
        in_specs += [self.tile(width), self.whole(1, width)]
        score_rows = seq
        if top is not None:
            ins.append(top)
            in_specs.append(self.tile(width))
            score_rows = 2 * seq
        outs += [
            jax.ShapeDtypeStruct((n, width), BF16),
            jax.ShapeDtypeStruct((n, 3 * width), BF16),
            jax.ShapeDtypeStruct((score_rows, hw), F32),
        ]
        out_specs += [self.tile(width), self.tile(3 * width), self.whole(score_rows, hw)]
        scratch = self.wq_scratch()
        if prev is not None:
            scratch += self.wo_scratch()
        if top is not None:
            outs.append(jax.ShapeDtypeStruct((n, width), BF16))
            out_specs.append(self.tile(width))
            scratch += self.wo_scratch()
        body = functools.partial(
            forward_kernel, prev is not None, top is not None, self.layout, self.scale, seq, width
        )
        return self.call(
            body,
            f"layer_in_{layer}",
            self.info(layer, max(layer - 1, 0)),
            ins,
            in_specs,
            outs,
            out_specs,
            scratch,
            2 * n * width * width * 5,
        )

    def backward(self, layer, scores, probs, qkv, dmix, x, gain, dy, v_prev):
        seq, width = self.seq, self.width
        n = self.rows * seq
        hw = HEADS * seq
        is_top, is_last = probs is None, layer == 0
        score_rows = scores[0].shape[0]
        ins = [scores[0], scores[1]]
        in_specs = [self.whole(score_rows, hw)] * 2
        if not is_top:
            ins.append(probs)
            in_specs.append(self.whole(seq, hw))
        ins += [qkv, dmix, x, gain]
        in_specs += [self.tile(3 * width), self.tile(width), self.tile(width), self.whole(1, width)]
        outs = [jax.ShapeDtypeStruct((n, 3 * width), BF16), jax.ShapeDtypeStruct((1, width), F32)]
        out_specs = [self.tile(3 * width), self.whole(1, width)]
        scratch = [pltpu.VMEM((seq, hw), BF16)] * 3
        if is_top:
            outs.append(jax.ShapeDtypeStruct((n, width), BF16))
            out_specs.append(self.tile(width))
            scratch.append(pltpu.VMEM((seq, hw), BF16))
        scratch = scratch + self.wq_scratch()
        if not is_last:
            ins += [dy, v_prev]
            in_specs += [self.tile(width), self.tile(width, 2)]
            outs += [
                jax.ShapeDtypeStruct((n, width), F32),
                jax.ShapeDtypeStruct((n, width), BF16),
                jax.ShapeDtypeStruct((n, width), BF16),
                jax.ShapeDtypeStruct((seq, hw), F32),
            ]
            out_specs += [self.tile(width)] * 3 + [self.whole(seq, hw)]
            scratch = scratch + self.wo_scratch()
        body = functools.partial(
            backward_kernel, is_top, is_last, self.layout, self.scale, seq, width
        )
        return self.call(
            body,
            f"layer_back_{layer}",
            self.info(layer, max(layer - 1, 0)),
            ins,
            in_specs,
            outs,
            out_specs,
            scratch,
            2 * n * width * width * 5,
        )


def group_swap(value, n_row, n_group):
    other = jnp.zeros_like(value)
    bit = 1
    while bit < n_group:
        if bit > 1:
            value = value + other
        other = lax.ppermute(value, "row", [(r, r ^ bit) for r in range(n_row)])
        bit *= 2
    return value, other


def gather_weights(wqkv, wout, n_section, n_row, n_group, member):
    width = wqkv.shape[0]
    part = width // n_group
    mine = jnp.concatenate(
        [
            lax.dynamic_slice_in_dim(wqkv, member * part, part, 0),
            lax.dynamic_slice_in_dim(wout, member * part, part, 0),
        ],
        axis=1,
    )
    got = {0: mine}
    for offset in sorted(range(1, n_section), key=lambda n: (n.bit_count(), n)):
        low = offset & -offset
        rest = offset ^ low
        if rest == 0:
            got[offset] = lax.ppermute(
                mine, "section", [(s, s ^ offset) for s in range(n_section)]
            )
        else:
            sends = jnp.where(member % 2 == 0, got[rest], got[low])
            perm = [
                (s * n_row + r, (s ^ (low if r % n_group % 2 == 0 else rest)) * n_row + r)
                for s in range(n_section)
                for r in range(n_row)
            ]
            got[offset] = lax.ppermute(sends, ("section", "row"), perm)
    pieces = {}
    for offset in range(1, n_section):
        have = [got[offset][None]]
        bit = 1
        while bit < n_group:
            send = have[0] if len(have) == 1 else jnp.concatenate(have, axis=0)
            have.append(lax.ppermute(send, "row", [(r, r ^ bit) for r in range(n_row)]))
            bit *= 2
        pieces[offset] = have
    return pieces


def local(tokens, embed, ln_gain, w_qkv, w_out, out_grad):
    n_section = lax.axis_size("section")
    n_row = lax.axis_size("row")
    section = lax.axis_index("section")
    place = lax.axis_index("row")
    micro, rows_here, seq = tokens.shape
    width = embed.shape[1]
    n_group = n_row // micro
    member = place % n_group
    rows = rows_here * micro
    scale = HEAD_DIM ** (-0.5) / math.sqrt(rows_here * n_row)
    gathered = gather_weights(w_qkv[0], w_out[0], n_section, n_row, n_group, member)
    same = [[m * n_group + g for m in range(micro)] for g in range(n_group)]
    exchange = functools.partial(
        lax.all_to_all,
        axis_name="row",
        split_axis=0,
        concat_axis=0,
        axis_index_groups=same,
        tiled=True,
    )
    tok = exchange(tokens).reshape(-1)
    top_grad = exchange(out_grad).reshape(rows * seq, width)
    gains = lax.all_gather(ln_gain[0], "section", axis=0, tiled=False)
    table = (jnp.arange(embed.shape[0], dtype=jnp.int32)[:, None] == tok[None, :]).astype(BF16)
    x = lax.dot_general(table, embed, TN, preferred_element_type=F32)

    chain = Chain(
        section, member, n_group, (w_qkv, w_out), gathered, seq, width, rows, scale
    )
    xs, hs, qkvs, probs, mixed = [], [], [], [], []
    scores = None
    dmix = None
    for layer in range(n_section):
        gain = gains[layer][None]
        prev = None if layer == 0 else (scores[0], scores[1], qkvs[-1])
        top = top_grad if layer == n_section - 1 else None
        outs = list(chain.forward(layer, x, gain, prev, top))
        if prev is not None:
            probs.append(outs.pop(0))
            mixed.append(outs.pop(0))
            x = outs.pop(0)
        if top is not None:
            dmix = outs.pop()
        xs.append(x)
        hs.append(outs[0])
        qkvs.append(outs[1])
        scores = group_swap(outs[2], n_row, n_group)
    probs.append(None)
    mixed.append(None)

    dy = top_grad
    ups = [None] * n_section
    dqkvs = [None] * n_section
    gain_parts = [None] * n_section
    ups[-1] = top_grad
    for layer in reversed(range(n_section)):
        v_prev = qkvs[layer - 1] if layer > 0 else None
        outs = list(
            chain.backward(
                layer, scores, probs[layer], qkvs[layer], dmix, xs[layer], gains[layer][None], dy, v_prev
            )
        )
        dqkvs[layer], gain_parts[layer] = outs[0], outs[1]
        outs = outs[2:]
        if probs[layer] is None:
            mixed[layer] = outs.pop(0)
        if layer > 0:
            dy, ups[layer - 1], dmix = outs[0], outs[1], outs[2]
            scores = group_swap(outs[3], n_row, n_group)

    def own_grads(layer):
        def run():
            g_qkv = lax.dot_general(hs[layer], dqkvs[layer], TN, preferred_element_type=F32)
            g_out = lax.dot_general(mixed[layer], ups[layer], TN, preferred_element_type=F32)
            return g_qkv.astype(BF16), g_out.astype(BF16), gain_parts[layer][0]

        return run

    g_qkv, g_out, g_gain = lax.switch(section, [own_grads(n) for n in range(n_section)])
    g_all = jnp.concatenate([g_qkv, g_out], axis=1)
    g_all = lax.psum_scatter(g_all, "row", scatter_dimension=0, tiled=True).astype(F32)
    g_gain = lax.psum_scatter(g_gain[None], "row", scatter_dimension=1, tiled=True)
    return (g_all[None, :, : 3 * width], g_all[None, :, 3 * width :], g_gain)


def solution(mesh):
    in_specs = (
        P(None, "row", None),
        P(),
        P("section", None),
        P("section", None, None),
        P("section", None, None),
        P(None, "row", None, None),
    )
    out_specs = (P("section", "row", None), P("section", "row", None), P("section", "row"))
    return jax.shard_map(local, mesh=mesh, in_specs=in_specs, out_specs=out_specs, check_vma=False)
```

time: 1330 us -> 415 us (0.31)
  waiting for transfers between devices: 561 us -> 176 us
  local copies, waits for them, and re-layouts: 221 us -> 15.3 us
  blocking collectives: 203 us -> 8.11 us
  matrix products: 174 us -> 11.7 us
  Pallas kernels: 0 us -> 155 us
  other arithmetic: 99.8 us -> 9.99 us
  starting transfers between devices: 35.1 us -> 17.9 us
    reduce_scatter x16 -> x1, waiting for transfers between devices: 400 us -> 54.1 us  [local(): lax.psum_scatter(g_all, 'row', scatter_dimension=0, tiled=True).astype(F32)]
    all_gather x14 -> x1, blocking collectives: 203 us -> 8.11 us  [local(): gains = lax.all_gather(ln_gain[0], 'section', axis=0, tiled=False)]
    dot_general x96 -> x3, matrix products: 174 us -> 11.7 us  [the longest x1 6.8 us: run(): lax.dot_general(hs[layer], dqkvs[layer], TN, preferred_element_type=F32)]
    pallas_call x0 -> x8, Pallas kernels: none -> 155 us  [call(): pl.pallas_call(body, name=name, out_shape=outs, grid_spec=pltpu.PrefetchS...]
    ppermute x12 -> x13, waiting for transfers between devices: 161 us -> 92.4 us  [the longest x2 51.4 us: gather_weights(): lax.ppermute(mine, 'section', [(s, s ^ offset) for s in range(n_section)])]
    convert_element_type x34 -> x0, local copies, waits for them, and re-layouts: 37.9 us -> none  [the longest x7 16.8 us: project_rows(): jnp.dot(normed.reshape(-1, width), wqkv, preferred_element_type=jnp.float32)]
    dynamic_update_slice x19 -> x0, other arithmetic: 34.2 us -> none  [store_slot(): lax.dynamic_update_index_in_dim(buffer, jnp.where(valid, value, previous)...]
    another operation x14 -> x2, local copies, waits for them, and re-layouts: 33.3 us -> 0.01 us  [the longest x7 24.8 us: split_heads(): parts = qkv.reshape(qkv.shape[0], qkv.shape[1], 3, HEADS, HEAD_DIM)]
  transfers between devices with their start and end apart: 29 -> 17, of which waited for: 28 -> 11; matrix products, arithmetic and copies ran while one was open for 17% -> 2% of each run, Pallas kernels for 0% -> 8%
where the time goes in v1:
time: 415 us; the launch traced here: 410 us
  waiting for transfers between devices  176 us (42%)
  Pallas kernels  155 us (37%)
  starting transfers between devices  17.9 us (4%)
  local copies, waits for them, and re-layouts  15.3 us (4%)
  between operations  14.6 us (4%)
  matrix products  11.7 us (3%)
  other arithmetic  9.99 us (2%)
  blocking collectives  8.11 us (2%)
    pallas_call x8, Pallas kernels, call(): pl.pallas_call(body, name=name, out_shape=outs, grid_spec=pltpu.PrefetchS...  155 us
    reduce_scatter x1, waiting for transfers between devices, local(): lax.psum_scatter(g_all, 'row', scatter_dimension=0, tiled=True).astype(F32)  54.1 us
    ppermute x2, waiting for transfers between devices, gather_weights(): lax.ppermute(mine, 'section', [(s, s ^ offset) for s in range(n_section)])  51.4 us
    unnamed x3, waiting for transfers between devices  29.3 us
    ppermute x1, waiting for transfers between devices, gather_weights(): got[offset] = lax.ppermute(sends, ('section', 'row'), perm)  26.9 us
    ppermute x7, waiting for transfers between devices, group_swap(): other = lax.ppermute(value, 'row', [(r, r ^ bit) for r in range(n_row)])  14 us
    unnamed x60, local copies, waits for them, and re-layouts  10.9 us
  transfers between devices with their start and end apart: 17, of which 11 were waited for; matrix products, arithmetic and copies ran while one was open for 2% of the time, Pallas kernels for 8%

profile of v1, /device:TPU:0, one launch (start us, length us, event | category | flops | bytes accessed | tf_op | source)
XLA Modules:
  0.0 410.1 jit_solution(17104611033038941052)
XLA Ops:
  7.2 1.1 dynamic-slice_bitcast_fusion.1
  8.3 1.6 dynamic-slice_bitcast_fusion
  9.9 1.7 pad_maximum_fusion.1
  11.6 3.0 collective-permute-start.2
  14.6 1.5 collective-permute-start
  16.1 50.1 %collective-permute-done.2 = bf16[384,3072]{1,0:T(8,128)(2,1)} collective-permute-done((bf16[384,3072]{1,0:T(8,128)(2,1)}, bf16[384,3072]{1,0:T(8,128)(2,1)}, u32[]{:S(2)}, u32[]{:S(2)}) %collective-permute-start.2) | collective-permute-done | bytes 2359328 | tf_op jit(solution)/shard_map/ppermute | solution.py:452
  66.2 1.4 collective-permute-done
  67.5 2.8 broadcast_select_fusion
  70.3 1.6 collective-permute-start.4
  72.4 26.9 %collective-permute-done.4 = bf16[384,3072]{1,0:T(8,128)(2,1)} collective-permute-done((bf16[384,3072]{1,0:T(8,128)(2,1)S(1)}, bf16[384,3072]{1,0:T(8,128)(2,1)}, u32[]{:S(2)}, u32[]{:S(2)}) %collective-permute-start.4) | collective-permute-done | bytes 2359328 | tf_op jit(solution)/shard_map/ppermute | solution.py:462
  99.3 4.9 %all-to-all-start = ((s32[4,2,128]{2,1,0:T(2,128)}), s32[4,2,128]{2,1,0:T(2,128)S(1)}, u32[]{:S(2)}, u32[]{:S(2)}) async-start(s32[4,2,128]{2,1,0:T(2,128)} %param.10), calls=%async_computation | async-start | bytes 8192 | tf_op jit(solution)/shard_map/all_to_all | solution.py:496
  104.2 8.1 %all-gather = f32[4,1,768]{2,1,0:T(1,128)S(1)} all-gather(f32[1,1,768]{2,1,0:T(1,128)S(1)} %bitcast.58), channel_id=1, replica_groups=mesh['section'=4,'row'=8] {'section'}, dimensions={0}, use_global_device_ids=true | all-gather | bytes 15360 | tf_op jit(solution)/shard_map/all_gather | solution.py:498
  112.4 2.4 fusion.refs_0_.refs_3_.refs_5_
  114.8 13.7 %layer_in_0.1 = (bf16[1024,768]{1,0:T(8,128)(2,1)}, bf16[1024,2304]{1,0:T(8,128)(2,1)}, f32[128,1536]{1,0:T(8,128)S(1)}) custom-call(s32[3]{0:T(128)S(1)} %add_add_fusion.info, f32[1024,768]{1,0:T(8,128)} %fusion.refs_0_.refs_3_.refs_5_, f32[1,768]{1,0:T(1,128)S(1)} %get-tuple-element.164.refs_1_.refs_6_, bf16[1,768,2304]{2,1,0:T(8,128)(2,1)} %refs_7_.3, ...), custom_call_target="tpu_custom_call" | custom-call | flops 6039797760 | bytes 10226688 | tf_op jit(solution)/shard_map/layer_in_0/pallas_call | solution.py:300
  128.6 5.2 %all-to-all-start.1 = ((bf16[4,2,128,768]{3,2,1,0:T(8,128)(2,1)}), bf16[4,2,128,768]{3,2,1,0:T(8,128)(2,1)}, u32[]{:S(2)}, u32[]{:S(2)}) async-start(bf16[4,2,128,768]{3,2,1,0:T(8,128)(2,1)} %param.15), calls=%async_computation.1 | async-start | bytes 3145728 | tf_op jit(solution)/shard_map/all_to_all | solution.py:497
  134.2 0.9 copy-done.7
  135.1 1.1 copy-done.8
  136.2 17.2 %layer_in_1.1 = (bf16[128,1536]{1,0:T(8,128)(2,1)S(1)}, bf16[1024,768]{1,0:T(8,128)(2,1)}, f32[1024,768]{1,0:T(8,128)}, bf16[1024,768]{1,0:T(8,128)(2,1)}, bf16[...) custom-call(s32[3]{0:T(128)S(1)} %add_add_fusion.1.info, f32[128,1536]{1,0:T(8,128)S(1)} %get-tuple-element.117.refs_0_, ...), custom_call_target="tpu_custom_call" | custom-call | flops 6039797760 | bytes 21629952 | tf_op jit(solution)/shard_map/layer_in_1/pallas_call | solution.py:300
  153.5 0.7 copy-done.9
  154.3 0.5 copy-done.13
  154.9 2.1 collective-permute-done.7.refs_1_
  157.1 17.2 %layer_in_2.1 = (bf16[128,1536]{1,0:T(8,128)(2,1)S(1)}, bf16[1024,768]{1,0:T(8,128)(2,1)}, f32[1024,768]{1,0:T(8,128)}, bf16[1024,768]{1,0:T(8,128)(2,1)}, bf16[...) custom-call(s32[3]{0:T(128)S(1)} %add_add_fusion.2.info, f32[128,1536]{1,0:T(8,128)S(1)} %get-tuple-element.119.refs_0_, ...), custom_call_target="tpu_custom_call" | custom-call | flops 6039797760 | bytes 21629952 | tf_op jit(solution)/shard_map/layer_in_2/pallas_call | solution.py:300
  174.3 0.7 copy-done.11
  175.3 2.1 collective-permute-done.8.refs_1_
  177.4 23.2 %layer_in_3.1 = (bf16[128,1536]{1,0:T(8,128)(2,1)S(1)}, bf16[1024,768]{1,0:T(8,128)(2,1)}, f32[1024,768]{1,0:T(8,128)}, bf16[1024,768]{1,0:T(8,128)(2,1)}, bf16[...) custom-call(s32[3]{0:T(128)S(1)} %add_add_fusion.3.info, ...), custom_call_target="tpu_custom_call" | custom-call | flops 6039797760 | bytes 25562112 | tf_op jit(solution)/shard_map/layer_in_3/pallas_call | solution.py:300
  200.8 3.3 collective-permute-done.9.refs_1_
  204.1 1.2 copy-done.19
  205.3 23.5 %layer_back_3.1 = (bf16[1024,2304]{1,0:T(8,128)(2,1)}, f32[1,768]{1,0:T(1,128)}, bf16[1024,768]{1,0:T(8,128)(2,1)}, f32[1024,768]{1,0:T(8,128)}, bf16[1024,768]{...) custom-call(s32[3]{0:T(128)S(1)} %add_add_fusion.3.info, ...), custom_call_target="tpu_custom_call" | custom-call | flops 6039797760 | bytes 32249856 | tf_op jit(solution)/shard_map/layer_back_3/pallas_call | solution.py:300
  228.8 1.2 copy-done.6
  230.1 2.1 collective-permute-done.10.refs_1_
  232.3 23.3 %layer_back_2.1 = (bf16[1024,2304]{1,0:T(8,128)(2,1)}, f32[1,768]{1,0:T(1,128)}, f32[1024,768]{1,0:T(8,128)}, bf16[1024,768]{1,0:T(8,128)(2,1)}, bf16[1024,768]{1,0:T(8,128)(2,1)S(1)}, /*index=5*/f32[128,1536]{1,0:T(8,128)S(1)}) custom-call(s32[3]{0:T(128)S(1)} %copy-done.16, f32[128,1536]{1,0:T(8,128)S(1)} %get-tuple-element.129.refs_0_, ...), custom_call_target="tpu_custom_call" | custom-call | flops 6039797760 | bytes 31070208 | tf_op jit(solution)/shard_map/layer_back_2/pallas_call | solution.py:300
  255.6 1.1 copy-done.5
  256.9 2.1 collective-permute-done.11.refs_1_
  259.1 22.5 %layer_back_1.1 = (bf16[1024,2304]{1,0:T(8,128)(2,1)}, f32[1,768]{1,0:T(1,128)}, f32[1024,768]{1,0:T(8,128)}, bf16[1024,768]{1,0:T(8,128)(2,1)}, bf16[1024,768]{1,0:T(8,128)(2,1)S(1)}, /*index=5*/f32[128,1536]{1,0:T(8,128)S(1)}) custom-call(s32[3]{0:T(128)S(1)} %copy-done.14, f32[128,1536]{1,0:T(8,128)S(1)} %get-tuple-element.133.refs_0_, ...), custom_call_target="tpu_custom_call" | custom-call | flops 6039797760 | bytes 31070208 | tf_op jit(solution)/shard_map/layer_back_1/pallas_call | solution.py:300
  281.8 2.3 collective-permute-done.12.refs_1_
  284.1 1.0 copy-done.10
  285.1 14.1 %layer_back_0.1 = (bf16[1024,2304]{1,0:T(8,128)(2,1)}, f32[1,768]{1,0:T(1,128)S(1)}) custom-call(s32[3]{0:T(128)S(1)} %copy-done.18, f32[128,1536]{1,0:T(8,128)S(1)} %get-tuple-element.137.refs_0_, f32[128,1536]{1,0:T(8,128)} %collective-permute-done.12.refs_1_, bf16[128,1536]{1,0:T(8,128)(2,1)S(1)} %copy-done.10, ...), custom_call_target="tpu_custom_call" | custom-call | flops 6039797760 | bytes 16128000 | tf_op jit(solution)/shard_map/layer_back_0/pallas_call | solution.py:300
  299.3 10.9 %conditional.2 = (bf16[768,2304]{1,0:T(8,128)(2,1)S(1)}, bf16[768,768]{1,0:T(8,128)(2,1)}, f32[1,768]{1,0:T(1,128)S(1)}) conditional(s32[]{:T(128)} %clamp.3, (bf16[1024,768]{1,0:T(8,128)(2,1)}, bf16[1024,2304]{1,0:T(8,128)(2,1)}, bf16[1024,768]{1,0:T(8,128)(2,1)S(1)}, bf16[1024,768]{1,0:T(8,128)(2,1)}, ...), branch_computations={%region_0.1_spmd, %region_1.2_spmd, %region_2.3_spmd, %region_3.4_... | conditional | flops 4831838208 | bytes 26744912
  299.4 6.8 %fusion.2 = bf16[768,2304]{1,0:T(8,128)(2,1)S(1)} fusion(bf16[1024,768]{1,0:T(8,128)(2,1)} %get-tuple-element.48, bf16[1024,2304]{1,0:T(8,128)(2,1)} %get-tuple-element.49), kind=kOutput, calls=%fused_computation.18 | convolution fusion | flops 3623878656 | bytes 9830400 | tf_op jit(solution)/shard_map/cond/branch_0_fun/dot_general | solution.py:548
  306.2 2.5 fusion.3
  310.2 0.9 copy.9
  311.2 4.0 pad_maximum_fusion
  315.3 29.3 %reduce-scatter.7.cloned.1.call-done = f32[96,1]{1,0:T(8,128)} async-done(((f32[768,1]{1,0:T(8,128)}), f32[96,1]{1,0:T(8,128)}) %reduce-scatter.7.cloned.1.call-update) | async-done | bytes 400
  344.6 1.4 copy.10
  345.9 54.1 %reduce-scatter.5.cloned.1.call-done = bf16[96,3072]{1,0:T(8,128)(2,1)} async-done(((bf16[768,3072]{1,0:T(8,128)(2,1)}), bf16[96,3072]{1,0:T(8,128)(2,1)}) %reduce-scatter.5.cloned.1.call-update) | async-done | bytes 589840 | tf_op jit(solution)/shard_map/reduce_scatter | solution.py:556
  400.1 1.2 convert_element_type.20
  401.3 0.7 slice_bitcast_fusion.1
  402.0 1.0 slice_bitcast_fusion
  (76 shorter events, 2.3 us)
Async XLA Ops:
  7.2 105.2 %copy-start = (bf16[33,768]{1,0:T(8,128)(2,1)S(1)}, bf16[33,768]{1,0:T(8,128)(2,1)}, u32[]{:S(2)}) copy-start(bf16[33,768]{1,0:T(8,128)(2,1)} %param.11) | copy-start | bytes 152068
  11.6 54.5 %collective-permute-start.2 = (bf16[384,3072]{1,0:T(8,128)(2,1)}, bf16[384,3072]{1,0:T(8,128)(2,1)}, u32[]{:S(2)}, u32[]{:S(2)}) collective-permute-start(bf16[384,3072]{1,0:T(8,128)(2,1)} %pad_maximum_fusion.1), channel_id=1, source_target_pairs={{0,16},{8,24},{16,0},{24,8},{1,17},{9,25},{17,1},{25,9},{2,18},{10... | collective-permute-start | bytes 7077896 | tf_op jit(solution)/shard_map/ppermute | solution.py:452
  14.6 52.9 %collective-permute-start = (bf16[384,3072]{1,0:T(8,128)(2,1)}, bf16[384,3072]{1,0:T(8,128)(2,1)S(1)}, u32[]{:S(2)}, u32[]{:S(2)}) collective-permute-start(bf16[384,3072]{1,0:T(8,128)(2,1)} %pad_maximum_fusion.1), channel_id=1, source_target_pairs={{0,8},{8,0},{16,24},{24,16},{1,9},{9,1},{17,25},{25,17},{2,10},{10... | collective-permute-start | bytes 7077896 | tf_op jit(solution)/shard_map/ppermute | solution.py:452
  16.1 88.1 %copy-start.23 = (f32[1,768]{1,0:T(1,128)S(1)}, f32[1,768]{1,0:T(1,128)}, u32[]{:S(2)}) copy-start(f32[1,768]{1,0:T(1,128)} %param.12) | copy-start | bytes 9220
  67.5 47.2 %copy-start.2 = (bf16[384,3072]{1,0:T(8,128)(2,1)}, bf16[384,3072]{1,0:T(8,128)(2,1)S(1)}, u32[]{:S(2)}) copy-start(bf16[384,3072]{1,0:T(8,128)(2,1)S(1)} %collective-permute-done) | copy-start | bytes 7077892
  70.3 29.0 %collective-permute-start.4 = (bf16[384,3072]{1,0:T(8,128)(2,1)S(1)}, bf16[384,3072]{1,0:T(8,128)(2,1)}, u32[]{:S(2)}, u32[]{:S(2)}) collective-permute-start(bf16[384,3072]{1,0:T(8,128)(2,1)S(1)} %broadcast_select_fusion), channel_id=1, source_target_pairs={{0,8},{1,17},{2,10},{3,19},{4,12},{5,21},{6,14},{7,23},{8,0},{9,25... | collective-permute-start | bytes 7077896 | tf_op jit(solution)/shard_map/ppermute | solution.py:462
  71.8 42.9 %collective-permute-start.3 = (bf16[1,384,3072]{2,1,0:T(8,128)(2,1)}, bf16[1,384,3072]{2,1,0:T(8,128)(2,1)}, u32[]{:S(2)}, u32[]{:S(2)}) collective-permute-start(bf16[1,384,3072]{2,1,0:T(8,128)(2,1)} %bitcast.8.refs_6_.refs_9_.refs_10_.refs_12_.refs_13_.refs_11_), channel_id=1, source_target_pairs={{0,1},{1,0},{2,3},{3,2},{4,5},{5,4},{6,7},{7,6},{8,9},{9,8},{10,11... | collective-permute-start | bytes 7077896 | tf_op jit(solution)/shard_map/ppermute | solution.py:469
  71.8 42.9 %collective-permute-start.1 = (bf16[1,384,3072]{2,1,0:T(8,128)(2,1)S(1)}, bf16[1,384,3072]{2,1,0:T(8,128)(2,1)}, u32[]{:S(2)}, u32[]{:S(2)}) collective-permute-start(bf16[1,384,3072]{2,1,0:T(8,128)(2,1)S(1)} %bitcast.46), channel_id=1, source_target_pairs={{0,1},{1,0},{2,3},{3,2},{4,5},{5,4},{6,7},{7,6},{8,9},{9,8},{10,11... | collective-permute-start | bytes 7077896 | tf_op jit(solution)/shard_map/ppermute | solution.py:469
  99.3 15.4 %collective-permute-start.5 = (bf16[1,384,3072]{2,1,0:T(8,128)(2,1)}, bf16[1,384,3072]{2,1,0:T(8,128)(2,1)}, u32[]{:S(2)}, u32[]{:S(2)}) collective-permute-start(bf16[1,384,3072]{2,1,0:T(8,128)(2,1)} %bitcast.9.refs_8_.refs_11_.refs_12_.refs_14_.refs_15_.refs_13_), channel_id=1, source_target_pairs={{0,1},{1,0},{2,3},{3,2},{4,5},{5,4},{6,7},{7,6},{8,9},{9,8},{10,11... | collective-permute-start | bytes 7077896 | tf_op jit(solution)/shard_map/ppermute | solution.py:469
  99.3 13.1 %all-to-all-start = ((s32[4,2,128]{2,1,0:T(2,128)}), s32[4,2,128]{2,1,0:T(2,128)S(1)}, u32[]{:S(2)}, u32[]{:S(2)}) async-start(s32[4,2,128]{2,1,0:T(2,128)} %param.10), calls=%async_computation | async-start | bytes 8192 | tf_op jit(solution)/shard_map/all_to_all | solution.py:496
  112.4 2.4 copy-start.17
  112.4 2.4 copy-start.3
  128.5 6.6 %copy-start.4 = (bf16[1,768,768]{2,1,0:T(8,128)(2,1)S(1)}, bf16[1,768,768]{2,1,0:T(8,128)(2,1)}, u32[]{:S(2)}) copy-start(bf16[1,768,768]{2,1,0:T(8,128)(2,1)} %refs_8_.3) | copy-start | bytes 3538948
  128.5 5.7 %collective-permute-start.6 = (f32[128,1536]{1,0:T(8,128)S(1)}, f32[128,1536]{1,0:T(8,128)S(1)}, u32[]{:S(2)}, u32[]{:S(2)}) collective-permute-start(f32[128,1536]{1,0:T(8,128)S(1)} %get-tuple-element.117.refs_0_), channel_id=1, source_target_pairs={{0,1},{1,0},{2,3},{3,2},{4,5},{5,4},{6,7},{7,6},{8,9},{9,8},{10,11... | collective-permute-start | bytes 2359304 | tf_op jit(solution)/shard_map/ppermute | solution.py:432
  128.6 46.7 %all-to-all-start.1 = ((bf16[4,2,128,768]{3,2,1,0:T(8,128)(2,1)}), bf16[4,2,128,768]{3,2,1,0:T(8,128)(2,1)}, u32[]{:S(2)}, u32[]{:S(2)}) async-start(bf16[4,2,128,768]{3,2,1,0:T(8,128)(2,1)} %param.15), calls=%async_computation.1 | async-start | bytes 3145728 | tf_op jit(solution)/shard_map/all_to_all | solution.py:497
  133.9 210.7 %reduce-scatter.7.cloned.1.call-start = ((), (), s32[]{:S(2)}) async-start(), calls=%async_computation.5 | async-start | bytes 442368
  134.2 0.9 copy-start.7
  135.1 1.1 copy-start.8
  153.5 0.8 copy-start.9
  154.3 0.5 copy-start.13
  154.8 2.3 collective-permute-start.7
  154.9 19.4 %copy-start.15 = (s32[3]{0:T(128)}, s32[3]{0:T(128)S(1)}, u32[]{:S(2)}) copy-start(s32[3]{0:T(128)S(1)} %add_add_fusion.2.info) | copy-start | bytes 40
  174.3 0.7 copy-start.11
  175.1 2.3 collective-permute-start.8
  200.6 3.5 collective-permute-start.9
  204.1 1.2 copy-start.19
  205.3 27.0 %copy-start.16 = (s32[3]{0:T(128)S(1)}, s32[3]{0:T(128)}, u32[]{:S(2)}) copy-start(s32[3]{0:T(128)} %copy-done.15) | copy-start | bytes 40
  228.8 1.2 copy-start.6
  230.0 2.3 collective-permute-start.10
  232.3 26.8 %copy-start.12 = (bf16[128,1536]{1,0:T(8,128)(2,1)S(1)}, bf16[128,1536]{1,0:T(8,128)(2,1)}, u32[]{:S(2)}) copy-start(bf16[128,1536]{1,0:T(8,128)(2,1)} %copy-done.11) | copy-start | bytes 1179652
  232.3 26.8 %copy-start.14 = (s32[3]{0:T(128)S(1)}, s32[3]{0:T(128)}, u32[]{:S(2)}) copy-start(s32[3]{0:T(128)} %copy-done.13) | copy-start | bytes 40
  255.6 1.1 copy-start.5
  256.8 2.3 collective-permute-start.11
  259.1 25.0 %copy-start.18 = (s32[3]{0:T(128)S(1)}, s32[3]{0:T(128)}, u32[]{:S(2)}) copy-start(s32[3]{0:T(128)} %copy-done.17) | copy-start | bytes 40
  281.6 2.5 collective-permute-start.12
  284.1 1.0 copy-start.10
  285.1 14.2 %copy-start.20 = (f32[1,768]{1,0:T(1,128)S(1)}, f32[1,768]{1,0:T(1,128)}, u32[]{:S(2)}) copy-start(f32[1,768]{1,0:T(1,128)} %get-tuple-element.157) | copy-start | bytes 9220
  285.1 14.2 %copy-start.21 = (f32[1,768]{1,0:T(1,128)S(1)}, f32[1,768]{1,0:T(1,128)}, u32[]{:S(2)}) copy-start(f32[1,768]{1,0:T(1,128)} %get-tuple-element.153) | copy-start | bytes 9220
  285.1 14.2 %copy-start.22 = (f32[1,768]{1,0:T(1,128)S(1)}, f32[1,768]{1,0:T(1,128)}, u32[]{:S(2)}) copy-start(f32[1,768]{1,0:T(1,128)} %get-tuple-element.148) | copy-start | bytes 9220
  285.1 14.2 %copy-start.24 = (bf16[1024,2304]{1,0:T(8,128)(2,1)S(1)}, bf16[1024,2304]{1,0:T(8,128)(2,1)}, u32[]{:S(2)}) copy-start(bf16[1024,2304]{1,0:T(8,128)(2,1)} %get-tuple-element.155) | copy-start | bytes 14155780
  285.1 14.2 %copy-start.25 = (bf16[1024,768]{1,0:T(8,128)(2,1)S(1)}, bf16[1024,768]{1,0:T(8,128)(2,1)}, u32[]{:S(2)}) copy-start(bf16[1024,768]{1,0:T(8,128)(2,1)} %get-tuple-element.141) | copy-start | bytes 4718596
  285.1 14.2 %copy-start.26 = (bf16[1024,768]{1,0:T(8,128)(2,1)S(1)}, bf16[1024,768]{1,0:T(8,128)(2,1)}, u32[]{:S(2)}) copy-start(bf16[1024,768]{1,0:T(8,128)(2,1)} %get-tuple-element.144) | copy-start | bytes 4718596
  285.1 14.2 %copy-start.27 = (bf16[1024,768]{1,0:T(8,128)(2,1)S(1)}, bf16[1024,768]{1,0:T(8,128)(2,1)}, u32[]{:S(2)}) copy-start(bf16[1024,768]{1,0:T(8,128)(2,1)} %get-tuple-element.146) | copy-start | bytes 4718596
  285.1 14.2 %copy-start.28 = (bf16[1024,768]{1,0:T(8,128)(2,1)S(1)}, bf16[1024,768]{1,0:T(8,128)(2,1)}, u32[]{:S(2)}) copy-start(bf16[1024,768]{1,0:T(8,128)(2,1)} %get-tuple-element.149) | copy-start | bytes 4718596
  299.3 6.8 %copy-start.33 = (bf16[1024,768]{1,0:T(8,128)(2,1)S(1)}, bf16[1024,768]{1,0:T(8,128)(2,1)}, u32[]{:S(2)}) copy-start(bf16[1024,768]{1,0:T(8,128)(2,1)} %get-tuple-element.51) | copy-start | bytes 4718596 | tf_op jit(solution)/shard_map/conditional
  311.2 88.9 %reduce-scatter.5.cloned.1.call-start = ((), (), s32[]{:S(2)}) async-start(), calls=%async_computation.4 | async-start | bytes 5308416 | tf_op jit(solution)/shard_map/reduce_scatter | solution.py:556
  400.1 2.9 copy-start.1
Sparse Core Ops, SparseCore 0:
  311.3 33.1 reduce-scatter.6
  347.0 53.0 reduce-scatter.4

commit v2 on v1

v2 whole, which is shorter than its diff:
```python
import functools
import math

import jax
import jax.numpy as jnp
from jax import lax
from jax.experimental import pallas as pl
from jax.experimental.pallas import tpu as pltpu
from jax.sharding import PartitionSpec as P

HEADS = 12
HEAD_DIM = 64
PACK = 2
F32 = jnp.float32
BF16 = jnp.bfloat16
VMEM_LIMIT = 48 * 1024 * 1024
NT = (((1,), (1,)), ((), ()))
TN = (((0,), (0,)), ((), ()))


def mm(a, b):
    return jnp.dot(a, b, preferred_element_type=F32)


def mm_nt(a, b):
    return lax.dot_general(a, b, NT, preferred_element_type=F32)


def head_lanes(ref, seq, head):
    width = PACK * HEAD_DIM
    first = head * width
    return jnp.concatenate(
        [ref[r * seq : (r + 1) * seq, first : first + width] for r in range(ref.shape[0] // seq)],
        axis=1,
    )


def regroup(blocks):
    return [
        jnp.concatenate([block[:, n * HEAD_DIM : (n + 1) * HEAD_DIM] for block in blocks], axis=1)
        for n in range(PACK)
    ]


def pack_rows(value, out, first, seq):
    width = PACK * HEAD_DIM
    for pair in range(value.shape[0] // seq // PACK):
        for p in range(value.shape[1] // width):
            blocks = [
                value[(pair * PACK + r) * seq : (pair * PACK + r + 1) * seq, p * width : (p + 1) * width]
                for r in range(PACK)
            ]
            for n, block in enumerate(regroup(blocks)):
                at = (first + p * PACK + n) * width
                out[pair * seq : (pair + 1) * seq, at : at + width] = block


class Weights:
    def __init__(self, choices, member, own, stages, columns, dst, sems):
        self.choices, self.member, self.own, self.stages = choices, member, own, stages
        self.columns, self.dst, self.sems = columns, dst, sems

    def each(self, act):
        @pl.when(self.choices[0] == 0)
        def _():
            act(pltpu.make_async_copy(self.own.at[0], self.dst, self.sems.at[0]))

        for stage, group in enumerate(self.stages):
            for parity in range(min(2, self.sems.shape[0])):

                @pl.when(self.choices[parity] == stage + 1)
                def _(group=group, parity=parity):
                    seen = 0
                    for ref in group:
                        rows = ref.shape[1]
                        for n in range(ref.shape[0]):
                            if seen % 2 == parity:
                                start = pl.multiple_of((self.member ^ seen) * rows, rows)
                                act(
                                    pltpu.make_async_copy(
                                        ref.at[n, :, self.columns],
                                        self.dst.at[pl.ds(start, rows)],
                                        self.sems.at[seen],
                                    )
                                )
                            seen += 1

    def start(self):
        self.each(lambda copy: copy.start())

    def wait(self):
        self.each(lambda copy: copy.wait())


def take_stages(it, layout):
    return [[next(it) for _ in range(count)] for count in layout]


def softmax_heads(la, lb, scale, keep):
    seq = la.shape[0]
    for h in range(HEADS):
        at = slice(h * seq, (h + 1) * seq)
        logits = (la[:, at] + lb[:, at]) * scale
        e = jnp.exp(logits - jnp.max(logits, axis=-1, keepdims=True))
        keep(h, e / jnp.sum(e, axis=-1, keepdims=True))


def norm_parts(x):
    centred = x - jnp.mean(x, axis=-1, keepdims=True)
    spread = jnp.mean(centred * centred, axis=-1, keepdims=True)
    rstd = lax.rsqrt(spread + 1e-05)
    return centred * rstd, rstd


def scores(ref_a, first_a, ref_b, first_b, out, out_row, seq, begin):
    parts = [
        mm_nt(head_lanes(ref_a, seq, first_a + h), head_lanes(ref_b, seq, first_b + h))
        for h in range(HEADS)
    ]
    rows = slice(out_row, out_row + seq)

    @pl.when(begin)
    def _():
        for h, part in enumerate(parts):
            out[rows, h * seq : (h + 1) * seq] = part

    @pl.when(jnp.logical_not(begin))
    def _():
        for h, part in enumerate(parts):
            out[rows, h * seq : (h + 1) * seq] += part


def mix(weights, ref_b, first_b, out, first_out, scale, seq):
    width = PACK * HEAD_DIM
    for p in range(HEADS // PACK):
        values = []
        for h in range(p * PACK, (p + 1) * PACK):
            value = mm(weights[:, h * seq : (h + 1) * seq], head_lanes(ref_b, seq, first_b + h))
            values.append((value if scale is None else value * scale).astype(BF16))
        at = first_out + p * width
        for pair in range(ref_b.shape[0] // seq):
            blocks = [value[:, pair * width : (pair + 1) * width] for value in values]
            for n, block in enumerate(regroup(blocks)):
                row = (pair * PACK + n) * seq
                out[row : row + seq, at : at + width] = block


def forward_kernel(has_prev, has_top, info, *refs, layout, scale, seq, width):
    it = iter(refs)
    if has_prev:
        la, lb, v_prev = next(it), next(it), next(it)
    x_in, gain = next(it), next(it)
    top = next(it) if has_top else None
    own_q, own_o = next(it), next(it)
    stages = take_stages(it, layout)
    if has_prev:
        probs_out, mixed_out, x_out = next(it), next(it), next(it)
    h_out, qkv_out, score_out = next(it), next(it), next(it)
    if has_top:
        dmix_out = next(it)
    wq, sem_q = next(it), next(it)
    if has_prev:
        wo, sem_o = next(it), next(it)
    if has_top:
        wt, sem_t = next(it), next(it)
    step = pl.program_id(0)
    qcols, ocols = slice(0, 3 * width), slice(3 * width, 4 * width)
    now, before = (info[0], info[1]), (info[2], info[3])
    get_q = Weights(now, info[4], own_q, stages, qcols, wq, sem_q)
    if has_prev:
        get_o = Weights(before, info[4], own_o, stages, ocols, wo, sem_o)
    if has_top:
        get_t = Weights(now, info[4], own_o, stages, ocols, wt, sem_t)

    @pl.when(step == 0)
    def _():
        if has_prev:
            get_o.start()
        get_q.start()
        if has_top:
            get_t.start()
        if has_prev:

            def keep(h, value):
                probs_out[:, h * seq : (h + 1) * seq] = value.astype(BF16)

            softmax_heads(la, lb, scale, keep)

    if has_prev:
        mix(probs_out, v_prev, 0, mixed_out, 0, None, seq)
        pl.when(step == 0)(get_o.wait)
        x = x_in[...] + mm(mixed_out[...], wo[...])
        x_out[...] = x
    else:
        x = x_in[...]
    hat, _ = norm_parts(x)
    h = (hat * gain[...]).astype(BF16)
    h_out[...] = h
    pl.when(step == 0)(get_q.wait)
    for t in range(3):
        part = mm(h_out[...], wq[:, t * width : (t + 1) * width]).astype(BF16)
        pack_rows(part, qkv_out, t * HEADS, seq)
    begin = step == 0
    scores(qkv_out, 0, qkv_out, HEADS, score_out, 0, seq, begin)
    if has_top:
        pl.when(step == 0)(get_t.wait)
        pack_rows(mm_nt(top[...], wt[...]).astype(BF16), dmix_out, 0, seq)
        scores(dmix_out, 0, qkv_out, 2 * HEADS, score_out, seq, seq, begin)


def backward_kernel(is_top, is_last, info, *refs, layout, scale, seq, width):
    it = iter(refs)
    sa, sb = next(it), next(it)
    if not is_top:
        probs = next(it)
    qkv, dmix = next(it), next(it)
    if not is_last:
        x_in, gain, dy, v_prev = next(it), next(it), next(it), next(it)
    own_q, own_o = next(it), next(it)
    stages = take_stages(it, layout)
    dqkv_out = next(it)
    if is_top:
        mixed_out = next(it)
    if not is_last:
        gain_out = next(it)
        dy_out, dyb_out, dmix_out, score_out = next(it), next(it), next(it), next(it)
    dl, dlt, pt = next(it), next(it), next(it)
    if is_top:
        probs = next(it)
    step = pl.program_id(0)
    if not is_last:
        wq, sem_q, wo, sem_o = next(it), next(it), next(it), next(it)
        qcols, ocols = slice(0, 3 * width), slice(3 * width, 4 * width)
        get_q = Weights((info[0], info[1]), info[4], own_q, stages, qcols, wq, sem_q)
        get_o = Weights((info[2], info[3]), info[4], own_o, stages, ocols, wo, sem_o)

    @pl.when(step == 0)
    def _():
        if not is_last:
            get_q.start()
            get_o.start()
        if is_top:

            def keep(h, value):
                probs[:, h * seq : (h + 1) * seq] = value.astype(BF16)

            softmax_heads(sa.at[0:seq], sb.at[0:seq], scale, keep)
        first = seq if is_top else 0
        for h in range(HEADS):
            at = slice(h * seq, (h + 1) * seq)
            prob = probs[:, at].astype(F32)
            d_prob = sa[first : first + seq, at] + sb[first : first + seq, at]
            d_logit = prob * (d_prob - jnp.sum(d_prob * prob, axis=-1, keepdims=True))
            dl[:, at] = d_logit.astype(BF16)
            dlt[:, at] = jnp.transpose(d_logit).astype(BF16)
            pt[:, at] = jnp.transpose(prob).astype(BF16)

    if is_top:
        mix(probs, qkv, 2 * HEADS, mixed_out, 0, None, seq)
    mix(dl, qkv, HEADS, dqkv_out, 0, scale, seq)
    mix(dlt, qkv, 0, dqkv_out, width, scale, seq)
    mix(pt, dmix, 0, dqkv_out, 2 * width, None, seq)
    if not is_last:
        pl.when(step == 0)(get_q.wait)
        d_h = mm_nt(dqkv_out[...], wq[...]).astype(BF16).astype(F32)
        hat, rstd = norm_parts(x_in[...])
        add_gain(gain_out, d_h, hat, step)
        d_hat = d_h * gain[...]
        mean_d = jnp.mean(d_hat, axis=-1, keepdims=True)
        mean_dh = jnp.mean(d_hat * hat, axis=-1, keepdims=True)
        d_x = dy[...].astype(F32) + rstd * (d_hat - mean_d - hat * mean_dh)
        dy_out[...] = d_x
        dyb_out[...] = d_x.astype(BF16)
        pl.when(step == 0)(get_o.wait)
        pack_rows(mm_nt(dyb_out[...], wo[...]).astype(BF16), dmix_out, 0, seq)
        scores(dmix_out, 0, v_prev, 0, score_out, 0, seq, step == 0)


def add_gain(gain_out, d_h, hat, step):
    part = jnp.sum(d_h * hat, axis=0, keepdims=True)

    @pl.when(step == 0)
    def _():
        gain_out[...] = part

    @pl.when(step > 0)
    def _():
        gain_out[...] += part


def gain_kernel(info, *refs, layout, width):
    it = iter(refs)
    dqkv, x_in, own_q, _ = next(it), next(it), next(it), next(it)
    stages = take_stages(it, layout)
    gain_out, wq, sem_q = next(it), next(it), next(it)
    step = pl.program_id(0)
    get_q = Weights(
        (info[0], info[1]), info[4], own_q, stages, slice(0, 3 * width), wq, sem_q
    )
    pl.when(step == 0)(get_q.start)
    hat, _ = norm_parts(x_in[...])
    pl.when(step == 0)(get_q.wait)
    d_h = mm_nt(dqkv[...], wq[...]).astype(BF16).astype(F32)
    add_gain(gain_out, d_h, hat, step)


class Chain:
    def __init__(self, fetched, member, n_group, own, seq, width, rows, scale):
        self.fetched, self.member, self.n_group = fetched, member, n_group
        self.own, self.seq, self.width, self.rows = own, seq, width, rows
        self.scale = scale
        per_step = 4 if rows % 4 == 0 else 2
        self.chunk = per_step * seq
        self.steps = rows // per_step

    def info(self, now, other):
        picks = self.fetched.choices(now) + self.fetched.choices(other) + [self.member]
        return jnp.stack(picks).astype(jnp.int32)

    def whole(self, rows, lanes):
        return pl.BlockSpec((rows, lanes), lambda i, s: (0, 0))

    def tile(self, lanes, column=0, part=1):
        return pl.BlockSpec((self.chunk // part, lanes), lambda i, s: (i, column))

    def packed(self, heads, column=0):
        return self.tile(heads * PACK * HEAD_DIM, column, PACK)

    def call(self, make_body, name, info, stages, ins, in_specs, outs, out_specs, scratch, flops):
        size = sum(math.prod(o.shape) * o.dtype.itemsize for o in outs)
        size += sum(math.prod(a.shape) * a.dtype.itemsize for a in ins)
        any_spec = pl.BlockSpec(memory_space=pl.ANY)
        groups = self.fetched.stages[:stages]
        weights = [*self.own] + [a for group in groups for a in group]
        return pl.pallas_call(
            make_body(layout=tuple(len(group) for group in groups)),
            name=name,
            out_shape=outs,
            grid_spec=pltpu.PrefetchScalarGridSpec(
                num_scalar_prefetch=1,
                grid=(self.steps,),
                in_specs=in_specs + [any_spec] * len(weights),
                out_specs=out_specs,
                scratch_shapes=scratch,
            ),
            compiler_params=pltpu.CompilerParams(
                dimension_semantics=("arbitrary",), vmem_limit_bytes=VMEM_LIMIT
            ),
            cost_estimate=pl.CostEstimate(flops=flops, bytes_accessed=size, transcendentals=0),
        )(info, *ins, *weights)

    def weight_scratch(self, columns):
        return [
            pltpu.VMEM((self.width, columns * self.width), BF16),
            pltpu.SemaphoreType.DMA((self.n_group,)),
        ]

    def forward(self, layer, x, gain, prev, top):
        seq, width = self.seq, self.width
        n = self.rows * seq
        hw = HEADS * seq
        ins, in_specs, outs, out_specs = [], [], [], []
        if prev is not None:
            ins += [prev[0], prev[1], prev[2]]
            in_specs += [self.whole(seq, hw), self.whole(seq, hw), self.packed(HEADS, 2)]
            outs += [
                jax.ShapeDtypeStruct((seq, hw), BF16),
                jax.ShapeDtypeStruct((n, width), BF16),
                jax.ShapeDtypeStruct((n, width), F32),
            ]
            out_specs += [self.whole(seq, hw), self.tile(width), self.tile(width)]
        ins += [x, gain]
        in_specs += [self.tile(width), self.whole(1, width)]
        score_rows = seq
        if top is not None:
            ins.append(top)
            in_specs.append(self.tile(width))
            score_rows = 2 * seq
        outs += [
            jax.ShapeDtypeStruct((n, width), BF16),
            jax.ShapeDtypeStruct((n // PACK, 3 * PACK * width), BF16),
            jax.ShapeDtypeStruct((score_rows, hw), F32),
        ]
        out_specs += [self.tile(width), self.packed(3 * HEADS), self.whole(score_rows, hw)]
        scratch = self.weight_scratch(3)
        if prev is not None:
            scratch += self.weight_scratch(1)
        if top is not None:
            outs.append(jax.ShapeDtypeStruct((n // PACK, PACK * width), BF16))
            out_specs.append(self.packed(HEADS))
            scratch += self.weight_scratch(1)
        body = functools.partial(
            functools.partial,
            forward_kernel,
            prev is not None,
            top is not None,
            scale=self.scale,
            seq=seq,
            width=width,
        )
        return self.call(
            body,
            f"layer_in_{layer}",
            self.info(layer, max(layer - 1, 0)),
            self.fetched.first_stages if layer == 0 else None,
            ins,
            in_specs,
            outs,
            out_specs,
            scratch,
            2 * n * width * width * 5,
        )

    def backward(self, layer, scores, probs, qkv, dmix, x, gain, dy, v_prev):
        seq, width = self.seq, self.width
        n = self.rows * seq
        hw = HEADS * seq
        is_top, is_last = probs is None, layer == 0
        score_rows = scores[0].shape[0]
        ins = [scores[0], scores[1]]
        in_specs = [self.whole(score_rows, hw)] * 2
        if not is_top:
            ins.append(probs)
            in_specs.append(self.whole(seq, hw))
        ins += [qkv, dmix]
        in_specs += [self.packed(3 * HEADS), self.packed(HEADS)]
        outs = [jax.ShapeDtypeStruct((n, 3 * width), BF16)]
        out_specs = [self.tile(3 * width)]
        scratch = [pltpu.VMEM((seq, hw), BF16)] * 3
        if is_top:
            outs.append(jax.ShapeDtypeStruct((n, width), BF16))
            out_specs.append(self.tile(width))
            scratch.append(pltpu.VMEM((seq, hw), BF16))
        if not is_last:
            ins += [x, gain, dy, v_prev]
            in_specs += [self.tile(width), self.whole(1, width)]
            in_specs += [self.tile(width), self.packed(HEADS, 2)]
            outs += [
                jax.ShapeDtypeStruct((1, width), F32),
                jax.ShapeDtypeStruct((n, width), F32),
                jax.ShapeDtypeStruct((n, width), BF16),
                jax.ShapeDtypeStruct((n // PACK, PACK * width), BF16),
                jax.ShapeDtypeStruct((seq, hw), F32),
            ]
            out_specs += [self.whole(1, width)] + [self.tile(width)] * 2
            out_specs += [self.packed(HEADS), self.whole(seq, hw)]
            scratch = scratch + self.weight_scratch(3) + self.weight_scratch(1)
        body = functools.partial(
            functools.partial,
            backward_kernel,
            is_top,
            is_last,
            scale=self.scale,
            seq=seq,
            width=width,
        )
        return self.call(
            body,
            f"layer_back_{layer}",
            self.info(layer, max(layer - 1, 0)),
            0 if is_last else None,
            ins,
            in_specs,
            outs,
            out_specs,
            scratch,
            2 * n * width * width * 5,
        )

    def gain_grad(self, layer, dqkv, x):
        width = self.width
        n = self.rows * self.seq
        return self.call(
            functools.partial(functools.partial, gain_kernel, width=width),
            f"gain_back_{layer}",
            self.info(layer, layer),
            None,
            [dqkv, x],
            [self.tile(3 * width), self.tile(width)],
            [jax.ShapeDtypeStruct((1, width), F32)],
            [self.whole(1, width)],
            self.weight_scratch(3),
            2 * n * width * width * 3,
        )[0]


def group_swap(value, n_row, n_group):
    other = jnp.zeros_like(value)
    bit = 1
    while bit < n_group:
        if bit > 1:
            value = value + other
        other = lax.ppermute(value, "row", [(r, r ^ bit) for r in range(n_row)])
        bit *= 2
    return value, other


class Fetched:
    first_stages = 2

    def __init__(self, wqkv, wout, section, n_section, n_row, n_group, member):
        assert n_section == 4
        self.section, self.n_row, self.n_group, self.member = section, n_row, n_group, member
        self.last = n_section - 1
        part = wqkv.shape[0] // n_group
        self.mine = jnp.concatenate(
            [
                lax.dynamic_slice_in_dim(wqkv, member * part, part, 0),
                lax.dynamic_slice_in_dim(wout, member * part, part, 0),
            ],
            axis=1,
        )
        even = member % 2 == 0
        self.to_last = section == (self.last ^ jnp.where(even, 2, 1))
        self.got = self.hop(self.mine, 1)
        self.stages = [self.share(self.got)]

    def hop(self, value, even_bit):
        perm = [
            (s * self.n_row + r, (s ^ (even_bit if r % 2 == 0 else 3 - even_bit)) * self.n_row + r)
            for s in range(self.last + 1)
            for r in range(self.n_row)
        ]
        return lax.ppermute(value, ("section", "row"), perm)

    def finish(self, *ready):
        second, *ready = lax.optimization_barrier(
            (jnp.where(self.to_last, self.got, self.mine), *ready)
        )
        second = self.hop(second, 2)
        third, second = lax.optimization_barrier(
            (jnp.where(self.to_last, self.mine, self.got), second)
        )
        third = self.hop(third, 2)
        self.stages += [self.share(second), self.share(third)]
        return ready

    def share(self, value):
        have = [value[None]]
        bit = 1
        while bit < self.n_group:
            send = have[0] if len(have) == 1 else jnp.concatenate(have, axis=0)
            have.append(lax.ppermute(send, "row", [(r, r ^ bit) for r in range(self.n_row)]))
            bit *= 2
        return have

    def choices(self, layer):
        offset = self.section ^ layer
        at_last = self.section == self.last
        picks = []
        for parity in (self.member % 2, 1 - self.member % 2):
            first = jnp.where(parity == 0, 1, 2)
            second = jnp.where(at_last, 3, 3 - first)
            pick = jnp.where(offset == first, 1, jnp.where(offset == second, 2, 3))
            picks.append(jnp.where(offset == 0, 0, pick))
        return picks


def local(tokens, embed, ln_gain, w_qkv, w_out, out_grad):
    n_section = lax.axis_size("section")
    n_row = lax.axis_size("row")
    section = lax.axis_index("section")
    place = lax.axis_index("row")
    micro, rows_here, seq = tokens.shape
    width = embed.shape[1]
    n_group = n_row // micro
    member = place % n_group
    rows = rows_here * micro
    scale = HEAD_DIM ** (-0.5) / math.sqrt(rows_here * n_row)
    fetched = Fetched(w_qkv[0], w_out[0], section, n_section, n_row, n_group, member)
    same = [[m * n_group + g for m in range(micro)] for g in range(n_group)]
    exchange = functools.partial(
        lax.all_to_all,
        axis_name="row",
        split_axis=0,
        concat_axis=0,
        axis_index_groups=same,
        tiled=True,
    )
    tok = exchange(tokens).reshape(-1)
    top_grad = exchange(out_grad).reshape(rows * seq, width)
    gains = lax.all_gather(ln_gain[0], "section", axis=0, tiled=False)
    table = (jnp.arange(embed.shape[0], dtype=jnp.int32)[:, None] == tok[None, :]).astype(BF16)
    x = lax.dot_general(table, embed, TN, preferred_element_type=F32)

    x, gains = fetched.finish(x, gains)
    chain = Chain(fetched, member, n_group, (w_qkv, w_out), seq, width, rows, scale)
    xs, hs, qkvs, probs, mixed = [], [], [], [], []
    scores = None
    dmix = None
    for layer in range(n_section):
        gain = gains[layer][None]
        prev = None if layer == 0 else (scores[0], scores[1], qkvs[-1])
        top = top_grad if layer == n_section - 1 else None
        outs = list(chain.forward(layer, x, gain, prev, top))
        if prev is not None:
            probs.append(outs.pop(0))
            mixed.append(outs.pop(0))
            x = outs.pop(0)
        if top is not None:
            dmix = outs.pop()
        xs.append(x)
        hs.append(outs[0])
        qkvs.append(outs[1])
        scores = group_swap(outs[2], n_row, n_group)
    probs.append(None)
    mixed.append(None)

    dy = top_grad
    ups = [None] * n_section
    dqkvs = [None] * n_section
    gain_parts = [None] * n_section
    ups[-1] = top_grad
    for layer in reversed(range(n_section)):
        v_prev = qkvs[layer - 1] if layer > 0 else None
        outs = list(
            chain.backward(
                layer, scores, probs[layer], qkvs[layer], dmix, xs[layer], gains[layer][None], dy, v_prev
            )
        )
        dqkvs[layer] = outs.pop(0)
        if probs[layer] is None:
            mixed[layer] = outs.pop(0)
        if layer > 0:
            gain_parts[layer], dy, ups[layer - 1], dmix, part = outs
            scores = group_swap(part, n_row, n_group)

    def own_grads(layer):
        def run():
            g_qkv = lax.dot_general(hs[layer], dqkvs[layer], TN, preferred_element_type=F32)
            g_out = lax.dot_general(mixed[layer], ups[layer], TN, preferred_element_type=F32)
            return jnp.concatenate([g_qkv.astype(BF16), g_out.astype(BF16)], axis=1)

        return run

    g_all = lax.switch(section, [own_grads(n) for n in range(n_section)])
    g_all = lax.psum_scatter(g_all, "row", scatter_dimension=0, tiled=True).astype(F32)
    gain_parts[0] = chain.gain_grad(0, dqkvs[0], xs[0])
    g_gain = lax.select_n(section, *gain_parts)
    bit = 1
    while bit < n_row:
        g_gain = g_gain + lax.ppermute(g_gain, "row", [(r, r ^ bit) for r in range(n_row)])
        bit *= 2
    g_gain = lax.dynamic_slice_in_dim(g_gain, place * (width // n_row), width // n_row, 1)
    return (g_all[None, :, : 3 * width], g_all[None, :, 3 * width :], g_gain)


def solution(mesh):
    in_specs = (
        P(None, "row", None),
        P(),
        P("section", None),
        P("section", None, None),
        P("section", None, None),
        P(None, "row", None, None),
    )
    out_specs = (P("section", "row", None), P("section", "row", None), P("section", "row"))
    return jax.shard_map(local, mesh=mesh, in_specs=in_specs, out_specs=out_specs, check_vma=False)
```

time: 415 us -> 361 us (0.87)
  waiting for transfers between devices: 176 us -> 109 us
  Pallas kernels: 155 us -> 137 us
  blocking collectives: 8.11 us -> 25.8 us
  loops' own time: 1.57 us -> 9.74 us
  starting transfers between devices: 17.9 us -> 22.6 us
    unnamed x3 -> x1, waiting for transfers between devices: 29.3 us -> 0.02 us
    ppermute x6 -> x9, waiting for transfers between devices: 78.4 us -> 59.3 us  [the longest x3 54.3 us: hop(): return lax.ppermute(value, ('section', 'row'), perm)]
    pallas_call x8 -> x9, Pallas kernels: 155 us -> 137 us  [call(): pl.pallas_call(make_body(layout=tuple((len(group) for group in groups))),...]
    reduce_scatter x1, waiting for transfers between devices: 54.1 us -> 35.9 us  [local(): lax.psum_scatter(g_all, 'row', scatter_dimension=0, tiled=True).astype(F32)]
    all_gather x1, blocking collectives: 8.11 us -> 25.8 us  [local(): gains = lax.all_gather(ln_gain[0], 'section', axis=0, tiled=False)]
    another operation x0 -> x1, loops' own time: none -> 9.74 us  [local(): g_all = lax.switch(section, [own_grads(n) for n in range(n_section)])]
    ppermute x6 -> x9, starting transfers between devices: 6.53 us -> 11.5 us  [the longest x3 6.04 us: hop(): return lax.ppermute(value, ('section', 'row'), perm)]
    unnamed x60 -> x59, local copies, waits for them, and re-layouts: 10.9 us -> 14.9 us
  transfers between devices with their start and end apart: 17 -> 19, of which waited for: 11 -> 13; matrix products, arithmetic and copies ran while one was open for 2% -> 1% of each run, Pallas kernels for 8% -> 14%
where the time goes in v2:
time: 361 us; the launch traced here: 356 us
  Pallas kernels  137 us (38%)
  waiting for transfers between devices  109 us (30%)
  blocking collectives  25.8 us (7%)
  starting transfers between devices  22.6 us (6%)
  local copies, waits for them, and re-layouts  19.2 us (5%)
  between operations  14.9 us (4%)
  matrix products  10.5 us (3%)
  loops' own time  9.74 us (3%)
  other arithmetic  7.68 us (2%)
    pallas_call x9, Pallas kernels, call(): pl.pallas_call(make_body(layout=tuple((len(group) for group in groups))),...  137 us
    ppermute x3, waiting for transfers between devices, hop(): return lax.ppermute(value, ('section', 'row'), perm)  54.3 us
    reduce_scatter x1, waiting for transfers between devices, local(): lax.psum_scatter(g_all, 'row', scatter_dimension=0, tiled=True).astype(F32)  35.9 us
    all_gather x1, blocking collectives, local(): gains = lax.all_gather(ln_gain[0], 'section', axis=0, tiled=False)  25.8 us
    unnamed x59, local copies, waits for them, and re-layouts  14.9 us
    ppermute x7, waiting for transfers between devices, group_swap(): other = lax.ppermute(value, 'row', [(r, r ^ bit) for r in range(n_row)])  13.4 us
    another operation x1, loops' own time, local(): g_all = lax.switch(section, [own_grads(n) for n in range(n_section)])  9.74 us
  transfers between devices with their start and end apart: 19, of which 13 were waited for; matrix products, arithmetic and copies ran while one was open for 1% of the time, Pallas kernels for 14%

profile of v2, /device:TPU:0, one launch (start us, length us, event | category | flops | bytes accessed | tf_op | source)
XLA Modules:
  0.0 355.9 jit_solution(549395727994023042)
XLA Ops:
  7.2 1.7 dynamic-slice_bitcast_fusion
  9.1 2.0 pad_maximum_fusion.4
  11.0 2.9 collective-permute-start
  14.0 4.9 %all-to-all-start = ((s32[4,2,128]{2,1,0:T(2,128)}), s32[4,2,128]{2,1,0:T(2,128)S(1)}, u32[]{:S(2)}, u32[]{:S(2)}) async-start(s32[4,2,128]{2,1,0:T(2,128)} %param.10), calls=%async_computation | async-start | bytes 8192 | tf_op jit(solution)/shard_map/all_to_all | solution.py:580
  18.8 25.8 %all-gather = f32[4,1,768]{2,1,0:T(1,128)S(1)} all-gather(f32[1,1,768]{2,1,0:T(1,128)S(1)} %bitcast.54), channel_id=1, replica_groups=mesh['section'=4,'row'=8] {'section'}, dimensions={0}, use_global_device_ids=true | all-gather | bytes 15360 | tf_op jit(solution)/shard_map/all_gather | solution.py:582
  44.7 2.4 fusion.refs_0_.refs_3_.refs_1_
  47.1 1.1 broadcast_select_fusion
  48.2 1.6 collective-permute-start.2
  49.8 27.4 %collective-permute-done.2 = bf16[384,3072]{1,0:T(8,128)(2,1)} collective-permute-done((bf16[384,3072]{1,0:T(8,128)(2,1)S(1)}, bf16[384,3072]{1,0:T(8,128)(2,1)}, u32[]{:S(2)}, u32[]{:S(2)}) %collective-permute-start.2) | collective-permute-done | bytes 2359328 | tf_op jit(solution)/shard_map/ppermute | solution.py:524
  77.3 1.5 collective-permute-start.5
  79.3 26.9 %collective-permute-done.5 = bf16[384,3072]{1,0:T(8,128)(2,1)} collective-permute-done((bf16[384,3072]{1,0:T(8,128)(2,1)S(1)}, bf16[384,3072]{1,0:T(8,128)(2,1)}, u32[]{:S(2)}, u32[]{:S(2)}) %collective-permute-start.5) | collective-permute-done | bytes 2359328 | tf_op jit(solution)/shard_map/ppermute | solution.py:524
  106.8 1.3 copy-done.5
  108.1 11.0 %layer_in_0.1 = (bf16[1024,768]{1,0:T(8,128)(2,1)}, bf16[512,4608]{1,0:T(8,128)(2,1)}, f32[128,1536]{1,0:T(8,128)S(1)}) custom-call(s32[5]{0:T(128)S(1)} %stack.29.info, f32[1024,768]{1,0:T(8,128)} %fusion.refs_0_.refs_3_.refs_1_, f32[1,768]{1,0:T(1,128)S(1)} %get-tuple-element.151.refs_1_, bf16[1,768,2304]{2,1,0:T(8,128)(2,1)} %refs_2_.3, ...), custom_call_target="tpu_custom_call" | custom-call | flops 6039797760 | bytes 10226688 | tf_op jit(solution)/shard_map/layer_in_0/pallas_call | solution.py:335
  119.7 4.9 %all-to-all-start.1 = ((bf16[4,2,128,768]{3,2,1,0:T(8,128)(2,1)}), bf16[4,2,128,768]{3,2,1,0:T(8,128)(2,1)}, u32[]{:S(2)}, u32[]{:S(2)}) async-start(bf16[4,2,128,768]{3,2,1,0:T(8,128)(2,1)} %param.15), calls=%async_computation.1 | async-start | bytes 3145728 | tf_op jit(solution)/shard_map/all_to_all | solution.py:581
  125.8 1.1 copy-done.11
  126.9 14.6 %layer_in_1.1 = (bf16[128,1536]{1,0:T(8,128)(2,1)S(1)}, bf16[1024,768]{1,0:T(8,128)(2,1)}, f32[1024,768]{1,0:T(8,128)}, bf16[1024,768]{1,0:T(8,128)(2,1)}, bf16[...) custom-call(s32[5]{0:T(128)S(1)} %stack.32.info, f32[128,1536]{1,0:T(8,128)S(1)} %get-tuple-element.106.refs_0_, ...), custom_call_target="tpu_custom_call" | custom-call | flops 6039797760 | bytes 21629952 | tf_op jit(solution)/shard_map/layer_in_1/pallas_call | solution.py:335
  142.9 1.7 collective-permute-done.7.refs_1_
  145.2 15.8 %layer_in_2.1 = (bf16[128,1536]{1,0:T(8,128)(2,1)S(1)}, bf16[1024,768]{1,0:T(8,128)(2,1)}, f32[1024,768]{1,0:T(8,128)}, bf16[1024,768]{1,0:T(8,128)(2,1)}, bf16[...) custom-call(s32[5]{0:T(128)S(1)} %copy-done.14, f32[128,1536]{1,0:T(8,128)S(1)} %get-tuple-element.109.refs_0_, ...), custom_call_target="tpu_custom_call" | custom-call | flops 6039797760 | bytes 21629952 | tf_op jit(solution)/shard_map/layer_in_2/pallas_call | solution.py:335
  162.0 2.0 collective-permute-done.8.refs_1_
  164.0 17.9 %layer_in_3.1 = (bf16[128,1536]{1,0:T(8,128)(2,1)S(1)}, bf16[1024,768]{1,0:T(8,128)(2,1)}, f32[1024,768]{1,0:T(8,128)}, bf16[1024,768]{1,0:T(8,128)(2,1)}, bf16[...) custom-call(s32[5]{0:T(128)S(1)} %stack.38.info, ...), custom_call_target="tpu_custom_call" | custom-call | flops 6039797760 | bytes 25562112 | tf_op jit(solution)/shard_map/layer_in_3/pallas_call | solution.py:335
  182.2 3.3 collective-permute-done.9.refs_1_
  185.4 1.2 copy-done.24
  186.6 20.9 %layer_back_3.1 = (bf16[1024,2304]{1,0:T(8,128)(2,1)}, bf16[1024,768]{1,0:T(8,128)(2,1)}, f32[1,768]{1,0:T(1,128)S(1)}, f32[1024,768]{1,0:T(8,128)}, bf16[1024,7...) custom-call(s32[5]{0:T(128)S(1)} %stack.38.info, ...), custom_call_target="tpu_custom_call" | custom-call | flops 6039797760 | bytes 32249856 | tf_op jit(solution)/shard_map/layer_back_3/pallas_call | solution.py:335
  207.5 1.2 copy-done.9
  208.8 2.2 collective-permute-done.10.refs_1_
  210.9 20.3 %layer_back_2.1 = (bf16[1024,2304]{1,0:T(8,128)(2,1)}, f32[1,768]{1,0:T(1,128)S(1)}, f32[1024,768]{1,0:T(8,128)}, bf16[1024,768]{1,0:T(8,128)(2,1)}, bf16[512,15...) custom-call(s32[5]{0:T(128)S(1)} %copy-done.15, f32[128,1536]{1,0:T(8,128)S(1)} %get-tuple-element.119.refs_0_, ...), custom_call_target="tpu_custom_call" | custom-call | flops 6039797760 | bytes 31070208 | tf_op jit(solution)/shard_map/layer_back_2/pallas_call | solution.py:335
  231.3 1.1 copy-done.8
  232.5 2.1 collective-permute-done.11.refs_1_
  234.7 20.2 %layer_back_1.1 = (bf16[1024,2304]{1,0:T(8,128)(2,1)}, f32[1,768]{1,0:T(1,128)S(1)}, f32[1024,768]{1,0:T(8,128)}, bf16[1024,768]{1,0:T(8,128)(2,1)}, bf16[512,15...) custom-call(s32[5]{0:T(128)S(1)} %stack.32.info, f32[128,1536]{1,0:T(8,128)S(1)} %get-tuple-element.123.refs_0_, ...), custom_call_target="tpu_custom_call" | custom-call | flops 6039797760 | bytes 31070208 | tf_op jit(solution)/shard_map/layer_back_1/pallas_call | solution.py:335
  254.9 1.1 copy-done.18
  256.2 2.1 collective-permute-done.12.refs_1_
  258.3 1.4 copy-done.19
  259.8 6.2 %layer_back_0.1.refs_0_ = bf16[1024,2304]{1,0:T(8,128)(2,1)} custom-call(s32[5]{0:T(128)S(1)} %copy-done.17, f32[128,1536]{1,0:T(8,128)S(1)} %get-tuple-element.127.refs_0_, f32[128,1536]{1,0:T(8,128)S(1)} %collective-permute-done.12.refs_1_, bf16[128,1536]{1,0:T(8,128)(2,1)S(1)} %copy-done.21, bf16[512,4608]{1,0:T(8,128)(2,1)} %get-tuple-element.107.refs_2_.refs_8_.refs_3_, ...), custom_call_target="tpu_custom_call" | custom-call | flops 6039797760 | bytes 12976128 | tf_op jit(solution)/shard_map/layer_back_0/pallas_call | solution.py:335
  266.0 20.7 %conditional.1 = (bf16[768,3072]{1,0:T(8,128)(2,1)}) conditional(s32[]{:T(128)} %clamp.3, (bf16[1024,768]{1,0:T(8,128)(2,1)S(1)}, bf16[1024,2304]{1,0:T(8,128)(2,1)}, bf16[1024,768]{1,0:T(8,128)(2,1)S(1)}, bf16[1024,768]{1,0:T(8,128)(2,1)S(1)}) %tuple.41, (bf16[1024,768]{1,0:T(8,128)(2,1)}, ...), branch_computations={%region_0.1_spmd, %region_1.2_spmd, %region_2.3_spmd, %region_3.4_... | conditional | flops 4843634688 | bytes 36175936 | solution.py:636
  266.0 6.7 %convolution_convert_fusion = bf16[768,2304]{1,0:T(8,128)(2,1)S(1)} fusion(bf16[1024,768]{1,0:T(8,128)(2,1)S(1)} %get-tuple-element.32, bf16[1024,2304]{1,0:T(8,128)(2,1)} %get-tuple-element.33), kind=kOutput, calls=%fused_computation | convolution fusion | flops 3625648128 | bytes 9830400 | tf_op jit(solution)/shard_map/cond/branch_0_fun/dot_general | solution.py:630
  272.7 1.5 convolution_convert_fusion.1
  274.1 2.8 pad_maximum_fusion
  286.7 1.6 copy-done.3
  288.3 1.3 copy-done.7
  289.6 9.7 %gain_back_0.1 = f32[1,768]{1,0:T(1,128)S(1)} custom-call(s32[5]{0:T(128)S(1)} %copy-done.17, bf16[1024,2304]{1,0:T(8,128)(2,1)} %layer_back_0.1.refs_0_, f32[1024,768]{1,0:T(8,128)} %fusion.refs_0_.refs_3_.refs_1_, bf16[1,768,2304]{2,1,0:T(8,128)(2,1)} %refs_2_.3, bf16[1,768,768]{2,1,0:T(8,128)(2,1)S(1)} %copy-done.7, bf16[1,384,3072]{2,1,0:T(8,128)(2,1)S(1)} %bitcast.51, ...), custom_call_target="tpu_custom_call" | custom-call | flops 3623878656 | bytes 7867392 | tf_op jit(solution)/shard_map/gain_back_0/pallas_call | solution.py:335
  299.5 1.0 collective-permute-done.13
  300.5 2.0 collective-permute-start.14
  302.6 1.8 collective-permute-done.14
  304.4 2.7 collective-permute-start.15
  307.1 2.1 collective-permute-done.15
  309.8 35.9 %reduce-scatter.2.cloned.1.call-done = bf16[96,3072]{1,0:T(8,128)(2,1)} async-done(((bf16[768,3072]{1,0:T(8,128)(2,1)}), bf16[96,3072]{1,0:T(8,128)(2,1)}) %reduce-scatter.2.cloned.1.call-update) | async-done | bytes 589840 | tf_op jit(solution)/shard_map/reduce_scatter | solution.py:637
  345.6 1.2 convert_element_type.28
  346.8 1.0 slice_bitcast_fusion
  (81 shorter events, 8.2 us)
Async XLA Ops:
  7.2 37.6 %copy-start = (bf16[33,768]{1,0:T(8,128)(2,1)S(1)}, bf16[33,768]{1,0:T(8,128)(2,1)}, u32[]{:S(2)}) copy-start(bf16[33,768]{1,0:T(8,128)(2,1)} %param.11) | copy-start | bytes 152068
  7.2 1.8 copy-start.4
  9.0 2.0 copy-start.22
  9.0 9.8 %copy-start.25 = (f32[1,768]{1,0:T(1,128)S(1)}, f32[1,768]{1,0:T(1,128)}, u32[]{:S(2)}) copy-start(f32[1,768]{1,0:T(1,128)} %param.12) | copy-start | bytes 9220
  11.0 36.1 %collective-permute-start = (bf16[384,3072]{1,0:T(8,128)(2,1)}, bf16[384,3072]{1,0:T(8,128)(2,1)S(1)}, u32[]{:S(2)}, u32[]{:S(2)}) collective-permute-start(bf16[384,3072]{1,0:T(8,128)(2,1)} %pad_maximum_fusion.4), channel_id=1, source_target_pairs={{0,8},{1,17},{2,10},{3,19},{4,12},{5,21},{6,14},{7,23},{8,0},{9,25... | collective-permute-start | bytes 7077896 | tf_op jit(solution)/shard_map/ppermute | solution.py:524
  14.0 30.7 %all-to-all-start = ((s32[4,2,128]{2,1,0:T(2,128)}), s32[4,2,128]{2,1,0:T(2,128)S(1)}, u32[]{:S(2)}, u32[]{:S(2)}) async-start(s32[4,2,128]{2,1,0:T(2,128)} %param.10), calls=%async_computation | async-start | bytes 8192 | tf_op jit(solution)/shard_map/all_to_all | solution.py:580
  44.7 2.4 copy-start.23
  47.1 59.2 %copy-start.2 = (bf16[384,3072]{1,0:T(8,128)(2,1)}, bf16[384,3072]{1,0:T(8,128)(2,1)S(1)}, u32[]{:S(2)}) copy-start(bf16[384,3072]{1,0:T(8,128)(2,1)S(1)} %collective-permute-done) | copy-start | bytes 7077892
  48.2 29.0 %collective-permute-start.2 = (bf16[384,3072]{1,0:T(8,128)(2,1)S(1)}, bf16[384,3072]{1,0:T(8,128)(2,1)}, u32[]{:S(2)}, u32[]{:S(2)}) collective-permute-start(bf16[384,3072]{1,0:T(8,128)(2,1)S(1)} %get-tuple-element.103), channel_id=1, source_target_pairs={{0,16},{1,9},{2,18},{3,11},{4,20},{5,13},{6,22},{7,15},{8,24},{9,1... | collective-permute-start | bytes 7077896 | tf_op jit(solution)/shard_map/ppermute | solution.py:524
  77.3 28.9 %collective-permute-start.5 = (bf16[384,3072]{1,0:T(8,128)(2,1)S(1)}, bf16[384,3072]{1,0:T(8,128)(2,1)}, u32[]{:S(2)}, u32[]{:S(2)}) collective-permute-start(bf16[384,3072]{1,0:T(8,128)(2,1)S(1)} %get-tuple-element.108), channel_id=1, source_target_pairs={{0,16},{1,9},{2,18},{3,11},{4,20},{5,13},{6,22},{7,15},{8,24},{9,1... | collective-permute-start | bytes 7077896 | tf_op jit(solution)/shard_map/ppermute | solution.py:524
  78.8 27.5 %collective-permute-start.1 = (bf16[1,384,3072]{2,1,0:T(8,128)(2,1)S(1)}, bf16[1,384,3072]{2,1,0:T(8,128)(2,1)}, u32[]{:S(2)}, u32[]{:S(2)}) collective-permute-start(bf16[1,384,3072]{2,1,0:T(8,128)(2,1)S(1)} %bitcast.43), channel_id=1, source_target_pairs={{0,1},{1,0},{2,3},{3,2},{4,5},{5,4},{6,7},{7,6},{8,9},{9,8},{10,11... | collective-permute-start | bytes 7077896 | tf_op jit(solution)/shard_map/ppermute | solution.py:543
  78.8 27.5 %collective-permute-start.3 = (bf16[1,384,3072]{2,1,0:T(8,128)(2,1)}, bf16[1,384,3072]{2,1,0:T(8,128)(2,1)}, u32[]{:S(2)}, u32[]{:S(2)}) collective-permute-start(bf16[1,384,3072]{2,1,0:T(8,128)(2,1)} %bitcast.8.refs_6_.refs_9_.refs_10_.refs_12_.refs_13_), channel_id=1, source_target_pairs={{0,1},{1,0},{2,3},{3,2},{4,5},{5,4},{6,7},{7,6},{8,9},{9,8},{10,11... | collective-permute-start | bytes 7077896 | tf_op jit(solution)/shard_map/ppermute | solution.py:543
  106.2 19.6 %collective-permute-start.6 = (bf16[1,384,3072]{2,1,0:T(8,128)(2,1)}, bf16[1,384,3072]{2,1,0:T(8,128)(2,1)}, u32[]{:S(2)}, u32[]{:S(2)}) collective-permute-start(bf16[1,384,3072]{2,1,0:T(8,128)(2,1)} %bitcast.15.refs_11_.refs_12_.refs_14_.refs_15_.refs_8_), channel_id=1, source_target_pairs={{0,1},{1,0},{2,3},{3,2},{4,5},{5,4},{6,7},{7,6},{8,9},{9,8},{10,11... | collective-permute-start | bytes 7077896 | tf_op jit(solution)/shard_map/ppermute | solution.py:543
  106.3 0.5 copy-start.16
  106.8 1.3 copy-start.5
  119.1 6.7 %copy-start.6 = (bf16[1,768,768]{2,1,0:T(8,128)(2,1)S(1)}, bf16[1,768,768]{2,1,0:T(8,128)(2,1)}, u32[]{:S(2)}) copy-start(bf16[1,768,768]{2,1,0:T(8,128)(2,1)} %refs_3_.3) | copy-start | bytes 3538948
  119.1 5.8 %collective-permute-start.4 = (f32[128,1536]{1,0:T(8,128)S(1)}, f32[128,1536]{1,0:T(8,128)S(1)}, u32[]{:S(2)}, u32[]{:S(2)}) collective-permute-start(f32[128,1536]{1,0:T(8,128)S(1)} %get-tuple-element.106.refs_0_), channel_id=1, source_target_pairs={{0,1},{1,0},{2,3},{3,2},{4,5},{5,4},{6,7},{7,6},{8,9},{9,8},{10,11... | collective-permute-start | bytes 2359304 | tf_op jit(solution)/shard_map/ppermute | solution.py:493
  119.7 42.3 %all-to-all-start.1 = ((bf16[4,2,128,768]{3,2,1,0:T(8,128)(2,1)}), bf16[4,2,128,768]{3,2,1,0:T(8,128)(2,1)}, u32[]{:S(2)}, u32[]{:S(2)}) async-start(bf16[4,2,128,768]{3,2,1,0:T(8,128)(2,1)} %param.15), calls=%async_computation.1 | async-start | bytes 3145728 | tf_op jit(solution)/shard_map/all_to_all | solution.py:581
  124.6 221.1 %reduce-scatter.2.cloned.1.call-start = ((), (), s32[]{:S(2)}) async-start(), calls=%async_computation.3 | async-start | bytes 5308416 | tf_op jit(solution)/shard_map/reduce_scatter | solution.py:637
  124.9 0.9 copy-start.10
  125.8 1.1 copy-start.11
  141.6 0.7 copy-start.20
  142.3 2.3 collective-permute-start.7
  144.6 0.6 copy-start.14
  161.0 0.7 copy-start.12
  161.7 2.3 collective-permute-start.8
  182.0 3.5 collective-permute-start.9
  185.4 1.2 copy-start.24
  186.6 24.3 %copy-start.15 = (s32[5]{0:T(128)S(1)}, s32[5]{0:T(128)}, u32[]{:S(2)}) copy-start(s32[5]{0:T(128)} %stack.35.info) | copy-start | bytes 64
  207.5 1.2 copy-start.9
  208.7 2.3 collective-permute-start.10
  210.9 23.8 %copy-start.13 = (bf16[128,1536]{1,0:T(8,128)(2,1)S(1)}, bf16[128,1536]{1,0:T(8,128)(2,1)}, u32[]{:S(2)}) copy-start(bf16[128,1536]{1,0:T(8,128)(2,1)} %copy-done.12) | copy-start | bytes 1179652
  231.3 1.1 copy-start.8
  232.4 2.3 collective-permute-start.11
  234.7 23.6 %copy-start.17 = (s32[5]{0:T(128)S(1)}, s32[5]{0:T(128)}, u32[]{:S(2)}) copy-start(s32[5]{0:T(128)} %copy-done.16) | copy-start | bytes 64
  234.7 23.6 %copy-start.21 = (bf16[128,1536]{1,0:T(8,128)(2,1)S(1)}, bf16[128,1536]{1,0:T(8,128)(2,1)}, u32[]{:S(2)}) copy-start(bf16[128,1536]{1,0:T(8,128)(2,1)} %copy-done.20) | copy-start | bytes 1179652
  254.9 1.1 copy-start.18
  256.1 2.3 collective-permute-start.12
  258.3 1.4 copy-start.19
  259.8 6.2 %copy-start.26 = (bf16[1024,768]{1,0:T(8,128)(2,1)S(1)}, bf16[1024,768]{1,0:T(8,128)(2,1)}, u32[]{:S(2)}) copy-start(bf16[1024,768]{1,0:T(8,128)(2,1)} %get-tuple-element.130) | copy-start | bytes 4718596
  259.8 6.2 %copy-start.32 = (bf16[1024,768]{1,0:T(8,128)(2,1)S(1)}, bf16[1024,768]{1,0:T(8,128)(2,1)}, u32[]{:S(2)}) copy-start(bf16[1024,768]{1,0:T(8,128)(2,1)} %get-tuple-element.131) | copy-start | bytes 4718596
  259.8 6.2 %copy-start.33 = (bf16[1024,768]{1,0:T(8,128)(2,1)S(1)}, bf16[1024,768]{1,0:T(8,128)(2,1)}, u32[]{:S(2)}) copy-start(bf16[1024,768]{1,0:T(8,128)(2,1)} %get-tuple-element.105) | copy-start | bytes 4718596
  286.7 1.7 copy-start.3
  288.3 1.3 copy-start.7
  289.6 58.9 %copy-start.1 = (bf16[33,768]{1,0:T(8,128)(2,1)S(1)}, bf16[33,768]{1,0:T(8,128)(2,1)}, u32[]{:S(2)}) copy-start(bf16[33,768]{1,0:T(8,128)(2,1)} %param.11) | copy-start | bytes 152068
  299.3 1.2 collective-permute-start.13
  300.5 3.9 %collective-permute-start.14 = (f32[1,768]{1,0:T(1,128)S(1)}, f32[1,768]{1,0:T(1,128)S(1)}, u32[]{:S(2)}, u32[]{:S(2)}) collective-permute-start(f32[1,768]{1,0:T(1,128)S(1)} %add.64), channel_id=1, source_target_pairs={{0,2},{1,3},{2,0},{3,1},{4,6},{5,7},{6,4},{7,5},{8,10},{9,11},{10,... | collective-permute-start | bytes 9224 | tf_op jit(solution)/shard_map/ppermute | solution.py:642
  304.4 4.8 %collective-permute-start.15 = (f32[1,768]{1,0:T(1,128)S(1)}, f32[1,768]{1,0:T(1,128)S(1)}, u32[]{:S(2)}, u32[]{:S(2)}) collective-permute-start(f32[1,768]{1,0:T(1,128)S(1)} %add.65), channel_id=1, source_target_pairs={{0,4},{1,5},{2,6},{3,7},{4,0},{5,1},{6,2},{7,3},{8,12},{9,13},{10,... | collective-permute-start | bytes 9224 | tf_op jit(solution)/shard_map/ppermute | solution.py:642
Sparse Core Ops, SparseCore 0:
  286.8 58.7 reduce-scatter.1

commit v3 on v2

v3 whole, which is shorter than its diff:
```python
import functools
import math

import jax
import jax.numpy as jnp
from jax import lax
from jax.experimental import pallas as pl
from jax.experimental.pallas import tpu as pltpu
from jax.sharding import PartitionSpec as P

HEADS = 12
HEAD_DIM = 64
PACK = 2
BLOCKS = 3
DIRECT, ACROSS, FULL = range(3)
F32 = jnp.float32
BF16 = jnp.bfloat16
VMEM_LIMIT = 60 * 1024 * 1024
NT = (((1,), (1,)), ((), ()))
TN = (((0,), (0,)), ((), ()))


def mm(a, b):
    return jnp.dot(a, b, preferred_element_type=F32)


def mm_nt(a, b):
    return lax.dot_general(a, b, NT, preferred_element_type=F32)


def head_lanes(ref, seq, head):
    width = PACK * HEAD_DIM
    first = head * width
    return jnp.concatenate(
        [ref[r * seq : (r + 1) * seq, first : first + width] for r in range(ref.shape[0] // seq)],
        axis=1,
    )


def regroup(blocks):
    return [
        jnp.concatenate([block[:, n * HEAD_DIM : (n + 1) * HEAD_DIM] for block in blocks], axis=1)
        for n in range(PACK)
    ]


def pack_rows(value, out, first, seq):
    width = PACK * HEAD_DIM
    for pair in range(value.shape[0] // seq // PACK):
        for p in range(value.shape[1] // width):
            blocks = [
                value[(pair * PACK + r) * seq : (pair * PACK + r + 1) * seq, p * width : (p + 1) * width]
                for r in range(PACK)
            ]
            for n, block in enumerate(regroup(blocks)):
                at = (first + p * PACK + n) * width
                out[pair * seq : (pair + 1) * seq, at : at + width] = block


class Weights:
    def __init__(self, info, first, own, stages, columns, dst, sems):
        self.choices = (info[first], info[first + 1])
        self.member, self.half = info[4], info[5]
        self.own, self.stages = own, stages
        self.columns, self.dst, self.sems = columns, dst, sems

    def each(self, act):
        @pl.when(self.choices[0] == 0)
        def _():
            act(pltpu.make_async_copy(self.own.at[0], self.dst, self.sems.at[0]))

        for stage, group in enumerate(self.stages):
            for parity in range(2):

                @pl.when(self.choices[parity] == stage + 1)
                def _(group=group, parity=parity):
                    for kind, refs in group:
                        self.shares(kind, refs, parity, act)

    def shares(self, kind, refs, parity, act):
        group = self.sems.shape[0] // BLOCKS
        block = self.dst.shape[0] // group // BLOCKS
        places = {DIRECT: (self.half, 2), ACROSS: (1 - self.half,), FULL: (0, 1, 2)}[kind]
        sems = {DIRECT: (0, 1), ACROSS: (2,), FULL: (0, 1, 2)}[kind]
        seen = 0
        for ref in refs:
            for n in range(ref.shape[0]):
                if seen % 2 == parity:
                    base = (self.member ^ seen) * BLOCKS
                    for j, place in enumerate(places):
                        start = pl.multiple_of((base + place) * block, block)
                        act(
                            pltpu.make_async_copy(
                                ref.at[n, j * block : (j + 1) * block, self.columns],
                                self.dst.at[pl.ds(start, block)],
                                self.sems.at[seen * BLOCKS + sems[j]],
                            )
                        )
                seen += 1

    def start(self):
        self.each(lambda copy: copy.start())

    def wait(self):
        self.each(lambda copy: copy.wait())


def take_stages(it, layout):
    return [[(kind, [next(it) for _ in range(count)]) for kind, count in group] for group in layout]


def softmax_heads(la, lb, scale, keep):
    seq = la.shape[0]
    for h in range(HEADS):
        at = slice(h * seq, (h + 1) * seq)
        logits = (la[:, at] + lb[:, at]) * scale
        e = jnp.exp(logits - jnp.max(logits, axis=-1, keepdims=True))
        keep(h, e / jnp.sum(e, axis=-1, keepdims=True))


def norm_parts(x):
    centred = x - jnp.mean(x, axis=-1, keepdims=True)
    spread = jnp.mean(centred * centred, axis=-1, keepdims=True)
    rstd = lax.rsqrt(spread + 1e-05)
    return centred * rstd, rstd


def scores(ref_a, first_a, ref_b, first_b, out, out_row, seq, begin):
    parts = [
        mm_nt(head_lanes(ref_a, seq, first_a + h), head_lanes(ref_b, seq, first_b + h))
        for h in range(HEADS)
    ]
    rows = slice(out_row, out_row + seq)

    @pl.when(begin)
    def _():
        for h, part in enumerate(parts):
            out[rows, h * seq : (h + 1) * seq] = part

    @pl.when(jnp.logical_not(begin))
    def _():
        for h, part in enumerate(parts):
            out[rows, h * seq : (h + 1) * seq] += part


def mix(weights, ref_b, first_b, out, first_out, scale, seq):
    width = PACK * HEAD_DIM
    for p in range(HEADS // PACK):
        values = []
        for h in range(p * PACK, (p + 1) * PACK):
            value = mm(weights[:, h * seq : (h + 1) * seq], head_lanes(ref_b, seq, first_b + h))
            values.append((value if scale is None else value * scale).astype(BF16))
        at = first_out + p * width
        for pair in range(ref_b.shape[0] // seq):
            blocks = [value[:, pair * width : (pair + 1) * width] for value in values]
            for n, block in enumerate(regroup(blocks)):
                row = (pair * PACK + n) * seq
                out[row : row + seq, at : at + width] = block


def forward_kernel(has_prev, has_top, info, *refs, layout, scale, seq, width):
    it = iter(refs)
    if has_prev:
        la, lb, v_prev = next(it), next(it), next(it)
    x_in, gain = next(it), next(it)
    top = next(it) if has_top else None
    own_q, own_o = next(it), next(it)
    stages = take_stages(it, layout)
    if has_prev:
        probs_out, x_out = next(it), next(it)
    qkv_out, score_out = next(it), next(it)
    if has_top:
        dmix_out = next(it)
    wq, sem_q = next(it), next(it)
    if has_prev:
        wo, sem_o, mixed = next(it), next(it), next(it)
    if has_top:
        wt, sem_t = next(it), next(it)
    step = pl.program_id(0)
    qcols, ocols = slice(0, 3 * width), slice(3 * width, 4 * width)
    get_q = Weights(info, 0, own_q, stages, qcols, wq, sem_q)
    if has_prev:
        get_o = Weights(info, 2, own_o, stages, ocols, wo, sem_o)
    if has_top:
        get_t = Weights(info, 0, own_o, stages, ocols, wt, sem_t)

    @pl.when(step == 0)
    def _():
        if has_prev:
            get_o.start()
        get_q.start()
        if has_top:
            get_t.start()
        if has_prev:

            def keep(h, value):
                probs_out[:, h * seq : (h + 1) * seq] = value.astype(BF16)

            softmax_heads(la, lb, scale, keep)

    if has_prev:
        mix(probs_out, v_prev, 0, mixed, 0, None, seq)
        pl.when(step == 0)(get_o.wait)
        x = x_in[...] + mm(mixed[...], wo[...])
        x_out[...] = x
    else:
        x = x_in[...]
    hat, _ = norm_parts(x)
    h = (hat * gain[...]).astype(BF16)
    pl.when(step == 0)(get_q.wait)
    pack_rows(mm(h, wq[...]).astype(BF16), qkv_out, 0, seq)
    begin = step == 0
    scores(qkv_out, 0, qkv_out, HEADS, score_out, 0, seq, begin)
    if has_top:
        pl.when(step == 0)(get_t.wait)
        pack_rows(mm_nt(top[...], wt[...]).astype(BF16), dmix_out, 0, seq)
        scores(dmix_out, 0, qkv_out, 2 * HEADS, score_out, seq, seq, begin)


def add_gain(gain_out, d_h, hat, step):
    part = jnp.sum(d_h * hat, axis=0, keepdims=True)

    @pl.when(step == 0)
    def _():
        gain_out[...] = part

    @pl.when(step > 0)
    def _():
        gain_out[...] += part


def add_product(a, b, total, column, step, steps, staged):
    at = slice(column, column + b.shape[1])
    part = lax.dot_general(a, b, TN, preferred_element_type=F32)

    @pl.when(step == 0)
    def _():
        total[:, at] = part

    @pl.when((step > 0) & (step < steps - 1))
    def _():
        total[:, at] += part

    @pl.when(step == steps - 1)
    def _():
        staged[:, at] = ((total[:, at] if steps > 1 else 0.0) + part).astype(BF16)


def logit_grads(probs, sa, sb, first, seq, dl, dlt):
    for h in range(HEADS):
        at = slice(h * seq, (h + 1) * seq)
        prob = probs[:, at].astype(F32)
        d_prob = sa[first : first + seq, at] + sb[first : first + seq, at]
        d_logit = prob * (d_prob - jnp.sum(d_prob * prob, axis=-1, keepdims=True))
        dl[:, at] = d_logit.astype(BF16)
        dlt[:, at] = jnp.transpose(d_logit).astype(BF16)


def turn_probs(probs, seq, pt):
    for h in range(HEADS):
        at = slice(h * seq, (h + 1) * seq)
        pt[:, at] = jnp.transpose(probs[:, at].astype(F32)).astype(BF16)


def backward_kernel(is_top, info, *refs, layout, scale, seq, width, steps):
    it = iter(refs)
    sa, sb = next(it), next(it)
    if not is_top:
        probs = next(it)
    qkv, dmix, x_in, gain, dy, v_prev = [next(it) for _ in range(6)]
    if not is_top:
        next(it), next(it)
    own_q, own_o = next(it), next(it)
    stages = take_stages(it, layout)
    gain_out, dy_out, dmix_out, score_out = [next(it) for _ in range(4)]
    grad_a, grad_b = next(it), next(it)
    dl, dlt, pt, dqkv, mixed = [next(it) for _ in range(5)]
    total_a, total_b, staged_a, staged_b, sem_g = [next(it) for _ in range(5)]
    wq, sem_q, wo, sem_o = [next(it) for _ in range(4)]
    if is_top:
        probs = next(it)
    step = pl.program_id(0)
    get_q = Weights(info, 0, own_q, stages, slice(0, 3 * width), wq, sem_q)
    get_o = Weights(info, 2, own_o, stages, slice(3 * width, 4 * width), wo, sem_o)
    own = info[0] == 0

    @pl.when(step == 0)
    def _():
        get_q.start()
        get_o.start()
        if is_top:

            def keep(h, value):
                probs[:, h * seq : (h + 1) * seq] = value.astype(BF16)

            softmax_heads(sa.at[0:seq], sb.at[0:seq], scale, keep)
        logit_grads(probs, sa, sb, seq if is_top else 0, seq, dl, dlt)
        turn_probs(probs, seq, pt)

    mix(dl, qkv, HEADS, dqkv, 0, scale, seq)
    mix(dlt, qkv, 0, dqkv, width, scale, seq)
    mix(pt, dmix, 0, dqkv, 2 * width, None, seq)
    pl.when(step == 0)(get_q.wait)
    d_h = mm_nt(dqkv[...], wq[...]).astype(BF16).astype(F32)
    hat, rstd = norm_parts(x_in[...])
    add_gain(gain_out, d_h, hat, step)
    d_hat = d_h * gain[...]
    mean_d = jnp.mean(d_hat, axis=-1, keepdims=True)
    mean_dh = jnp.mean(d_hat * hat, axis=-1, keepdims=True)
    d_x = dy[...].astype(F32) + rstd * (d_hat - mean_d - hat * mean_dh)
    dy_out[...] = d_x
    pl.when(step == 0)(get_o.wait)
    pack_rows(mm_nt(d_x.astype(BF16), wo[...]).astype(BF16), dmix_out, 0, seq)
    scores(dmix_out, 0, v_prev, 0, score_out, 0, seq, step == 0)

    @pl.when(own)
    def _():
        mix(probs, qkv, 2 * HEADS, mixed, 0, None, seq)
        h = (norm_parts(x_in[...])[0] * gain[...]).astype(BF16)
        add_product(mixed[...], dy[...].astype(BF16), total_a, 0, step, steps, staged_a)
        add_product(h, dqkv[:, 2 * width :], total_a, width, step, steps, staged_a)
        add_product(h, dqkv[:, : 2 * width], total_b, 0, step, steps, staged_b)

    @pl.when(own & (step == steps - 1))
    def _():
        copies = [
            pltpu.make_async_copy(staged_a, grad_a, sem_g.at[0]),
            pltpu.make_async_copy(staged_b, grad_b, sem_g.at[1]),
        ]
        for copy in copies:
            copy.start()
        for copy in copies:
            copy.wait()


def early_kernel(info, *refs, layout, seq, width, steps):
    probs, v, dmix, x_in, gain, dy, _, dv_out, grad_a, pt, mixed, total, staged, sem = refs
    step = pl.program_id(0)
    own = info[0] == 0

    @pl.when(own)
    def _():
        @pl.when(step == 0)
        def _():
            turn_probs(probs, seq, pt)

        mix(probs, v, 0, mixed, 0, None, seq)
        mix(pt, dmix, 0, dv_out, 0, None, seq)
        h = (norm_parts(x_in[...])[0] * gain[...]).astype(BF16)
        add_product(mixed[...], dy[...].astype(BF16), total, 0, step, steps, staged)
        add_product(h, dv_out[...], total, width, step, steps, staged)

    @pl.when(own & (step == steps - 1))
    def _():
        copy = pltpu.make_async_copy(staged, grad_a, sem.at[0])
        copy.start()
        copy.wait()


def late_kernel(info, *refs, layout, scale, seq, width, steps):
    sa, sb, probs, qk, x_in, gain, _, dqk_out, grad_b, dl, dlt, total, staged, sem = refs
    step = pl.program_id(0)
    own = info[0] == 0

    @pl.when(own)
    def _():
        @pl.when(step == 0)
        def _():
            logit_grads(probs, sa, sb, 0, seq, dl, dlt)

        h = (norm_parts(x_in[...])[0] * gain[...]).astype(BF16)
        mix(dl, qk, HEADS, dqk_out, 0, scale, seq)
        mix(dlt, qk, 0, dqk_out, width, scale, seq)
        add_product(h, dqk_out[...], total, 0, step, steps, staged)

    @pl.when(own & (step == steps - 1))
    def _():
        copy = pltpu.make_async_copy(staged, grad_b, sem.at[0])
        copy.start()
        copy.wait()


def gain_kernel(info, *refs, layout, width):
    dqk, dv, x_in, own_q, gain_out, wq, sem = refs
    step = pl.program_id(0)

    @pl.when(info[0] == 0)
    def _():
        @pl.when(step == 0)
        def _():
            copy = pltpu.make_async_copy(own_q.at[0], wq, sem.at[0])
            copy.start()
            copy.wait()

        hat, _ = norm_parts(x_in[...])
        d_h = mm_nt(dqk[...], wq[:, : 2 * width]) + mm_nt(dv[...], wq[:, 2 * width :])
        add_gain(gain_out, d_h.astype(BF16).astype(F32), hat, step)


class Chain:
    def __init__(self, fetched, member, n_group, own, seq, width, rows, scale):
        self.fetched, self.member, self.n_group = fetched, member, n_group
        self.own, self.seq, self.width, self.rows = own, seq, width, rows
        self.scale = scale
        per_step = 4 if rows % 4 == 0 else 2
        self.chunk = per_step * seq
        self.steps = rows // per_step

    def info(self, now, other):
        picks = self.fetched.choices(now) + self.fetched.choices(other)
        return jnp.stack(picks + [self.member, self.fetched.half]).astype(jnp.int32)

    def whole(self, rows, lanes):
        return pl.BlockSpec((rows, lanes), lambda i, s: (0, 0))

    def tile(self, lanes, column=0, part=1):
        return pl.BlockSpec((self.chunk // part, lanes), lambda i, s: (i, column))

    def packed(self, heads, column=0):
        return self.tile(heads * PACK * HEAD_DIM, column, PACK)

    def call(self, body, name, info, stages, ins, outs, scratch, flops, carried=(), own=None):
        any_spec = pl.BlockSpec(memory_space=pl.ANY)
        groups = self.fetched.stages[:stages]
        weights = list(self.own if own is None else own)
        weights += [a for group in groups for _, arrays in group for a in arrays]
        arrays = [a for a, _ in ins] + list(carried)
        shapes = [o for o, _ in outs]
        size = sum(math.prod(a.shape) * a.dtype.itemsize for a in arrays + shapes)
        aliases = {
            1 + len(ins) + n: len(outs) - len(carried) + n for n in range(len(carried))
        }
        layout = tuple(tuple((kind, len(arrays)) for kind, arrays in group) for group in groups)
        return pl.pallas_call(
            functools.partial(body, layout=layout),
            name=name,
            out_shape=shapes,
            grid_spec=pltpu.PrefetchScalarGridSpec(
                num_scalar_prefetch=1,
                grid=(self.steps,),
                in_specs=[spec for _, spec in ins] + [any_spec] * (len(carried) + len(weights)),
                out_specs=[spec for _, spec in outs],
                scratch_shapes=scratch,
            ),
            input_output_aliases=aliases,
            compiler_params=pltpu.CompilerParams(
                dimension_semantics=("arbitrary",), vmem_limit_bytes=VMEM_LIMIT
            ),
            cost_estimate=pl.CostEstimate(flops=flops, bytes_accessed=size, transcendentals=0),
        )(info, *arrays, *weights)

    def weight_scratch(self, columns):
        return [
            pltpu.VMEM((self.width, columns * self.width), BF16),
            pltpu.SemaphoreType.DMA((self.n_group * BLOCKS,)),
        ]

    def shape(self, rows, lanes, dtype):
        return jax.ShapeDtypeStruct((rows, lanes), dtype)

    def grad_out(self):
        any_spec = pl.BlockSpec(memory_space=pl.ANY)
        return (self.shape(self.width, 2 * self.width, BF16), any_spec)

    def grad_scratch(self, copies):
        shape = (self.width, 2 * self.width)
        scratch = [pltpu.VMEM(shape, F32)] * copies + [pltpu.VMEM(shape, BF16)] * copies
        return scratch + [pltpu.SemaphoreType.DMA((copies,))]

    def forward(self, layer, x, gain, prev, top):
        seq, width = self.seq, self.width
        n = self.rows * seq
        hw = HEADS * seq
        score_rows = seq if top is None else 2 * seq
        ins = [(x, self.tile(width)), (gain, self.whole(1, width))]
        outs = [
            (self.shape(n // PACK, 3 * PACK * width, BF16), self.packed(3 * HEADS)),
            (self.shape(score_rows, hw, F32), self.whole(score_rows, hw)),
        ]
        scratch = self.weight_scratch(3)
        if prev is not None:
            ins = [
                (prev[0], self.whole(seq, hw)),
                (prev[1], self.whole(seq, hw)),
                (prev[2], self.packed(HEADS, 2)),
            ] + ins
            outs = [
                (self.shape(seq, hw, BF16), self.whole(seq, hw)),
                (self.shape(n, width, F32), self.tile(width)),
            ] + outs
            scratch += self.weight_scratch(1) + [pltpu.VMEM((self.chunk, width), BF16)]
        if top is not None:
            ins.append((top, self.tile(width)))
            outs.append((self.shape(n // PACK, PACK * width, BF16), self.packed(HEADS)))
            scratch += self.weight_scratch(1)
        body = functools.partial(
            forward_kernel, prev is not None, top is not None, scale=self.scale, seq=seq, width=width
        )
        return self.call(
            body,
            f"layer_in_{layer}",
            self.info(layer, max(layer - 1, 0)),
            self.fetched.first_stages if layer == 0 else None,
            ins,
            outs,
            scratch,
            2 * n * width * width * 5,
        )

    def backward(self, layer, scores, probs, qkv, dmix, x, gain, dy, v_prev, grads):
        seq, width = self.seq, self.width
        n = self.rows * seq
        hw = HEADS * seq
        is_top = probs is None
        score_rows = scores[0].shape[0]
        square = pltpu.VMEM((seq, hw), BF16)
        ins = [(s, self.whole(score_rows, hw)) for s in scores]
        if not is_top:
            ins.append((probs, self.whole(seq, hw)))
        ins += [
            (qkv, self.packed(3 * HEADS)),
            (dmix, self.packed(HEADS)),
            (x, self.tile(width)),
            (gain, self.whole(1, width)),
            (dy, self.tile(width)),
            (v_prev, self.packed(HEADS, 2)),
        ]
        outs = [
            (self.shape(1, width, F32), self.whole(1, width)),
            (self.shape(n, width, F32), self.tile(width)),
            (self.shape(n // PACK, PACK * width, BF16), self.packed(HEADS)),
            (self.shape(seq, hw, F32), self.whole(seq, hw)),
            self.grad_out(),
            self.grad_out(),
        ]
        scratch = [square] * 3
        scratch += [pltpu.VMEM((self.chunk, lanes * width), BF16) for lanes in (3, 1)]
        scratch += self.grad_scratch(2) + self.weight_scratch(3) + self.weight_scratch(1)
        if is_top:
            scratch.append(square)
        body = functools.partial(
            backward_kernel, is_top, scale=self.scale, seq=seq, width=width, steps=self.steps
        )
        return self.call(
            body,
            f"layer_back_{layer}",
            self.info(layer, layer - 1),
            None,
            ins,
            outs,
            scratch,
            2 * n * width * width * 5,
            carried=grads,
        )

    def early(self, probs, qkv, dmix, x, gain, dy, grad):
        seq, width = self.seq, self.width
        n, hw = self.rows * seq, HEADS * seq
        ins = [
            (probs, self.whole(seq, hw)),
            (qkv, self.packed(HEADS, 2)),
            (dmix, self.packed(HEADS)),
            (x, self.tile(width)),
            (gain, self.whole(1, width)),
            (dy, self.tile(width)),
        ]
        outs = [(self.shape(n, width, BF16), self.tile(width)), self.grad_out()]
        scratch = [pltpu.VMEM((seq, hw), BF16), pltpu.VMEM((self.chunk, width), BF16)]
        return self.call(
            functools.partial(early_kernel, seq=seq, width=width, steps=self.steps),
            "early_back_0",
            self.info(0, 0),
            0,
            ins,
            outs,
            scratch + self.grad_scratch(1),
            2 * n * width * width * 3,
            carried=(grad,),
            own=(),
        )

    def late(self, scores, probs, qkv, x, gain, grad):
        seq, width = self.seq, self.width
        n, hw = self.rows * seq, HEADS * seq
        ins = [
            (scores[0], self.whole(seq, hw)),
            (scores[1], self.whole(seq, hw)),
            (probs, self.whole(seq, hw)),
            (qkv, self.packed(2 * HEADS)),
            (x, self.tile(width)),
            (gain, self.whole(1, width)),
        ]
        outs = [(self.shape(n, 2 * width, BF16), self.tile(2 * width)), self.grad_out()]
        return self.call(
            functools.partial(
                late_kernel, scale=self.scale, seq=seq, width=width, steps=self.steps
            ),
            "late_back_0",
            self.info(0, 0),
            0,
            ins,
            outs,
            [pltpu.VMEM((seq, hw), BF16)] * 2 + self.grad_scratch(1),
            2 * n * width * width * 3,
            carried=(grad,),
            own=(),
        )

    def gain_grad(self, dqk, dv, x):
        width = self.width
        n = self.rows * self.seq
        return self.call(
            functools.partial(gain_kernel, width=width),
            "gain_back_0",
            self.info(0, 0),
            0,
            [(dqk, self.tile(2 * width)), (dv, self.tile(width)), (x, self.tile(width))],
            [(self.shape(1, width, F32), self.whole(1, width))],
            self.weight_scratch(3),
            2 * n * width * width * 3,
            own=self.own[:1],
        )[0]


def group_swap(value, n_row, n_group):
    other = jnp.zeros_like(value)
    bit = 1
    while bit < n_group:
        if bit > 1:
            value = value + other
        other = lax.ppermute(value, "row", [(r, r ^ bit) for r in range(n_row)])
        bit *= 2
    return value, other


class Fetched:
    first_stages = 2

    def __init__(self, wqkv, wout, section, place, n_section, n_row, n_group):
        assert n_section == 4 and n_group % 2 == 0
        self.section, self.n_row, self.n_group = section, n_row, n_group
        self.member, self.half = place % n_group, place // n_group % 2
        self.last = n_section - 1
        self.block = wqkv.shape[0] // n_group // BLOCKS
        self.own = (wqkv, wout)
        self.to_last = section == (self.last ^ jnp.where(self.member % 2 == 0, 2, 1))
        self.mine = jnp.concatenate([self.own_block(self.half), self.own_block(2)], axis=0)
        self.got = self.hop(self.mine, 1)
        self.across = self.cross(self.got)
        self.stages = [self.halves(self.got, self.across)]

    def own_block(self, place, count=1):
        start = (self.member * BLOCKS + place) * self.block
        rows = [lax.dynamic_slice_in_dim(w, start, count * self.block, 0) for w in self.own]
        return jnp.concatenate(rows, axis=1)

    def hop(self, value, even_bit):
        perm = [
            (s * self.n_row + r, (s ^ (even_bit if r % 2 == 0 else 3 - even_bit)) * self.n_row + r)
            for s in range(self.last + 1)
            for r in range(self.n_row)
        ]
        return lax.ppermute(value, ("section", "row"), perm)

    def cross(self, value):
        perm = [(r, r ^ self.n_group) for r in range(self.n_row)]
        return lax.ppermute(value[: self.block], "row", perm)

    def halves(self, got, across):
        return [(DIRECT, self.share(got)), (ACROSS, self.share(across))]

    def second(self, *ready):
        second, *ready = lax.optimization_barrier(
            (jnp.where(self.to_last, self.got, self.mine), *ready)
        )
        second = self.hop(second, 2)
        self.stages.append(self.halves(second, self.cross(second)))
        low = jnp.where(self.half == 0, self.got[: self.block], self.across)
        high = jnp.where(self.half == 0, self.across, self.got[: self.block])
        relayed = jnp.concatenate([low, high, self.got[self.block :]], axis=0)
        third, _ = lax.optimization_barrier(
            (jnp.where(self.to_last, self.own_block(0, BLOCKS), relayed), second)
        )
        self.third = self.hop(third, 2)
        return ready

    def finish(self, ready):
        third, ready = lax.optimization_barrier((self.third, ready))
        self.stages.append([(FULL, self.share(third))])
        return ready

    def share(self, value):
        have = [value[None]]
        bit = 1
        while bit < self.n_group:
            send = have[0] if len(have) == 1 else jnp.concatenate(have, axis=0)
            have.append(lax.ppermute(send, "row", [(r, r ^ bit) for r in range(self.n_row)]))
            bit *= 2
        return have

    def choices(self, layer):
        offset = self.section ^ layer
        at_last = self.section == self.last
        picks = []
        for parity in (self.member % 2, 1 - self.member % 2):
            first = jnp.where(parity == 0, 1, 2)
            second = jnp.where(at_last, 3, 3 - first)
            pick = jnp.where(offset == first, 1, jnp.where(offset == second, 2, 3))
            picks.append(jnp.where(offset == 0, 0, pick))
        return picks


def local(tokens, embed, ln_gain, w_qkv, w_out, out_grad):
    n_section = lax.axis_size("section")
    n_row = lax.axis_size("row")
    section = lax.axis_index("section")
    place = lax.axis_index("row")
    micro, rows_here, seq = tokens.shape
    width = embed.shape[1]
    n_group = n_row // micro
    member = place % n_group
    rows = rows_here * micro
    scale = HEAD_DIM ** (-0.5) / math.sqrt(rows_here * n_row)
    fetched = Fetched(w_qkv[0], w_out[0], section, place, n_section, n_row, n_group)
    same = [[m * n_group + g for m in range(micro)] for g in range(n_group)]
    exchange = functools.partial(
        lax.all_to_all,
        axis_name="row",
        split_axis=0,
        concat_axis=0,
        axis_index_groups=same,
        tiled=True,
    )
    tok = exchange(tokens).reshape(-1)
    top_grad = exchange(out_grad).reshape(rows * seq, width)
    gains = lax.all_gather(ln_gain[0], "section", axis=0, tiled=False)
    table = (jnp.arange(embed.shape[0], dtype=jnp.int32)[:, None] == tok[None, :]).astype(BF16)
    x = lax.dot_general(table, embed, TN, preferred_element_type=F32)

    x, gains = fetched.second(x, gains)
    chain = Chain(fetched, member, n_group, (w_qkv, w_out), seq, width, rows, scale)
    xs, qkvs, probs = [], [], []
    scores = None
    dmix = None
    for layer in range(n_section):
        prev = None if layer == 0 else (*scores, qkvs[-1])
        top = top_grad if layer == n_section - 1 else None
        outs = list(chain.forward(layer, x, gains[layer][None], prev, top))
        if prev is not None:
            probs.append(outs.pop(0))
            x = outs.pop(0)
        xs.append(x)
        qkvs.append(outs[0])
        if top is not None:
            dmix = outs[2]
        scores = group_swap(outs[1], n_row, n_group)
        if layer == 0:
            scores = (scores[0], fetched.finish(scores[1]))
    probs.append(None)

    dy = top_grad
    gain_parts = [None] * n_section
    grads = ()
    for layer in range(n_section - 1, 0, -1):
        gain_parts[layer], dy, dmix, part, *grads = chain.backward(
            layer,
            scores,
            probs[layer],
            qkvs[layer],
            dmix,
            xs[layer],
            gains[layer][None],
            dy,
            qkvs[layer - 1],
            grads,
        )
        scores = group_swap(part, n_row, n_group)
    sum_rows = functools.partial(
        lax.psum_scatter, axis_name="row", scatter_dimension=0, tiled=True
    )
    gain = gains[0][None]
    d_v, grad_a = chain.early(probs[0], qkvs[0], dmix, xs[0], gain, dy, grads[0])
    grad_a = sum_rows(grad_a).astype(F32)
    d_qk, grad_b = chain.late(scores, probs[0], qkvs[0], xs[0], gain, grads[1])
    grad_b = sum_rows(grad_b).astype(F32)
    gain_parts[0] = chain.gain_grad(d_qk, d_v, xs[0])
    g_gain = lax.select_n(section, *gain_parts)
    bit = 1
    while bit < n_row:
        g_gain = g_gain + lax.ppermute(g_gain, "row", [(r, r ^ bit) for r in range(n_row)])
        bit *= 2
    g_gain = lax.dynamic_slice_in_dim(g_gain, place * (width // n_row), width // n_row, 1)
    g_qkv = jnp.concatenate([grad_b, grad_a[:, width:]], axis=1)
    return (g_qkv[None], grad_a[None, :, :width], g_gain)


def solution(mesh):
    in_specs = (
        P(None, "row", None),
        P(),
        P("section", None),
        P("section", None, None),
        P("section", None, None),
        P(None, "row", None, None),
    )
    out_specs = (P("section", "row", None), P("section", "row", None), P("section", "row"))
    return jax.shard_map(local, mesh=mesh, in_specs=in_specs, out_specs=out_specs, check_vma=False)
```

time: 361 us -> 345 us (0.956)
  Pallas kernels: 137 us -> 158 us
  waiting for transfers between devices: 109 us -> 90.3 us
  loops' own time: 9.74 us -> 0 us
  blocking collectives: 25.8 us -> 17.4 us
  matrix products: 10.5 us -> 2.33 us
  starting transfers between devices: 22.6 us -> 26.5 us
    ppermute x3, waiting for transfers between devices: 54.3 us -> 14.2 us  [hop(): return lax.ppermute(value, ('section', 'row'), perm)]
    pallas_call x9 -> x10, Pallas kernels: 137 us -> 158 us  [call(): pl.pallas_call(functools.partial(body, layout=layout), name=name, out_sha...]
    ppermute x0 -> x2, waiting for transfers between devices: none -> 13.3 us  [cross(): return lax.ppermute(value[:self.block], 'row', perm)]
    another operation x1 -> x0, loops' own time: 9.74 us -> none  [local(): g_all = lax.switch(section, [own_grads(n) for n in range(n_section)])]
    all_gather x1, blocking collectives: 25.8 us -> 17.4 us  [local(): gains = lax.all_gather(ln_gain[0], 'section', axis=0, tiled=False)]
    dot_general x2 -> x0, matrix products: 8.11 us -> none  [the longest x1 6.66 us: run(): lax.dot_general(hs[layer], dqkvs[layer], TN, preferred_element_type=F32)]
    unnamed x59 -> x35, local copies, waits for them, and re-layouts: 14.9 us -> 8.11 us
    reduce_scatter x1 -> x2, waiting for transfers between devices: 35.9 us -> 42 us  [the longest x1 35.2 us: local(): grad_b = sum_rows(grad_b).astype(F32)]
  transfers between devices with their start and end apart: 19 -> 24, of which waited for: 13 -> 17; matrix products, arithmetic and copies ran while one was open for 1% -> 5% of each run, Pallas kernels for 14% -> 19%
where the time goes in v3:
time: 345 us; the launch traced here: 340 us
  Pallas kernels  158 us (46%)
  waiting for transfers between devices  90.3 us (26%)
  starting transfers between devices  26.5 us (8%)
  local copies, waits for them, and re-layouts  19 us (6%)
  blocking collectives  17.4 us (5%)
  between operations  14.9 us (4%)
  other arithmetic  11 us (3%)
    pallas_call x10, Pallas kernels, call(): pl.pallas_call(functools.partial(body, layout=layout), name=name, out_sha...  158 us
    reduce_scatter x1, waiting for transfers between devices, local(): grad_b = sum_rows(grad_b).astype(F32)  35.2 us
    all_gather x1, blocking collectives, local(): gains = lax.all_gather(ln_gain[0], 'section', axis=0, tiled=False)  17.4 us
    ppermute x7, waiting for transfers between devices, group_swap(): other = lax.ppermute(value, 'row', [(r, r ^ bit) for r in range(n_row)])  15.2 us
    ppermute x3, waiting for transfers between devices, hop(): return lax.ppermute(value, ('section', 'row'), perm)  14.2 us
    ppermute x2, waiting for transfers between devices, cross(): return lax.ppermute(value[:self.block], 'row', perm)  13.3 us
    unnamed x35, local copies, waits for them, and re-layouts  8.11 us
  transfers between devices with their start and end apart: 24, of which 17 were waited for; matrix products, arithmetic and copies ran while one was open for 5% of the time, Pallas kernels for 19%

profile of v3, /device:TPU:0, one launch (start us, length us, event | category | flops | bytes accessed | tf_op | source)
XLA Modules:
  0.0 339.6 jit_solution(5752923898845067063)
XLA Ops:
  7.2 1.1 dynamic-slice_bitcast_fusion.5
  8.3 1.3 dynamic-slice_bitcast_fusion.3
  9.6 1.4 maximum_maximum_fusion
  11.0 2.9 collective-permute-start
  13.9 4.9 %all-to-all-start = ((s32[4,2,128]{2,1,0:T(2,128)}), s32[4,2,128]{2,1,0:T(2,128)S(1)}, u32[]{:S(2)}, u32[]{:S(2)}) async-start(s32[4,2,128]{2,1,0:T(2,128)} %param.6), calls=%async_computation | async-start | bytes 8192 | tf_op jit(solution)/shard_map/all_to_all | solution.py:734
  18.8 17.4 %all-gather = f32[4,1,768]{2,1,0:T(1,128)S(1)} all-gather(f32[1,1,768]{2,1,0:T(1,128)S(1)} %bitcast.56), channel_id=1, replica_groups=mesh['section'=4,'row'=8] {'section'}, dimensions={0}, use_global_device_ids=true | all-gather | bytes 15360 | tf_op jit(solution)/shard_map/all_gather | solution.py:736
  36.2 2.3 fusion.refs_0_.refs_3_.refs_4_.refs_2_
  38.6 1.7 broadcast_select_fusion
  40.3 1.5 collective-permute-start.4
  42.7 1.6 collective-permute-start.2
  44.3 1.1 dynamic-slice_bitcast_fusion.1
  45.4 1.6 dynamic-slice_bitcast_fusion
  47.1 13.8 %collective-permute-done.4 = bf16[256,3072]{1,0:T(8,128)(2,1)S(1)} collective-permute-done((bf16[256,3072]{1,0:T(8,128)(2,1)}, bf16[256,3072]{1,0:T(8,128)(2,1)S(1)}, u32[]{:S(2)}, u32[]{:S(2)}) %collective-permute-start.4) | collective-permute-done | bytes 1572896 | tf_op jit(solution)/shard_map/ppermute | solution.py:663
  61.0 1.6 collective-permute-start.6
  62.6 1.4 broadcast_select_fusion.2
  64.0 2.3 maximum_select_fusion
  66.3 1.5 collective-permute-start.8
  67.8 13.3 %collective-permute-done.6 = bf16[128,3072]{1,0:T(8,128)(2,1)} collective-permute-done((bf16[128,3072]{1,0:T(8,128)(2,1)S(1)}, bf16[128,3072]{1,0:T(8,128)(2,1)}, u32[]{:S(2)}, u32[]{:S(2)}) %collective-permute-start.6) | collective-permute-done | bytes 786464 | tf_op jit(solution)/shard_map/ppermute | solution.py:667
  82.4 1.3 collective-permute-done.7.refs_11_.refs_14_.refs_15_.refs_17_.refs_20_
  83.7 11.1 %layer_in_0.1 = (bf16[512,4608]{1,0:T(8,128)(2,1)}, f32[128,1536]{1,0:T(8,128)}) custom-call(s32[6]{0:T(128)} %stack.32.info, f32[1024,768]{1,0:T(8,128)} %fusion.refs_0_.refs_3_.refs_4_.refs_2_, f32[1,768]{1,0:T(1,128)} %get-tuple-element.99.refs_1_.refs_5_.refs_4_, bf16[1,768,2304]{2,1,0:T(8,128)(2,1)} %refs_3_.3, bf16[1,768,768]{2,1,0:T(8,128)(2,1)} %refs_12_.3, ...), custom_call_target="tpu_custom_call" | custom-call | flops 6039797760 | bytes 8653824 | tf_op jit(solution)/shard_map/layer_in_0/pallas_call | solution.py:434
  95.4 2.0 collective-permute-done.9.refs_1_
  97.5 4.9 %all-to-all-start.1 = ((bf16[4,2,128,768]{3,2,1,0:T(8,128)(2,1)}), bf16[4,2,128,768]{3,2,1,0:T(8,128)(2,1)}, u32[]{:S(2)}, u32[]{:S(2)}) async-start(bf16[4,2,128,768]{3,2,1,0:T(8,128)(2,1)} %param.11), calls=%async_computation.1 | async-start | bytes 3145728 | tf_op jit(solution)/shard_map/all_to_all | solution.py:735
  103.3 1.4 copy-done.3
  104.7 15.0 %layer_in_1.1 = (bf16[128,1536]{1,0:T(8,128)(2,1)}, f32[1024,768]{1,0:T(8,128)}, bf16[512,4608]{1,0:T(8,128)(2,1)}, f32[128,1536]{1,0:T(8,128)}) custom-call(s32[6]{0:T(128)} %stack.35.info, f32[128,1536]{1,0:T(8,128)} %get-tuple-element.49.refs_0_, f32[128,1536]{1,0:T(8,128)} %copy-done.6, ...), custom_call_target="tpu_custom_call" | custom-call | flops 6039797760 | bytes 18484224 | tf_op jit(solution)/shard_map/layer_in_1/pallas_call | solution.py:434
  120.5 1.8 collective-permute-done.11.refs_1_
  123.2 15.8 %layer_in_2.1 = (bf16[128,1536]{1,0:T(8,128)(2,1)}, f32[1024,768]{1,0:T(8,128)}, bf16[512,4608]{1,0:T(8,128)(2,1)}, f32[128,1536]{1,0:T(8,128)}) custom-call(s32[6]{0:T(128)} %stack.38.info, f32[128,1536]{1,0:T(8,128)} %get-tuple-element.54.refs_0_, f32[128,1536]{1,0:T(8,128)} %copy-done.7, bf16[512,4608]{1,0:T(8,128)(2,1)} %get-tuple-element.55.refs_2_.refs_8_.refs_3_, ...), custom_call_target="tpu_custom_call" | custom-call | flops 6039797760 | bytes 18484224 | tf_op jit(solution)/shard_map/layer_in_2/pallas_call | solution.py:434
  140.0 1.5 collective-permute-done.12.refs_1_
  142.4 19.1 %layer_in_3.1 = (bf16[128,1536]{1,0:T(8,128)(2,1)}, f32[1024,768]{1,0:T(8,128)}, bf16[512,4608]{1,0:T(8,128)(2,1)}, f32[256,1536]{1,0:T(8,128)}, bf16[512,1536]{1,0:T(8,128)(2,1)}) custom-call(s32[6]{0:T(128)} %stack.41.info, f32[128,1536]{1,0:T(8,128)} %get-tuple-element.57.refs_0_, f32[128,1536]{1,0:T(8,128)} %copy-done.8, ...), custom_call_target="tpu_custom_call" | custom-call | flops 6039797760 | bytes 22416384 | tf_op jit(solution)/shard_map/layer_in_3/pallas_call | solution.py:434
  161.7 3.5 %collective-permute-done.13.refs_1_ = f32[256,1536]{1,0:T(8,128)S(1)} collective-permute-done((f32[256,1536]{1,0:T(8,128)}, f32[256,1536]{1,0:T(8,128)S(1)}, u32[]{:S(2)}, u32[]{:S(2)}) %collective-permute-start.13) | collective-permute-done | bytes 1572896 | tf_op jit(solution)/shard_map/ppermute | solution.py:631
  165.2 1.2 copy-done.5
  166.4 21.3 %layer_back_3.1 = (f32[1,768]{1,0:T(1,128)}, f32[1024,768]{1,0:T(8,128)}, bf16[512,1536]{1,0:T(8,128)(2,1)}, f32[128,1536]{1,0:T(8,128)}, bf16[768,1536]{1,0:T(8,128)(2,1)}, /*index=5*/bf16[768,1536]{1,0:T(8,128)(2,1)}) custom-call(s32[6]{0:T(128)} %stack.41.info, f32[256,1536]{1,0:T(8,128)} %get-tuple-element.60.refs_0_, f32[256,1536]{1,0:T(8,128)} %copy-done.5, ...), custom_call_target="tpu_custom_call" | custom-call | flops 6039797760 | bytes 29104128 | tf_op jit(solution)/shard_map/layer_back_3/pallas_call | solution.py:434
  188.0 2.4 collective-permute-done.14.refs_1_
  191.2 20.9 %layer_back_2.1 = (f32[1,768]{1,0:T(1,128)}, f32[1024,768]{1,0:T(8,128)}, bf16[512,1536]{1,0:T(8,128)(2,1)}, f32[128,1536]{1,0:T(8,128)}, bf16[768,1536]{1,0:T(8,128)(2,1)}, /*index=5*/bf16[768,1536]{1,0:T(8,128)(2,1)}) custom-call(s32[6]{0:T(128)} %stack.38.info, ...), custom_call_target="tpu_custom_call", output_to_operand_aliasing={{4}: (10, {}), {5}: (11, {})} | custom-call | flops 6039797760 | bytes 34215936 | tf_op jit(solution)/shard_map/layer_back_2/pallas_call | solution.py:434
  212.6 2.1 collective-permute-done.15.refs_1_
  215.6 21.2 %layer_back_1.1 = (f32[1,768]{1,0:T(1,128)}, f32[1024,768]{1,0:T(8,128)}, bf16[512,1536]{1,0:T(8,128)(2,1)}, f32[128,1536]{1,0:T(8,128)}, bf16[768,1536]{1,0:T(8,128)(2,1)}, /*index=5*/bf16[768,1536]{1,0:T(8,128)(2,1)}) custom-call(s32[6]{0:T(128)} %stack.35.info, ...), custom_call_target="tpu_custom_call", output_to_operand_aliasing={{4}: (10, {}), {5}: (11, {})} | custom-call | flops 6039797760 | bytes 34215936 | tf_op jit(solution)/shard_map/layer_back_1/pallas_call | solution.py:434
  236.8 12.0 %early_back_0.1 = (bf16[1024,768]{1,0:T(8,128)(2,1)}, bf16[768,1536]{1,0:T(8,128)(2,1)}) custom-call(s32[6]{0:T(128)} %stack.32.info, bf16[128,1536]{1,0:T(8,128)(2,1)} %get-tuple-element.77.refs_2_.refs_0_, bf16[512,4608]{1,0:T(8,128)(2,1)} %get-tuple-element.52.refs_2_.refs_8_.refs_3_.refs_1_, ...), custom_call_target="tpu_custom_call", output_to_operand_aliasing={{1}: (7, {})} | custom-call | flops 3623878656 | bytes 19270656 | tf_op jit(solution)/shard_map/early_back_0/pallas_call | solution.py:434
  248.9 1.0 copy-done.15
  250.4 1.9 collective-permute-done.16.refs_1_
  253.2 11.5 %late_back_0.1 = (bf16[1024,1536]{1,0:T(8,128)(2,1)}, bf16[768,1536]{1,0:T(8,128)(2,1)}) custom-call(s32[6]{0:T(128)} %stack.32.info, f32[128,1536]{1,0:T(8,128)} %get-tuple-element.76.refs_0_, f32[128,1536]{1,0:T(8,128)} %copy-done.16, bf16[128,1536]{1,0:T(8,128)(2,1)} %get-tuple-element.77.refs_2_.refs_0_, ...), custom_call_target="tpu_custom_call", output_to_operand_aliasing={{1}: (7, {})} | custom-call | flops 3623878656 | bytes 17697792 | tf_op jit(solution)/shard_map/late_back_0/pallas_call | solution.py:434
  264.7 10.3 %gain_back_0.1 = f32[1,768]{1,0:T(1,128)} custom-call(s32[6]{0:T(128)} %stack.32.info, bf16[1024,1536]{1,0:T(8,128)(2,1)} %get-tuple-element.84.refs_0_, bf16[1024,768]{1,0:T(8,128)(2,1)} %get-tuple-element.85.refs_1_, f32[1024,768]{1,0:T(8,128)} %fusion.refs_0_.refs_3_.refs_4_.refs_2_, bf16[1,768,2304]{2,1,0:T(8,128)(2,1)} %refs_3_.3), custom_call_target="tpu_custom_call" | custom-call | flops 3623878656 | bytes 7867392 | tf_op jit(solution)/shard_map/gain_back_0/pallas_call | solution.py:434
  277.0 2.0 collective-permute-start.18
  279.0 1.6 collective-permute-done.18
  280.6 2.9 collective-permute-start.19
  283.5 1.6 collective-permute-done.19
  285.7 6.7 %reduce-scatter.5.cloned.1.call-done = bf16[96,1536]{1,0:T(8,128)(2,1)} async-done(((bf16[768,1536]{1,0:T(8,128)(2,1)}), bf16[96,1536]{1,0:T(8,128)(2,1)}) %reduce-scatter.5.cloned.1.call-update) | async-done | bytes 294928 | tf_op jit(solution)/shard_map/reduce_scatter | solution.py:783
  293.4 1.0 convert_element_type.8
  295.2 35.2 %reduce-scatter.3.cloned.1.call-done = bf16[96,1536]{1,0:T(8,128)(2,1)} async-done(((bf16[768,1536]{1,0:T(8,128)(2,1)}), bf16[96,1536]{1,0:T(8,128)(2,1)}) %reduce-scatter.3.cloned.1.call-update) | async-done | bytes 294928 | tf_op jit(solution)/shard_map/reduce_scatter | solution.py:785
  330.4 1.0 convert_element_type.7
  (73 shorter events, 16.7 us)
Async XLA Ops:
  7.2 29.1 %copy-start = (bf16[33,768]{1,0:T(8,128)(2,1)S(1)}, bf16[33,768]{1,0:T(8,128)(2,1)}, u32[]{:S(2)}) copy-start(bf16[33,768]{1,0:T(8,128)(2,1)} %param.7) | copy-start | bytes 152068
  8.3 10.5 %copy-start.11 = (f32[1,768]{1,0:T(1,128)S(1)}, f32[1,768]{1,0:T(1,128)}, u32[]{:S(2)}) copy-start(f32[1,768]{1,0:T(1,128)} %param.8) | copy-start | bytes 9220
  11.0 27.6 %collective-permute-start = (bf16[256,3072]{1,0:T(8,128)(2,1)}, bf16[256,3072]{1,0:T(8,128)(2,1)S(1)}, u32[]{:S(2)}, u32[]{:S(2)}) collective-permute-start(bf16[256,3072]{1,0:T(8,128)(2,1)} %maximum_maximum_fusion), channel_id=1, source_target_pairs={{0,8},{1,17},{2,10},{3,19},{4,12},{5,21},{6,14},{7,23},{8,0},{9,25... | collective-permute-start | bytes 4718600 | tf_op jit(solution)/shard_map/ppermute | solution.py:663
  13.9 22.3 %all-to-all-start = ((s32[4,2,128]{2,1,0:T(2,128)}), s32[4,2,128]{2,1,0:T(2,128)S(1)}, u32[]{:S(2)}, u32[]{:S(2)}) async-start(s32[4,2,128]{2,1,0:T(2,128)} %param.6), calls=%async_computation | async-start | bytes 8192 | tf_op jit(solution)/shard_map/all_to_all | solution.py:734
  38.6 24.0 %copy-start.2 = (bf16[256,3072]{1,0:T(8,128)(2,1)}, bf16[256,3072]{1,0:T(8,128)(2,1)S(1)}, u32[]{:S(2)}) copy-start(bf16[256,3072]{1,0:T(8,128)(2,1)S(1)} %collective-permute-done) | copy-start | bytes 4718596
  40.3 20.6 %collective-permute-start.4 = (bf16[256,3072]{1,0:T(8,128)(2,1)}, bf16[256,3072]{1,0:T(8,128)(2,1)S(1)}, u32[]{:S(2)}, u32[]{:S(2)}) collective-permute-start(bf16[256,3072]{1,0:T(8,128)(2,1)} %broadcast_select_fusion), channel_id=1, source_target_pairs={{0,16},{1,9},{2,18},{3,11},{4,20},{5,13},{6,22},{7,15},{8,24},{9,1... | collective-permute-start | bytes 4718600 | tf_op jit(solution)/shard_map/ppermute | solution.py:663
  42.7 19.9 %collective-permute-start.2 = (bf16[128,3072]{1,0:T(8,128)(2,1)}, bf16[128,3072]{1,0:T(8,128)(2,1)}, u32[]{:S(2)}, u32[]{:S(2)}) collective-permute-start(bf16[128,3072]{1,0:T(8,128)(2,1)} %slice.42), channel_id=1, source_target_pairs={{0,2},{1,3},{2,0},{3,1},{4,6},{5,7},{6,4},{7,5},{8,10},{9,11},{10,... | collective-permute-start | bytes 2359304 | tf_op jit(solution)/shard_map/ppermute | solution.py:667
  47.0 35.4 %collective-permute-start.1 = (bf16[1,256,3072]{2,1,0:T(8,128)(2,1)S(1)}, bf16[1,256,3072]{2,1,0:T(8,128)(2,1)}, u32[]{:S(2)}, u32[]{:S(2)}) collective-permute-start(bf16[1,256,3072]{2,1,0:T(8,128)(2,1)S(1)} %bitcast.38), channel_id=1, source_target_pairs={{0,1},{1,0},{2,3},{3,2},{4,5},{5,4},{6,7},{7,6},{8,9},{9,8},{10,11... | collective-permute-start | bytes 4718600 | tf_op jit(solution)/shard_map/ppermute | solution.py:697
  60.9 3.1 copy-start.4
  60.9 21.5 %collective-permute-start.5 = (bf16[1,256,3072]{2,1,0:T(8,128)(2,1)S(1)}, bf16[1,256,3072]{2,1,0:T(8,128)(2,1)}, u32[]{:S(2)}, u32[]{:S(2)}) collective-permute-start(bf16[1,256,3072]{2,1,0:T(8,128)(2,1)S(1)} %bitcast.46), channel_id=1, source_target_pairs={{0,1},{1,0},{2,3},{3,2},{4,5},{5,4},{6,7},{7,6},{8,9},{9,8},{10,11... | collective-permute-start | bytes 4718600 | tf_op jit(solution)/shard_map/ppermute | solution.py:697
  61.0 20.1 %collective-permute-start.6 = (bf16[128,3072]{1,0:T(8,128)(2,1)S(1)}, bf16[128,3072]{1,0:T(8,128)(2,1)}, u32[]{:S(2)}, u32[]{:S(2)}) collective-permute-start(bf16[128,3072]{1,0:T(8,128)(2,1)S(1)} %slice.43), channel_id=1, source_target_pairs={{0,2},{1,3},{2,0},{3,1},{4,6},{5,7},{6,4},{7,5},{8,10},{9,11},{10,... | collective-permute-start | bytes 2359304 | tf_op jit(solution)/shard_map/ppermute | solution.py:667
  66.3 29.2 %collective-permute-start.8 = (bf16[384,3072]{1,0:T(8,128)(2,1)}, bf16[384,3072]{1,0:T(8,128)(2,1)}, u32[]{:S(2)}, u32[]{:S(2)}) collective-permute-start(bf16[384,3072]{1,0:T(8,128)(2,1)} %maximum_select_fusion), channel_id=1, source_target_pairs={{0,16},{1,9},{2,18},{3,11},{4,20},{5,13},{6,22},{7,15},{8,24},{9,1... | collective-permute-start | bytes 7077896 | tf_op jit(solution)/shard_map/ppermute | solution.py:663
  67.8 14.6 %collective-permute-start.3 = (bf16[1,128,3072]{2,1,0:T(8,128)(2,1)}, bf16[1,128,3072]{2,1,0:T(8,128)(2,1)}, u32[]{:S(2)}, u32[]{:S(2)}) collective-permute-start(bf16[1,128,3072]{2,1,0:T(8,128)(2,1)} %bitcast.17.refs_6_.refs_9_.refs_10_.refs_12_.refs_15_), channel_id=1, source_target_pairs={{0,1},{1,0},{2,3},{3,2},{4,5},{5,4},{6,7},{7,6},{8,9},{9,8},{10,11... | collective-permute-start | bytes 2359304 | tf_op jit(solution)/shard_map/ppermute | solution.py:697
  81.1 2.6 collective-permute-start.7
  94.8 2.6 collective-permute-start.9
  97.4 5.9 %copy-start.6 = (f32[128,1536]{1,0:T(8,128)}, f32[128,1536]{1,0:T(8,128)S(1)}, u32[]{:S(2)}) copy-start(f32[128,1536]{1,0:T(8,128)S(1)} %collective-permute-done.9.refs_1_) | copy-start | bytes 2359300
  97.4 5.9 %collective-permute-start.10 = (bf16[1,384,3072]{2,1,0:T(8,128)(2,1)}, bf16[1,384,3072]{2,1,0:T(8,128)(2,1)S(1)}, u32[]{:S(2)}, u32[]{:S(2)}) collective-permute-start(bf16[1,384,3072]{2,1,0:T(8,128)(2,1)} %bitcast.22.refs_15_.refs_16_.refs_18_.refs_21_), channel_id=1, source_target_pairs={{0,1},{1,0},{2,3},{3,2},{4,5},{5,4},{6,7},{7,6},{8,9},{9,8},{10,11... | collective-permute-start | bytes 7077896 | tf_op jit(solution)/shard_map/ppermute | solution.py:697
  97.5 42.5 %all-to-all-start.1 = ((bf16[4,2,128,768]{3,2,1,0:T(8,128)(2,1)}), bf16[4,2,128,768]{3,2,1,0:T(8,128)(2,1)}, u32[]{:S(2)}, u32[]{:S(2)}) async-start(bf16[4,2,128,768]{3,2,1,0:T(8,128)(2,1)} %param.11), calls=%async_computation.1 | async-start | bytes 3145728 | tf_op jit(solution)/shard_map/all_to_all | solution.py:735
  102.4 190.1 %reduce-scatter.5.cloned.1.call-start = ((), (), s32[]{:S(2)}) async-start(), calls=%async_computation.5 | async-start | bytes 2654208 | tf_op jit(solution)/shard_map/reduce_scatter | solution.py:783
  103.3 1.4 copy-start.3
  119.7 2.6 collective-permute-start.11
  122.3 0.9 copy-start.7
  139.0 2.6 collective-permute-start.12
  141.5 0.9 copy-start.8
  161.5 3.7 %collective-permute-start.13 = (f32[256,1536]{1,0:T(8,128)}, f32[256,1536]{1,0:T(8,128)S(1)}, u32[]{:S(2)}, u32[]{:S(2)}) collective-permute-start(f32[256,1536]{1,0:T(8,128)} %get-tuple-element.60.refs_0_), channel_id=1, source_target_pairs={{0,1},{1,0},{2,3},{3,2},{4,5},{5,4},{6,7},{7,6},{8,9},{9,8},{10,11... | collective-permute-start | bytes 4718600 | tf_op jit(solution)/shard_map/ppermute | solution.py:631
  165.2 1.2 copy-start.5
  187.8 2.6 collective-permute-start.14
  190.3 0.9 copy-start.10
  212.1 2.6 collective-permute-start.15
  214.7 0.9 copy-start.9
  248.8 1.1 copy-start.15
  248.9 81.5 %reduce-scatter.3.cloned.1.call-start = ((), (), s32[]{:S(2)}) async-start(), calls=%async_computation.4 | async-start | bytes 2654208 | tf_op jit(solution)/shard_map/reduce_scatter | solution.py:785
  250.0 2.3 collective-permute-start.16
  252.3 0.9 copy-start.16
  264.7 10.3 %copy-start.12 = (f32[1,768]{1,0:T(1,128)S(1)}, f32[1,768]{1,0:T(1,128)}, u32[]{:S(2)}) copy-start(f32[1,768]{1,0:T(1,128)} %get-tuple-element.88) | copy-start | bytes 9220
  264.7 10.3 %copy-start.13 = (f32[1,768]{1,0:T(1,128)S(1)}, f32[1,768]{1,0:T(1,128)}, u32[]{:S(2)}) copy-start(f32[1,768]{1,0:T(1,128)} %get-tuple-element.87) | copy-start | bytes 9220
  264.7 10.3 %copy-start.14 = (f32[1,768]{1,0:T(1,128)S(1)}, f32[1,768]{1,0:T(1,128)}, u32[]{:S(2)}) copy-start(f32[1,768]{1,0:T(1,128)} %get-tuple-element.86) | copy-start | bytes 9220
  275.8 1.2 collective-permute-start.17
  277.0 3.6 %collective-permute-start.18 = (f32[1,768]{1,0:T(1,128)S(1)}, f32[1,768]{1,0:T(1,128)S(1)}, u32[]{:S(2)}, u32[]{:S(2)}) collective-permute-start(f32[1,768]{1,0:T(1,128)S(1)} %add.94), channel_id=1, source_target_pairs={{0,2},{1,3},{2,0},{3,1},{4,6},{5,7},{6,4},{7,5},{8,10},{9,11},{10,... | collective-permute-start | bytes 9224 | tf_op jit(solution)/shard_map/ppermute | solution.py:790
  280.6 4.5 %collective-permute-start.19 = (f32[1,768]{1,0:T(1,128)S(1)}, f32[1,768]{1,0:T(1,128)S(1)}, u32[]{:S(2)}, u32[]{:S(2)}) collective-permute-start(f32[1,768]{1,0:T(1,128)S(1)} %add.95), channel_id=1, source_target_pairs={{0,4},{1,5},{2,6},{3,7},{4,0},{5,1},{6,2},{7,3},{8,12},{9,13},{10,... | collective-permute-start | bytes 9224 | tf_op jit(solution)/shard_map/ppermute | solution.py:790
  285.1 47.2 %copy-start.1 = (bf16[33,768]{1,0:T(8,128)(2,1)S(1)}, bf16[33,768]{1,0:T(8,128)(2,1)}, u32[]{:S(2)}) copy-start(bf16[33,768]{1,0:T(8,128)(2,1)} %param.7) | copy-start | bytes 152068
Sparse Core Ops, SparseCore 0:
  249.0 43.4 reduce-scatter.4
  294.8 35.5 reduce-scatter.2

commit v4 on v3

--- a/solution.py
+++ b/solution.py
@@ -12,6 +12,7 @@
 HEAD_DIM = 64
 PACK = 2
 BLOCKS = 3
+TILE = 256
 DIRECT, ACROSS, FULL = range(3)
 F32 = jnp.float32
 BF16 = jnp.bfloat16
@@ -22,6 +23,12 @@
 
 def mm(a, b):
     return jnp.dot(a, b, preferred_element_type=F32)
+
+
+def column_loop(columns, body):
+    @pl.loop(0, columns // TILE)
+    def _(n):
+        body(pl.multiple_of(n * TILE, TILE))
 
 
 def mm_nt(a, b):
@@ -53,8 +60,8 @@
                 for r in range(PACK)
             ]
             for n, block in enumerate(regroup(blocks)):
-                at = (first + p * PACK + n) * width
-                out[pair * seq : (pair + 1) * seq, at : at + width] = block
+                at = pl.multiple_of(first + (p * PACK + n) * width, width)
+                out[pair * seq : (pair + 1) * seq, pl.ds(at, width)] = block
 
 
 class Weights:
@@ -171,7 +178,7 @@
     qkv_out, score_out = next(it), next(it)
     if has_top:
         dmix_out = next(it)
-    wq, sem_q = next(it), next(it)
+    wq, sem_q, h = next(it), next(it), next(it)
     if has_prev:
         wo, sem_o, mixed = next(it), next(it), next(it)
     if has_top:
@@ -201,19 +208,31 @@
     if has_prev:
         mix(probs_out, v_prev, 0, mixed, 0, None, seq)
         pl.when(step == 0)(get_o.wait)
-        x = x_in[...] + mm(mixed[...], wo[...])
-        x_out[...] = x
-    else:
-        x = x_in[...]
-    hat, _ = norm_parts(x)
-    h = (hat * gain[...]).astype(BF16)
+
+        @functools.partial(column_loop, width)
+        def _(at):
+            cols = pl.ds(at, TILE)
+            x_out[:, cols] = x_in[:, cols] + mm(mixed[...], wo[:, cols])
+
+    hat, _ = norm_parts(x_out[...] if has_prev else x_in[...])
+    h[...] = (hat * gain[...]).astype(BF16)
     pl.when(step == 0)(get_q.wait)
-    pack_rows(mm(h, wq[...]).astype(BF16), qkv_out, 0, seq)
+
+    @functools.partial(column_loop, 3 * width)
+    def _(at):
+        part = mm(h[...], wq[:, pl.ds(at, TILE)]).astype(BF16)
+        pack_rows(part, qkv_out, PACK * at, seq)
+
     begin = step == 0
     scores(qkv_out, 0, qkv_out, HEADS, score_out, 0, seq, begin)
     if has_top:
         pl.when(step == 0)(get_t.wait)
-        pack_rows(mm_nt(top[...], wt[...]).astype(BF16), dmix_out, 0, seq)
+
+        @functools.partial(column_loop, width)
+        def _(at):
+            part = mm_nt(top[...], wt[pl.ds(at, TILE), :]).astype(BF16)
+            pack_rows(part, dmix_out, PACK * at, seq)
+
         scores(dmix_out, 0, qkv_out, 2 * HEADS, score_out, seq, seq, begin)
 
 
@@ -229,21 +248,24 @@
         gain_out[...] += part
 
 
-def add_product(a, b, total, column, step, steps, staged):
-    at = slice(column, column + b.shape[1])
-    part = lax.dot_general(a, b, TN, preferred_element_type=F32)
-
-    @pl.when(step == 0)
-    def _():
-        total[:, at] = part
-
-    @pl.when((step > 0) & (step < steps - 1))
-    def _():
-        total[:, at] += part
-
-    @pl.when(step == steps - 1)
-    def _():
-        staged[:, at] = ((total[:, at] if steps > 1 else 0.0) + part).astype(BF16)
+def add_product(a, b, first, columns, total, place, step, steps, staged):
+    @functools.partial(column_loop, columns)
+    def _(at):
+        there = pl.ds(pl.multiple_of(place + at, TILE), TILE)
+        right = b[:, pl.ds(pl.multiple_of(first + at, TILE), TILE)].astype(BF16)
+        part = lax.dot_general(a[...], right, TN, preferred_element_type=F32)
+
+        @pl.when(step == 0)
+        def _():
+            total[:, there] = part
+
+        @pl.when((step > 0) & (step < steps - 1))
+        def _():
+            total[:, there] += part
+
+        @pl.when(step == steps - 1)
+        def _():
+            staged[:, there] = ((total[:, there] if steps > 1 else 0.0) + part).astype(BF16)
 
 
 def logit_grads(probs, sa, sb, first, seq, dl, dlt):
@@ -274,7 +296,7 @@
     stages = take_stages(it, layout)
     gain_out, dy_out, dmix_out, score_out = [next(it) for _ in range(4)]
     grad_a, grad_b = next(it), next(it)
-    dl, dlt, pt, dqkv, mixed = [next(it) for _ in range(5)]
+    dl, dlt, pt, dqkv, d_hs, mixed = [next(it) for _ in range(6)]
     total_a, total_b, staged_a, staged_b, sem_g = [next(it) for _ in range(5)]
     wq, sem_q, wo, sem_o = [next(it) for _ in range(4)]
     if is_top:
@@ -301,7 +323,12 @@
     mix(dlt, qkv, 0, dqkv, width, scale, seq)
     mix(pt, dmix, 0, dqkv, 2 * width, None, seq)
     pl.when(step == 0)(get_q.wait)
-    d_h = mm_nt(dqkv[...], wq[...]).astype(BF16).astype(F32)
+
+    @functools.partial(column_loop, width)
+    def _(at):
+        d_hs[:, pl.ds(at, TILE)] = mm_nt(dqkv[...], wq[pl.ds(at, TILE), :]).astype(BF16)
+
+    d_h = d_hs[...].astype(F32)
     hat, rstd = norm_parts(x_in[...])
     add_gain(gain_out, d_h, hat, step)
     d_hat = d_h * gain[...]
@@ -309,17 +336,23 @@
     mean_dh = jnp.mean(d_hat * hat, axis=-1, keepdims=True)
     d_x = dy[...].astype(F32) + rstd * (d_hat - mean_d - hat * mean_dh)
     dy_out[...] = d_x
+    d_hs[...] = d_x.astype(BF16)
     pl.when(step == 0)(get_o.wait)
-    pack_rows(mm_nt(d_x.astype(BF16), wo[...]).astype(BF16), dmix_out, 0, seq)
+
+    @functools.partial(column_loop, width)
+    def _(at):
+        part = mm_nt(d_hs[...], wo[pl.ds(at, TILE), :]).astype(BF16)
+        pack_rows(part, dmix_out, PACK * at, seq)
+
     scores(dmix_out, 0, v_prev, 0, score_out, 0, seq, step == 0)
 
     @pl.when(own)
     def _():
         mix(probs, qkv, 2 * HEADS, mixed, 0, None, seq)
-        h = (norm_parts(x_in[...])[0] * gain[...]).astype(BF16)
-        add_product(mixed[...], dy[...].astype(BF16), total_a, 0, step, steps, staged_a)
-        add_product(h, dqkv[:, 2 * width :], total_a, width, step, steps, staged_a)
-        add_product(h, dqkv[:, : 2 * width], total_b, 0, step, steps, staged_b)
+        add_product(mixed, dy, 0, width, total_a, 0, step, steps, staged_a)
+        mixed[...] = (norm_parts(x_in[...])[0] * gain[...]).astype(BF16)
+        add_product(mixed, dqkv, 2 * width, width, total_a, width, step, steps, staged_a)
+        add_product(mixed, dqkv, 0, 2 * width, total_b, 0, step, steps, staged_b)
 
     @pl.when(own & (step == steps - 1))
     def _():
@@ -346,9 +379,9 @@
 
         mix(probs, v, 0, mixed, 0, None, seq)
         mix(pt, dmix, 0, dv_out, 0, None, seq)
-        h = (norm_parts(x_in[...])[0] * gain[...]).astype(BF16)
-        add_product(mixed[...], dy[...].astype(BF16), total, 0, step, steps, staged)
-        add_product(h, dv_out[...], total, width, step, steps, staged)
+        add_product(mixed, dy, 0, width, total, 0, step, steps, staged)
+        mixed[...] = (norm_parts(x_in[...])[0] * gain[...]).astype(BF16)
+        add_product(mixed, dv_out, 0, width, total, width, step, steps, staged)
 
     @pl.when(own & (step == steps - 1))
     def _():
@@ -358,7 +391,7 @@
 
 
 def late_kernel(info, *refs, layout, scale, seq, width, steps):
-    sa, sb, probs, qk, x_in, gain, _, dqk_out, grad_b, dl, dlt, total, staged, sem = refs
+    sa, sb, probs, qk, x_in, gain, _, dqk_out, grad_b, dl, dlt, h, total, staged, sem = refs
     step = pl.program_id(0)
     own = info[0] == 0
 
@@ -368,10 +401,10 @@
         def _():
             logit_grads(probs, sa, sb, 0, seq, dl, dlt)
 
-        h = (norm_parts(x_in[...])[0] * gain[...]).astype(BF16)
+        h[...] = (norm_parts(x_in[...])[0] * gain[...]).astype(BF16)
         mix(dl, qk, HEADS, dqk_out, 0, scale, seq)
         mix(dlt, qk, 0, dqk_out, width, scale, seq)
-        add_product(h, dqk_out[...], total, 0, step, steps, staged)
+        add_product(h, dqk_out, 0, 2 * width, total, 0, step, steps, staged)
 
     @pl.when(own & (step == steps - 1))
     def _():
@@ -381,7 +414,7 @@
 
 
 def gain_kernel(info, *refs, layout, width):
-    dqk, dv, x_in, own_q, gain_out, wq, sem = refs
+    dqk, dv, x_in, own_q, gain_out, d_h, wq, sem = refs
     step = pl.program_id(0)
 
     @pl.when(info[0] == 0)
@@ -393,8 +426,14 @@
             copy.wait()
 
         hat, _ = norm_parts(x_in[...])
-        d_h = mm_nt(dqk[...], wq[:, : 2 * width]) + mm_nt(dv[...], wq[:, 2 * width :])
-        add_gain(gain_out, d_h.astype(BF16).astype(F32), hat, step)
+
+        @functools.partial(column_loop, width)
+        def _(at):
+            rows = pl.ds(at, TILE)
+            part = mm_nt(dqk[...], wq[rows, : 2 * width]) + mm_nt(dv[...], wq[rows, 2 * width :])
+            d_h[:, rows] = part.astype(BF16)
+
+        add_gain(gain_out, d_h[...].astype(F32), hat, step)
 
 
 class Chain:
@@ -477,7 +516,7 @@
             (self.shape(n // PACK, 3 * PACK * width, BF16), self.packed(3 * HEADS)),
             (self.shape(score_rows, hw, F32), self.whole(score_rows, hw)),
         ]
-        scratch = self.weight_scratch(3)
+        scratch = self.weight_scratch(3) + [pltpu.VMEM((self.chunk, width), BF16)]
         if prev is not None:
             ins = [
                 (prev[0], self.whole(seq, hw)),
@@ -534,7 +573,7 @@
             self.grad_out(),
         ]
         scratch = [square] * 3
-        scratch += [pltpu.VMEM((self.chunk, lanes * width), BF16) for lanes in (3, 1)]
+        scratch += [pltpu.VMEM((self.chunk, lanes * width), BF16) for lanes in (3, 1, 1)]
         scratch += self.grad_scratch(2) + self.weight_scratch(3) + self.weight_scratch(1)
         if is_top:
             scratch.append(square)
@@ -600,7 +639,9 @@
             0,
             ins,
             outs,
-            [pltpu.VMEM((seq, hw), BF16)] * 2 + self.grad_scratch(1),
+            [pltpu.VMEM((seq, hw), BF16)] * 2
+            + [pltpu.VMEM((self.chunk, width), BF16)]
+            + self.grad_scratch(1),
             2 * n * width * width * 3,
             carried=(grad,),
             own=(),
@@ -616,7 +657,7 @@
             0,
             [(dqk, self.tile(2 * width)), (dv, self.tile(width)), (x, self.tile(width))],
             [(self.shape(1, width, F32), self.whole(1, width))],
-            self.weight_scratch(3),
+            [pltpu.VMEM((self.chunk, width), BF16)] + self.weight_scratch(3),
             2 * n * width * width * 3,
             own=self.own[:1],
         )[0]
@@ -631,6 +672,22 @@
         other = lax.ppermute(value, "row", [(r, r ^ bit) for r in range(n_row)])
         bit *= 2
     return value, other
+
+
+def sum_rows(grad, place, n_row, n_group):
+    rows = grad.shape[0] // n_row
+    spans = [1 << n for n in range(n_row.bit_length() - 1)]
+    value = grad.reshape(n_row, rows, grad.shape[1])
+    for bit in spans:
+        mine = (place // bit) % 2
+        pair = value.reshape(value.shape[0] // 2, 2, *value.shape[1:])
+        keep = lax.dynamic_index_in_dim(pair, mine, 1, keepdims=False)
+        send = lax.dynamic_index_in_dim(pair, 1 - mine, 1, keepdims=False)
+        other = lax.ppermute(
+            send.astype(BF16), "row", [(r, r ^ bit) for r in range(n_row)]
+        )
+        value = keep.astype(F32) + other.astype(F32)
+    return value[0]
 
 
 class Fetched:
@@ -669,20 +726,17 @@
     def halves(self, got, across):
         return [(DIRECT, self.share(got)), (ACROSS, self.share(across))]
 
-    def second(self, *ready):
-        second, *ready = lax.optimization_barrier(
-            (jnp.where(self.to_last, self.got, self.mine), *ready)
-        )
+    def second(self, x, gains):
+        second, x = lax.optimization_barrier((jnp.where(self.to_last, self.got, self.mine), x))
         second = self.hop(second, 2)
         self.stages.append(self.halves(second, self.cross(second)))
         low = jnp.where(self.half == 0, self.got[: self.block], self.across)
         high = jnp.where(self.half == 0, self.across, self.got[: self.block])
         relayed = jnp.concatenate([low, high, self.got[self.block :]], axis=0)
-        third, _ = lax.optimization_barrier(
-            (jnp.where(self.to_last, self.own_block(0, BLOCKS), relayed), second)
-        )
+        third = jnp.where(self.to_last, self.own_block(0, BLOCKS), relayed)
+        third, gains, _ = lax.optimization_barrier((third, gains, second))
         self.third = self.hop(third, 2)
-        return ready
+        return x, gains
 
     def finish(self, ready):
         third, ready = lax.optimization_barrier((self.third, ready))
@@ -775,14 +829,11 @@
             grads,
         )
         scores = group_swap(part, n_row, n_group)
-    sum_rows = functools.partial(
-        lax.psum_scatter, axis_name="row", scatter_dimension=0, tiled=True
-    )
     gain = gains[0][None]
     d_v, grad_a = chain.early(probs[0], qkvs[0], dmix, xs[0], gain, dy, grads[0])
-    grad_a = sum_rows(grad_a).astype(F32)
+    grad_a = sum_rows(grad_a, place, n_row, n_group)
     d_qk, grad_b = chain.late(scores, probs[0], qkvs[0], xs[0], gain, grads[1])
-    grad_b = sum_rows(grad_b).astype(F32)
+    grad_b = sum_rows(grad_b, place, n_row, n_group)
     gain_parts[0] = chain.gain_grad(d_qk, d_v, xs[0])
     g_gain = lax.select_n(section, *gain_parts)
     bit = 1

time: 345 us -> 365 us (1.058)
  Pallas kernels: 158 us -> 186 us
  between operations: 14.9 us -> 1.26 us
  waiting for transfers between devices: 90.3 us -> 82.9 us
  starting transfers between devices: 26.5 us -> 32.8 us
    reduce_scatter x2 -> x0, waiting for transfers between devices: 42 us -> none  [the longest x1 35.2 us: local(): grad_b = sum_rows(grad_b).astype(F32)]
    ppermute x0 -> x6, waiting for transfers between devices: none -> 39.1 us  [sum_rows(): lax.ppermute(send.astype(BF16), 'row', [(r, r ^ bit) for r in range(n_row)])]
    pallas_call x10, Pallas kernels: 158 us -> 186 us  [call(): pl.pallas_call(functools.partial(body, layout=layout), name=name, out_sha...]
    ppermute x3, waiting for transfers between devices: 14.2 us -> 5.84 us  [hop(): return lax.ppermute(value, ('section', 'row'), perm)]
    ppermute x0 -> x6, starting transfers between devices: none -> 5.7 us  [sum_rows(): lax.ppermute(send.astype(BF16), 'row', [(r, r ^ bit) for r in range(n_row)])]
    all_to_all x1, waiting for transfers between devices: 0.01 us -> 5.57 us  [local(): tok = exchange(tokens).reshape(-1)]
    squeeze x0 -> x2, local copies, waits for them, and re-layouts: none -> 4.78 us  [sum_rows(): send = lax.dynamic_index_in_dim(pair, 1 - mine, 1, keepdims=False)]
    add x0 -> x4, other arithmetic: none -> 3.69 us  [sum_rows(): value = keep.astype(F32) + other.astype(F32)]
  transfers between devices with their start and end apart: 24 -> 28, of which waited for: 17 -> 16; matrix products, arithmetic and copies ran while one was open for 5% -> 7% of each run, Pallas kernels for 19% -> 27%
where the time goes in v4:
time: 365 us; the launch traced here: 360 us
  Pallas kernels  186 us (51%)
  waiting for transfers between devices  82.9 us (23%)
  starting transfers between devices  32.8 us (9%)
  local copies, waits for them, and re-layouts  22 us (6%)
  blocking collectives  19.9 us (5%)
  other arithmetic  12.7 us (3%)
    pallas_call x10, Pallas kernels, call(): pl.pallas_call(functools.partial(body, layout=layout), name=name, out_sha...  186 us
    ppermute x6, waiting for transfers between devices, sum_rows(): lax.ppermute(send.astype(BF16), 'row', [(r, r ^ bit) for r in range(n_row)])  39.1 us
    all_gather x1, blocking collectives, local(): gains = lax.all_gather(ln_gain[0], 'section', axis=0, tiled=False)  19.9 us
    ppermute x7, waiting for transfers between devices, group_swap(): other = lax.ppermute(value, 'row', [(r, r ^ bit) for r in range(n_row)])  14 us
    ppermute x2, waiting for transfers between devices, cross(): return lax.ppermute(value[:self.block], 'row', perm)  13 us
  transfers between devices with their start and end apart: 28, of which 16 were waited for; matrix products, arithmetic and copies ran while one was open for 7% of the time, Pallas kernels for 27%

profile of v4, /device:TPU:0, one launch (start us, length us, event | category | flops | bytes accessed | tf_op | source)
XLA Modules:
  0.0 360.2 jit_solution(793276073908100087)
XLA Ops:
  1.8 1.3 dynamic-slice_bitcast_fusion.5
  3.1 1.4 maximum_maximum_fusion
  4.5 2.9 collective-permute-start
  7.4 4.9 %all-to-all-start = ((s32[4,2,128]{2,1,0:T(2,128)}), s32[4,2,128]{2,1,0:T(2,128)S(1)}, u32[]{:S(2)}, u32[]{:S(2)}) async-start(s32[4,2,128]{2,1,0:T(2,128)} %param.6), calls=%async_computation | async-start | bytes 8192 | tf_op jit(solution)/shard_map/all_to_all | solution.py:788
  12.3 5.6 %all-to-all-done = s32[4,2,128]{2,1,0:T(2,128)S(1)} async-done(((s32[4,2,128]{2,1,0:T(2,128)}), s32[4,2,128]{2,1,0:T(2,128)S(1)}, u32[]{:S(2)}, u32[]{:S(2)}) %all-to-all-start) | async-done | bytes 4128 | tf_op jit(solution)/shard_map/all_to_all | solution.py:788
  17.8 2.3 fusion.2.refs_0_.refs_3_.refs_4_.refs_2_
  20.2 5.8 %collective-permute-done = bf16[256,3072]{1,0:T(8,128)(2,1)S(1)} collective-permute-done((bf16[256,3072]{1,0:T(8,128)(2,1)}, bf16[256,3072]{1,0:T(8,128)(2,1)S(1)}, u32[]{:S(2)}, u32[]{:S(2)}) %collective-permute-start) | collective-permute-done | bytes 1572896 | tf_op jit(solution)/shard_map/ppermute | solution.py:720
  26.0 1.7 broadcast_select_fusion
  27.7 2.1 collective-permute-start.2
  30.7 1.6 collective-permute-start.1
  32.3 19.9 %all-gather = f32[4,1,768]{2,1,0:T(1,128)S(1)} all-gather(f32[1,1,768]{2,1,0:T(1,128)S(1)} %bitcast.98), channel_id=1, replica_groups=mesh['section'=4,'row'=8] {'section'}, dimensions={0}, use_global_device_ids=true | all-gather | bytes 15360 | tf_op jit(solution)/shard_map/all_gather | solution.py:790
  53.2 1.6 dynamic-slice_bitcast_fusion
  55.5 1.6 collective-permute-start.6
  57.1 1.4 broadcast_select_fusion.2
  58.5 2.2 maximum_select_fusion
  60.7 1.5 collective-permute-start.8
  62.2 13.0 %collective-permute-done.6 = bf16[128,3072]{1,0:T(8,128)(2,1)} collective-permute-done((bf16[128,3072]{1,0:T(8,128)(2,1)S(1)}, bf16[128,3072]{1,0:T(8,128)(2,1)}, u32[]{:S(2)}, u32[]{:S(2)}) %collective-permute-start.6) | collective-permute-done | bytes 786464 | tf_op jit(solution)/shard_map/ppermute | solution.py:724
  77.8 15.5 %layer_in_0.1 = (bf16[512,4608]{1,0:T(8,128)(2,1)}, f32[128,1536]{1,0:T(8,128)}) custom-call(s32[6]{0:T(128)} %stack.32.info, f32[1024,768]{1,0:T(8,128)} %fusion.2.refs_0_.refs_3_.refs_4_.refs_2_, f32[1,768]{1,0:T(1,128)} %get-tuple-element.101.refs_1_.refs_5_.refs_4_, bf16[1,768,2304]{2,1,0:T(8,128)(2,1)} %refs_3_.3, bf16[1,768,768]{2,1,0:T(8,128)(2,1)} %refs_12_.3, ...), custom_call_target="tpu_custom_call" | custom-call | flops 6039797760 | bytes 8653824 | tf_op jit(solution)/shard_map/layer_in_0/pallas_call | solution.py:473
  93.5 2.4 collective-permute-done.9.refs_1_
  96.0 5.1 %all-to-all-start.1 = ((bf16[4,2,128,768]{3,2,1,0:T(8,128)(2,1)}), bf16[4,2,128,768]{3,2,1,0:T(8,128)(2,1)}, u32[]{:S(2)}, u32[]{:S(2)}) async-start(bf16[4,2,128,768]{3,2,1,0:T(8,128)(2,1)} %param.11), calls=%async_computation.1 | async-start | bytes 3145728 | tf_op jit(solution)/shard_map/all_to_all | solution.py:789
  101.7 1.4 copy-done.3
  103.1 19.6 %layer_in_1.1 = (bf16[128,1536]{1,0:T(8,128)(2,1)}, f32[1024,768]{1,0:T(8,128)}, bf16[512,4608]{1,0:T(8,128)(2,1)}, f32[128,1536]{1,0:T(8,128)}) custom-call(s32[6]{0:T(128)} %stack.35.info, f32[128,1536]{1,0:T(8,128)} %get-tuple-element.49.refs_0_, f32[128,1536]{1,0:T(8,128)} %copy-done.8, ...), custom_call_target="tpu_custom_call" | custom-call | flops 6039797760 | bytes 18484224 | tf_op jit(solution)/shard_map/layer_in_1/pallas_call | solution.py:473
  123.5 1.7 collective-permute-done.11.refs_1_
  126.1 20.4 %layer_in_2.1 = (bf16[128,1536]{1,0:T(8,128)(2,1)}, f32[1024,768]{1,0:T(8,128)}, bf16[512,4608]{1,0:T(8,128)(2,1)}, f32[128,1536]{1,0:T(8,128)}) custom-call(s32[6]{0:T(128)} %stack.38.info, f32[128,1536]{1,0:T(8,128)} %get-tuple-element.54.refs_0_, f32[128,1536]{1,0:T(8,128)} %copy-done.9, bf16[512,4608]{1,0:T(8,128)(2,1)} %get-tuple-element.55.refs_2_.refs_8_.refs_3_, ...), custom_call_target="tpu_custom_call" | custom-call | flops 6039797760 | bytes 18484224 | tf_op jit(solution)/shard_map/layer_in_2/pallas_call | solution.py:473
  147.2 1.8 collective-permute-done.12.refs_1_
  150.0 24.4 %layer_in_3.1 = (bf16[128,1536]{1,0:T(8,128)(2,1)}, f32[1024,768]{1,0:T(8,128)}, bf16[512,4608]{1,0:T(8,128)(2,1)}, f32[256,1536]{1,0:T(8,128)}, bf16[512,1536]{1,0:T(8,128)(2,1)}) custom-call(s32[6]{0:T(128)} %stack.41.info, f32[128,1536]{1,0:T(8,128)} %get-tuple-element.57.refs_0_, f32[128,1536]{1,0:T(8,128)} %copy-done.10, ...), custom_call_target="tpu_custom_call" | custom-call | flops 6039797760 | bytes 22416384 | tf_op jit(solution)/shard_map/layer_in_3/pallas_call | solution.py:473
  174.6 3.5 collective-permute-done.13.refs_1_
  179.3 21.7 %layer_back_3.1 = (f32[1,768]{1,0:T(1,128)}, f32[1024,768]{1,0:T(8,128)}, bf16[512,1536]{1,0:T(8,128)(2,1)}, f32[128,1536]{1,0:T(8,128)}, bf16[768,1536]{1,0:T(8,128)(2,1)}, /*index=5*/bf16[768,1536]{1,0:T(8,128)(2,1)}) custom-call(s32[6]{0:T(128)} %stack.41.info, f32[256,1536]{1,0:T(8,128)} %get-tuple-element.60.refs_0_, f32[256,1536]{1,0:T(8,128)} %copy-done.7, ...), custom_call_target="tpu_custom_call" | custom-call | flops 6039797760 | bytes 29104128 | tf_op jit(solution)/shard_map/layer_back_3/pallas_call | solution.py:473
  201.2 2.4 collective-permute-done.14.refs_1_
  204.5 21.4 %layer_back_2.1 = (f32[1,768]{1,0:T(1,128)}, f32[1024,768]{1,0:T(8,128)}, bf16[512,1536]{1,0:T(8,128)(2,1)}, f32[128,1536]{1,0:T(8,128)}, bf16[768,1536]{1,0:T(8,128)(2,1)}, /*index=5*/bf16[768,1536]{1,0:T(8,128)(2,1)}) custom-call(s32[6]{0:T(128)} %stack.38.info, ...), custom_call_target="tpu_custom_call", output_to_operand_aliasing={{4}: (10, {}), {5}: (11, {})} | custom-call | flops 6039797760 | bytes 34215936 | tf_op jit(solution)/shard_map/layer_back_2/pallas_call | solution.py:473
  226.3 2.2 collective-permute-done.15.refs_1_
  229.4 22.0 %layer_back_1.1 = (f32[1,768]{1,0:T(1,128)}, f32[1024,768]{1,0:T(8,128)}, bf16[512,1536]{1,0:T(8,128)(2,1)}, f32[128,1536]{1,0:T(8,128)}, bf16[768,1536]{1,0:T(8,128)(2,1)}, /*index=5*/bf16[768,1536]{1,0:T(8,128)(2,1)}) custom-call(s32[6]{0:T(128)} %stack.35.info, ...), custom_call_target="tpu_custom_call", output_to_operand_aliasing={{4}: (10, {}), {5}: (11, {})} | custom-call | flops 6039797760 | bytes 34215936 | tf_op jit(solution)/shard_map/layer_back_1/pallas_call | solution.py:473
  251.8 14.2 %early_back_0.1 = (bf16[1024,768]{1,0:T(8,128)(2,1)}, bf16[768,1536]{1,0:T(8,128)(2,1)}) custom-call(s32[6]{0:T(128)} %stack.32.info, bf16[128,1536]{1,0:T(8,128)(2,1)} %get-tuple-element.77.refs_2_.refs_0_, bf16[512,4608]{1,0:T(8,128)(2,1)} %get-tuple-element.52.refs_2_.refs_8_.refs_3_.refs_1_, ...), custom_call_target="tpu_custom_call", output_to_operand_aliasing={{1}: (7, {})} | custom-call | flops 3623878656 | bytes 19270656 | tf_op jit(solution)/shard_map/early_back_0/pallas_call | solution.py:473
  266.1 2.4 dynamic-slice_bitcast_fusion.1
  269.6 14.6 %late_back_0.1 = (bf16[1024,1536]{1,0:T(8,128)(2,1)}, bf16[768,1536]{1,0:T(8,128)(2,1)}) custom-call(s32[6]{0:T(128)} %stack.32.info, f32[128,1536]{1,0:T(8,128)} %get-tuple-element.76.refs_0_, f32[128,1536]{1,0:T(8,128)} %copy-done.17, bf16[128,1536]{1,0:T(8,128)(2,1)} %get-tuple-element.77.refs_2_.refs_0_, ...), custom_call_target="tpu_custom_call", output_to_operand_aliasing={{1}: (7, {})} | custom-call | flops 3623878656 | bytes 17697792 | tf_op jit(solution)/shard_map/late_back_0/pallas_call | solution.py:473
  284.2 2.4 dynamic-slice_bitcast_fusion.2
  286.9 12.5 %gain_back_0.1 = f32[1,768]{1,0:T(1,128)} custom-call(s32[6]{0:T(128)} %stack.32.info, bf16[1024,1536]{1,0:T(8,128)(2,1)} %get-tuple-element.84.refs_0_, bf16[1024,768]{1,0:T(8,128)(2,1)} %get-tuple-element.85.refs_1_, f32[1024,768]{1,0:T(8,128)} %fusion.2.refs_0_.refs_3_.refs_4_.refs_2_, bf16[1,768,2304]{2,1,0:T(8,128)(2,1)} %refs_3_.3), custom_call_target="tpu_custom_call" | custom-call | flops 3623878656 | bytes 7867392 | tf_op jit(solution)/shard_map/gain_back_0/pallas_call | solution.py:473
  301.3 2.0 collective-permute-start.24
  303.3 1.6 collective-permute-done.24
  304.9 2.9 collective-permute-start.25
  307.8 1.6 collective-permute-done.25
  310.0 1.8 convert_add_fusion
  311.8 2.1 collective-permute-start.21
  313.9 1.6 convert_add_fusion.1
  315.8 15.6 %collective-permute-done.21 = bf16[2,96,1536]{2,1,0:T(8,128)(2,1)S(1)} collective-permute-done((bf16[2,96,1536]{2,1,0:T(8,128)(2,1)S(1)}, bf16[2,96,1536]{2,1,0:T(8,128)(2,1)S(1)}, u32[]{:S(2)}, u32[]{:S(2)}) %collective-permute-start.21) | collective-permute-done | bytes 589856 | tf_op jit(solution)/shard_map/ppermute | solution.py:686
  331.5 2.0 collective-permute-start.22
  333.5 10.8 %collective-permute-done.18 = bf16[2,96,1536]{2,1,0:T(8,128)(2,1)S(1)} collective-permute-done((bf16[2,96,1536]{2,1,0:T(8,128)(2,1)S(1)}, bf16[2,96,1536]{2,1,0:T(8,128)(2,1)S(1)}, u32[]{:S(2)}, u32[]{:S(2)}) %collective-permute-start.18) | collective-permute-done | bytes 589856 | tf_op jit(solution)/shard_map/ppermute | solution.py:686
  346.3 12.7 %collective-permute-done.19 = bf16[1,96,1536]{2,1,0:T(8,128)(2,1)S(1)} collective-permute-done((bf16[1,96,1536]{2,1,0:T(8,128)(2,1)S(1)}, bf16[1,96,1536]{2,1,0:T(8,128)(2,1)S(1)}, u32[]{:S(2)}, u32[]{:S(2)}) %collective-permute-start.19) | collective-permute-done | bytes 294944 | tf_op jit(solution)/shard_map/ppermute | solution.py:686
  (90 shorter events, 22.0 us)
Async XLA Ops:
  0.6 17.2 %copy-start = (bf16[33,768]{1,0:T(8,128)(2,1)S(1)}, bf16[33,768]{1,0:T(8,128)(2,1)}, u32[]{:S(2)}) copy-start(bf16[33,768]{1,0:T(8,128)(2,1)} %param.7) | copy-start | bytes 152068
  4.5 21.5 %collective-permute-start = (bf16[256,3072]{1,0:T(8,128)(2,1)}, bf16[256,3072]{1,0:T(8,128)(2,1)S(1)}, u32[]{:S(2)}, u32[]{:S(2)}) collective-permute-start(bf16[256,3072]{1,0:T(8,128)(2,1)} %maximum_maximum_fusion), channel_id=1, source_target_pairs={{0,8},{1,17},{2,10},{3,19},{4,12},{5,21},{6,14},{7,23},{8,0},{9,25... | collective-permute-start | bytes 4718600 | tf_op jit(solution)/shard_map/ppermute | solution.py:720
  7.4 10.4 %all-to-all-start = ((s32[4,2,128]{2,1,0:T(2,128)}), s32[4,2,128]{2,1,0:T(2,128)S(1)}, u32[]{:S(2)}, u32[]{:S(2)}) async-start(s32[4,2,128]{2,1,0:T(2,128)} %param.6), calls=%async_computation | async-start | bytes 8192 | tf_op jit(solution)/shard_map/all_to_all | solution.py:788
  20.2 12.1 %copy-start.13 = (f32[1,768]{1,0:T(1,128)S(1)}, f32[1,768]{1,0:T(1,128)}, u32[]{:S(2)}) copy-start(f32[1,768]{1,0:T(1,128)} %param.8) | copy-start | bytes 9220
  26.0 31.1 %copy-start.2 = (bf16[256,3072]{1,0:T(8,128)(2,1)}, bf16[256,3072]{1,0:T(8,128)(2,1)S(1)}, u32[]{:S(2)}) copy-start(bf16[256,3072]{1,0:T(8,128)(2,1)S(1)} %collective-permute-done) | copy-start | bytes 4718596
  27.7 27.2 %collective-permute-start.2 = (bf16[256,3072]{1,0:T(8,128)(2,1)}, bf16[256,3072]{1,0:T(8,128)(2,1)S(1)}, u32[]{:S(2)}, u32[]{:S(2)}) collective-permute-start(bf16[256,3072]{1,0:T(8,128)(2,1)} %broadcast_select_fusion), channel_id=1, source_target_pairs={{0,16},{1,9},{2,18},{3,11},{4,20},{5,13},{6,22},{7,15},{8,24},{9,1... | collective-permute-start | bytes 4718600 | tf_op jit(solution)/shard_map/ppermute | solution.py:720
  30.7 26.4 %collective-permute-start.1 = (bf16[128,3072]{1,0:T(8,128)(2,1)}, bf16[128,3072]{1,0:T(8,128)(2,1)}, u32[]{:S(2)}, u32[]{:S(2)}) collective-permute-start(bf16[128,3072]{1,0:T(8,128)(2,1)} %slice.42), channel_id=1, source_target_pairs={{0,2},{1,3},{2,0},{3,1},{4,6},{5,7},{6,4},{7,5},{8,10},{9,11},{10,... | collective-permute-start | bytes 2359304 | tf_op jit(solution)/shard_map/ppermute | solution.py:724
  54.8 21.6 %collective-permute-start.3 = (bf16[1,256,3072]{2,1,0:T(8,128)(2,1)S(1)}, bf16[1,256,3072]{2,1,0:T(8,128)(2,1)}, u32[]{:S(2)}, u32[]{:S(2)}) collective-permute-start(bf16[1,256,3072]{2,1,0:T(8,128)(2,1)S(1)} %bitcast.72), channel_id=1, source_target_pairs={{0,1},{1,0},{2,3},{3,2},{4,5},{5,4},{6,7},{7,6},{8,9},{9,8},{10,11... | collective-permute-start | bytes 4718600 | tf_op jit(solution)/shard_map/ppermute | solution.py:751
  54.9 3.6 copy-start.4
  54.9 21.5 %collective-permute-start.5 = (bf16[1,256,3072]{2,1,0:T(8,128)(2,1)S(1)}, bf16[1,256,3072]{2,1,0:T(8,128)(2,1)}, u32[]{:S(2)}, u32[]{:S(2)}) collective-permute-start(bf16[1,256,3072]{2,1,0:T(8,128)(2,1)S(1)} %bitcast.80), channel_id=1, source_target_pairs={{0,1},{1,0},{2,3},{3,2},{4,5},{5,4},{6,7},{7,6},{8,9},{9,8},{10,11... | collective-permute-start | bytes 4718600 | tf_op jit(solution)/shard_map/ppermute | solution.py:751
  55.5 19.7 %collective-permute-start.6 = (bf16[128,3072]{1,0:T(8,128)(2,1)S(1)}, bf16[128,3072]{1,0:T(8,128)(2,1)}, u32[]{:S(2)}, u32[]{:S(2)}) collective-permute-start(bf16[128,3072]{1,0:T(8,128)(2,1)S(1)} %slice.44), channel_id=1, source_target_pairs={{0,2},{1,3},{2,0},{3,1},{4,6},{5,7},{6,4},{7,5},{8,10},{9,11},{10,... | collective-permute-start | bytes 2359304 | tf_op jit(solution)/shard_map/ppermute | solution.py:724
  60.7 32.8 %collective-permute-start.8 = (bf16[384,3072]{1,0:T(8,128)(2,1)}, bf16[384,3072]{1,0:T(8,128)(2,1)}, u32[]{:S(2)}, u32[]{:S(2)}) collective-permute-start(bf16[384,3072]{1,0:T(8,128)(2,1)} %maximum_select_fusion), channel_id=1, source_target_pairs={{0,16},{1,9},{2,18},{3,11},{4,20},{5,13},{6,22},{7,15},{8,24},{9,1... | collective-permute-start | bytes 7077896 | tf_op jit(solution)/shard_map/ppermute | solution.py:720
  62.2 14.3 %collective-permute-start.4 = (bf16[1,128,3072]{2,1,0:T(8,128)(2,1)}, bf16[1,128,3072]{2,1,0:T(8,128)(2,1)}, u32[]{:S(2)}, u32[]{:S(2)}) collective-permute-start(bf16[1,128,3072]{2,1,0:T(8,128)(2,1)} %bitcast.19.refs_6_.refs_9_.refs_10_.refs_12_.refs_15_), channel_id=1, source_target_pairs={{0,1},{1,0},{2,3},{3,2},{4,5},{5,4},{6,7},{7,6},{8,9},{9,8},{10,11... | collective-permute-start | bytes 2359304 | tf_op jit(solution)/shard_map/ppermute | solution.py:751
  75.2 2.6 collective-permute-start.7
  93.3 2.6 collective-permute-start.9
  95.9 5.8 %copy-start.8 = (f32[128,1536]{1,0:T(8,128)}, f32[128,1536]{1,0:T(8,128)S(1)}, u32[]{:S(2)}) copy-start(f32[128,1536]{1,0:T(8,128)S(1)} %collective-permute-done.9.refs_1_) | copy-start | bytes 2359300
  95.9 5.8 %collective-permute-start.10 = (bf16[1,384,3072]{2,1,0:T(8,128)(2,1)}, bf16[1,384,3072]{2,1,0:T(8,128)(2,1)S(1)}, u32[]{:S(2)}, u32[]{:S(2)}) collective-permute-start(bf16[1,384,3072]{2,1,0:T(8,128)(2,1)} %bitcast.22.refs_15_.refs_16_.refs_18_.refs_21_), channel_id=1, source_target_pairs={{0,1},{1,0},{2,3},{3,2},{4,5},{5,4},{6,7},{7,6},{8,9},{9,8},{10,11... | collective-permute-start | bytes 7077896 | tf_op jit(solution)/shard_map/ppermute | solution.py:751
  96.0 51.2 %all-to-all-start.1 = ((bf16[4,2,128,768]{3,2,1,0:T(8,128)(2,1)}), bf16[4,2,128,768]{3,2,1,0:T(8,128)(2,1)}, u32[]{:S(2)}, u32[]{:S(2)}) async-start(bf16[4,2,128,768]{3,2,1,0:T(8,128)(2,1)} %param.11), calls=%async_computation.1 | async-start | bytes 3145728 | tf_op jit(solution)/shard_map/all_to_all | solution.py:789
  101.7 1.4 copy-start.3
  122.7 2.6 collective-permute-start.11
  125.3 0.9 copy-start.9
  146.5 2.6 collective-permute-start.12
  149.1 0.9 copy-start.10
  174.4 3.7 %collective-permute-start.13 = (f32[256,1536]{1,0:T(8,128)}, f32[256,1536]{1,0:T(8,128)S(1)}, u32[]{:S(2)}, u32[]{:S(2)}) collective-permute-start(f32[256,1536]{1,0:T(8,128)} %get-tuple-element.60.refs_0_), channel_id=1, source_target_pairs={{0,1},{1,0},{2,3},{3,2},{4,5},{5,4},{6,7},{7,6},{8,9},{9,8},{10,11... | collective-permute-start | bytes 4718600 | tf_op jit(solution)/shard_map/ppermute | solution.py:672
  178.1 1.2 copy-start.7
  201.1 2.6 collective-permute-start.14
  203.6 0.9 copy-start.12
  226.0 2.6 collective-permute-start.15
  228.5 0.9 copy-start.11
  251.4 17.2 %collective-permute-start.16 = (f32[128,1536]{1,0:T(8,128)}, f32[128,1536]{1,0:T(8,128)S(1)}, u32[]{:S(2)}, u32[]{:S(2)}) collective-permute-start(f32[128,1536]{1,0:T(8,128)} %get-tuple-element.76.refs_0_), channel_id=1, source_target_pairs={{0,1},{1,0},{2,3},{3,2},{4,5},{5,4},{6,7},{7,6},{8,9},{9,8},{10,11... | collective-permute-start | bytes 2359304 | tf_op jit(solution)/shard_map/ppermute | solution.py:672
  268.5 41.5 %collective-permute-start.20 = (bf16[4,96,1536]{2,1,0:T(8,128)(2,1)}, bf16[4,96,1536]{2,1,0:T(8,128)(2,1)}, u32[]{:S(2)}, u32[]{:S(2)}) collective-permute-start(bf16[4,96,1536]{2,1,0:T(8,128)(2,1)} %dynamic-slice_bitcast_fusion.1), channel_id=1, source_target_pairs={{0,1},{1,0},{2,3},{3,2},{4,5},{5,4},{6,7},{7,6},{8,9},{9,8},{10,11... | collective-permute-start | bytes 3538952 | tf_op jit(solution)/shard_map/ppermute | solution.py:686
  268.7 0.9 copy-start.17
  286.5 27.4 %collective-permute-start.17 = (bf16[4,96,1536]{2,1,0:T(8,128)(2,1)}, bf16[4,96,1536]{2,1,0:T(8,128)(2,1)}, u32[]{:S(2)}, u32[]{:S(2)}) collective-permute-start(bf16[4,96,1536]{2,1,0:T(8,128)(2,1)} %dynamic-slice_bitcast_fusion.2), channel_id=1, source_target_pairs={{0,1},{1,0},{2,3},{3,2},{4,5},{5,4},{6,7},{7,6},{8,9},{9,8},{10,11... | collective-permute-start | bytes 3538952 | tf_op jit(solution)/shard_map/ppermute | solution.py:686
  286.9 12.5 %copy-start.14 = (f32[1,768]{1,0:T(1,128)S(1)}, f32[1,768]{1,0:T(1,128)}, u32[]{:S(2)}) copy-start(f32[1,768]{1,0:T(1,128)} %get-tuple-element.88) | copy-start | bytes 9220
  286.9 12.5 %copy-start.15 = (f32[1,768]{1,0:T(1,128)S(1)}, f32[1,768]{1,0:T(1,128)}, u32[]{:S(2)}) copy-start(f32[1,768]{1,0:T(1,128)} %get-tuple-element.87) | copy-start | bytes 9220
  286.9 12.5 %copy-start.16 = (f32[1,768]{1,0:T(1,128)S(1)}, f32[1,768]{1,0:T(1,128)}, u32[]{:S(2)}) copy-start(f32[1,768]{1,0:T(1,128)} %get-tuple-element.86) | copy-start | bytes 9220
  286.9 23.1 %copy-start.5 = (bf16[768,1536]{1,0:T(8,128)(2,1)S(1)}, bf16[768,1536]{1,0:T(8,128)(2,1)}, u32[]{:S(2)}) copy-start(bf16[768,1536]{1,0:T(8,128)(2,1)} %get-tuple-element.83) | copy-start | bytes 7077892
  300.1 1.2 collective-permute-start.23
  301.3 3.6 collective-permute-start.24
  304.9 4.5 %collective-permute-start.25 = (f32[1,768]{1,0:T(1,128)S(1)}, f32[1,768]{1,0:T(1,128)S(1)}, u32[]{:S(2)}, u32[]{:S(2)}) collective-permute-start(f32[1,768]{1,0:T(1,128)S(1)} %add.162), channel_id=1, source_target_pairs={{0,4},{1,5},{2,6},{3,7},{4,0},{5,1},{6,2},{7,3},{8,12},{9,13},{10,... | collective-permute-start | bytes 9224 | tf_op jit(solution)/shard_map/ppermute | solution.py:841
  309.9 4.0 %copy-start.6 = (bf16[768,1536]{1,0:T(8,128)(2,1)S(1)}, bf16[768,1536]{1,0:T(8,128)(2,1)}, u32[]{:S(2)}) copy-start(bf16[768,1536]{1,0:T(8,128)(2,1)} %get-tuple-element.79) | copy-start | bytes 7077892
  311.8 19.5 %collective-permute-start.21 = (bf16[2,96,1536]{2,1,0:T(8,128)(2,1)S(1)}, bf16[2,96,1536]{2,1,0:T(8,128)(2,1)S(1)}, u32[]{:S(2)}, u32[]{:S(2)}) collective-permute-start(bf16[2,96,1536]{2,1,0:T(8,128)(2,1)S(1)} %fusion.1), channel_id=1, source_target_pairs={{0,2},{1,3},{2,0},{3,1},{4,6},{5,7},{6,4},{7,5},{8,10},{9,11},{10,... | collective-permute-start | bytes 1769480 | tf_op jit(solution)/shard_map/ppermute | solution.py:686
  315.6 28.6 %collective-permute-start.18 = (bf16[2,96,1536]{2,1,0:T(8,128)(2,1)S(1)}, bf16[2,96,1536]{2,1,0:T(8,128)(2,1)S(1)}, u32[]{:S(2)}, u32[]{:S(2)}) collective-permute-start(bf16[2,96,1536]{2,1,0:T(8,128)(2,1)S(1)} %fusion), channel_id=1, source_target_pairs={{0,2},{1,3},{2,0},{3,1},{4,6},{5,7},{6,4},{7,5},{8,10},{9,11},{10,... | collective-permute-start | bytes 1769480 | tf_op jit(solution)/shard_map/ppermute | solution.py:686
  331.5 14.0 %collective-permute-start.22 = (bf16[1,96,1536]{2,1,0:T(8,128)(2,1)S(1)}, bf16[1,96,1536]{2,1,0:T(8,128)(2,1)S(1)}, u32[]{:S(2)}, u32[]{:S(2)}) collective-permute-start(bf16[1,96,1536]{2,1,0:T(8,128)(2,1)S(1)} %dynamic-slice_convert_fusion.1), channel_id=1, source_target_pairs={{0,4},{1,5},{2,6},{3,7},{4,0},{5,1},{6,2},{7,3},{8,12},{9,13},{10,... | collective-permute-start | bytes 884744 | tf_op jit(solution)/shard_map/ppermute | solution.py:686
  344.5 14.5 %collective-permute-start.19 = (bf16[1,96,1536]{2,1,0:T(8,128)(2,1)S(1)}, bf16[1,96,1536]{2,1,0:T(8,128)(2,1)S(1)}, u32[]{:S(2)}, u32[]{:S(2)}) collective-permute-start(bf16[1,96,1536]{2,1,0:T(8,128)(2,1)S(1)} %dynamic-slice_convert_fusion.2), channel_id=1, source_target_pairs={{0,4},{1,5},{2,6},{3,7},{4,0},{5,1},{6,2},{7,3},{8,12},{9,13},{10,... | collective-permute-start | bytes 884744 | tf_op jit(solution)/shard_map/ppermute | solution.py:686
  345.5 14.6 %copy-start.1 = (bf16[33,768]{1,0:T(8,128)(2,1)S(1)}, bf16[33,768]{1,0:T(8,128)(2,1)}, u32[]{:S(2)}) copy-start(bf16[33,768]{1,0:T(8,128)(2,1)} %param.7) | copy-start | bytes 152068

commit v5 on v3

--- a/solution.py
+++ b/solution.py
@@ -206,7 +206,7 @@
     else:
         x = x_in[...]
     hat, _ = norm_parts(x)
-    h = (hat * gain[...]).astype(BF16)
+    h = (hat * gain[pl.ds(info[6], 1), :]).astype(BF16)
     pl.when(step == 0)(get_q.wait)
     pack_rows(mm(h, wq[...]).astype(BF16), qkv_out, 0, seq)
     begin = step == 0
@@ -217,18 +217,6 @@
         scores(dmix_out, 0, qkv_out, 2 * HEADS, score_out, seq, seq, begin)
 
 
-def add_gain(gain_out, d_h, hat, step):
-    part = jnp.sum(d_h * hat, axis=0, keepdims=True)
-
-    @pl.when(step == 0)
-    def _():
-        gain_out[...] = part
-
-    @pl.when(step > 0)
-    def _():
-        gain_out[...] += part
-
-
 def add_product(a, b, total, column, step, steps, staged):
     at = slice(column, column + b.shape[1])
     part = lax.dot_general(a, b, TN, preferred_element_type=F32)
@@ -243,7 +231,7 @@
 
     @pl.when(step == steps - 1)
     def _():
-        staged[:, at] = ((total[:, at] if steps > 1 else 0.0) + part).astype(BF16)
+        staged[:, at] = ((total[:, at] if steps > 1 else 0.0) + part).astype(staged.dtype)
 
 
 def logit_grads(probs, sa, sb, first, seq, dl, dlt):
@@ -262,20 +250,40 @@
         pt[:, at] = jnp.transpose(probs[:, at].astype(F32)).astype(BF16)
 
 
+def ship(staged, keep, send, member, sems):
+    count, rows = keep.shape[0], keep.shape[1]
+    copies = []
+    for n in range(count):
+        for k, dst in enumerate((keep, send)):
+            start = pl.multiple_of((2 * n + (member + k) % 2) * rows, rows)
+            copies.append(
+                pltpu.make_async_copy(staged.at[pl.ds(start, rows)], dst.at[n], sems.at[2 * n + k])
+            )
+    return copies
+
+
+def run_copies(copies):
+    for copy in copies:
+        copy.start()
+    for copy in copies:
+        copy.wait()
+
+
 def backward_kernel(is_top, info, *refs, layout, scale, seq, width, steps):
     it = iter(refs)
     sa, sb = next(it), next(it)
     if not is_top:
         probs = next(it)
-    qkv, dmix, x_in, gain, dy, v_prev = [next(it) for _ in range(6)]
+    qkv, dmix, x_in, gains, dy, v_prev = [next(it) for _ in range(6)]
     if not is_top:
-        next(it), next(it)
+        for _ in range(4):
+            next(it)
     own_q, own_o = next(it), next(it)
     stages = take_stages(it, layout)
-    gain_out, dy_out, dmix_out, score_out = [next(it) for _ in range(4)]
-    grad_a, grad_b = next(it), next(it)
+    dy_out, dmix_out, score_out, send_out = [next(it) for _ in range(4)]
+    keep_a, send_a, keep_b, send_b = [next(it) for _ in range(4)]
     dl, dlt, pt, dqkv, mixed = [next(it) for _ in range(5)]
-    total_a, total_b, staged_a, staged_b, sem_g = [next(it) for _ in range(5)]
+    total_a, staged_a, sem_a, total_b, staged_b, sem_b = [next(it) for _ in range(6)]
     wq, sem_q, wo, sem_o = [next(it) for _ in range(4)]
     if is_top:
         probs = next(it)
@@ -283,6 +291,7 @@
     get_q = Weights(info, 0, own_q, stages, slice(0, 3 * width), wq, sem_q)
     get_o = Weights(info, 2, own_o, stages, slice(3 * width, 4 * width), wo, sem_o)
     own = info[0] == 0
+    gain = gains[pl.ds(info[6], 1), :]
 
     @pl.when(step == 0)
     def _():
@@ -301,10 +310,8 @@
     mix(dlt, qkv, 0, dqkv, width, scale, seq)
     mix(pt, dmix, 0, dqkv, 2 * width, None, seq)
     pl.when(step == 0)(get_q.wait)
-    d_h = mm_nt(dqkv[...], wq[...]).astype(BF16).astype(F32)
+    d_hat = mm_nt(dqkv[...], wq[...]).astype(BF16).astype(F32) * gain
     hat, rstd = norm_parts(x_in[...])
-    add_gain(gain_out, d_h, hat, step)
-    d_hat = d_h * gain[...]
     mean_d = jnp.mean(d_hat, axis=-1, keepdims=True)
     mean_dh = jnp.mean(d_hat * hat, axis=-1, keepdims=True)
     d_x = dy[...].astype(F32) + rstd * (d_hat - mean_d - hat * mean_dh)
@@ -313,28 +320,26 @@
     pack_rows(mm_nt(d_x.astype(BF16), wo[...]).astype(BF16), dmix_out, 0, seq)
     scores(dmix_out, 0, v_prev, 0, score_out, 0, seq, step == 0)
 
+    @pl.when(step == steps - 1)
+    def _():
+        send_out[...] = score_out[...].astype(BF16)
+
     @pl.when(own)
     def _():
         mix(probs, qkv, 2 * HEADS, mixed, 0, None, seq)
-        h = (norm_parts(x_in[...])[0] * gain[...]).astype(BF16)
+        h = (norm_parts(x_in[...])[0] * gain).astype(BF16)
         add_product(mixed[...], dy[...].astype(BF16), total_a, 0, step, steps, staged_a)
         add_product(h, dqkv[:, 2 * width :], total_a, width, step, steps, staged_a)
         add_product(h, dqkv[:, : 2 * width], total_b, 0, step, steps, staged_b)
 
     @pl.when(own & (step == steps - 1))
     def _():
-        copies = [
-            pltpu.make_async_copy(staged_a, grad_a, sem_g.at[0]),
-            pltpu.make_async_copy(staged_b, grad_b, sem_g.at[1]),
-        ]
-        for copy in copies:
-            copy.start()
-        for copy in copies:
-            copy.wait()
+        copies = ship(staged_a, keep_a, send_a, info[4], sem_a)
+        run_copies(copies + ship(staged_b, keep_b, send_b, info[4], sem_b))
 
 
 def early_kernel(info, *refs, layout, seq, width, steps):
-    probs, v, dmix, x_in, gain, dy, _, dv_out, grad_a, pt, mixed, total, staged, sem = refs
+    probs, v, dmix, x_in, gains, dy, _, _, keep, send, pt, mixed, dv, total, staged, sem = refs
     step = pl.program_id(0)
     own = info[0] == 0
 
@@ -345,20 +350,18 @@
             turn_probs(probs, seq, pt)
 
         mix(probs, v, 0, mixed, 0, None, seq)
-        mix(pt, dmix, 0, dv_out, 0, None, seq)
-        h = (norm_parts(x_in[...])[0] * gain[...]).astype(BF16)
+        mix(pt, dmix, 0, dv, 0, None, seq)
+        h = (norm_parts(x_in[...])[0] * gains[pl.ds(info[6], 1), :]).astype(BF16)
         add_product(mixed[...], dy[...].astype(BF16), total, 0, step, steps, staged)
-        add_product(h, dv_out[...], total, width, step, steps, staged)
+        add_product(h, dv[...], total, width, step, steps, staged)
 
     @pl.when(own & (step == steps - 1))
     def _():
-        copy = pltpu.make_async_copy(staged, grad_a, sem.at[0])
-        copy.start()
-        copy.wait()
+        run_copies(ship(staged, keep, send, info[4], sem))
 
 
 def late_kernel(info, *refs, layout, scale, seq, width, steps):
-    sa, sb, probs, qk, x_in, gain, _, dqk_out, grad_b, dl, dlt, total, staged, sem = refs
+    sa, sb, probs, qk, x_in, gains, _, _, keep, send, dl, dlt, dqk, total, staged, sem = refs
     step = pl.program_id(0)
     own = info[0] == 0
 
@@ -368,38 +371,20 @@
         def _():
             logit_grads(probs, sa, sb, 0, seq, dl, dlt)
 
-        h = (norm_parts(x_in[...])[0] * gain[...]).astype(BF16)
-        mix(dl, qk, HEADS, dqk_out, 0, scale, seq)
-        mix(dlt, qk, 0, dqk_out, width, scale, seq)
-        add_product(h, dqk_out[...], total, 0, step, steps, staged)
+        mix(dl, qk, HEADS, dqk, 0, scale, seq)
+        mix(dlt, qk, 0, dqk, width, scale, seq)
+        h = (norm_parts(x_in[...])[0] * gains[pl.ds(info[6], 1), :]).astype(BF16)
+        add_product(h, dqk[...], total, 0, step, steps, staged)
 
     @pl.when(own & (step == steps - 1))
     def _():
-        copy = pltpu.make_async_copy(staged, grad_b, sem.at[0])
-        copy.start()
-        copy.wait()
-
-
-def gain_kernel(info, *refs, layout, width):
-    dqk, dv, x_in, own_q, gain_out, wq, sem = refs
-    step = pl.program_id(0)
-
-    @pl.when(info[0] == 0)
-    def _():
-        @pl.when(step == 0)
-        def _():
-            copy = pltpu.make_async_copy(own_q.at[0], wq, sem.at[0])
-            copy.start()
-            copy.wait()
-
-        hat, _ = norm_parts(x_in[...])
-        d_h = mm_nt(dqk[...], wq[:, : 2 * width]) + mm_nt(dv[...], wq[:, 2 * width :])
-        add_gain(gain_out, d_h.astype(BF16).astype(F32), hat, step)
+        run_copies(ship(staged, keep, send, info[4], sem))
 
 
 class Chain:
-    def __init__(self, fetched, member, n_group, own, seq, width, rows, scale):
-        self.fetched, self.member, self.n_group = fetched, member, n_group
+    def __init__(self, fetched, member, n_row, n_group, own, gains, seq, width, rows, scale):
+        self.fetched, self.member, self.n_row, self.n_group = fetched, member, n_row, n_group
+        self.gains = (gains, self.whole(*gains.shape))
         self.own, self.seq, self.width, self.rows = own, seq, width, rows
         self.scale = scale
         per_step = 4 if rows % 4 == 0 else 2
@@ -408,7 +393,8 @@
 
     def info(self, now, other):
         picks = self.fetched.choices(now) + self.fetched.choices(other)
-        return jnp.stack(picks + [self.member, self.fetched.half]).astype(jnp.int32)
+        picks += [self.member, self.fetched.half, self.fetched.section ^ now]
+        return jnp.stack(picks).astype(jnp.int32)
 
     def whole(self, rows, lanes):
         return pl.BlockSpec((rows, lanes), lambda i, s: (0, 0))
@@ -458,21 +444,26 @@
     def shape(self, rows, lanes, dtype):
         return jax.ShapeDtypeStruct((rows, lanes), dtype)
 
-    def grad_out(self):
+    def grad_outs(self):
         any_spec = pl.BlockSpec(memory_space=pl.ANY)
-        return (self.shape(self.width, 2 * self.width, BF16), any_spec)
-
-    def grad_scratch(self, copies):
+        rows = self.width // self.n_row
+        shape = (self.n_row // 2, rows, 2 * self.width)
+        return [(jax.ShapeDtypeStruct(shape, self.grad_type()), any_spec)] * 2
+
+    def grad_type(self):
+        return BF16 if self.width // self.n_row % 16 == 0 else F32
+
+    def grad_scratch(self):
         shape = (self.width, 2 * self.width)
-        scratch = [pltpu.VMEM(shape, F32)] * copies + [pltpu.VMEM(shape, BF16)] * copies
-        return scratch + [pltpu.SemaphoreType.DMA((copies,))]
-
-    def forward(self, layer, x, gain, prev, top):
+        scratch = [pltpu.VMEM(shape, F32), pltpu.VMEM(shape, self.grad_type())]
+        return scratch + [pltpu.SemaphoreType.DMA((self.n_row,))]
+
+    def forward(self, layer, x, prev, top):
         seq, width = self.seq, self.width
         n = self.rows * seq
         hw = HEADS * seq
         score_rows = seq if top is None else 2 * seq
-        ins = [(x, self.tile(width)), (gain, self.whole(1, width))]
+        ins = [(x, self.tile(width)), self.gains]
         outs = [
             (self.shape(n // PACK, 3 * PACK * width, BF16), self.packed(3 * HEADS)),
             (self.shape(score_rows, hw, F32), self.whole(score_rows, hw)),
@@ -507,7 +498,7 @@
             2 * n * width * width * 5,
         )
 
-    def backward(self, layer, scores, probs, qkv, dmix, x, gain, dy, v_prev, grads):
+    def backward(self, layer, scores, probs, qkv, dmix, x, dy, v_prev, grads):
         seq, width = self.seq, self.width
         n = self.rows * seq
         hw = HEADS * seq
@@ -521,21 +512,21 @@
             (qkv, self.packed(3 * HEADS)),
             (dmix, self.packed(HEADS)),
             (x, self.tile(width)),
-            (gain, self.whole(1, width)),
+            self.gains,
             (dy, self.tile(width)),
             (v_prev, self.packed(HEADS, 2)),
         ]
         outs = [
-            (self.shape(1, width, F32), self.whole(1, width)),
             (self.shape(n, width, F32), self.tile(width)),
             (self.shape(n // PACK, PACK * width, BF16), self.packed(HEADS)),
             (self.shape(seq, hw, F32), self.whole(seq, hw)),
-            self.grad_out(),
-            self.grad_out(),
+            (self.shape(seq, hw, BF16), self.whole(seq, hw)),
+            *self.grad_outs(),
+            *self.grad_outs(),
         ]
         scratch = [square] * 3
         scratch += [pltpu.VMEM((self.chunk, lanes * width), BF16) for lanes in (3, 1)]
-        scratch += self.grad_scratch(2) + self.weight_scratch(3) + self.weight_scratch(1)
+        scratch += self.grad_scratch() * 2 + self.weight_scratch(3) + self.weight_scratch(1)
         if is_top:
             scratch.append(square)
         body = functools.partial(
@@ -553,7 +544,7 @@
             carried=grads,
         )
 
-    def early(self, probs, qkv, dmix, x, gain, dy, grad):
+    def early(self, probs, qkv, dmix, x, dy, grads):
         seq, width = self.seq, self.width
         n, hw = self.rows * seq, HEADS * seq
         ins = [
@@ -561,25 +552,24 @@
             (qkv, self.packed(HEADS, 2)),
             (dmix, self.packed(HEADS)),
             (x, self.tile(width)),
-            (gain, self.whole(1, width)),
+            self.gains,
             (dy, self.tile(width)),
         ]
-        outs = [(self.shape(n, width, BF16), self.tile(width)), self.grad_out()]
-        scratch = [pltpu.VMEM((seq, hw), BF16), pltpu.VMEM((self.chunk, width), BF16)]
+        scratch = [pltpu.VMEM((seq, hw), BF16)] + [pltpu.VMEM((self.chunk, width), BF16)] * 2
         return self.call(
             functools.partial(early_kernel, seq=seq, width=width, steps=self.steps),
             "early_back_0",
             self.info(0, 0),
             0,
             ins,
-            outs,
-            scratch + self.grad_scratch(1),
+            self.grad_outs(),
+            scratch + self.grad_scratch(),
             2 * n * width * width * 3,
-            carried=(grad,),
+            carried=grads,
             own=(),
         )
 
-    def late(self, scores, probs, qkv, x, gain, grad):
+    def late(self, scores, probs, qkv, x, grads):
         seq, width = self.seq, self.width
         n, hw = self.rows * seq, HEADS * seq
         ins = [
@@ -588,9 +578,9 @@
             (probs, self.whole(seq, hw)),
             (qkv, self.packed(2 * HEADS)),
             (x, self.tile(width)),
-            (gain, self.whole(1, width)),
+            self.gains,
         ]
-        outs = [(self.shape(n, 2 * width, BF16), self.tile(2 * width)), self.grad_out()]
+        scratch = [pltpu.VMEM((seq, hw), BF16)] * 2 + [pltpu.VMEM((self.chunk, 2 * width), BF16)]
         return self.call(
             functools.partial(
                 late_kernel, scale=self.scale, seq=seq, width=width, steps=self.steps
@@ -599,38 +589,48 @@
             self.info(0, 0),
             0,
             ins,
-            outs,
-            [pltpu.VMEM((seq, hw), BF16)] * 2 + self.grad_scratch(1),
+            self.grad_outs(),
+            scratch + self.grad_scratch(),
             2 * n * width * width * 3,
-            carried=(grad,),
+            carried=grads,
             own=(),
         )
 
-    def gain_grad(self, dqk, dv, x):
-        width = self.width
-        n = self.rows * self.seq
-        return self.call(
-            functools.partial(gain_kernel, width=width),
-            "gain_back_0",
-            self.info(0, 0),
-            0,
-            [(dqk, self.tile(2 * width)), (dv, self.tile(width)), (x, self.tile(width))],
-            [(self.shape(1, width, F32), self.whole(1, width))],
-            self.weight_scratch(3),
-            2 * n * width * width * 3,
-            own=self.own[:1],
-        )[0]
-
-
-def group_swap(value, n_row, n_group):
-    other = jnp.zeros_like(value)
+
+def group_swap(value, send, n_row, n_group):
+    other = jnp.zeros_like(send)
     bit = 1
     while bit < n_group:
         if bit > 1:
             value = value + other
-        other = lax.ppermute(value, "row", [(r, r ^ bit) for r in range(n_row)])
+            send = value.astype(send.dtype)
+        other = lax.ppermute(send, "row", [(r, r ^ bit) for r in range(n_row)])
         bit *= 2
     return value, other
+
+
+class RowSum:
+    def __init__(self, keep, send, place, n_row):
+        self.keep, self.send, self.place, self.n_row, self.bit = keep, send, place, n_row, 1
+
+    def step(self):
+        perm = [(r, r ^ self.bit) for r in range(self.n_row)]
+        other = lax.ppermute(self.send.astype(BF16), "row", perm)
+        value = self.keep.astype(F32) + other.astype(F32)
+        self.bit *= 2
+        if self.bit == self.n_row:
+            return value[0]
+        mine = self.place // self.bit % 2
+        pair = value.reshape(value.shape[0] // 2, 2, *value.shape[1:])
+        self.keep = lax.dynamic_index_in_dim(pair, mine, 1, keepdims=False)
+        self.send = lax.dynamic_index_in_dim(pair, 1 - mine, 1, keepdims=False).astype(BF16)
+        return None
+
+    def finish(self):
+        value = None
+        while value is None:
+            value = self.step()
+        return value
 
 
 class Fetched:
@@ -669,20 +669,16 @@
     def halves(self, got, across):
         return [(DIRECT, self.share(got)), (ACROSS, self.share(across))]
 
-    def second(self, *ready):
-        second, *ready = lax.optimization_barrier(
-            (jnp.where(self.to_last, self.got, self.mine), *ready)
-        )
+    def second(self, x):
+        second, x = lax.optimization_barrier((jnp.where(self.to_last, self.got, self.mine), x))
         second = self.hop(second, 2)
         self.stages.append(self.halves(second, self.cross(second)))
         low = jnp.where(self.half == 0, self.got[: self.block], self.across)
         high = jnp.where(self.half == 0, self.across, self.got[: self.block])
         relayed = jnp.concatenate([low, high, self.got[self.block :]], axis=0)
-        third, _ = lax.optimization_barrier(
-            (jnp.where(self.to_last, self.own_block(0, BLOCKS), relayed), second)
-        )
+        third = jnp.where(self.to_last, self.own_block(0, BLOCKS), relayed)
         self.third = self.hop(third, 2)
-        return ready
+        return x
 
     def finish(self, ready):
         third, ready = lax.optimization_barrier((self.third, ready))
@@ -733,19 +729,28 @@
     )
     tok = exchange(tokens).reshape(-1)
     top_grad = exchange(out_grad).reshape(rows * seq, width)
-    gains = lax.all_gather(ln_gain[0], "section", axis=0, tiled=False)
+    gains = jnp.concatenate(
+        [ln_gain]
+        + [
+            lax.ppermute(ln_gain, "section", [(s, s ^ offset) for s in range(n_section)])
+            for offset in range(1, n_section)
+        ],
+        axis=0,
+    )
     table = (jnp.arange(embed.shape[0], dtype=jnp.int32)[:, None] == tok[None, :]).astype(BF16)
     x = lax.dot_general(table, embed, TN, preferred_element_type=F32)
 
-    x, gains = fetched.second(x, gains)
-    chain = Chain(fetched, member, n_group, (w_qkv, w_out), seq, width, rows, scale)
+    x, gains = fetched.second((x, gains))
+    chain = Chain(
+        fetched, member, n_row, n_group, (w_qkv, w_out), gains, seq, width, rows, scale
+    )
     xs, qkvs, probs = [], [], []
     scores = None
     dmix = None
     for layer in range(n_section):
         prev = None if layer == 0 else (*scores, qkvs[-1])
         top = top_grad if layer == n_section - 1 else None
-        outs = list(chain.forward(layer, x, gains[layer][None], prev, top))
+        outs = list(chain.forward(layer, x, prev, top))
         if prev is not None:
             probs.append(outs.pop(0))
             x = outs.pop(0)
@@ -753,45 +758,38 @@
         qkvs.append(outs[0])
         if top is not None:
             dmix = outs[2]
-        scores = group_swap(outs[1], n_row, n_group)
+        scores = group_swap(outs[1], outs[1], n_row, n_group)
         if layer == 0:
             scores = (scores[0], fetched.finish(scores[1]))
     probs.append(None)
 
     dy = top_grad
-    gain_parts = [None] * n_section
     grads = ()
     for layer in range(n_section - 1, 0, -1):
-        gain_parts[layer], dy, dmix, part, *grads = chain.backward(
+        dy, dmix, part, send, *grads = chain.backward(
             layer,
             scores,
             probs[layer],
             qkvs[layer],
             dmix,
             xs[layer],
-            gains[layer][None],
             dy,
             qkvs[layer - 1],
             grads,
         )
-        scores = group_swap(part, n_row, n_group)
-    sum_rows = functools.partial(
-        lax.psum_scatter, axis_name="row", scatter_dimension=0, tiled=True
-    )
-    gain = gains[0][None]
-    d_v, grad_a = chain.early(probs[0], qkvs[0], dmix, xs[0], gain, dy, grads[0])
-    grad_a = sum_rows(grad_a).astype(F32)
-    d_qk, grad_b = chain.late(scores, probs[0], qkvs[0], xs[0], gain, grads[1])
-    grad_b = sum_rows(grad_b).astype(F32)
-    gain_parts[0] = chain.gain_grad(d_qk, d_v, xs[0])
-    g_gain = lax.select_n(section, *gain_parts)
-    bit = 1
-    while bit < n_row:
-        g_gain = g_gain + lax.ppermute(g_gain, "row", [(r, r ^ bit) for r in range(n_row)])
-        bit *= 2
-    g_gain = lax.dynamic_slice_in_dim(g_gain, place * (width // n_row), width // n_row, 1)
-    g_qkv = jnp.concatenate([grad_b, grad_a[:, width:]], axis=1)
-    return (g_qkv[None], grad_a[None, :, :width], g_gain)
+        scores = group_swap(part, send, n_row, n_group)
+    early = RowSum(*chain.early(probs[0], qkvs[0], dmix, xs[0], dy, grads[:2]), place, n_row)
+    early.step()
+    early.send, other = lax.optimization_barrier((early.send, scores[1]))
+    late = chain.late((scores[0], other), probs[0], qkvs[0], xs[0], grads[2:])
+    g_early = early.finish()
+    g_late = RowSum(*late, place, n_row).finish()
+    g_qkv = jnp.concatenate([g_late, g_early[:, width:]], axis=1)
+    block = width // n_row
+    w_here = lax.dynamic_slice_in_dim(w_qkv[0], place * block, block, 0).astype(F32)
+    gain_here = lax.dynamic_slice_in_dim(ln_gain, place * block, block, 1)
+    g_gain = jnp.sum(g_qkv * w_here, axis=1)[None] / gain_here
+    return (g_qkv[None], g_early[None, :, :width], g_gain)
 
 
 def solution(mesh):

time: 345 us -> 313 us (0.907)
  blocking collectives: 17.4 us -> 0 us
  Pallas kernels: 158 us -> 144 us
  between operations: 14.9 us -> 1.57 us
  starting transfers between devices: 26.5 us -> 33 us
  waiting for transfers between devices: 90.3 us -> 94.3 us
    ppermute x10 -> x16, waiting for transfers between devices: 19.2 us -> 63.6 us  [the longest x6 43.4 us: step(): other = lax.ppermute(self.send.astype(BF16), 'row', perm)]
    reduce_scatter x2 -> x0, waiting for transfers between devices: 42 us -> none  [the longest x1 35.2 us: local(): grad_b = sum_rows(grad_b).astype(F32)]
    all_gather x1 -> x0, blocking collectives: 17.4 us -> none  [local(): gains = lax.all_gather(ln_gain[0], 'section', axis=0, tiled=False)]
    pallas_call x10 -> x9, Pallas kernels: 158 us -> 144 us  [call(): pl.pallas_call(functools.partial(body, layout=layout), name=name, out_sha...]
    ppermute x10 -> x16, starting transfers between devices: 7.05 us -> 12.7 us  [the longest x6 7.33 us: step(): other = lax.ppermute(self.send.astype(BF16), 'row', perm)]
    ppermute x2, waiting for transfers between devices: 13.3 us -> 7.74 us  [cross(): return lax.ppermute(value[:self.block], 'row', perm)]
    ppermute x3, waiting for transfers between devices: 14.2 us -> 19.2 us  [hop(): return lax.ppermute(value, ('section', 'row'), perm)]
    unnamed x35 -> x42, local copies, waits for them, and re-layouts: 8.11 us -> 7.01 us
  transfers between devices with their start and end apart: 24 -> 28, of which waited for: 17 -> 15; matrix products, arithmetic and copies ran while one was open for 5% -> 6% of each run, Pallas kernels for 19% -> 14%
where the time goes in v5:
time: 313 us; the launch traced here: 307 us
  Pallas kernels  144 us (46%)
  waiting for transfers between devices  94.3 us (30%)
  starting transfers between devices  33 us (11%)
  local copies, waits for them, and re-layouts  18.5 us (6%)
  other arithmetic  12.7 us (4%)
    pallas_call x9, Pallas kernels, call(): pl.pallas_call(functools.partial(body, layout=layout), name=name, out_sha...  144 us
    ppermute x6, waiting for transfers between devices, step(): other = lax.ppermute(self.send.astype(BF16), 'row', perm)  43.4 us
    ppermute x3, waiting for transfers between devices, hop(): return lax.ppermute(value, ('section', 'row'), perm)  19.2 us
    ppermute x3, waiting for transfers between devices, local(): lax.ppermute(ln_gain, 'section', [(s, s ^ offset) for s in range(n_sectio...  11.6 us
    ppermute x7, waiting for transfers between devices, group_swap(): other = lax.ppermute(send, 'row', [(r, r ^ bit) for r in range(n_row)])  8.54 us
    ppermute x2, waiting for transfers between devices, cross(): return lax.ppermute(value[:self.block], 'row', perm)  7.74 us
    ppermute x6, starting transfers between devices, step(): other = lax.ppermute(self.send.astype(BF16), 'row', perm)  7.33 us
    unnamed x42, local copies, waits for them, and re-layouts  7.01 us
  transfers between devices with their start and end apart: 28, of which 15 were waited for; matrix products, arithmetic and copies ran while one was open for 6% of the time, Pallas kernels for 14%

profile of v5, /device:TPU:0, one launch (start us, length us, event | category | flops | bytes accessed | tf_op | source)
XLA Modules:
  0.0 306.7 jit_solution(11372184700960555110)
XLA Ops:
  1.8 1.5 dynamic-slice_bitcast_fusion.3
  4.2 2.9 collective-permute-start
  7.2 1.5 collective-permute-start.3
  8.7 2.0 collective-permute-start.1
  10.7 4.9 %all-to-all-start = ((s32[4,2,128]{2,1,0:T(2,128)}), s32[4,2,128]{2,1,0:T(2,128)S(1)}, u32[]{:S(2)}, u32[]{:S(2)}) async-start(s32[4,2,128]{2,1,0:T(2,128)} %param.6), calls=%async_computation | async-start | bytes 8192 | tf_op jit(solution)/shard_map/all_to_all | solution.py:730
  15.6 11.6 %collective-permute-done.3 = f32[1,768]{1,0:T(1,128)S(1)} collective-permute-done((f32[1,768]{1,0:T(1,128)S(1)}, f32[1,768]{1,0:T(1,128)S(1)}, u32[]{:S(2)}, u32[]{:S(2)}) %collective-permute-start.3) | collective-permute-done | bytes 3104 | tf_op jit(solution)/shard_map/ppermute | solution.py:735
  27.8 2.3 fusion.4.refs_0_.refs_3_.refs_4_
  30.2 1.6 broadcast_select_fusion
  32.4 2.1 slice.22
  34.5 1.6 collective-permute-start.5
  36.1 1.1 dynamic-slice_bitcast_fusion.1
  37.4 15.1 %collective-permute-done.7 = bf16[256,3072]{1,0:T(8,128)(2,1)} collective-permute-done((bf16[256,3072]{1,0:T(8,128)(2,1)}, bf16[256,3072]{1,0:T(8,128)(2,1)}, u32[]{:S(2)}, u32[]{:S(2)}) %collective-permute-start.7) | collective-permute-done | bytes 1572896 | tf_op jit(solution)/shard_map/ppermute | solution.py:663
  52.5 1.2 slice.23
  53.7 1.6 collective-permute-start.9
  55.4 1.8 broadcast_select_fusion.2
  57.1 2.2 maximum_select_fusion
  60.0 2.6 collective-permute-start.6
  62.6 7.7 %collective-permute-done.9 = bf16[128,3072]{1,0:T(8,128)(2,1)S(1)} collective-permute-done((bf16[128,3072]{1,0:T(8,128)(2,1)S(1)}, bf16[128,3072]{1,0:T(8,128)(2,1)S(1)}, u32[]{:S(2)}, u32[]{:S(2)}) %collective-permute-start.9) | collective-permute-done | bytes 786464 | tf_op jit(solution)/shard_map/ppermute | solution.py:667
  71.1 1.6 collective-permute-done.10.refs_11_.refs_14_.refs_15_.refs_17_.refs_22_
  72.8 11.4 %layer_in_0.1 = (bf16[512,4608]{1,0:T(8,128)(2,1)}, f32[128,1536]{1,0:T(8,128)}) custom-call(s32[7]{0:T(128)} %stack.41.info, f32[1024,768]{1,0:T(8,128)} %fusion.4.refs_0_.refs_3_.refs_4_, f32[4,768]{1,0:T(4,128)} %pad_maximum_fusion.1.refs_1_.refs_4_.refs_5_.refs_6_, bf16[1,768,2304]{2,1,0:T(8,128)(2,1)} %refs_13_.3, bf16[1,768,768]{2,1,0:T(8,128)(2,1)} %refs_14_.3, ...), custom_call_target="tpu_custom_call" | custom-call | flops 6039797760 | bytes 8663040 | tf_op jit(solution)/shard_map/layer_in_0/pallas_call | solution.py:420
  84.4 4.0 %collective-permute-done.11 = bf16[384,3072]{1,0:T(8,128)(2,1)S(1)} collective-permute-done((bf16[384,3072]{1,0:T(8,128)(2,1)}, bf16[384,3072]{1,0:T(8,128)(2,1)S(1)}, u32[]{:S(2)}, u32[]{:S(2)}) %collective-permute-start.11) | collective-permute-done | bytes 2359328 | tf_op jit(solution)/shard_map/ppermute | solution.py:663
  90.0 4.6 %all-to-all-start.1 = ((bf16[4,2,128,768]{3,2,1,0:T(8,128)(2,1)}), bf16[4,2,128,768]{3,2,1,0:T(8,128)(2,1)}, u32[]{:S(2)}, u32[]{:S(2)}) async-start(bf16[4,2,128,768]{3,2,1,0:T(8,128)(2,1)} %param.11), calls=%async_computation.1 | async-start | bytes 3145728 | tf_op jit(solution)/shard_map/all_to_all | solution.py:731
  95.3 14.9 %layer_in_1.1 = (bf16[128,1536]{1,0:T(8,128)(2,1)}, f32[1024,768]{1,0:T(8,128)}, bf16[512,4608]{1,0:T(8,128)(2,1)}, f32[128,1536]{1,0:T(8,128)}) custom-call(s32[7]{0:T(128)} %stack.45.info, f32[128,1536]{1,0:T(8,128)} %get-tuple-element.56.refs_0_, f32[128,1536]{1,0:T(8,128)} %copy-done.14, ...), custom_call_target="tpu_custom_call" | custom-call | flops 6039797760 | bytes 18493440 | tf_op jit(solution)/shard_map/layer_in_1/pallas_call | solution.py:420
  111.6 1.5 collective-permute-done.14.refs_1_
  114.1 15.8 %layer_in_2.1 = (bf16[128,1536]{1,0:T(8,128)(2,1)}, f32[1024,768]{1,0:T(8,128)}, bf16[512,4608]{1,0:T(8,128)(2,1)}, f32[128,1536]{1,0:T(8,128)}) custom-call(s32[7]{0:T(128)} %stack.49.info, f32[128,1536]{1,0:T(8,128)} %get-tuple-element.60.refs_0_, f32[128,1536]{1,0:T(8,128)} %copy-done.15, bf16[512,4608]{1,0:T(8,128)(2,1)} %get-tuple-element.61.refs_2_.refs_8_.refs_3_, ...), custom_call_target="tpu_custom_call" | custom-call | flops 6039797760 | bytes 18493440 | tf_op jit(solution)/shard_map/layer_in_2/pallas_call | solution.py:420
  130.6 2.1 all-to-all-done.1
  133.6 19.1 %layer_in_3.1 = (bf16[128,1536]{1,0:T(8,128)(2,1)}, f32[1024,768]{1,0:T(8,128)}, bf16[512,4608]{1,0:T(8,128)(2,1)}, f32[256,1536]{1,0:T(8,128)}, bf16[512,1536]{1,0:T(8,128)(2,1)}) custom-call(s32[7]{0:T(128)} %stack.53.info, f32[128,1536]{1,0:T(8,128)} %get-tuple-element.63.refs_0_, f32[128,1536]{1,0:T(8,128)} %copy-done.16, ...), custom_call_target="tpu_custom_call" | custom-call | flops 6039797760 | bytes 22425600 | tf_op jit(solution)/shard_map/layer_in_3/pallas_call | solution.py:420
  152.8 3.6 %collective-permute-done.16.refs_1_ = f32[256,1536]{1,0:T(8,128)S(1)} collective-permute-done((f32[256,1536]{1,0:T(8,128)}, f32[256,1536]{1,0:T(8,128)S(1)}, u32[]{:S(2)}, u32[]{:S(2)}) %collective-permute-start.16) | collective-permute-done | bytes 1572896 | tf_op jit(solution)/shard_map/ppermute | solution.py:607
  156.4 1.2 copy-done.13
  157.6 20.9 %layer_back_3.1 = (f32[1024,768]{1,0:T(8,128)}, bf16[512,1536]{1,0:T(8,128)(2,1)}, f32[128,1536]{1,0:T(8,128)}, bf16[128,1536]{1,0:T(8,128)(2,1)}, bf16[4,96,153...) custom-call(s32[7]{0:T(128)} %stack.53.info, ...), custom_call_target="tpu_custom_call" | custom-call | flops 6039797760 | bytes 29503488 | tf_op jit(solution)/shard_map/layer_back_3/pallas_call | solution.py:420
  178.7 1.8 collective-permute-done.17.refs_1_
  181.3 20.4 %layer_back_2.1 = (f32[1024,768]{1,0:T(8,128)}, bf16[512,1536]{1,0:T(8,128)(2,1)}, f32[128,1536]{1,0:T(8,128)}, bf16[128,1536]{1,0:T(8,128)(2,1)}, bf16[4,96,153...) custom-call(s32[7]{0:T(128)} %stack.49.info, ...), custom_call_target="tpu_custom_call", output_to_operand_aliasing={{4}: (10, {}), {5}: (11, {}), {6}: (12, {}), {7}: (13, {})} | custom-call | flops 6039797760 | bytes 34222080 | tf_op jit(solution)/shard_map/layer_back_2/pallas_call | solution.py:420
  202.1 1.6 collective-permute-done.18.refs_1_
  204.4 20.7 %layer_back_1.1 = (f32[1024,768]{1,0:T(8,128)}, bf16[512,1536]{1,0:T(8,128)(2,1)}, f32[128,1536]{1,0:T(8,128)}, bf16[128,1536]{1,0:T(8,128)(2,1)}, bf16[4,96,153...) custom-call(s32[7]{0:T(128)} %stack.45.info, ...), custom_call_target="tpu_custom_call", output_to_operand_aliasing={{4}: (10, {}), {5}: (11, {}), {6}: (12, {}), {7}: (13, {})} | custom-call | flops 6039797760 | bytes 34222080 | tf_op jit(solution)/shard_map/layer_back_1/pallas_call | solution.py:420
  225.2 10.9 %early_back_0.1 = (bf16[4,96,1536]{2,1,0:T(8,128)(2,1)}, bf16[4,96,1536]{2,1,0:T(8,128)(2,1)}) custom-call(s32[7]{0:T(128)} %stack.41.info, bf16[128,1536]{1,0:T(8,128)(2,1)} %get-tuple-element.89.refs_0_.refs_2_, bf16[512,4608]{1,0:T(8,128)(2,1)} %get-tuple-element.58.refs_2_.refs_8_.refs_1_.refs_3_, ...), custom_call_target="tpu_custom_call", output_to_operand_aliasing={{0}: (7, {}), {1}: (8, {})} | custom-call | flops 3623878656 | bytes 17707008 | tf_op jit(solution)/shard_map/early_back_0/pallas_call | solution.py:420
  236.7 2.5 collective-permute-done.19
  239.2 1.6 convert_add_fusion.1
  242.5 10.3 %late_back_0.1 = (bf16[4,96,1536]{2,1,0:T(8,128)(2,1)}, bf16[4,96,1536]{2,1,0:T(8,128)(2,1)}) custom-call(s32[7]{0:T(128)} %stack.41.info, f32[128,1536]{1,0:T(8,128)} %get-tuple-element.88.refs_0_, bf16[128,1536]{1,0:T(8,128)(2,1)} %copy-done.20, bf16[128,1536]{1,0:T(8,128)(2,1)} %get-tuple-element.89.refs_0_.refs_2_, ...), custom_call_target="tpu_custom_call", output_to_operand_aliasing={{0}: (7, {}), {1}: (8, {})} | custom-call | flops 3623878656 | bytes 14168064 | tf_op jit(solution)/shard_map/late_back_0/pallas_call | solution.py:420
  253.1 1.4 collective-permute-start.24
  254.5 1.3 collective-permute-done.21
  255.8 1.6 convert_add_fusion
  257.5 1.5 collective-permute-start.22
  259.0 10.5 %collective-permute-done.24 = bf16[2,96,1536]{2,1,0:T(8,128)(2,1)S(1)} collective-permute-done((bf16[2,96,1536]{2,1,0:T(8,128)(2,1)}, bf16[2,96,1536]{2,1,0:T(8,128)(2,1)S(1)}, u32[]{:S(2)}, u32[]{:S(2)}) %collective-permute-start.24) | collective-permute-done | bytes 589856 | tf_op jit(solution)/shard_map/ppermute | solution.py:618
  269.7 2.4 collective-permute-start.25
  272.0 15.7 %collective-permute-done.22 = bf16[2,96,1536]{2,1,0:T(8,128)(2,1)S(1)} collective-permute-done((bf16[2,96,1536]{2,1,0:T(8,128)(2,1)S(1)}, bf16[2,96,1536]{2,1,0:T(8,128)(2,1)S(1)}, u32[]{:S(2)}, u32[]{:S(2)}) %collective-permute-start.22) | collective-permute-done | bytes 589856 | tf_op jit(solution)/shard_map/ppermute | solution.py:618
  287.9 1.3 collective-permute-start.23
  290.1 13.4 %collective-permute-done.23 = bf16[1,96,1536]{2,1,0:T(8,128)(2,1)S(1)} collective-permute-done((bf16[1,96,1536]{2,1,0:T(8,128)(2,1)S(1)}, bf16[1,96,1536]{2,1,0:T(8,128)(2,1)S(1)}, u32[]{:S(2)}, u32[]{:S(2)}) %collective-permute-start.23) | collective-permute-done | bytes 294944 | tf_op jit(solution)/shard_map/ppermute | solution.py:618
  303.5 2.1 fusion
  (88 shorter events, 18.0 us)
Async XLA Ops:
  0.6 27.2 %copy-start = (bf16[33,768]{1,0:T(8,128)(2,1)S(1)}, bf16[33,768]{1,0:T(8,128)(2,1)}, u32[]{:S(2)}) copy-start(bf16[33,768]{1,0:T(8,128)(2,1)} %param.7) | copy-start | bytes 152068
  1.8 1.7 copy-start.9
  1.8 1.7 copy-start.11
  3.2 0.8 copy-start.5
  3.2 1.0 copy-start.7
  3.3 3.9 %copy-start.19 = (f32[1,768]{1,0:T(1,128)S(1)}, f32[1,768]{1,0:T(1,128)}, u32[]{:S(2)}) copy-start(f32[1,768]{1,0:T(1,128)} %param.8) | copy-start | bytes 9220
  4.2 25.9 %collective-permute-start = (bf16[256,3072]{1,0:T(8,128)(2,1)S(1)}, bf16[256,3072]{1,0:T(8,128)(2,1)}, u32[]{:S(2)}, u32[]{:S(2)}) collective-permute-start(bf16[256,3072]{1,0:T(8,128)(2,1)S(1)} %maximum_maximum_fusion), channel_id=1, source_target_pairs={{0,8},{1,17},{2,10},{3,19},{4,12},{5,21},{6,14},{7,23},{8,0},{9,25... | collective-permute-start | bytes 4718600 | tf_op jit(solution)/shard_map/ppermute | solution.py:663
  7.2 20.0 %collective-permute-start.3 = (f32[1,768]{1,0:T(1,128)S(1)}, f32[1,768]{1,0:T(1,128)S(1)}, u32[]{:S(2)}, u32[]{:S(2)}) collective-permute-start(f32[1,768]{1,0:T(1,128)S(1)} %copy-done.19), channel_id=1, source_target_pairs={{0,24},{8,16},{16,8},{24,0},{1,25},{9,17},{17,9},{25,1},{2,26},{10... | collective-permute-start | bytes 9224 | tf_op jit(solution)/shard_map/ppermute | solution.py:735
  8.7 18.5 %collective-permute-start.2 = (f32[1,768]{1,0:T(1,128)S(1)}, f32[1,768]{1,0:T(1,128)S(1)}, u32[]{:S(2)}, u32[]{:S(2)}) collective-permute-start(f32[1,768]{1,0:T(1,128)S(1)} %copy-done.19), channel_id=1, source_target_pairs={{0,16},{8,24},{16,0},{24,8},{1,17},{9,25},{17,1},{25,9},{2,18},{10... | collective-permute-start | bytes 9224 | tf_op jit(solution)/shard_map/ppermute | solution.py:735
  8.7 18.5 %collective-permute-start.1 = (f32[1,768]{1,0:T(1,128)S(1)}, f32[1,768]{1,0:T(1,128)S(1)}, u32[]{:S(2)}, u32[]{:S(2)}) collective-permute-start(f32[1,768]{1,0:T(1,128)S(1)} %copy-done.19), channel_id=1, source_target_pairs={{0,8},{8,0},{16,24},{24,16},{1,9},{9,1},{17,25},{25,17},{2,10},{10... | collective-permute-start | bytes 9224 | tf_op jit(solution)/shard_map/ppermute | solution.py:735
  10.7 17.1 %all-to-all-start = ((s32[4,2,128]{2,1,0:T(2,128)}), s32[4,2,128]{2,1,0:T(2,128)S(1)}, u32[]{:S(2)}, u32[]{:S(2)}) async-start(s32[4,2,128]{2,1,0:T(2,128)} %param.6), calls=%async_computation | async-start | bytes 8192 | tf_op jit(solution)/shard_map/all_to_all | solution.py:730
  27.8 2.4 copy-start.6
  27.8 2.4 copy-start.8
  27.8 2.4 copy-start.10
  27.8 2.4 copy-start.12
  30.2 7.0 %copy-start.2 = (bf16[1,768,2304]{2,1,0:T(8,128)(2,1)S(1)}, bf16[1,768,2304]{2,1,0:T(8,128)(2,1)}, u32[]{:S(2)}) copy-start(bf16[1,768,2304]{2,1,0:T(8,128)(2,1)} %refs_13_.3) | copy-start | bytes 10616836
  31.8 20.7 %collective-permute-start.7 = (bf16[256,3072]{1,0:T(8,128)(2,1)}, bf16[256,3072]{1,0:T(8,128)(2,1)}, u32[]{:S(2)}, u32[]{:S(2)}) collective-permute-start(bf16[256,3072]{1,0:T(8,128)(2,1)} %broadcast_select_fusion), channel_id=1, source_target_pairs={{0,16},{1,9},{2,18},{3,11},{4,20},{5,13},{6,22},{7,15},{8,24},{9,1... | collective-permute-start | bytes 4718600 | tf_op jit(solution)/shard_map/ppermute | solution.py:663
  34.5 20.9 %collective-permute-start.5 = (bf16[128,3072]{1,0:T(8,128)(2,1)}, bf16[128,3072]{1,0:T(8,128)(2,1)}, u32[]{:S(2)}, u32[]{:S(2)}) collective-permute-start(bf16[128,3072]{1,0:T(8,128)(2,1)} %slice.22), channel_id=1, source_target_pairs={{0,2},{1,3},{2,0},{3,1},{4,6},{5,7},{6,4},{7,5},{8,10},{9,11},{10,... | collective-permute-start | bytes 2359304 | tf_op jit(solution)/shard_map/ppermute | solution.py:667
  37.3 33.8 %collective-permute-start.4 = (bf16[1,256,3072]{2,1,0:T(8,128)(2,1)}, bf16[1,256,3072]{2,1,0:T(8,128)(2,1)}, u32[]{:S(2)}, u32[]{:S(2)}) collective-permute-start(bf16[1,256,3072]{2,1,0:T(8,128)(2,1)} %bitcast.19.refs_4_.refs_7_.refs_8_.refs_10_.refs_15_), channel_id=1, source_target_pairs={{0,1},{1,0},{2,3},{3,2},{4,5},{5,4},{6,7},{7,6},{8,9},{9,8},{10,11... | collective-permute-start | bytes 4718600 | tf_op jit(solution)/shard_map/ppermute | solution.py:693
  53.7 16.6 %collective-permute-start.9 = (bf16[128,3072]{1,0:T(8,128)(2,1)S(1)}, bf16[128,3072]{1,0:T(8,128)(2,1)S(1)}, u32[]{:S(2)}, u32[]{:S(2)}) collective-permute-start(bf16[128,3072]{1,0:T(8,128)(2,1)S(1)} %slice.23), channel_id=1, source_target_pairs={{0,2},{1,3},{2,0},{3,1},{4,6},{5,7},{6,4},{7,5},{8,10},{9,11},{10,... | collective-permute-start | bytes 2359304 | tf_op jit(solution)/shard_map/ppermute | solution.py:667
  55.4 17.4 %collective-permute-start.8 = (bf16[1,256,3072]{2,1,0:T(8,128)(2,1)}, bf16[1,256,3072]{2,1,0:T(8,128)(2,1)}, u32[]{:S(2)}, u32[]{:S(2)}) collective-permute-start(bf16[1,256,3072]{2,1,0:T(8,128)(2,1)} %bitcast.21.refs_8_.refs_11_.refs_12_.refs_14_.refs_19_), channel_id=1, source_target_pairs={{0,1},{1,0},{2,3},{3,2},{4,5},{5,4},{6,7},{7,6},{8,9},{9,8},{10,11... | collective-permute-start | bytes 4718600 | tf_op jit(solution)/shard_map/ppermute | solution.py:693
  59.3 29.1 %collective-permute-start.11 = (bf16[384,3072]{1,0:T(8,128)(2,1)}, bf16[384,3072]{1,0:T(8,128)(2,1)S(1)}, u32[]{:S(2)}, u32[]{:S(2)}) collective-permute-start(bf16[384,3072]{1,0:T(8,128)(2,1)} %maximum_select_fusion), channel_id=1, source_target_pairs={{0,16},{1,9},{2,18},{3,11},{4,20},{5,13},{6,22},{7,15},{8,24},{9,1... | collective-permute-start | bytes 7077896 | tf_op jit(solution)/shard_map/ppermute | solution.py:663
  60.0 11.2 %collective-permute-start.6 = (bf16[1,128,3072]{2,1,0:T(8,128)(2,1)}, bf16[1,128,3072]{2,1,0:T(8,128)(2,1)}, u32[]{:S(2)}, u32[]{:S(2)}) collective-permute-start(bf16[1,128,3072]{2,1,0:T(8,128)(2,1)} %bitcast.20.refs_6_.refs_9_.refs_10_.refs_12_.refs_17_), channel_id=1, source_target_pairs={{0,1},{1,0},{2,3},{3,2},{4,5},{5,4},{6,7},{7,6},{8,9},{9,8},{10,11... | collective-permute-start | bytes 2359304 | tf_op jit(solution)/shard_map/ppermute | solution.py:693
  70.3 2.4 copy-start.4
  70.3 2.4 collective-permute-start.10
  84.2 4.2 %collective-permute-start.12 = (f32[128,1536]{1,0:T(8,128)}, f32[128,1536]{1,0:T(8,128)S(1)}, u32[]{:S(2)}, u32[]{:S(2)}) collective-permute-start(f32[128,1536]{1,0:T(8,128)} %get-tuple-element.56.refs_0_), channel_id=1, source_target_pairs={{0,1},{1,0},{2,3},{3,2},{4,5},{5,4},{6,7},{7,6},{8,9},{9,8},{10,11... | collective-permute-start | bytes 2359304 | tf_op jit(solution)/shard_map/ppermute | solution.py:607
  88.4 1.5 copy-start.3
  88.4 1.6 copy-start.14
  88.4 6.9 %collective-permute-start.13 = (bf16[1,384,3072]{2,1,0:T(8,128)(2,1)S(1)}, bf16[1,384,3072]{2,1,0:T(8,128)(2,1)}, u32[]{:S(2)}, u32[]{:S(2)}) collective-permute-start(bf16[1,384,3072]{2,1,0:T(8,128)(2,1)S(1)} %bitcast.65), channel_id=1, source_target_pairs={{0,1},{1,0},{2,3},{3,2},{4,5},{5,4},{6,7},{7,6},{8,9},{9,8},{10,11... | collective-permute-start | bytes 7077896 | tf_op jit(solution)/shard_map/ppermute | solution.py:693
  90.0 42.7 %all-to-all-start.1 = ((bf16[4,2,128,768]{3,2,1,0:T(8,128)(2,1)}), bf16[4,2,128,768]{3,2,1,0:T(8,128)(2,1)}, u32[]{:S(2)}, u32[]{:S(2)}) async-start(bf16[4,2,128,768]{3,2,1,0:T(8,128)(2,1)} %param.11), calls=%async_computation.1 | async-start | bytes 3145728 | tf_op jit(solution)/shard_map/all_to_all | solution.py:731
  110.3 2.9 collective-permute-start.14
  113.1 0.9 copy-start.15
  129.8 2.9 collective-permute-start.15
  132.7 0.9 copy-start.16
  152.7 3.7 %collective-permute-start.16 = (f32[256,1536]{1,0:T(8,128)}, f32[256,1536]{1,0:T(8,128)S(1)}, u32[]{:S(2)}, u32[]{:S(2)}) collective-permute-start(f32[256,1536]{1,0:T(8,128)} %get-tuple-element.66.refs_0_), channel_id=1, source_target_pairs={{0,1},{1,0},{2,3},{3,2},{4,5},{5,4},{6,7},{7,6},{8,9},{9,8},{10,11... | collective-permute-start | bytes 4718600 | tf_op jit(solution)/shard_map/ppermute | solution.py:607
  156.4 1.2 copy-start.13
  178.5 2.0 collective-permute-start.17
  180.5 0.8 copy-start.18
  201.7 2.0 collective-permute-start.18
  203.7 0.8 copy-start.17
  236.1 3.1 %collective-permute-start.19 = (bf16[4,96,1536]{2,1,0:T(8,128)(2,1)}, bf16[4,96,1536]{2,1,0:T(8,128)(2,1)S(1)}, u32[]{:S(2)}, u32[]{:S(2)}) collective-permute-start(bf16[4,96,1536]{2,1,0:T(8,128)(2,1)} %get-tuple-element.95), channel_id=1, source_target_pairs={{0,1},{1,0},{2,3},{3,2},{4,5},{5,4},{6,7},{7,6},{8,9},{9,8},{10,11... | collective-permute-start | bytes 3538952 | tf_op jit(solution)/shard_map/ppermute | solution.py:618
  236.5 5.2 %collective-permute-start.20 = (bf16[128,1536]{1,0:T(8,128)(2,1)}, bf16[128,1536]{1,0:T(8,128)(2,1)S(1)}, u32[]{:S(2)}, u32[]{:S(2)}) collective-permute-start(bf16[128,1536]{1,0:T(8,128)(2,1)} %get-tuple-element.96), channel_id=1, source_target_pairs={{0,1},{1,0},{2,3},{3,2},{4,5},{5,4},{6,7},{7,6},{8,9},{9,8},{10,11... | collective-permute-start | bytes 1179656 | tf_op jit(solution)/shard_map/ppermute | solution.py:607
  252.7 3.1 %collective-permute-start.21 = (bf16[4,96,1536]{2,1,0:T(8,128)(2,1)}, bf16[4,96,1536]{2,1,0:T(8,128)(2,1)S(1)}, u32[]{:S(2)}, u32[]{:S(2)}) collective-permute-start(bf16[4,96,1536]{2,1,0:T(8,128)(2,1)} %get-tuple-element.101), channel_id=1, source_target_pairs={{0,1},{1,0},{2,3},{3,2},{4,5},{5,4},{6,7},{7,6},{8,9},{9,8},{10,11... | collective-permute-start | bytes 3538952 | tf_op jit(solution)/shard_map/ppermute | solution.py:618
  253.1 16.4 %collective-permute-start.24 = (bf16[2,96,1536]{2,1,0:T(8,128)(2,1)}, bf16[2,96,1536]{2,1,0:T(8,128)(2,1)S(1)}, u32[]{:S(2)}, u32[]{:S(2)}) collective-permute-start(bf16[2,96,1536]{2,1,0:T(8,128)(2,1)} %fusion.2), channel_id=1, source_target_pairs={{0,2},{1,3},{2,0},{3,1},{4,6},{5,7},{6,4},{7,5},{8,10},{9,11},{10,... | collective-permute-start | bytes 1769480 | tf_op jit(solution)/shard_map/ppermute | solution.py:618
  257.5 30.2 %collective-permute-start.22 = (bf16[2,96,1536]{2,1,0:T(8,128)(2,1)S(1)}, bf16[2,96,1536]{2,1,0:T(8,128)(2,1)S(1)}, u32[]{:S(2)}, u32[]{:S(2)}) collective-permute-start(bf16[2,96,1536]{2,1,0:T(8,128)(2,1)S(1)} %fusion.3), channel_id=1, source_target_pairs={{0,2},{1,3},{2,0},{3,1},{4,6},{5,7},{6,4},{7,5},{8,10},{9,11},{10,... | collective-permute-start | bytes 1769480 | tf_op jit(solution)/shard_map/ppermute | solution.py:618
  269.7 19.6 %collective-permute-start.25 = (bf16[1,96,1536]{2,1,0:T(8,128)(2,1)S(1)}, bf16[1,96,1536]{2,1,0:T(8,128)(2,1)S(1)}, u32[]{:S(2)}, u32[]{:S(2)}) collective-permute-start(bf16[1,96,1536]{2,1,0:T(8,128)(2,1)S(1)} %dynamic-slice_convert_fusion), channel_id=1, source_target_pairs={{0,4},{1,5},{2,6},{3,7},{4,0},{5,1},{6,2},{7,3},{8,12},{9,13},{10,... | collective-permute-start | bytes 884744 | tf_op jit(solution)/shard_map/ppermute | solution.py:618
  287.9 15.6 %collective-permute-start.23 = (bf16[1,96,1536]{2,1,0:T(8,128)(2,1)S(1)}, bf16[1,96,1536]{2,1,0:T(8,128)(2,1)S(1)}, u32[]{:S(2)}, u32[]{:S(2)}) collective-permute-start(bf16[1,96,1536]{2,1,0:T(8,128)(2,1)S(1)} %dynamic-slice_convert_fusion.1), channel_id=1, source_target_pairs={{0,4},{1,5},{2,6},{3,7},{4,0},{5,1},{6,2},{7,3},{8,12},{9,13},{10,... | collective-permute-start | bytes 884744 | tf_op jit(solution)/shard_map/ppermute | solution.py:618
  289.3 16.9 %copy-start.1 = (bf16[33,768]{1,0:T(8,128)(2,1)S(1)}, bf16[33,768]{1,0:T(8,128)(2,1)}, u32[]{:S(2)}) copy-start(bf16[33,768]{1,0:T(8,128)(2,1)} %param.7) | copy-start | bytes 152068
  (1 other events, 0.7 us)

commit v6 on v5

--- a/solution.py
+++ b/solution.py
@@ -613,9 +613,11 @@
     def __init__(self, keep, send, place, n_row):
         self.keep, self.send, self.place, self.n_row, self.bit = keep, send, place, n_row, 1
 
-    def step(self):
+    def exchange(self):
         perm = [(r, r ^ self.bit) for r in range(self.n_row)]
-        other = lax.ppermute(self.send.astype(BF16), "row", perm)
+        return lax.ppermute(self.send.astype(BF16), "row", perm)
+
+    def add(self, other):
         value = self.keep.astype(F32) + other.astype(F32)
         self.bit *= 2
         if self.bit == self.n_row:
@@ -629,30 +631,106 @@
     def finish(self):
         value = None
         while value is None:
-            value = self.step()
+            value = self.add(self.exchange())
         return value
+
+
+def copy_call(body, name, scalars, outs, arrays):
+    any_spec = pl.BlockSpec(memory_space=pl.ANY)
+    return pl.pallas_call(
+        body,
+        name=name,
+        out_shape=outs,
+        grid_spec=pltpu.PrefetchScalarGridSpec(
+            num_scalar_prefetch=1,
+            grid=(1,),
+            in_specs=[any_spec] * len(arrays),
+            out_specs=[any_spec] * len(outs),
+            scratch_shapes=[pltpu.SemaphoreType.DMA((2 * BLOCKS + 1,))],
+        ),
+        compiler_params=pltpu.CompilerParams(vmem_limit_bytes=VMEM_LIMIT),
+        cost_estimate=pl.CostEstimate(flops=0, bytes_accessed=0, transcendentals=0),
+    )(jnp.stack(scalars).astype(jnp.int32), *arrays)
+
+
+def own_blocks(own, places, block, out, sems):
+    copies, column = [], 0
+    for k, ref in enumerate(own):
+        columns = ref.shape[2]
+        for n, place in enumerate(places):
+            start = pl.multiple_of(place * block, block)
+            copies.append(
+                pltpu.make_async_copy(
+                    ref.at[0, pl.ds(start, block)],
+                    out.at[n * block : (n + 1) * block, column : column + columns],
+                    sems.at[2 * n + k],
+                )
+            )
+        column += columns
+    return copies
+
+
+def first_kernel(block, info, own_q, own_o, out, sems):
+    base = info[0] * BLOCKS
+    run_copies(own_blocks((own_q, own_o), (base + info[1], base + 2), block, out, sems))
+
+
+def second_kernel(block, info, got, mine, *refs):
+    out, cross, sems = refs[-3:]
+    copy = pltpu.make_async_copy(got.at[:block], cross, sems.at[1])
+    copy.start()
+    for flag, source in ((1, got), (0, mine)):
+
+        @pl.when(info[2] == flag)
+        def _(source=source):
+            run_copies([pltpu.make_async_copy(source, out, sems.at[0])])
+
+    copy.wait()
+
+
+def third_kernel(block, info, got, across, own_q, own_o, second, out, cross, sems):
+    copy = pltpu.make_async_copy(second.at[:block], cross, sems.at[2 * BLOCKS])
+    copy.start()
+
+    @pl.when(info[2] == 1)
+    def _():
+        base = info[0] * BLOCKS
+        places = [base + n for n in range(BLOCKS)]
+        run_copies(own_blocks((own_q, own_o), places, block, out, sems))
+
+    @pl.when(info[2] == 0)
+    def _():
+        copies = []
+        for n, (source, place) in enumerate(
+            ((got.at[:block], info[1]), (across, 1 - info[1]), (got.at[block:], 2))
+        ):
+            start = pl.multiple_of(place * block, block)
+            copies.append(pltpu.make_async_copy(source, out.at[pl.ds(start, block)], sems.at[n]))
+        run_copies(copies)
+
+    copy.wait()
 
 
 class Fetched:
     first_stages = 2
 
-    def __init__(self, wqkv, wout, section, place, n_section, n_row, n_group):
+    def __init__(self, own, section, place, n_section, n_row, n_group):
         assert n_section == 4 and n_group % 2 == 0
         self.section, self.n_row, self.n_group = section, n_row, n_group
         self.member, self.half = place % n_group, place // n_group % 2
         self.last = n_section - 1
-        self.block = wqkv.shape[0] // n_group // BLOCKS
-        self.own = (wqkv, wout)
-        self.to_last = section == (self.last ^ jnp.where(self.member % 2 == 0, 2, 1))
-        self.mine = jnp.concatenate([self.own_block(self.half), self.own_block(2)], axis=0)
+        self.block = own[0].shape[1] // n_group // BLOCKS
+        self.own = own
+        to_last = section == (self.last ^ jnp.where(self.member % 2 == 0, 2, 1))
+        self.scalars = [self.member, self.half, to_last]
+        (self.mine,) = self.copies(first_kernel, "share_first", [2], own)
         self.got = self.hop(self.mine, 1)
-        self.across = self.cross(self.got)
-        self.stages = [self.halves(self.got, self.across)]
-
-    def own_block(self, place, count=1):
-        start = (self.member * BLOCKS + place) * self.block
-        rows = [lax.dynamic_slice_in_dim(w, start, count * self.block, 0) for w in self.own]
-        return jnp.concatenate(rows, axis=1)
+
+    def copies(self, body, name, blocks, arrays):
+        columns = sum(w.shape[2] for w in self.own)
+        outs = [jax.ShapeDtypeStruct((n * self.block, columns), BF16) for n in blocks]
+        body = functools.partial(body, self.block)
+        return copy_call(body, name, self.scalars, outs, arrays)
 
     def hop(self, value, even_bit):
         perm = [
@@ -664,21 +742,21 @@
 
     def cross(self, value):
         perm = [(r, r ^ self.n_group) for r in range(self.n_row)]
-        return lax.ppermute(value[: self.block], "row", perm)
+        return lax.ppermute(value, "row", perm)
 
     def halves(self, got, across):
         return [(DIRECT, self.share(got)), (ACROSS, self.share(across))]
 
-    def second(self, x):
-        second, x = lax.optimization_barrier((jnp.where(self.to_last, self.got, self.mine), x))
+    def second(self, *ready):
+        arrays = [self.got, self.mine, *ready]
+        second, cross = self.copies(second_kernel, "share_second", [2, 1], arrays)
         second = self.hop(second, 2)
-        self.stages.append(self.halves(second, self.cross(second)))
-        low = jnp.where(self.half == 0, self.got[: self.block], self.across)
-        high = jnp.where(self.half == 0, self.across, self.got[: self.block])
-        relayed = jnp.concatenate([low, high, self.got[self.block :]], axis=0)
-        third = jnp.where(self.to_last, self.own_block(0, BLOCKS), relayed)
+        across = self.cross(cross)
+        self.stages = [self.halves(self.got, across)]
+        arrays = [self.got, across, *self.own, second]
+        third, cross = self.copies(third_kernel, "share_third", [BLOCKS, 1], arrays)
         self.third = self.hop(third, 2)
-        return x
+        self.stages.append(self.halves(second, self.cross(cross)))
 
     def finish(self, ready):
         third, ready = lax.optimization_barrier((self.third, ready))
@@ -717,7 +795,7 @@
     member = place % n_group
     rows = rows_here * micro
     scale = HEAD_DIM ** (-0.5) / math.sqrt(rows_here * n_row)
-    fetched = Fetched(w_qkv[0], w_out[0], section, place, n_section, n_row, n_group)
+    fetched = Fetched((w_qkv, w_out), section, place, n_section, n_row, n_group)
     same = [[m * n_group + g for m in range(micro)] for g in range(n_group)]
     exchange = functools.partial(
         lax.all_to_all,
@@ -729,18 +807,15 @@
     )
     tok = exchange(tokens).reshape(-1)
     top_grad = exchange(out_grad).reshape(rows * seq, width)
-    gains = jnp.concatenate(
-        [ln_gain]
-        + [
-            lax.ppermute(ln_gain, "section", [(s, s ^ offset) for s in range(n_section)])
-            for offset in range(1, n_section)
-        ],
-        axis=0,
-    )
+    gain_parts = [ln_gain] + [
+        lax.ppermute(ln_gain, "section", [(s, s ^ offset) for s in range(n_section)])
+        for offset in range(1, n_section)
+    ]
+    gains = jnp.concatenate(gain_parts, axis=0)
     table = (jnp.arange(embed.shape[0], dtype=jnp.int32)[:, None] == tok[None, :]).astype(BF16)
     x = lax.dot_general(table, embed, TN, preferred_element_type=F32)
 
-    x, gains = fetched.second((x, gains))
+    fetched.second(x, *gain_parts[1:])
     chain = Chain(
         fetched, member, n_row, n_group, (w_qkv, w_out), gains, seq, width, rows, scale
     )
@@ -779,11 +854,14 @@
         )
         scores = group_swap(part, send, n_row, n_group)
     early = RowSum(*chain.early(probs[0], qkvs[0], dmix, xs[0], dy, grads[:2]), place, n_row)
-    early.step()
+    early.add(early.exchange())
     early.send, other = lax.optimization_barrier((early.send, scores[1]))
-    late = chain.late((scores[0], other), probs[0], qkvs[0], xs[0], grads[2:])
+    moved = early.exchange()
+    late = RowSum(*chain.late((scores[0], other), probs[0], qkvs[0], xs[0], grads[2:]), place, n_row)
+    late.send, moved = lax.optimization_barrier((late.send, moved))
+    early.add(moved)
     g_early = early.finish()
-    g_late = RowSum(*late, place, n_row).finish()
+    g_late = late.finish()
     g_qkv = jnp.concatenate([g_late, g_early[:, width:]], axis=1)
     block = width // n_row
     w_here = lax.dynamic_slice_in_dim(w_qkv[0], place * block, block, 0).astype(F32)

time: 313 us -> 526 us (1.68)
  Pallas kernels: 144 us -> 365 us
  local copies, waits for them, and re-layouts: 18.5 us -> 12.8 us
    pallas_call x0 -> x3, Pallas kernels: none -> 220 us  [copy_call(): pl.pallas_call(body, name=name, out_shape=outs, grid_spec=pltpu.PrefetchS...]
    ppermute x8, waiting for transfers between devices: 51.2 us -> 68.7 us  [the longest x6 38.6 us: exchange(): return lax.ppermute(self.send.astype(BF16), 'row', perm)]
    ppermute x3, waiting for transfers between devices: 19.2 us -> 1.73 us  [hop(): return lax.ppermute(value, ('section', 'row'), perm)]
    select_n x3 -> x0, other arithmetic: 5.57 us -> none  [the longest x1 2.2 us: second(): third = jnp.where(self.to_last, self.own_block(0, BLOCKS), relayed)]
  transfers between devices with their start and end apart: 28 -> 28, of which waited for: 15 -> 18; matrix products, arithmetic and copies ran while one was open for 6% -> 2% of each run, Pallas kernels for 14% -> 29%
where the time goes in v6:
time: 526 us; the launch traced here: 517 us
  Pallas kernels  365 us (69%)
  waiting for transfers between devices  93.8 us (18%)
  starting transfers between devices  32.4 us (6%)
  local copies, waits for them, and re-layouts  12.8 us (2%)
  other arithmetic  9.41 us (2%)
    pallas_call x3, Pallas kernels, copy_call(): pl.pallas_call(body, name=name, out_shape=outs, grid_spec=pltpu.PrefetchS...  220 us
    pallas_call x9, Pallas kernels, call(): pl.pallas_call(functools.partial(body, layout=layout), name=name, out_sha...  145 us
    ppermute x6, waiting for transfers between devices, exchange(): return lax.ppermute(self.send.astype(BF16), 'row', perm)  38.6 us
    ppermute x2, waiting for transfers between devices, cross(): return lax.ppermute(value, 'row', perm)  30.1 us
    ppermute x7, waiting for transfers between devices, group_swap(): other = lax.ppermute(send, 'row', [(r, r ^ bit) for r in range(n_row)])  11.2 us
  transfers between devices with their start and end apart: 28, of which 18 were waited for; matrix products, arithmetic and copies ran while one was open for 2% of the time, Pallas kernels for 29%

profile of v6, /device:TPU:0, one launch (start us, length us, event | category | flops | bytes accessed | tf_op | source)
XLA Modules:
  0.0 516.7 jit_solution(3796429658107427435)
XLA Ops:
  1.4 49.6 %share_first.1.mine = bf16[256,3072]{1,0:T(8,128)(2,1)} custom-call(s32[3]{0:T(128)} %pad_add_fusion.info, bf16[1,768,2304]{2,1,0:T(8,128)(2,1)} %refs_13_.3, bf16[1,768,768]{2,1,0:T(8,128)(2,1)} %refs_14_.3), custom_call_target="tpu_custom_call" | custom-call | tf_op jit(solution)/shard_map/share_first/pallas_call | solution.py:640
  51.0 3.0 collective-permute-start.3
  54.0 4.9 all-to-all-start
  58.9 1.5 collective-permute-start.2
  60.9 1.5 collective-permute-start
  62.4 2.1 all-to-all-done
  64.4 2.3 fusion.4.refs_0_.refs_3_.refs_4_
  66.8 7.4 %collective-permute-done.2.refs_3_ = f32[1,768]{1,0:T(1,128)S(1)} collective-permute-done((f32[1,768]{1,0:T(1,128)S(1)}, f32[1,768]{1,0:T(1,128)S(1)}, u32[]{:S(2)}, u32[]{:S(2)}) %collective-permute-start.2) | collective-permute-done | bytes 3104 | tf_op jit(solution)/shard_map/ppermute | solution.py:811
  74.8 1.1 copy-done.2
  75.9 73.3 %share_second.1 = (bf16[256,3072]{1,0:T(8,128)(2,1)}, bf16[128,3072]{1,0:T(8,128)(2,1)}) custom-call(s32[3]{0:T(128)} %pad_add_fusion.info, bf16[256,3072]{1,0:T(8,128)(2,1)} %copy-done.2, bf16[256,3072]{1,0:T(8,128)(2,1)} %share_first.1.mine, f32[1024,768]{1,0:T(8,128)} %fusion.4.refs_0_.refs_3_.refs_4_, f32[1,768]{1,0:T(1,128)} %copy-done.18, ...), custom_call_target="tpu_custom_call" | custom-call | tf_op jit(solution)/shard_map/share_second/pallas_call | solution.py:640
  149.9 1.6 collective-permute-start.5
  151.5 16.7 %collective-permute-done.5.across = bf16[128,3072]{1,0:T(8,128)(2,1)S(1)} collective-permute-done((bf16[128,3072]{1,0:T(8,128)(2,1)}, bf16[128,3072]{1,0:T(8,128)(2,1)S(1)}, u32[]{:S(2)}, u32[]{:S(2)}) %collective-permute-start.5) | collective-permute-done | bytes 786464 | tf_op jit(solution)/shard_map/ppermute | solution.py:745
  168.2 1.7 collective-permute-done.7.second
  169.9 1.1 copy-done.4
  171.1 97.1 %share_third.1 = (bf16[384,3072]{1,0:T(8,128)(2,1)}, bf16[128,3072]{1,0:T(8,128)(2,1)}) custom-call(s32[3]{0:T(128)} %pad_add_fusion.info, bf16[256,3072]{1,0:T(8,128)(2,1)} %copy-done.2, bf16[128,3072]{1,0:T(8,128)(2,1)} %copy-done.5, bf16[1,768,2304]{2,1,0:T(8,128)(2,1)} %refs_13_.3, bf16[1,768,768]{2,1,0:T(8,128)(2,1)} %refs_14_.3, ...), custom_call_target="tpu_custom_call" | custom-call | tf_op jit(solution)/shard_map/share_third/pallas_call | solution.py:640
  268.2 1.6 collective-permute-start.9
  270.5 1.1 collective-permute-start.6
  271.6 13.4 %collective-permute-done.9 = bf16[128,3072]{1,0:T(8,128)(2,1)S(1)} collective-permute-done((bf16[128,3072]{1,0:T(8,128)(2,1)}, bf16[128,3072]{1,0:T(8,128)(2,1)S(1)}, u32[]{:S(2)}, u32[]{:S(2)}) %collective-permute-start.9) | collective-permute-done | bytes 786464 | tf_op jit(solution)/shard_map/ppermute | solution.py:745
  287.4 11.4 %layer_in_0.1 = (bf16[512,4608]{1,0:T(8,128)(2,1)}, f32[128,1536]{1,0:T(8,128)}) custom-call(s32[7]{0:T(128)} %stack.48.info, f32[1024,768]{1,0:T(8,128)} %fusion.4.refs_0_.refs_3_.refs_4_, f32[4,768]{1,0:T(4,128)} %pad_maximum_fusion.1.refs_1_.refs_4_.refs_5_.refs_6_, bf16[1,768,2304]{2,1,0:T(8,128)(2,1)} %refs_13_.3, bf16[1,768,768]{2,1,0:T(8,128)(2,1)} %refs_14_.3, ...), custom_call_target="tpu_custom_call" | custom-call | flops 6039797760 | bytes 8663040 | tf_op jit(solution)/shard_map/layer_in_0/pallas_call | solution.py:420
  299.0 2.4 collective-permute-done.12.refs_1_
  302.2 5.6 %all-to-all-start.1 = ((bf16[4,2,128,768]{3,2,1,0:T(8,128)(2,1)}), bf16[4,2,128,768]{3,2,1,0:T(8,128)(2,1)}, u32[]{:S(2)}, u32[]{:S(2)}) async-start(bf16[4,2,128,768]{3,2,1,0:T(8,128)(2,1)} %param.11), calls=%async_computation.1 | async-start | bytes 3145728 | tf_op jit(solution)/shard_map/all_to_all | solution.py:809
  308.5 15.0 %layer_in_1.1 = (bf16[128,1536]{1,0:T(8,128)(2,1)}, f32[1024,768]{1,0:T(8,128)}, bf16[512,4608]{1,0:T(8,128)(2,1)}, f32[128,1536]{1,0:T(8,128)}) custom-call(s32[7]{0:T(128)} %stack.52.info, f32[128,1536]{1,0:T(8,128)} %get-tuple-element.59.refs_0_, f32[128,1536]{1,0:T(8,128)} %copy-done.9, ...), custom_call_target="tpu_custom_call" | custom-call | flops 6039797760 | bytes 18493440 | tf_op jit(solution)/shard_map/layer_in_1/pallas_call | solution.py:420
  324.3 1.8 collective-permute-done.14.refs_1_
  327.0 15.8 %layer_in_2.1 = (bf16[128,1536]{1,0:T(8,128)(2,1)}, f32[1024,768]{1,0:T(8,128)}, bf16[512,4608]{1,0:T(8,128)(2,1)}, f32[128,1536]{1,0:T(8,128)}) custom-call(s32[7]{0:T(128)} %stack.56.info, f32[128,1536]{1,0:T(8,128)} %get-tuple-element.64.refs_0_, f32[128,1536]{1,0:T(8,128)} %copy-done.10, bf16[512,4608]{1,0:T(8,128)(2,1)} %get-tuple-element.65.refs_2_.refs_8_.refs_3_, ...), custom_call_target="tpu_custom_call" | custom-call | flops 6039797760 | bytes 18493440 | tf_op jit(solution)/shard_map/layer_in_2/pallas_call | solution.py:420
  343.5 1.7 all-to-all-done.1
  346.2 19.0 %layer_in_3.1 = (bf16[128,1536]{1,0:T(8,128)(2,1)}, f32[1024,768]{1,0:T(8,128)}, bf16[512,4608]{1,0:T(8,128)(2,1)}, f32[256,1536]{1,0:T(8,128)}, bf16[512,1536]{1,0:T(8,128)(2,1)}) custom-call(s32[7]{0:T(128)} %stack.60.info, f32[128,1536]{1,0:T(8,128)} %get-tuple-element.67.refs_0_, f32[128,1536]{1,0:T(8,128)} %copy-done.11, ...), custom_call_target="tpu_custom_call" | custom-call | flops 6039797760 | bytes 22425600 | tf_op jit(solution)/shard_map/layer_in_3/pallas_call | solution.py:420
  365.4 3.5 collective-permute-done.16.refs_1_
  368.9 1.2 copy-done.7
  370.1 20.7 %layer_back_3.1 = (f32[1024,768]{1,0:T(8,128)}, bf16[512,1536]{1,0:T(8,128)(2,1)}, f32[128,1536]{1,0:T(8,128)}, bf16[128,1536]{1,0:T(8,128)(2,1)}, bf16[4,96,153...) custom-call(s32[7]{0:T(128)} %stack.60.info, ...), custom_call_target="tpu_custom_call" | custom-call | flops 6039797760 | bytes 29503488 | tf_op jit(solution)/shard_map/layer_back_3/pallas_call | solution.py:420
  391.1 1.8 collective-permute-done.17.refs_1_
  393.6 20.7 %layer_back_2.1 = (f32[1024,768]{1,0:T(8,128)}, bf16[512,1536]{1,0:T(8,128)(2,1)}, f32[128,1536]{1,0:T(8,128)}, bf16[128,1536]{1,0:T(8,128)(2,1)}, bf16[4,96,153...) custom-call(s32[7]{0:T(128)} %stack.56.info, ...), custom_call_target="tpu_custom_call", output_to_operand_aliasing={{4}: (10, {}), {5}: (11, {}), {6}: (12, {}), {7}: (13, {})} | custom-call | flops 6039797760 | bytes 34222080 | tf_op jit(solution)/shard_map/layer_back_2/pallas_call | solution.py:420
  414.8 1.6 collective-permute-done.18.refs_1_
  417.1 20.8 %layer_back_1.1 = (f32[1024,768]{1,0:T(8,128)}, bf16[512,1536]{1,0:T(8,128)(2,1)}, f32[128,1536]{1,0:T(8,128)}, bf16[128,1536]{1,0:T(8,128)(2,1)}, bf16[4,96,153...) custom-call(s32[7]{0:T(128)} %stack.52.info, ...), custom_call_target="tpu_custom_call", output_to_operand_aliasing={{4}: (10, {}), {5}: (11, {}), {6}: (12, {}), {7}: (13, {})} | custom-call | flops 6039797760 | bytes 34222080 | tf_op jit(solution)/shard_map/layer_back_1/pallas_call | solution.py:420
  437.9 10.9 %early_back_0.1 = (bf16[4,96,1536]{2,1,0:T(8,128)(2,1)}, bf16[4,96,1536]{2,1,0:T(8,128)(2,1)}) custom-call(s32[7]{0:T(128)} %stack.48.info, bf16[128,1536]{1,0:T(8,128)(2,1)} %get-tuple-element.93.refs_0_.refs_2_, bf16[512,4608]{1,0:T(8,128)(2,1)} %get-tuple-element.62.refs_2_.refs_8_.refs_1_.refs_3_, ...), custom_call_target="tpu_custom_call", output_to_operand_aliasing={{0}: (7, {}), {1}: (8, {})} | custom-call | flops 3623878656 | bytes 17707008 | tf_op jit(solution)/shard_map/early_back_0/pallas_call | solution.py:420
  449.4 2.5 collective-permute-done.19
  452.9 2.0 convert_add_fusion.1
  455.0 2.1 collective-permute-start.21
  457.1 10.3 %late_back_0.1 = (bf16[4,96,1536]{2,1,0:T(8,128)(2,1)}, bf16[4,96,1536]{2,1,0:T(8,128)(2,1)}) custom-call(s32[7]{0:T(128)} %stack.48.info, f32[128,1536]{1,0:T(8,128)} %get-tuple-element.92.refs_0_, bf16[128,1536]{1,0:T(8,128)(2,1)} %copy-done.21, bf16[128,1536]{1,0:T(8,128)(2,1)} %get-tuple-element.93.refs_0_.refs_2_, ...), custom_call_target="tpu_custom_call", output_to_operand_aliasing={{0}: (7, {}), {1}: (8, {})} | custom-call | flops 3623878656 | bytes 14168064 | tf_op jit(solution)/shard_map/late_back_0/pallas_call | solution.py:420
  467.3 3.6 collective-permute-done.21
  471.0 3.2 collective-permute-done.22
  474.2 2.0 convert_add_fusion
  476.2 1.8 collective-permute-start.23
  478.0 1.2 bitcast_add_fusion
  479.3 2.4 collective-permute-start.25
  481.7 16.3 %collective-permute-done.23 = bf16[2,96,1536]{2,1,0:T(8,128)(2,1)S(1)} collective-permute-done((bf16[2,96,1536]{2,1,0:T(8,128)(2,1)S(1)}, bf16[2,96,1536]{2,1,0:T(8,128)(2,1)S(1)}, u32[]{:S(2)}, u32[]{:S(2)}) %collective-permute-start.23) | collective-permute-done | bytes 589856 | tf_op jit(solution)/shard_map/ppermute | solution.py:618
  498.2 1.7 collective-permute-start.24
  500.7 13.0 %collective-permute-done.24 = bf16[1,96,1536]{2,1,0:T(8,128)(2,1)S(1)} collective-permute-done((bf16[1,96,1536]{2,1,0:T(8,128)(2,1)S(1)}, bf16[1,96,1536]{2,1,0:T(8,128)(2,1)S(1)}, u32[]{:S(2)}, u32[]{:S(2)}) %collective-permute-start.24) | collective-permute-done | bytes 294944 | tf_op jit(solution)/shard_map/ppermute | solution.py:618
  513.8 2.1 fusion
  (84 shorter events, 16.5 us)
Async XLA Ops:
  0.6 63.8 %copy-start = (bf16[33,768]{1,0:T(8,128)(2,1)S(1)}, bf16[33,768]{1,0:T(8,128)(2,1)}, u32[]{:S(2)}) copy-start(bf16[33,768]{1,0:T(8,128)(2,1)} %param.7) | copy-start | bytes 152068
  1.4 57.5 %copy-start.20 = (f32[1,768]{1,0:T(1,128)S(1)}, f32[1,768]{1,0:T(1,128)}, u32[]{:S(2)}) copy-start(f32[1,768]{1,0:T(1,128)} %param.8) | copy-start | bytes 9220
  51.0 23.2 %collective-permute-start.3 = (bf16[256,3072]{1,0:T(8,128)(2,1)}, bf16[256,3072]{1,0:T(8,128)(2,1)S(1)}, u32[]{:S(2)}, u32[]{:S(2)}) collective-permute-start(bf16[256,3072]{1,0:T(8,128)(2,1)} %share_first.1.mine), channel_id=1, source_target_pairs={{0,8},{1,17},{2,10},{3,19},{4,12},{5,21},{6,14},{7,23},{8,0},{9,25... | collective-permute-start | bytes 4718600 | tf_op jit(solution)/shard_map/ppermute | solution.py:741
  54.0 10.4 %all-to-all-start = ((s32[4,2,128]{2,1,0:T(2,128)}), s32[4,2,128]{2,1,0:T(2,128)S(1)}, u32[]{:S(2)}, u32[]{:S(2)}) async-start(s32[4,2,128]{2,1,0:T(2,128)} %param.6), calls=%async_computation | async-start | bytes 8192 | tf_op jit(solution)/shard_map/all_to_all | solution.py:808
  58.9 15.3 %collective-permute-start.2 = (f32[1,768]{1,0:T(1,128)S(1)}, f32[1,768]{1,0:T(1,128)S(1)}, u32[]{:S(2)}, u32[]{:S(2)}) collective-permute-start(f32[1,768]{1,0:T(1,128)S(1)} %copy-done.20), channel_id=1, source_target_pairs={{0,24},{8,16},{16,8},{24,0},{1,25},{9,17},{17,9},{25,1},{2,26},{10... | collective-permute-start | bytes 9224 | tf_op jit(solution)/shard_map/ppermute | solution.py:811
  60.4 13.8 %collective-permute-start.1 = (f32[1,768]{1,0:T(1,128)S(1)}, f32[1,768]{1,0:T(1,128)S(1)}, u32[]{:S(2)}, u32[]{:S(2)}) collective-permute-start(f32[1,768]{1,0:T(1,128)S(1)} %copy-done.20), channel_id=1, source_target_pairs={{0,16},{8,24},{16,0},{24,8},{1,17},{9,25},{17,1},{25,9},{2,18},{10... | collective-permute-start | bytes 9224 | tf_op jit(solution)/shard_map/ppermute | solution.py:811
  60.9 13.3 %collective-permute-start = (f32[1,768]{1,0:T(1,128)S(1)}, f32[1,768]{1,0:T(1,128)S(1)}, u32[]{:S(2)}, u32[]{:S(2)}) collective-permute-start(f32[1,768]{1,0:T(1,128)S(1)} %copy-done.20), channel_id=1, source_target_pairs={{0,8},{8,0},{16,24},{24,16},{1,9},{9,1},{17,25},{25,17},{2,10},{10... | collective-permute-start | bytes 9224 | tf_op jit(solution)/shard_map/ppermute | solution.py:811
  74.2 0.6 copy-start.16
  74.8 1.1 copy-start.2
  149.2 20.7 %collective-permute-start.7 = (bf16[256,3072]{1,0:T(8,128)(2,1)}, bf16[256,3072]{1,0:T(8,128)(2,1)S(1)}, u32[]{:S(2)}, u32[]{:S(2)}) collective-permute-start(bf16[256,3072]{1,0:T(8,128)(2,1)} %get-tuple-element.57), channel_id=1, source_target_pairs={{0,16},{1,9},{2,18},{3,11},{4,20},{5,13},{6,22},{7,15},{8,24},{9,1... | collective-permute-start | bytes 4718600 | tf_op jit(solution)/shard_map/ppermute | solution.py:741
  149.9 18.3 %collective-permute-start.5 = (bf16[128,3072]{1,0:T(8,128)(2,1)}, bf16[128,3072]{1,0:T(8,128)(2,1)S(1)}, u32[]{:S(2)}, u32[]{:S(2)}) collective-permute-start(bf16[128,3072]{1,0:T(8,128)(2,1)} %get-tuple-element.56), channel_id=1, source_target_pairs={{0,2},{1,3},{2,0},{3,1},{4,6},{5,7},{6,4},{7,5},{8,10},{9,11},{10,... | collective-permute-start | bytes 2359304 | tf_op jit(solution)/shard_map/ppermute | solution.py:745
  151.5 134.2 %copy-start.15 = (f32[1,768]{1,0:T(1,128)S(1)}, f32[1,768]{1,0:T(1,128)}, u32[]{:S(2)}) copy-start(f32[1,768]{1,0:T(1,128)} %copy-done.14) | copy-start | bytes 9220
  151.5 134.2 %copy-start.17 = (f32[1,768]{1,0:T(1,128)S(1)}, f32[1,768]{1,0:T(1,128)}, u32[]{:S(2)}) copy-start(f32[1,768]{1,0:T(1,128)} %copy-done.16) | copy-start | bytes 9220
  151.5 134.2 %copy-start.19 = (f32[1,768]{1,0:T(1,128)S(1)}, f32[1,768]{1,0:T(1,128)}, u32[]{:S(2)}) copy-start(f32[1,768]{1,0:T(1,128)} %copy-done.18) | copy-start | bytes 9220
  151.5 134.8 %collective-permute-start.4 = (bf16[1,256,3072]{2,1,0:T(8,128)(2,1)}, bf16[1,256,3072]{2,1,0:T(8,128)(2,1)}, u32[]{:S(2)}, u32[]{:S(2)}) collective-permute-start(bf16[1,256,3072]{2,1,0:T(8,128)(2,1)} %bitcast.54), channel_id=1, source_target_pairs={{0,1},{1,0},{2,3},{3,2},{4,5},{5,4},{6,7},{7,6},{8,9},{9,8},{10,11... | collective-permute-start | bytes 4718600 | tf_op jit(solution)/shard_map/ppermute | solution.py:771
  168.2 1.7 copy-start.5
  169.9 1.1 copy-start.4
  268.2 16.7 %collective-permute-start.9 = (bf16[128,3072]{1,0:T(8,128)(2,1)}, bf16[128,3072]{1,0:T(8,128)(2,1)S(1)}, u32[]{:S(2)}, u32[]{:S(2)}) collective-permute-start(bf16[128,3072]{1,0:T(8,128)(2,1)} %get-tuple-element.58), channel_id=1, source_target_pairs={{0,2},{1,3},{2,0},{3,1},{4,6},{5,7},{6,4},{7,5},{8,10},{9,11},{10,... | collective-permute-start | bytes 2359304 | tf_op jit(solution)/shard_map/ppermute | solution.py:745
  269.8 16.5 %collective-permute-start.8 = (bf16[1,256,3072]{2,1,0:T(8,128)(2,1)}, bf16[1,256,3072]{2,1,0:T(8,128)(2,1)}, u32[]{:S(2)}, u32[]{:S(2)}) collective-permute-start(bf16[1,256,3072]{2,1,0:T(8,128)(2,1)} %bitcast.69), channel_id=1, source_target_pairs={{0,1},{1,0},{2,3},{3,2},{4,5},{5,4},{6,7},{7,6},{8,9},{9,8},{10,11... | collective-permute-start | bytes 4718600 | tf_op jit(solution)/shard_map/ppermute | solution.py:771
  269.9 29.1 %collective-permute-start.11 = (bf16[384,3072]{1,0:T(8,128)(2,1)}, bf16[384,3072]{1,0:T(8,128)(2,1)S(1)}, u32[]{:S(2)}, u32[]{:S(2)}) collective-permute-start(bf16[384,3072]{1,0:T(8,128)(2,1)} %get-tuple-element.60), channel_id=1, source_target_pairs={{0,16},{1,9},{2,18},{3,11},{4,20},{5,13},{6,22},{7,15},{8,24},{9,1... | collective-permute-start | bytes 7077896 | tf_op jit(solution)/shard_map/ppermute | solution.py:741
  270.5 15.8 %collective-permute-start.6 = (bf16[1,128,3072]{2,1,0:T(8,128)(2,1)}, bf16[1,128,3072]{2,1,0:T(8,128)(2,1)}, u32[]{:S(2)}, u32[]{:S(2)}) collective-permute-start(bf16[1,128,3072]{2,1,0:T(8,128)(2,1)} %bitcast.77), channel_id=1, source_target_pairs={{0,1},{1,0},{2,3},{3,2},{4,5},{5,4},{6,7},{7,6},{8,9},{9,8},{10,11... | collective-permute-start | bytes 2359304 | tf_op jit(solution)/shard_map/ppermute | solution.py:771
  284.9 2.4 copy-start.6
  284.9 2.4 collective-permute-start.10
  298.8 2.6 collective-permute-start.12
  299.0 2.5 copy-start.3
  301.3 0.9 copy-start.9
  301.3 7.2 %collective-permute-start.13 = (bf16[1,384,3072]{2,1,0:T(8,128)(2,1)S(1)}, bf16[1,384,3072]{2,1,0:T(8,128)(2,1)}, u32[]{:S(2)}, u32[]{:S(2)}) collective-permute-start(bf16[1,384,3072]{2,1,0:T(8,128)(2,1)S(1)} %bitcast.62), channel_id=1, source_target_pairs={{0,1},{1,0},{2,3},{3,2},{4,5},{5,4},{6,7},{7,6},{8,9},{9,8},{10,11... | collective-permute-start | bytes 7077896 | tf_op jit(solution)/shard_map/ppermute | solution.py:771
  302.2 42.9 %all-to-all-start.1 = ((bf16[4,2,128,768]{3,2,1,0:T(8,128)(2,1)}), bf16[4,2,128,768]{3,2,1,0:T(8,128)(2,1)}, u32[]{:S(2)}, u32[]{:S(2)}) async-start(bf16[4,2,128,768]{3,2,1,0:T(8,128)(2,1)} %param.11), calls=%async_computation.1 | async-start | bytes 3145728 | tf_op jit(solution)/shard_map/all_to_all | solution.py:809
  323.5 2.6 collective-permute-start.14
  326.0 0.9 copy-start.10
  342.8 2.6 collective-permute-start.15
  345.3 0.9 copy-start.11
  365.2 3.7 collective-permute-start.16
  368.9 1.2 copy-start.7
  390.8 2.0 collective-permute-start.17
  392.8 0.8 copy-start.13
  414.4 2.0 collective-permute-start.18
  416.4 0.8 copy-start.12
  448.8 3.1 collective-permute-start.19
  449.2 5.8 %collective-permute-start.20 = (bf16[128,1536]{1,0:T(8,128)(2,1)}, bf16[128,1536]{1,0:T(8,128)(2,1)S(1)}, u32[]{:S(2)}, u32[]{:S(2)}) collective-permute-start(bf16[128,1536]{1,0:T(8,128)(2,1)} %get-tuple-element.100), channel_id=1, source_target_pairs={{0,1},{1,0},{2,3},{3,2},{4,5},{5,4},{6,7},{7,6},{8,9},{9,8},{10,11... | collective-permute-start | bytes 1179656 | tf_op jit(solution)/shard_map/ppermute | solution.py:607
  451.9 1.0 copy-start.8
  455.0 2.1 copy-start.21
  455.0 16.0 %collective-permute-start.21 = (bf16[2,96,1536]{2,1,0:T(8,128)(2,1)S(1)}, bf16[2,96,1536]{2,1,0:T(8,128)(2,1)}, u32[]{:S(2)}, u32[]{:S(2)}) collective-permute-start(bf16[2,96,1536]{2,1,0:T(8,128)(2,1)S(1)} %fusion.2), channel_id=1, source_target_pairs={{0,2},{1,3},{2,0},{3,1},{4,6},{5,7},{6,4},{7,5},{8,10},{9,11},{10,... | collective-permute-start | bytes 1769480 | tf_op jit(solution)/shard_map/ppermute | solution.py:618
  471.0 3.2 collective-permute-start.22
  476.2 21.8 %collective-permute-start.23 = (bf16[2,96,1536]{2,1,0:T(8,128)(2,1)S(1)}, bf16[2,96,1536]{2,1,0:T(8,128)(2,1)S(1)}, u32[]{:S(2)}, u32[]{:S(2)}) collective-permute-start(bf16[2,96,1536]{2,1,0:T(8,128)(2,1)S(1)} %fusion.3), channel_id=1, source_target_pairs={{0,2},{1,3},{2,0},{3,1},{4,6},{5,7},{6,4},{7,5},{8,10},{9,11},{10,... | collective-permute-start | bytes 1769480 | tf_op jit(solution)/shard_map/ppermute | solution.py:618
  479.3 20.6 %collective-permute-start.25 = (bf16[1,96,1536]{2,1,0:T(8,128)(2,1)S(1)}, bf16[1,96,1536]{2,1,0:T(8,128)(2,1)S(1)}, u32[]{:S(2)}, u32[]{:S(2)}) collective-permute-start(bf16[1,96,1536]{2,1,0:T(8,128)(2,1)S(1)} %dynamic-slice_convert_fusion), channel_id=1, source_target_pairs={{0,4},{1,5},{2,6},{3,7},{4,0},{5,1},{6,2},{7,3},{8,12},{9,13},{10,... | collective-permute-start | bytes 884744 | tf_op jit(solution)/shard_map/ppermute | solution.py:618
  498.2 15.5 %collective-permute-start.24 = (bf16[1,96,1536]{2,1,0:T(8,128)(2,1)S(1)}, bf16[1,96,1536]{2,1,0:T(8,128)(2,1)S(1)}, u32[]{:S(2)}, u32[]{:S(2)}) collective-permute-start(bf16[1,96,1536]{2,1,0:T(8,128)(2,1)S(1)} %dynamic-slice_convert_fusion.1), channel_id=1, source_target_pairs={{0,4},{1,5},{2,6},{3,7},{4,0},{5,1},{6,2},{7,3},{8,12},{9,13},{10,... | collective-permute-start | bytes 884744 | tf_op jit(solution)/shard_map/ppermute | solution.py:618
  499.9 16.6 %copy-start.1 = (bf16[33,768]{1,0:T(8,128)(2,1)S(1)}, bf16[33,768]{1,0:T(8,128)(2,1)}, u32[]{:S(2)}) copy-start(bf16[33,768]{1,0:T(8,128)(2,1)} %param.7) | copy-start | bytes 152068
  (2 other events, 1.2 us)

commit v7 on v6

--- a/solution.py
+++ b/solution.py
@@ -645,7 +645,7 @@
             num_scalar_prefetch=1,
             grid=(1,),
             in_specs=[any_spec] * len(arrays),
-            out_specs=[any_spec] * len(outs),
+            out_specs=[pl.BlockSpec(o.shape, lambda i, s: (0, 0)) for o in outs],
             scratch_shapes=[pltpu.SemaphoreType.DMA((2 * BLOCKS + 1,))],
         ),
         compiler_params=pltpu.CompilerParams(vmem_limit_bytes=VMEM_LIMIT),

time: 526 us -> 318 us (0.60)
  the two profiles are of different devices: /device:TPU:0 before, /device:TPU:6 now
where the time goes in v7:
time: 318 us; the launch traced here: 313 us
  Pallas kernels  156 us (49%)
  waiting for transfers between devices  99.9 us (31%)
  starting transfers between devices  31.3 us (10%)
  local copies, waits for them, and re-layouts  12.8 us (4%)
  other arithmetic  9.41 us (3%)
    pallas_call x9, Pallas kernels, call(): pl.pallas_call(functools.partial(body, layout=layout), name=name, out_sha...  145 us
    ppermute x6, waiting for transfers between devices, exchange(): return lax.ppermute(self.send.astype(BF16), 'row', perm)  44.7 us
    ppermute x2, waiting for transfers between devices, cross(): return lax.ppermute(value, 'row', perm)  30.6 us
    pallas_call x3, Pallas kernels, copy_call(): pl.pallas_call(body, name=name, out_shape=outs, grid_spec=pltpu.PrefetchS...  11.4 us
    ppermute x7, waiting for transfers between devices, group_swap(): other = lax.ppermute(send, 'row', [(r, r ^ bit) for r in range(n_row)])  11.1 us
    unnamed x44, local copies, waits for them, and re-layouts  9.15 us
    ppermute x6, starting transfers between devices, exchange(): return lax.ppermute(self.send.astype(BF16), 'row', perm)  8.22 us
    ppermute x3, waiting for transfers between devices, local(): lax.ppermute(ln_gain, 'section', [(s, s ^ offset) for s in range(n_sectio...  7.46 us
  transfers between devices with their start and end apart: 28, of which 19 were waited for; matrix products, arithmetic and copies ran while one was open for 3% of the time, Pallas kernels for 16%

profile of v7, /device:TPU:6, one launch (start us, length us, event | category | flops | bytes accessed | tf_op | source)
XLA Modules:
  0.0 313.2 jit_solution(16140202211287819272)
XLA Ops:
  1.4 3.3 %share_first.1.mine = bf16[256,3072]{1,0:T(8,128)(2,1)} custom-call(s32[3]{0:T(128)} %pad_add_fusion.info, bf16[1,768,2304]{2,1,0:T(8,128)(2,1)} %refs_13_.3, bf16[1,768,768]{2,1,0:T(8,128)(2,1)} %refs_14_.3), custom_call_target="tpu_custom_call" | custom-call | tf_op jit(solution)/shard_map/share_first/pallas_call | solution.py:640
  5.3 4.9 %all-to-all-start = ((s32[4,2,128]{2,1,0:T(2,128)}), s32[4,2,128]{2,1,0:T(2,128)S(1)}, u32[]{:S(2)}, u32[]{:S(2)}) async-start(s32[4,2,128]{2,1,0:T(2,128)} %param.6), calls=%async_computation | async-start | bytes 8192 | tf_op jit(solution)/shard_map/all_to_all | solution.py:808
  10.2 1.4 collective-permute-start.2
  11.6 1.5 collective-permute-start.1
  13.7 2.1 all-to-all-done
  15.8 2.3 fusion.4.refs_0_.refs_3_.refs_4_
  18.1 7.4 %collective-permute-done.2.refs_3_ = f32[1,768]{1,0:T(1,128)S(1)} collective-permute-done((f32[1,768]{1,0:T(1,128)S(1)}, f32[1,768]{1,0:T(1,128)S(1)}, u32[]{:S(2)}, u32[]{:S(2)}) %collective-permute-start.2) | collective-permute-done | bytes 3104 | tf_op jit(solution)/shard_map/ppermute | solution.py:811
  26.2 1.1 copy-done.2
  27.3 3.8 %share_second.1 = (bf16[256,3072]{1,0:T(8,128)(2,1)}, bf16[128,3072]{1,0:T(8,128)(2,1)}) custom-call(s32[3]{0:T(128)} %pad_add_fusion.info, bf16[256,3072]{1,0:T(8,128)(2,1)} %copy-done.2, bf16[256,3072]{1,0:T(8,128)(2,1)} %share_first.1.mine, f32[1024,768]{1,0:T(8,128)} %fusion.4.refs_0_.refs_3_.refs_4_, f32[1,768]{1,0:T(1,128)} %copy-done.18, ...), custom_call_target="tpu_custom_call" | custom-call | tf_op jit(solution)/shard_map/share_second/pallas_call | solution.py:640
  31.1 1.5 collective-permute-start.7
  32.6 1.6 collective-permute-start.5
  34.2 15.8 %collective-permute-done.5.across = bf16[128,3072]{1,0:T(8,128)(2,1)S(1)} collective-permute-done((bf16[128,3072]{1,0:T(8,128)(2,1)}, bf16[128,3072]{1,0:T(8,128)(2,1)S(1)}, u32[]{:S(2)}, u32[]{:S(2)}) %collective-permute-start.5) | collective-permute-done | bytes 786464 | tf_op jit(solution)/shard_map/ppermute | solution.py:745
  50.0 1.7 collective-permute-done.7.second
  51.8 1.1 copy-done.4
  52.9 4.3 %share_third.1 = (bf16[384,3072]{1,0:T(8,128)(2,1)}, bf16[128,3072]{1,0:T(8,128)(2,1)}) custom-call(s32[3]{0:T(128)} %pad_add_fusion.info, bf16[256,3072]{1,0:T(8,128)(2,1)} %copy-done.2, bf16[128,3072]{1,0:T(8,128)(2,1)} %copy-done.5, bf16[1,768,2304]{2,1,0:T(8,128)(2,1)} %refs_13_.3, bf16[1,768,768]{2,1,0:T(8,128)(2,1)} %refs_14_.3, ...), custom_call_target="tpu_custom_call" | custom-call | tf_op jit(solution)/shard_map/share_third/pallas_call | solution.py:640
  57.2 1.6 collective-permute-start.9
  58.8 1.4 collective-permute-start.11
  60.2 14.8 %collective-permute-done.9 = bf16[128,3072]{1,0:T(8,128)(2,1)S(1)} collective-permute-done((bf16[128,3072]{1,0:T(8,128)(2,1)}, bf16[128,3072]{1,0:T(8,128)(2,1)S(1)}, u32[]{:S(2)}, u32[]{:S(2)}) %collective-permute-start.9) | collective-permute-done | bytes 786464 | tf_op jit(solution)/shard_map/ppermute | solution.py:745
  77.4 11.4 %layer_in_0.1 = (bf16[512,4608]{1,0:T(8,128)(2,1)}, f32[128,1536]{1,0:T(8,128)}) custom-call(s32[7]{0:T(128)} %stack.48.info, f32[1024,768]{1,0:T(8,128)} %fusion.4.refs_0_.refs_3_.refs_4_, f32[4,768]{1,0:T(4,128)} %pad_maximum_fusion.1.refs_1_.refs_4_.refs_5_.refs_6_, bf16[1,768,2304]{2,1,0:T(8,128)(2,1)} %refs_13_.3, bf16[1,768,768]{2,1,0:T(8,128)(2,1)} %refs_14_.3, ...), custom_call_target="tpu_custom_call" | custom-call | flops 6039797760 | bytes 8663040 | tf_op jit(solution)/shard_map/layer_in_0/pallas_call | solution.py:420
  89.0 2.4 collective-permute-done.12.refs_1_
  92.2 5.4 %all-to-all-start.1 = ((bf16[4,2,128,768]{3,2,1,0:T(8,128)(2,1)}), bf16[4,2,128,768]{3,2,1,0:T(8,128)(2,1)}, u32[]{:S(2)}, u32[]{:S(2)}) async-start(bf16[4,2,128,768]{3,2,1,0:T(8,128)(2,1)} %param.11), calls=%async_computation.1 | async-start | bytes 3145728 | tf_op jit(solution)/shard_map/all_to_all | solution.py:809
  98.4 15.5 %layer_in_1.1 = (bf16[128,1536]{1,0:T(8,128)(2,1)}, f32[1024,768]{1,0:T(8,128)}, bf16[512,4608]{1,0:T(8,128)(2,1)}, f32[128,1536]{1,0:T(8,128)}) custom-call(s32[7]{0:T(128)} %stack.52.info, f32[128,1536]{1,0:T(8,128)} %get-tuple-element.59.refs_0_, f32[128,1536]{1,0:T(8,128)} %copy-done.9, ...), custom_call_target="tpu_custom_call" | custom-call | flops 6039797760 | bytes 18493440 | tf_op jit(solution)/shard_map/layer_in_1/pallas_call | solution.py:420
  114.7 1.8 collective-permute-done.14.refs_1_
  117.3 15.3 %layer_in_2.1 = (bf16[128,1536]{1,0:T(8,128)(2,1)}, f32[1024,768]{1,0:T(8,128)}, bf16[512,4608]{1,0:T(8,128)(2,1)}, f32[128,1536]{1,0:T(8,128)}) custom-call(s32[7]{0:T(128)} %stack.56.info, f32[128,1536]{1,0:T(8,128)} %get-tuple-element.64.refs_0_, f32[128,1536]{1,0:T(8,128)} %copy-done.10, bf16[512,4608]{1,0:T(8,128)(2,1)} %get-tuple-element.65.refs_2_.refs_8_.refs_3_, ...), custom_call_target="tpu_custom_call" | custom-call | flops 6039797760 | bytes 18493440 | tf_op jit(solution)/shard_map/layer_in_2/pallas_call | solution.py:420
  133.9 1.1 all-to-all-done.1
  136.4 20.3 %layer_in_3.1 = (bf16[128,1536]{1,0:T(8,128)(2,1)}, f32[1024,768]{1,0:T(8,128)}, bf16[512,4608]{1,0:T(8,128)(2,1)}, f32[256,1536]{1,0:T(8,128)}, bf16[512,1536]{1,0:T(8,128)(2,1)}) custom-call(s32[7]{0:T(128)} %stack.60.info, f32[128,1536]{1,0:T(8,128)} %get-tuple-element.67.refs_0_, f32[128,1536]{1,0:T(8,128)} %copy-done.11, ...), custom_call_target="tpu_custom_call" | custom-call | flops 6039797760 | bytes 22425600 | tf_op jit(solution)/shard_map/layer_in_3/pallas_call | solution.py:420
  157.1 3.2 %collective-permute-done.16.refs_1_ = f32[256,1536]{1,0:T(8,128)S(1)} collective-permute-done((f32[256,1536]{1,0:T(8,128)}, f32[256,1536]{1,0:T(8,128)S(1)}, u32[]{:S(2)}, u32[]{:S(2)}) %collective-permute-start.16) | collective-permute-done | bytes 1572896 | tf_op jit(solution)/shard_map/ppermute | solution.py:607
  160.3 1.2 copy-done.7
  161.5 31.9 %layer_back_3.1 = (f32[1024,768]{1,0:T(8,128)}, bf16[512,1536]{1,0:T(8,128)(2,1)}, f32[128,1536]{1,0:T(8,128)}, bf16[128,1536]{1,0:T(8,128)(2,1)}, bf16[4,96,153...) custom-call(s32[7]{0:T(128)} %stack.60.info, ...), custom_call_target="tpu_custom_call" | custom-call | flops 6039797760 | bytes 29503488 | tf_op jit(solution)/shard_map/layer_back_3/pallas_call | solution.py:420
  193.8 1.6 collective-permute-done.17.refs_1_
  196.2 20.9 %layer_back_2.1 = (f32[1024,768]{1,0:T(8,128)}, bf16[512,1536]{1,0:T(8,128)(2,1)}, f32[128,1536]{1,0:T(8,128)}, bf16[128,1536]{1,0:T(8,128)(2,1)}, bf16[4,96,153...) custom-call(s32[7]{0:T(128)} %stack.56.info, ...), custom_call_target="tpu_custom_call", output_to_operand_aliasing={{4}: (10, {}), {5}: (11, {}), {6}: (12, {}), {7}: (13, {})} | custom-call | flops 6039797760 | bytes 34222080 | tf_op jit(solution)/shard_map/layer_back_2/pallas_call | solution.py:420
  217.3 1.8 collective-permute-done.18.refs_1_
  219.8 20.8 %layer_back_1.1 = (f32[1024,768]{1,0:T(8,128)}, bf16[512,1536]{1,0:T(8,128)(2,1)}, f32[128,1536]{1,0:T(8,128)}, bf16[128,1536]{1,0:T(8,128)(2,1)}, bf16[4,96,153...) custom-call(s32[7]{0:T(128)} %stack.52.info, ...), custom_call_target="tpu_custom_call", output_to_operand_aliasing={{4}: (10, {}), {5}: (11, {}), {6}: (12, {}), {7}: (13, {})} | custom-call | flops 6039797760 | bytes 34222080 | tf_op jit(solution)/shard_map/layer_back_1/pallas_call | solution.py:420
  240.6 4.9 %early_back_0.1 = (bf16[4,96,1536]{2,1,0:T(8,128)(2,1)}, bf16[4,96,1536]{2,1,0:T(8,128)(2,1)}) custom-call(s32[7]{0:T(128)} %stack.48.info, bf16[128,1536]{1,0:T(8,128)(2,1)} %get-tuple-element.93.refs_0_.refs_2_, bf16[512,4608]{1,0:T(8,128)(2,1)} %get-tuple-element.62.refs_2_.refs_8_.refs_1_.refs_3_, ...), custom_call_target="tpu_custom_call", output_to_operand_aliasing={{0}: (7, {}), {1}: (8, {})} | custom-call | flops 3623878656 | bytes 17707008 | tf_op jit(solution)/shard_map/early_back_0/pallas_call | solution.py:420
  246.1 2.5 collective-permute-done.19
  249.6 2.0 convert_add_fusion.1
  251.7 2.1 collective-permute-start.21
  253.7 4.1 %late_back_0.1 = (bf16[4,96,1536]{2,1,0:T(8,128)(2,1)}, bf16[4,96,1536]{2,1,0:T(8,128)(2,1)}) custom-call(s32[7]{0:T(128)} %stack.48.info, f32[128,1536]{1,0:T(8,128)} %get-tuple-element.92.refs_0_, bf16[128,1536]{1,0:T(8,128)(2,1)} %copy-done.21, bf16[128,1536]{1,0:T(8,128)(2,1)} %get-tuple-element.93.refs_0_.refs_2_, ...), custom_call_target="tpu_custom_call", output_to_operand_aliasing={{0}: (7, {}), {1}: (8, {})} | custom-call | flops 3623878656 | bytes 14168064 | tf_op jit(solution)/shard_map/late_back_0/pallas_call | solution.py:420
  257.8 9.7 %collective-permute-done.21 = bf16[2,96,1536]{2,1,0:T(8,128)(2,1)} collective-permute-done((bf16[2,96,1536]{2,1,0:T(8,128)(2,1)S(1)}, bf16[2,96,1536]{2,1,0:T(8,128)(2,1)}, u32[]{:S(2)}, u32[]{:S(2)}) %collective-permute-start.21) | collective-permute-done | bytes 589856 | tf_op jit(solution)/shard_map/ppermute | solution.py:618
  267.5 3.2 %collective-permute-done.22 = bf16[4,96,1536]{2,1,0:T(8,128)(2,1)} collective-permute-done((bf16[4,96,1536]{2,1,0:T(8,128)(2,1)}, bf16[4,96,1536]{2,1,0:T(8,128)(2,1)}, u32[]{:S(2)}, u32[]{:S(2)}) %collective-permute-start.22) | collective-permute-done | bytes 1179680 | tf_op jit(solution)/shard_map/ppermute | solution.py:618
  270.7 2.0 convert_add_fusion
  272.8 1.8 collective-permute-start.23
  274.6 1.2 bitcast_add_fusion
  275.8 2.4 collective-permute-start.25
  278.2 16.3 %collective-permute-done.23 = bf16[2,96,1536]{2,1,0:T(8,128)(2,1)S(1)} collective-permute-done((bf16[2,96,1536]{2,1,0:T(8,128)(2,1)S(1)}, bf16[2,96,1536]{2,1,0:T(8,128)(2,1)S(1)}, u32[]{:S(2)}, u32[]{:S(2)}) %collective-permute-start.23) | collective-permute-done | bytes 589856 | tf_op jit(solution)/shard_map/ppermute | solution.py:618
  294.7 1.7 collective-permute-start.24
  297.2 13.0 %collective-permute-done.24 = bf16[1,96,1536]{2,1,0:T(8,128)(2,1)S(1)} collective-permute-done((bf16[1,96,1536]{2,1,0:T(8,128)(2,1)S(1)}, bf16[1,96,1536]{2,1,0:T(8,128)(2,1)S(1)}, u32[]{:S(2)}, u32[]{:S(2)}) %collective-permute-start.24) | collective-permute-done | bytes 294944 | tf_op jit(solution)/shard_map/ppermute | solution.py:618
  310.3 2.1 fusion
  (84 shorter events, 17.1 us)
Async XLA Ops:
  0.6 15.2 %copy-start = (bf16[33,768]{1,0:T(8,128)(2,1)S(1)}, bf16[33,768]{1,0:T(8,128)(2,1)}, u32[]{:S(2)}) copy-start(bf16[33,768]{1,0:T(8,128)(2,1)} %param.7) | copy-start | bytes 152068
  1.4 8.8 %copy-start.20 = (f32[1,768]{1,0:T(1,128)S(1)}, f32[1,768]{1,0:T(1,128)}, u32[]{:S(2)}) copy-start(f32[1,768]{1,0:T(1,128)} %param.8) | copy-start | bytes 9220
  4.7 20.8 %collective-permute-start.3 = (bf16[256,3072]{1,0:T(8,128)(2,1)}, bf16[256,3072]{1,0:T(8,128)(2,1)S(1)}, u32[]{:S(2)}, u32[]{:S(2)}) collective-permute-start(bf16[256,3072]{1,0:T(8,128)(2,1)} %share_first.1.mine), channel_id=1, source_target_pairs={{0,8},{1,17},{2,10},{3,19},{4,12},{5,21},{6,14},{7,23},{8,0},{9,25... | collective-permute-start | bytes 4718600 | tf_op jit(solution)/shard_map/ppermute | solution.py:741
  5.3 10.4 %all-to-all-start = ((s32[4,2,128]{2,1,0:T(2,128)}), s32[4,2,128]{2,1,0:T(2,128)S(1)}, u32[]{:S(2)}, u32[]{:S(2)}) async-start(s32[4,2,128]{2,1,0:T(2,128)} %param.6), calls=%async_computation | async-start | bytes 8192 | tf_op jit(solution)/shard_map/all_to_all | solution.py:808
  10.2 15.3 %collective-permute-start.2 = (f32[1,768]{1,0:T(1,128)S(1)}, f32[1,768]{1,0:T(1,128)S(1)}, u32[]{:S(2)}, u32[]{:S(2)}) collective-permute-start(f32[1,768]{1,0:T(1,128)S(1)} %copy-done.20), channel_id=1, source_target_pairs={{0,24},{8,16},{16,8},{24,0},{1,25},{9,17},{17,9},{25,1},{2,26},{10... | collective-permute-start | bytes 9224 | tf_op jit(solution)/shard_map/ppermute | solution.py:811
  11.6 13.8 %collective-permute-start.1 = (f32[1,768]{1,0:T(1,128)S(1)}, f32[1,768]{1,0:T(1,128)S(1)}, u32[]{:S(2)}, u32[]{:S(2)}) collective-permute-start(f32[1,768]{1,0:T(1,128)S(1)} %copy-done.20), channel_id=1, source_target_pairs={{0,16},{8,24},{16,0},{24,8},{1,17},{9,25},{17,1},{25,9},{2,18},{10... | collective-permute-start | bytes 9224 | tf_op jit(solution)/shard_map/ppermute | solution.py:811
  13.2 12.4 %collective-permute-start = (f32[1,768]{1,0:T(1,128)S(1)}, f32[1,768]{1,0:T(1,128)S(1)}, u32[]{:S(2)}, u32[]{:S(2)}) collective-permute-start(f32[1,768]{1,0:T(1,128)S(1)} %copy-done.20), channel_id=1, source_target_pairs={{0,8},{8,0},{16,24},{24,16},{1,9},{9,1},{17,25},{25,17},{2,10},{10... | collective-permute-start | bytes 9224 | tf_op jit(solution)/shard_map/ppermute | solution.py:811
  25.5 0.6 copy-start.16
  26.2 1.1 copy-start.2
  31.1 20.7 %collective-permute-start.7 = (bf16[256,3072]{1,0:T(8,128)(2,1)}, bf16[256,3072]{1,0:T(8,128)(2,1)S(1)}, u32[]{:S(2)}, u32[]{:S(2)}) collective-permute-start(bf16[256,3072]{1,0:T(8,128)(2,1)} %get-tuple-element.57), channel_id=1, source_target_pairs={{0,16},{1,9},{2,18},{3,11},{4,20},{5,13},{6,22},{7,15},{8,24},{9,1... | collective-permute-start | bytes 4718600 | tf_op jit(solution)/shard_map/ppermute | solution.py:741
  32.6 17.4 %collective-permute-start.5 = (bf16[128,3072]{1,0:T(8,128)(2,1)}, bf16[128,3072]{1,0:T(8,128)(2,1)S(1)}, u32[]{:S(2)}, u32[]{:S(2)}) collective-permute-start(bf16[128,3072]{1,0:T(8,128)(2,1)} %get-tuple-element.56), channel_id=1, source_target_pairs={{0,2},{1,3},{2,0},{3,1},{4,6},{5,7},{6,4},{7,5},{8,10},{9,11},{10,... | collective-permute-start | bytes 2359304 | tf_op jit(solution)/shard_map/ppermute | solution.py:745
  34.2 41.6 %copy-start.15 = (f32[1,768]{1,0:T(1,128)S(1)}, f32[1,768]{1,0:T(1,128)}, u32[]{:S(2)}) copy-start(f32[1,768]{1,0:T(1,128)} %copy-done.14) | copy-start | bytes 9220
  34.2 41.6 %copy-start.17 = (f32[1,768]{1,0:T(1,128)S(1)}, f32[1,768]{1,0:T(1,128)}, u32[]{:S(2)}) copy-start(f32[1,768]{1,0:T(1,128)} %copy-done.16) | copy-start | bytes 9220
  34.2 41.6 %copy-start.19 = (f32[1,768]{1,0:T(1,128)S(1)}, f32[1,768]{1,0:T(1,128)}, u32[]{:S(2)}) copy-start(f32[1,768]{1,0:T(1,128)} %copy-done.18) | copy-start | bytes 9220
  34.2 42.2 %collective-permute-start.4 = (bf16[1,256,3072]{2,1,0:T(8,128)(2,1)}, bf16[1,256,3072]{2,1,0:T(8,128)(2,1)}, u32[]{:S(2)}, u32[]{:S(2)}) collective-permute-start(bf16[1,256,3072]{2,1,0:T(8,128)(2,1)} %bitcast.54), channel_id=1, source_target_pairs={{0,1},{1,0},{2,3},{3,2},{4,5},{5,4},{6,7},{7,6},{8,9},{9,8},{10,11... | collective-permute-start | bytes 4718600 | tf_op jit(solution)/shard_map/ppermute | solution.py:771
  50.0 1.8 copy-start.5
  51.8 1.1 copy-start.4
  57.2 17.8 %collective-permute-start.9 = (bf16[128,3072]{1,0:T(8,128)(2,1)}, bf16[128,3072]{1,0:T(8,128)(2,1)S(1)}, u32[]{:S(2)}, u32[]{:S(2)}) collective-permute-start(bf16[128,3072]{1,0:T(8,128)(2,1)} %get-tuple-element.58), channel_id=1, source_target_pairs={{0,2},{1,3},{2,0},{3,1},{4,6},{5,7},{6,4},{7,5},{8,10},{9,11},{10,... | collective-permute-start | bytes 2359304 | tf_op jit(solution)/shard_map/ppermute | solution.py:745
  58.8 17.6 %collective-permute-start.8 = (bf16[1,256,3072]{2,1,0:T(8,128)(2,1)}, bf16[1,256,3072]{2,1,0:T(8,128)(2,1)}, u32[]{:S(2)}, u32[]{:S(2)}) collective-permute-start(bf16[1,256,3072]{2,1,0:T(8,128)(2,1)} %bitcast.69), channel_id=1, source_target_pairs={{0,1},{1,0},{2,3},{3,2},{4,5},{5,4},{6,7},{7,6},{8,9},{9,8},{10,11... | collective-permute-start | bytes 4718600 | tf_op jit(solution)/shard_map/ppermute | solution.py:771
  58.8 30.2 %collective-permute-start.11 = (bf16[384,3072]{1,0:T(8,128)(2,1)}, bf16[384,3072]{1,0:T(8,128)(2,1)S(1)}, u32[]{:S(2)}, u32[]{:S(2)}) collective-permute-start(bf16[384,3072]{1,0:T(8,128)(2,1)} %get-tuple-element.60), channel_id=1, source_target_pairs={{0,16},{1,9},{2,18},{3,11},{4,20},{5,13},{6,22},{7,15},{8,24},{9,1... | collective-permute-start | bytes 7077896 | tf_op jit(solution)/shard_map/ppermute | solution.py:741
  60.2 16.2 %collective-permute-start.6 = (bf16[1,128,3072]{2,1,0:T(8,128)(2,1)}, bf16[1,128,3072]{2,1,0:T(8,128)(2,1)}, u32[]{:S(2)}, u32[]{:S(2)}) collective-permute-start(bf16[1,128,3072]{2,1,0:T(8,128)(2,1)} %bitcast.77), channel_id=1, source_target_pairs={{0,1},{1,0},{2,3},{3,2},{4,5},{5,4},{6,7},{7,6},{8,9},{9,8},{10,11... | collective-permute-start | bytes 2359304 | tf_op jit(solution)/shard_map/ppermute | solution.py:771
  75.0 2.4 copy-start.6
  75.0 2.4 collective-permute-start.10
  88.8 2.6 collective-permute-start.12
  89.0 2.5 copy-start.3
  91.4 0.9 copy-start.9
  91.4 7.0 %collective-permute-start.13 = (bf16[1,384,3072]{2,1,0:T(8,128)(2,1)S(1)}, bf16[1,384,3072]{2,1,0:T(8,128)(2,1)}, u32[]{:S(2)}, u32[]{:S(2)}) collective-permute-start(bf16[1,384,3072]{2,1,0:T(8,128)(2,1)S(1)} %bitcast.62), channel_id=1, source_target_pairs={{0,1},{1,0},{2,3},{3,2},{4,5},{5,4},{6,7},{7,6},{8,9},{9,8},{10,11... | collective-permute-start | bytes 7077896 | tf_op jit(solution)/shard_map/ppermute | solution.py:771
  92.2 42.8 %all-to-all-start.1 = ((bf16[4,2,128,768]{3,2,1,0:T(8,128)(2,1)}), bf16[4,2,128,768]{3,2,1,0:T(8,128)(2,1)}, u32[]{:S(2)}, u32[]{:S(2)}) async-start(bf16[4,2,128,768]{3,2,1,0:T(8,128)(2,1)} %param.11), calls=%async_computation.1 | async-start | bytes 3145728 | tf_op jit(solution)/shard_map/all_to_all | solution.py:809
  113.8 2.6 collective-permute-start.14
  116.4 0.9 copy-start.10
  132.6 2.8 collective-permute-start.15
  135.5 0.9 copy-start.11
  156.6 3.7 %collective-permute-start.16 = (f32[256,1536]{1,0:T(8,128)}, f32[256,1536]{1,0:T(8,128)S(1)}, u32[]{:S(2)}, u32[]{:S(2)}) collective-permute-start(f32[256,1536]{1,0:T(8,128)} %get-tuple-element.70.refs_0_), channel_id=1, source_target_pairs={{0,1},{1,0},{2,3},{3,2},{4,5},{5,4},{6,7},{7,6},{8,9},{9,8},{10,11... | collective-permute-start | bytes 4718600 | tf_op jit(solution)/shard_map/ppermute | solution.py:607
  160.3 1.2 copy-start.7
  193.4 2.0 collective-permute-start.17
  195.4 0.8 copy-start.13
  217.1 2.0 collective-permute-start.18
  219.1 0.8 copy-start.12
  245.5 3.1 collective-permute-start.19
  245.7 5.9 %collective-permute-start.20 = (bf16[128,1536]{1,0:T(8,128)(2,1)}, bf16[128,1536]{1,0:T(8,128)(2,1)S(1)}, u32[]{:S(2)}, u32[]{:S(2)}) collective-permute-start(bf16[128,1536]{1,0:T(8,128)(2,1)} %get-tuple-element.100), channel_id=1, source_target_pairs={{0,1},{1,0},{2,3},{3,2},{4,5},{5,4},{6,7},{7,6},{8,9},{9,8},{10,11... | collective-permute-start | bytes 1179656 | tf_op jit(solution)/shard_map/ppermute | solution.py:607
  248.6 1.0 copy-start.8
  251.6 2.1 copy-start.21
  251.7 15.9 %collective-permute-start.21 = (bf16[2,96,1536]{2,1,0:T(8,128)(2,1)S(1)}, bf16[2,96,1536]{2,1,0:T(8,128)(2,1)}, u32[]{:S(2)}, u32[]{:S(2)}) collective-permute-start(bf16[2,96,1536]{2,1,0:T(8,128)(2,1)S(1)} %fusion.2), channel_id=1, source_target_pairs={{0,2},{1,3},{2,0},{3,1},{4,6},{5,7},{6,4},{7,5},{8,10},{9,11},{10,... | collective-permute-start | bytes 1769480 | tf_op jit(solution)/shard_map/ppermute | solution.py:618
  267.5 3.2 %collective-permute-start.22 = (bf16[4,96,1536]{2,1,0:T(8,128)(2,1)}, bf16[4,96,1536]{2,1,0:T(8,128)(2,1)}, u32[]{:S(2)}, u32[]{:S(2)}) collective-permute-start(bf16[4,96,1536]{2,1,0:T(8,128)(2,1)} %get-tuple-element.107), channel_id=1, source_target_pairs={{0,1},{1,0},{2,3},{3,2},{4,5},{5,4},{6,7},{7,6},{8,9},{9,8},{10,11... | collective-permute-start | bytes 3538952 | tf_op jit(solution)/shard_map/ppermute | solution.py:618
  272.8 21.8 %collective-permute-start.23 = (bf16[2,96,1536]{2,1,0:T(8,128)(2,1)S(1)}, bf16[2,96,1536]{2,1,0:T(8,128)(2,1)S(1)}, u32[]{:S(2)}, u32[]{:S(2)}) collective-permute-start(bf16[2,96,1536]{2,1,0:T(8,128)(2,1)S(1)} %fusion.3), channel_id=1, source_target_pairs={{0,2},{1,3},{2,0},{3,1},{4,6},{5,7},{6,4},{7,5},{8,10},{9,11},{10,... | collective-permute-start | bytes 1769480 | tf_op jit(solution)/shard_map/ppermute | solution.py:618
  275.8 20.6 %collective-permute-start.25 = (bf16[1,96,1536]{2,1,0:T(8,128)(2,1)S(1)}, bf16[1,96,1536]{2,1,0:T(8,128)(2,1)S(1)}, u32[]{:S(2)}, u32[]{:S(2)}) collective-permute-start(bf16[1,96,1536]{2,1,0:T(8,128)(2,1)S(1)} %dynamic-slice_convert_fusion), channel_id=1, source_target_pairs={{0,4},{1,5},{2,6},{3,7},{4,0},{5,1},{6,2},{7,3},{8,12},{9,13},{10,... | collective-permute-start | bytes 884744 | tf_op jit(solution)/shard_map/ppermute | solution.py:618
  294.7 15.5 %collective-permute-start.24 = (bf16[1,96,1536]{2,1,0:T(8,128)(2,1)S(1)}, bf16[1,96,1536]{2,1,0:T(8,128)(2,1)S(1)}, u32[]{:S(2)}, u32[]{:S(2)}) collective-permute-start(bf16[1,96,1536]{2,1,0:T(8,128)(2,1)S(1)} %dynamic-slice_convert_fusion.1), channel_id=1, source_target_pairs={{0,4},{1,5},{2,6},{3,7},{4,0},{5,1},{6,2},{7,3},{8,12},{9,13},{10,... | collective-permute-start | bytes 884744 | tf_op jit(solution)/shard_map/ppermute | solution.py:618
  296.5 16.5 %copy-start.1 = (bf16[33,768]{1,0:T(8,128)(2,1)S(1)}, bf16[33,768]{1,0:T(8,128)(2,1)}, u32[]{:S(2)}) copy-start(bf16[33,768]{1,0:T(8,128)(2,1)} %param.7) | copy-start | bytes 152068
  (2 other events, 1.2 us)

commit v8 on v5

--- a/solution.py
+++ b/solution.py
@@ -15,7 +15,7 @@
 DIRECT, ACROSS, FULL = range(3)
 F32 = jnp.float32
 BF16 = jnp.bfloat16
-VMEM_LIMIT = 60 * 1024 * 1024
+VMEM_LIMIT = 50 * 1024 * 1024
 NT = (((1,), (1,)), ((), ()))
 TN = (((0,), (0,)), ((), ()))
 
@@ -269,7 +269,15 @@
         copy.wait()
 
 
-def backward_kernel(is_top, info, *refs, layout, scale, seq, width, steps):
+def backward_kernel(is_top, info, *refs, **sizes):
+    step = pl.program_id(0)
+
+    @pl.when(info[7] == 1)
+    def _():
+        backward_body(is_top, step, info, *refs, **sizes)
+
+
+def backward_body(is_top, step, info, *refs, layout, scale, seq, width, steps):
     it = iter(refs)
     sa, sb = next(it), next(it)
     if not is_top:
@@ -287,7 +295,6 @@
     wq, sem_q, wo, sem_o = [next(it) for _ in range(4)]
     if is_top:
         probs = next(it)
-    step = pl.program_id(0)
     get_q = Weights(info, 0, own_q, stages, slice(0, 3 * width), wq, sem_q)
     get_o = Weights(info, 2, own_o, stages, slice(3 * width, 4 * width), wo, sem_o)
     own = info[0] == 0
@@ -394,6 +401,7 @@
     def info(self, now, other):
         picks = self.fetched.choices(now) + self.fetched.choices(other)
         picks += [self.member, self.fetched.half, self.fetched.section ^ now]
+        picks.append(self.fetched.section <= now)
         return jnp.stack(picks).astype(jnp.int32)
 
     def whole(self, rows, lanes):
@@ -430,7 +438,7 @@
             ),
             input_output_aliases=aliases,
             compiler_params=pltpu.CompilerParams(
-                dimension_semantics=("arbitrary",), vmem_limit_bytes=VMEM_LIMIT
+                dimension_semantics=("arbitrary",), vmem_limit_bytes=VMEM_LIMIT + self.wide_bytes()
             ),
             cost_estimate=pl.CostEstimate(flops=flops, bytes_accessed=size, transcendentals=0),
         )(info, *arrays, *weights)
@@ -452,6 +460,9 @@
 
     def grad_type(self):
         return BF16 if self.width // self.n_row % 16 == 0 else F32
+
+    def wide_bytes(self):
+        return 0 if self.grad_type() == BF16 else 10 * 1024 * 1024
 
     def grad_scratch(self):
         shape = (self.width, 2 * self.width)
@@ -613,9 +624,11 @@
     def __init__(self, keep, send, place, n_row):
         self.keep, self.send, self.place, self.n_row, self.bit = keep, send, place, n_row, 1
 
-    def step(self):
+    def exchange(self):
         perm = [(r, r ^ self.bit) for r in range(self.n_row)]
-        other = lax.ppermute(self.send.astype(BF16), "row", perm)
+        return lax.ppermute(self.send.astype(BF16), "row", perm)
+
+    def add(self, other):
         value = self.keep.astype(F32) + other.astype(F32)
         self.bit *= 2
         if self.bit == self.n_row:
@@ -629,7 +642,7 @@
     def finish(self):
         value = None
         while value is None:
-            value = self.step()
+            value = self.add(self.exchange())
         return value
 
 
@@ -729,14 +742,11 @@
     )
     tok = exchange(tokens).reshape(-1)
     top_grad = exchange(out_grad).reshape(rows * seq, width)
-    gains = jnp.concatenate(
-        [ln_gain]
-        + [
-            lax.ppermute(ln_gain, "section", [(s, s ^ offset) for s in range(n_section)])
-            for offset in range(1, n_section)
-        ],
-        axis=0,
-    )
+    gain_parts = [ln_gain] + [
+        lax.ppermute(ln_gain, "section", [(s, s ^ offset) for s in range(n_section)])
+        for offset in range(1, n_section)
+    ]
+    gains = jnp.concatenate(gain_parts, axis=0)
     table = (jnp.arange(embed.shape[0], dtype=jnp.int32)[:, None] == tok[None, :]).astype(BF16)
     x = lax.dot_general(table, embed, TN, preferred_element_type=F32)
 
@@ -779,11 +789,14 @@
         )
         scores = group_swap(part, send, n_row, n_group)
     early = RowSum(*chain.early(probs[0], qkvs[0], dmix, xs[0], dy, grads[:2]), place, n_row)
-    early.step()
+    early.add(early.exchange())
     early.send, other = lax.optimization_barrier((early.send, scores[1]))
-    late = chain.late((scores[0], other), probs[0], qkvs[0], xs[0], grads[2:])
+    moved = early.exchange()
+    late = RowSum(*chain.late((scores[0], other), probs[0], qkvs[0], xs[0], grads[2:]), place, n_row)
+    late.send, moved = lax.optimization_barrier((late.send, moved))
+    early.add(moved)
     g_early = early.finish()
-    g_late = RowSum(*late, place, n_row).finish()
+    g_late = late.finish()
     g_qkv = jnp.concatenate([g_late, g_early[:, width:]], axis=1)
     block = width // n_row
     w_here = lax.dynamic_slice_in_dim(w_qkv[0], place * block, block, 0).astype(F32)

time: 313 us -> 307 us (0.981)
  the two profiles are of different devices: /device:TPU:0 before, /device:TPU:3 now
where the time goes in v8:
time: 307 us; the launch traced here: 302 us
  Pallas kernels  136 us (44%)
  waiting for transfers between devices  96 us (31%)
  starting transfers between devices  37.4 us (12%)
  local copies, waits for them, and re-layouts  15.4 us (5%)
  other arithmetic  12.7 us (4%)
    pallas_call x9, Pallas kernels, call(): pl.pallas_call(functools.partial(body, layout=layout), name=name, out_sha...  136 us
    ppermute x6, waiting for transfers between devices, exchange(): return lax.ppermute(self.send.astype(BF16), 'row', perm)  49.6 us
    ppermute x3, waiting for transfers between devices, hop(): return lax.ppermute(value, ('section', 'row'), perm)  16.3 us
    ppermute x5, starting transfers between devices, share(): lax.ppermute(send, 'row', [(r, r ^ bit) for r in range(self.n_row)])  15.1 us
    ppermute x3, waiting for transfers between devices, local(): lax.ppermute(ln_gain, 'section', [(s, s ^ offset) for s in range(n_sectio...  11.3 us
    ppermute x7, waiting for transfers between devices, group_swap(): other = lax.ppermute(send, 'row', [(r, r ^ bit) for r in range(n_row)])  7.94 us
    unnamed x50, local copies, waits for them, and re-layouts  7.58 us
  transfers between devices with their start and end apart: 28, of which 15 were waited for; matrix products, arithmetic and copies ran while one was open for 5% of the time, Pallas kernels for 14%

profile of v8, /device:TPU:3, one launch (start us, length us, event | category | flops | bytes accessed | tf_op | source)
XLA Modules:
  0.0 301.6 jit_solution(7238967562772482482)
XLA Ops:
  1.8 1.3 dynamic-slice_bitcast_fusion.3
  3.3 1.3 collective-permute-start
  6.0 1.2 collective-permute-start.1
  7.2 4.6 %all-to-all-start = ((s32[4,2,128]{2,1,0:T(2,128)}), s32[4,2,128]{2,1,0:T(2,128)S(1)}, u32[]{:S(2)}, u32[]{:S(2)}) async-start(s32[4,2,128]{2,1,0:T(2,128)} %param.6), calls=%async_computation | async-start | bytes 8192 | tf_op jit(solution)/shard_map/all_to_all | solution.py:743
  11.8 11.3 %collective-permute-done.2 = f32[1,768]{1,0:T(1,128)S(1)} collective-permute-done((f32[1,768]{1,0:T(1,128)S(1)}, f32[1,768]{1,0:T(1,128)S(1)}, u32[]{:S(2)}, u32[]{:S(2)}) %collective-permute-start.2) | collective-permute-done | bytes 3104 | tf_op jit(solution)/shard_map/ppermute | solution.py:746
  23.2 2.3 fusion.4.refs_0_.refs_3_.refs_4_
  25.5 1.6 broadcast_select_fusion
  27.1 1.3 slice.22
  28.4 1.6 collective-permute-start.5
  30.0 1.6 dynamic-slice_bitcast_fusion
  31.6 3.9 %collective-permute-start.4 = (bf16[1,256,3072]{2,1,0:T(8,128)(2,1)}, bf16[1,256,3072]{2,1,0:T(8,128)(2,1)}, u32[]{:S(2)}, u32[]{:S(2)}) collective-permute-start(bf16[1,256,3072]{2,1,0:T(8,128)(2,1)} %bitcast.23.refs_4_.refs_7_.refs_8_.refs_10_.refs_15_), channel_id=1, source_target_pairs={{0,1},{1,0},{2,3},{3,2},{4,5},{5,4},{6,7},{7,6},{8,9},{9,8},{10,11... | collective-permute-start | bytes 4718600 | tf_op jit(solution)/shard_map/ppermute | solution.py:706
  35.5 11.4 %collective-permute-done.7 = bf16[256,3072]{1,0:T(8,128)(2,1)} collective-permute-done((bf16[256,3072]{1,0:T(8,128)(2,1)}, bf16[256,3072]{1,0:T(8,128)(2,1)}, u32[]{:S(2)}, u32[]{:S(2)}) %collective-permute-start.7) | collective-permute-done | bytes 1572896 | tf_op jit(solution)/shard_map/ppermute | solution.py:676
  47.0 1.2 slice.23
  48.2 1.4 collective-permute-start.9
  49.5 4.9 %collective-permute-start.8 = (bf16[1,256,3072]{2,1,0:T(8,128)(2,1)}, bf16[1,256,3072]{2,1,0:T(8,128)(2,1)}, u32[]{:S(2)}, u32[]{:S(2)}) collective-permute-start(bf16[1,256,3072]{2,1,0:T(8,128)(2,1)} %bitcast.25.refs_8_.refs_11_.refs_12_.refs_14_.refs_19_), channel_id=1, source_target_pairs={{0,1},{1,0},{2,3},{3,2},{4,5},{5,4},{6,7},{7,6},{8,9},{9,8},{10,11... | collective-permute-start | bytes 4718600 | tf_op jit(solution)/shard_map/ppermute | solution.py:706
  54.5 1.6 broadcast_select_fusion.2
  56.1 2.3 maximum_select_fusion
  58.4 4.4 %collective-permute-done.9 = bf16[128,3072]{1,0:T(8,128)(2,1)S(1)} collective-permute-done((bf16[128,3072]{1,0:T(8,128)(2,1)S(1)}, bf16[128,3072]{1,0:T(8,128)(2,1)S(1)}, u32[]{:S(2)}, u32[]{:S(2)}) %collective-permute-start.9) | collective-permute-done | bytes 786464 | tf_op jit(solution)/shard_map/ppermute | solution.py:680
  62.7 5.5 %collective-permute-start.10 = (bf16[1,128,3072]{2,1,0:T(8,128)(2,1)S(1)}, bf16[1,128,3072]{2,1,0:T(8,128)(2,1)S(1)}, u32[]{:S(2)}, u32[]{:S(2)}) collective-permute-start(bf16[1,128,3072]{2,1,0:T(8,128)(2,1)S(1)} %bitcast.77), channel_id=1, source_target_pairs={{0,1},{1,0},{2,3},{3,2},{4,5},{5,4},{6,7},{7,6},{8,9},{9,8},{10,11... | collective-permute-start | bytes 2359304 | tf_op jit(solution)/shard_map/ppermute | solution.py:706
  68.3 1.8 collective-permute-done.10.refs_11_.refs_14_.refs_15_.refs_17_.refs_22_
  70.1 10.4 %layer_in_0.1 = (bf16[512,4608]{1,0:T(8,128)(2,1)}, f32[128,1536]{1,0:T(8,128)S(1)}) custom-call(s32[8]{0:T(128)S(1)} %stack.63.info, f32[1024,768]{1,0:T(8,128)} %fusion.4.refs_0_.refs_3_.refs_4_, f32[4,768]{1,0:T(4,128)S(1)} %pad_maximum_fusion.1.refs_1_.refs_4_.refs_5_.refs_6_, bf16[1,768,2304]{2,1,0:T(8,128)(2,1)} %refs_13_.3, ...), custom_call_target="tpu_custom_call" | custom-call | flops 6039797760 | bytes 8663040 | tf_op jit(solution)/shard_map/layer_in_0/pallas_call | solution.py:428
  81.9 4.8 %collective-permute-done.11 = bf16[384,3072]{1,0:T(8,128)(2,1)} collective-permute-done((bf16[384,3072]{1,0:T(8,128)(2,1)}, bf16[384,3072]{1,0:T(8,128)(2,1)}, u32[]{:S(2)}, u32[]{:S(2)}) %collective-permute-start.11) | collective-permute-done | bytes 2359328 | tf_op jit(solution)/shard_map/ppermute | solution.py:676
  87.5 4.6 %all-to-all-start.1 = ((bf16[4,2,128,768]{3,2,1,0:T(8,128)(2,1)}), bf16[4,2,128,768]{3,2,1,0:T(8,128)(2,1)}, u32[]{:S(2)}, u32[]{:S(2)}) async-start(bf16[4,2,128,768]{3,2,1,0:T(8,128)(2,1)} %param.11), calls=%async_computation.1 | async-start | bytes 3145728 | tf_op jit(solution)/shard_map/all_to_all | solution.py:744
  92.2 14.0 %layer_in_1.1 = (bf16[128,1536]{1,0:T(8,128)(2,1)S(1)}, f32[1024,768]{1,0:T(8,128)}, bf16[512,4608]{1,0:T(8,128)(2,1)}, f32[128,1536]{1,0:T(8,128)S(1)}) custom-call(s32[8]{0:T(128)S(1)} %stack.69.info, f32[128,1536]{1,0:T(8,128)S(1)} %copy-done.12, f32[128,1536]{1,0:T(8,128)S(1)} %collective-permute-done.12.refs_1_, ...), custom_call_target="tpu_custom_call" | custom-call | flops 6039797760 | bytes 18493440 | tf_op jit(solution)/shard_map/layer_in_1/pallas_call | solution.py:428
  107.3 2.0 collective-permute-done.14.refs_1_
  109.3 14.1 %layer_in_2.1 = (bf16[128,1536]{1,0:T(8,128)(2,1)S(1)}, f32[1024,768]{1,0:T(8,128)}, bf16[512,4608]{1,0:T(8,128)(2,1)}, f32[128,1536]{1,0:T(8,128)}) custom-call(s32[8]{0:T(128)S(1)} %stack.75.info, f32[128,1536]{1,0:T(8,128)S(1)} %get-tuple-element.62.refs_0_, f32[128,1536]{1,0:T(8,128)S(1)} %collective-permute-done.14.refs_1_, ...), custom_call_target="tpu_custom_call" | custom-call | flops 6039797760 | bytes 18493440 | tf_op jit(solution)/shard_map/layer_in_2/pallas_call | solution.py:428
  124.5 4.7 %all-to-all-done.1 = bf16[4,2,128,768]{3,2,1,0:T(8,128)(2,1)} async-done(((bf16[4,2,128,768]{3,2,1,0:T(8,128)(2,1)}), bf16[4,2,128,768]{3,2,1,0:T(8,128)(2,1)}, u32[]{:S(2)}, u32[]{:S(2)}) %all-to-all-start.1) | async-done | bytes 1572896 | tf_op jit(solution)/shard_map/all_to_all | solution.py:744
  129.1 19.0 %layer_in_3.1 = (bf16[128,1536]{1,0:T(8,128)(2,1)S(1)}, f32[1024,768]{1,0:T(8,128)}, bf16[512,4608]{1,0:T(8,128)(2,1)}, f32[256,1536]{1,0:T(8,128)}, bf16[512,1536]{1,0:T(8,128)(2,1)}) custom-call(s32[8]{0:T(128)S(1)} %stack.162.info, f32[128,1536]{1,0:T(8,128)} %get-tuple-element.65.refs_0_, f32[128,1536]{1,0:T(8,128)S(1)} %collective-permute-done.15.refs_1_, ...), custom_call_target="tpu_custom_call" | custom-call | flops 6039797760 | bytes 22425600 | tf_op jit(solution)/shard_map/layer_in_3/pallas_call | solution.py:428
  149.2 3.2 %collective-permute-done.16.refs_1_ = f32[256,1536]{1,0:T(8,128)S(1)} collective-permute-done((f32[256,1536]{1,0:T(8,128)}, f32[256,1536]{1,0:T(8,128)S(1)}, u32[]{:S(2)}, u32[]{:S(2)}) %collective-permute-start.16) | collective-permute-done | bytes 1572896 | tf_op jit(solution)/shard_map/ppermute | solution.py:618
  152.4 1.2 copy-done.22
  153.6 20.3 %layer_back_3.1 = (f32[1024,768]{1,0:T(8,128)}, bf16[512,1536]{1,0:T(8,128)(2,1)}, f32[128,1536]{1,0:T(8,128)S(1)}, bf16[128,1536]{1,0:T(8,128)(2,1)S(1)}, bf16[...) custom-call(s32[8]{0:T(128)S(1)} %stack.162.info, ...), custom_call_target="tpu_custom_call" | custom-call | flops 6039797760 | bytes 29503488 | tf_op jit(solution)/shard_map/layer_back_3/pallas_call | solution.py:428
  174.4 1.3 collective-permute-done.17.refs_1_
  175.8 19.4 %layer_back_2.1 = (f32[1024,768]{1,0:T(8,128)}, bf16[512,1536]{1,0:T(8,128)(2,1)}, f32[128,1536]{1,0:T(8,128)S(1)}, bf16[128,1536]{1,0:T(8,128)(2,1)S(1)}, bf16[...) custom-call(s32[8]{0:T(128)S(1)} %stack.75.info, ...), custom_call_target="tpu_custom_call", output_to_operand_aliasing={{4}: (10, {}), {5}: (11, {}), {6}: (12, {}), {7}: (13, {})} | custom-call | flops 6039797760 | bytes 34222080 | tf_op jit(solution)/shard_map/layer_back_2/pallas_call | solution.py:428
  195.7 1.3 collective-permute-done.18.refs_1_
  197.0 30.9 %layer_back_1.1 = (f32[1024,768]{1,0:T(8,128)}, bf16[512,1536]{1,0:T(8,128)(2,1)}, f32[128,1536]{1,0:T(8,128)S(1)}, bf16[128,1536]{1,0:T(8,128)(2,1)S(1)}, bf16[...) custom-call(s32[8]{0:T(128)S(1)} %stack.69.info, ...), custom_call_target="tpu_custom_call", output_to_operand_aliasing={{4}: (10, {}), {5}: (11, {}), {6}: (12, {}), {7}: (13, {})} | custom-call | flops 6039797760 | bytes 34222080 | tf_op jit(solution)/shard_map/layer_back_1/pallas_call | solution.py:428
  228.0 1.5 copy-done.7
  229.5 4.6 %early_back_0.1 = (bf16[4,96,1536]{2,1,0:T(8,128)(2,1)S(1)}, bf16[4,96,1536]{2,1,0:T(8,128)(2,1)}) custom-call(s32[8]{0:T(128)S(1)} %stack.63.info, bf16[128,1536]{1,0:T(8,128)(2,1)S(1)} %copy-done.16, bf16[512,4608]{1,0:T(8,128)(2,1)} %get-tuple-element.60.refs_2_.refs_8_.refs_1_.refs_3_, ...), custom_call_target="tpu_custom_call", output_to_operand_aliasing={{0}: (7, {}), {1}: (8, {})} | custom-call | flops 3623878656 | bytes 17707008 | tf_op jit(solution)/shard_map/early_back_0/pallas_call | solution.py:428
  235.7 2.8 collective-permute-done.19
  239.6 2.1 convert_add_fusion.1
  242.1 3.5 %late_back_0.1 = (bf16[4,96,1536]{2,1,0:T(8,128)(2,1)S(1)}, bf16[4,96,1536]{2,1,0:T(8,128)(2,1)S(1)}) custom-call(s32[8]{0:T(128)S(1)} %stack.63.info, f32[128,1536]{1,0:T(8,128)S(1)} %copy-done.18, bf16[128,1536]{1,0:T(8,128)(2,1)S(1)} %collective-permute-done.20.refs_1_, ...), custom_call_target="tpu_custom_call", output_to_operand_aliasing={{0}: (7, {}), {1}: (8, {})} | custom-call | flops 3623878656 | bytes 14168064 | tf_op jit(solution)/shard_map/late_back_0/pallas_call | solution.py:428
  245.6 10.8 %collective-permute-done.21 = bf16[2,96,1536]{2,1,0:T(8,128)(2,1)S(1)} collective-permute-done((bf16[2,96,1536]{2,1,0:T(8,128)(2,1)S(1)}, bf16[2,96,1536]{2,1,0:T(8,128)(2,1)S(1)}, u32[]{:S(2)}, u32[]{:S(2)}) %collective-permute-start.21) | collective-permute-done | bytes 589856 | tf_op jit(solution)/shard_map/ppermute | solution.py:629
  256.4 1.2 collective-permute-start.22
  257.6 2.6 collective-permute-done.22
  260.2 1.7 convert_add_fusion
  262.5 1.4 collective-permute-start.25
  263.9 19.1 %collective-permute-done.23 = bf16[2,96,1536]{2,1,0:T(8,128)(2,1)S(1)} collective-permute-done((bf16[2,96,1536]{2,1,0:T(8,128)(2,1)S(1)}, bf16[2,96,1536]{2,1,0:T(8,128)(2,1)S(1)}, u32[]{:S(2)}, u32[]{:S(2)}) %collective-permute-start.23) | collective-permute-done | bytes 589856 | tf_op jit(solution)/shard_map/ppermute | solution.py:629
  284.1 14.3 %collective-permute-done.24 = bf16[1,96,1536]{2,1,0:T(8,128)(2,1)S(1)} collective-permute-done((bf16[1,96,1536]{2,1,0:T(8,128)(2,1)S(1)}, bf16[1,96,1536]{2,1,0:T(8,128)(2,1)S(1)}, u32[]{:S(2)}, u32[]{:S(2)}) %collective-permute-start.24) | collective-permute-done | bytes 294944 | tf_op jit(solution)/shard_map/ppermute | solution.py:629
  298.5 2.1 fusion
  (96 shorter events, 14.4 us)
Async XLA Ops:
  0.6 22.5 %copy-start = (bf16[33,768]{1,0:T(8,128)(2,1)S(1)}, bf16[33,768]{1,0:T(8,128)(2,1)}, u32[]{:S(2)}) copy-start(bf16[33,768]{1,0:T(8,128)(2,1)} %param.7) | copy-start | bytes 152068
  3.1 1.5 copy-start.24
  3.3 22.2 %collective-permute-start = (bf16[256,3072]{1,0:T(8,128)(2,1)S(1)}, bf16[256,3072]{1,0:T(8,128)(2,1)}, u32[]{:S(2)}, u32[]{:S(2)}) collective-permute-start(bf16[256,3072]{1,0:T(8,128)(2,1)S(1)} %maximum_maximum_fusion), channel_id=1, source_target_pairs={{0,8},{1,17},{2,10},{3,19},{4,12},{5,21},{6,14},{7,23},{8,0},{9,25... | collective-permute-start | bytes 4718600 | tf_op jit(solution)/shard_map/ppermute | solution.py:676
  4.6 7.2 %collective-permute-start.3 = (f32[1,768]{1,0:T(1,128)S(1)}, f32[1,768]{1,0:T(1,128)S(1)}, u32[]{:S(2)}, u32[]{:S(2)}) collective-permute-start(f32[1,768]{1,0:T(1,128)S(1)} %copy-done.24), channel_id=1, source_target_pairs={{0,24},{8,16},{16,8},{24,0},{1,25},{9,17},{17,9},{25,1},{2,26},{10... | collective-permute-start | bytes 9224 | tf_op jit(solution)/shard_map/ppermute | solution.py:746
  5.0 18.1 %collective-permute-start.2 = (f32[1,768]{1,0:T(1,128)S(1)}, f32[1,768]{1,0:T(1,128)S(1)}, u32[]{:S(2)}, u32[]{:S(2)}) collective-permute-start(f32[1,768]{1,0:T(1,128)S(1)} %copy-done.24), channel_id=1, source_target_pairs={{0,16},{8,24},{16,0},{24,8},{1,17},{9,25},{17,1},{25,9},{2,18},{10... | collective-permute-start | bytes 9224 | tf_op jit(solution)/shard_map/ppermute | solution.py:746
  6.0 17.1 %collective-permute-start.1 = (f32[1,768]{1,0:T(1,128)S(1)}, f32[1,768]{1,0:T(1,128)S(1)}, u32[]{:S(2)}, u32[]{:S(2)}) collective-permute-start(f32[1,768]{1,0:T(1,128)S(1)} %copy-done.24), channel_id=1, source_target_pairs={{0,8},{8,0},{16,24},{24,16},{1,9},{9,1},{17,25},{25,17},{2,10},{10... | collective-permute-start | bytes 9224 | tf_op jit(solution)/shard_map/ppermute | solution.py:746
  7.2 15.9 %all-to-all-start = ((s32[4,2,128]{2,1,0:T(2,128)}), s32[4,2,128]{2,1,0:T(2,128)S(1)}, u32[]{:S(2)}, u32[]{:S(2)}) async-start(s32[4,2,128]{2,1,0:T(2,128)} %param.6), calls=%async_computation | async-start | bytes 8192 | tf_op jit(solution)/shard_map/all_to_all | solution.py:743
  27.1 2.9 copy-start.19
  27.1 19.9 %collective-permute-start.7 = (bf16[256,3072]{1,0:T(8,128)(2,1)}, bf16[256,3072]{1,0:T(8,128)(2,1)}, u32[]{:S(2)}, u32[]{:S(2)}) collective-permute-start(bf16[256,3072]{1,0:T(8,128)(2,1)} %broadcast_select_fusion), channel_id=1, source_target_pairs={{0,16},{1,9},{2,18},{3,11},{4,20},{5,13},{6,22},{7,15},{8,24},{9,1... | collective-permute-start | bytes 4718600 | tf_op jit(solution)/shard_map/ppermute | solution.py:676
  28.4 26.0 %collective-permute-start.5 = (bf16[128,3072]{1,0:T(8,128)(2,1)S(1)}, bf16[128,3072]{1,0:T(8,128)(2,1)S(1)}, u32[]{:S(2)}, u32[]{:S(2)}) collective-permute-start(bf16[128,3072]{1,0:T(8,128)(2,1)S(1)} %slice.22), channel_id=1, source_target_pairs={{0,2},{1,3},{2,0},{3,1},{4,6},{5,7},{6,4},{7,5},{8,10},{9,11},{10,... | collective-permute-start | bytes 2359304 | tf_op jit(solution)/shard_map/ppermute | solution.py:680
  31.6 36.6 %collective-permute-start.4 = (bf16[1,256,3072]{2,1,0:T(8,128)(2,1)}, bf16[1,256,3072]{2,1,0:T(8,128)(2,1)}, u32[]{:S(2)}, u32[]{:S(2)}) collective-permute-start(bf16[1,256,3072]{2,1,0:T(8,128)(2,1)} %bitcast.23.refs_4_.refs_7_.refs_8_.refs_10_.refs_15_), channel_id=1, source_target_pairs={{0,1},{1,0},{2,3},{3,2},{4,5},{5,4},{6,7},{7,6},{8,9},{9,8},{10,11... | collective-permute-start | bytes 4718600 | tf_op jit(solution)/shard_map/ppermute | solution.py:706
  48.2 14.6 %collective-permute-start.9 = (bf16[128,3072]{1,0:T(8,128)(2,1)S(1)}, bf16[128,3072]{1,0:T(8,128)(2,1)S(1)}, u32[]{:S(2)}, u32[]{:S(2)}) collective-permute-start(bf16[128,3072]{1,0:T(8,128)(2,1)S(1)} %slice.23), channel_id=1, source_target_pairs={{0,2},{1,3},{2,0},{3,1},{4,6},{5,7},{6,4},{7,5},{8,10},{9,11},{10,... | collective-permute-start | bytes 2359304 | tf_op jit(solution)/shard_map/ppermute | solution.py:680
  49.5 20.6 %collective-permute-start.8 = (bf16[1,256,3072]{2,1,0:T(8,128)(2,1)}, bf16[1,256,3072]{2,1,0:T(8,128)(2,1)}, u32[]{:S(2)}, u32[]{:S(2)}) collective-permute-start(bf16[1,256,3072]{2,1,0:T(8,128)(2,1)} %bitcast.25.refs_8_.refs_11_.refs_12_.refs_14_.refs_19_), channel_id=1, source_target_pairs={{0,1},{1,0},{2,3},{3,2},{4,5},{5,4},{6,7},{7,6},{8,9},{9,8},{10,11... | collective-permute-start | bytes 4718600 | tf_op jit(solution)/shard_map/ppermute | solution.py:706
  58.4 28.3 %collective-permute-start.11 = (bf16[384,3072]{1,0:T(8,128)(2,1)}, bf16[384,3072]{1,0:T(8,128)(2,1)}, u32[]{:S(2)}, u32[]{:S(2)}) collective-permute-start(bf16[384,3072]{1,0:T(8,128)(2,1)} %maximum_select_fusion), channel_id=1, source_target_pairs={{0,16},{1,9},{2,18},{3,11},{4,20},{5,13},{6,22},{7,15},{8,24},{9,1... | collective-permute-start | bytes 7077896 | tf_op jit(solution)/shard_map/ppermute | solution.py:676
  58.4 9.9 %collective-permute-start.6 = (bf16[1,128,3072]{2,1,0:T(8,128)(2,1)S(1)}, bf16[1,128,3072]{2,1,0:T(8,128)(2,1)S(1)}, u32[]{:S(2)}, u32[]{:S(2)}) collective-permute-start(bf16[1,128,3072]{2,1,0:T(8,128)(2,1)S(1)} %bitcast.69), channel_id=1, source_target_pairs={{0,1},{1,0},{2,3},{3,2},{4,5},{5,4},{6,7},{7,6},{8,9},{9,8},{10,11... | collective-permute-start | bytes 2359304 | tf_op jit(solution)/shard_map/ppermute | solution.py:706
  62.7 17.8 %copy-start.2 = (bf16[128,3072]{1,0:T(8,128)(2,1)}, bf16[128,3072]{1,0:T(8,128)(2,1)S(1)}, u32[]{:S(2)}) copy-start(bf16[128,3072]{1,0:T(8,128)(2,1)S(1)} %collective-permute-done.9) | copy-start | bytes 2359300
  62.7 7.4 %collective-permute-start.10 = (bf16[1,128,3072]{2,1,0:T(8,128)(2,1)S(1)}, bf16[1,128,3072]{2,1,0:T(8,128)(2,1)S(1)}, u32[]{:S(2)}, u32[]{:S(2)}) collective-permute-start(bf16[1,128,3072]{2,1,0:T(8,128)(2,1)S(1)} %bitcast.77), channel_id=1, source_target_pairs={{0,1},{1,0},{2,3},{3,2},{4,5},{5,4},{6,7},{7,6},{8,9},{9,8},{10,11... | collective-permute-start | bytes 2359304 | tf_op jit(solution)/shard_map/ppermute | solution.py:706
  68.3 12.2 %copy-start.4 = (bf16[1,128,3072]{2,1,0:T(8,128)(2,1)}, bf16[1,128,3072]{2,1,0:T(8,128)(2,1)S(1)}, u32[]{:S(2)}) copy-start(bf16[1,128,3072]{2,1,0:T(8,128)(2,1)S(1)} %collective-permute-done.6.refs_7_.refs_10_.refs_11_.refs_13_.refs_18_) | copy-start | bytes 2359300
  70.1 10.4 %copy-start.6 = (bf16[1,128,3072]{2,1,0:T(8,128)(2,1)}, bf16[1,128,3072]{2,1,0:T(8,128)(2,1)S(1)}, u32[]{:S(2)}) copy-start(bf16[1,128,3072]{2,1,0:T(8,128)(2,1)S(1)} %collective-permute-done.10.refs_11_.refs_14_.refs_15_.refs_17_.refs_22_) | copy-start | bytes 2359300
  80.5 6.1 %collective-permute-start.12 = (f32[128,1536]{1,0:T(8,128)S(1)}, f32[128,1536]{1,0:T(8,128)S(1)}, u32[]{:S(2)}, u32[]{:S(2)}) collective-permute-start(f32[128,1536]{1,0:T(8,128)S(1)} %get-tuple-element.58.refs_0_), channel_id=1, source_target_pairs={{0,1},{1,0},{2,3},{3,2},{4,5},{5,4},{6,7},{7,6},{8,9},{9,8},{10,11... | collective-permute-start | bytes 2359304 | tf_op jit(solution)/shard_map/ppermute | solution.py:618
  86.7 5.6 %copy-start.12 = (f32[128,1536]{1,0:T(8,128)S(1)}, f32[128,1536]{1,0:T(8,128)}, u32[]{:S(2)}) copy-start(f32[128,1536]{1,0:T(8,128)} %copy-done.11) | copy-start | bytes 2359300
  86.7 5.6 %collective-permute-start.13 = (bf16[1,384,3072]{2,1,0:T(8,128)(2,1)}, bf16[1,384,3072]{2,1,0:T(8,128)(2,1)}, u32[]{:S(2)}, u32[]{:S(2)}) collective-permute-start(bf16[1,384,3072]{2,1,0:T(8,128)(2,1)} %bitcast.29.refs_15_.refs_16_.refs_18_.refs_23_), channel_id=1, source_target_pairs={{0,1},{1,0},{2,3},{3,2},{4,5},{5,4},{6,7},{7,6},{8,9},{9,8},{10,11... | collective-permute-start | bytes 7077896 | tf_op jit(solution)/shard_map/ppermute | solution.py:706
  87.5 41.6 %all-to-all-start.1 = ((bf16[4,2,128,768]{3,2,1,0:T(8,128)(2,1)}), bf16[4,2,128,768]{3,2,1,0:T(8,128)(2,1)}, u32[]{:S(2)}, u32[]{:S(2)}) async-start(bf16[4,2,128,768]{3,2,1,0:T(8,128)(2,1)} %param.11), calls=%async_computation.1 | async-start | bytes 3145728 | tf_op jit(solution)/shard_map/all_to_all | solution.py:744
  107.0 2.3 collective-permute-start.14
  109.3 19.8 %copy-start.5 = (bf16[1,128,3072]{2,1,0:T(8,128)(2,1)S(1)}, bf16[1,128,3072]{2,1,0:T(8,128)(2,1)}, u32[]{:S(2)}) copy-start(bf16[1,128,3072]{2,1,0:T(8,128)(2,1)} %copy-done.4) | copy-start | bytes 2359300
  124.2 5.0 %collective-permute-start.15 = (f32[128,1536]{1,0:T(8,128)}, f32[128,1536]{1,0:T(8,128)S(1)}, u32[]{:S(2)}, u32[]{:S(2)}) collective-permute-start(f32[128,1536]{1,0:T(8,128)} %get-tuple-element.65.refs_0_), channel_id=1, source_target_pairs={{0,1},{1,0},{2,3},{3,2},{4,5},{5,4},{6,7},{7,6},{8,9},{9,8},{10,11... | collective-permute-start | bytes 2359304 | tf_op jit(solution)/shard_map/ppermute | solution.py:618
  129.1 24.5 %copy-start.3 = (bf16[128,3072]{1,0:T(8,128)(2,1)S(1)}, bf16[128,3072]{1,0:T(8,128)(2,1)}, u32[]{:S(2)}) copy-start(bf16[128,3072]{1,0:T(8,128)(2,1)} %copy-done.2) | copy-start | bytes 2359300
  148.1 4.3 %collective-permute-start.16 = (f32[256,1536]{1,0:T(8,128)}, f32[256,1536]{1,0:T(8,128)S(1)}, u32[]{:S(2)}, u32[]{:S(2)}) collective-permute-start(f32[256,1536]{1,0:T(8,128)} %get-tuple-element.68.refs_0_), channel_id=1, source_target_pairs={{0,1},{1,0},{2,3},{3,2},{4,5},{5,4},{6,7},{7,6},{8,9},{9,8},{10,11... | collective-permute-start | bytes 4718600 | tf_op jit(solution)/shard_map/ppermute | solution.py:618
  152.4 1.2 copy-start.22
  173.9 1.8 collective-permute-start.17
  175.8 21.2 %copy-start.14 = (bf16[128,1536]{1,0:T(8,128)(2,1)S(1)}, bf16[128,1536]{1,0:T(8,128)(2,1)}, u32[]{:S(2)}) copy-start(bf16[128,1536]{1,0:T(8,128)(2,1)} %copy-done.13) | copy-start | bytes 1179652
  195.2 1.8 collective-permute-start.18
  197.0 31.0 %copy-start.16 = (bf16[128,1536]{1,0:T(8,128)(2,1)S(1)}, bf16[128,1536]{1,0:T(8,128)(2,1)}, u32[]{:S(2)}) copy-start(bf16[128,1536]{1,0:T(8,128)(2,1)} %copy-done.15) | copy-start | bytes 1179652
  228.0 6.2 %copy-start.17 = (f32[128,1536]{1,0:T(8,128)}, f32[128,1536]{1,0:T(8,128)S(1)}, u32[]{:S(2)}) copy-start(f32[128,1536]{1,0:T(8,128)S(1)} %get-tuple-element.90.refs_0_) | copy-start | bytes 2359300
  228.0 1.6 copy-start.7
  235.2 3.3 %collective-permute-start.19 = (bf16[4,96,1536]{2,1,0:T(8,128)(2,1)}, bf16[4,96,1536]{2,1,0:T(8,128)(2,1)S(1)}, u32[]{:S(2)}, u32[]{:S(2)}) collective-permute-start(bf16[4,96,1536]{2,1,0:T(8,128)(2,1)} %get-tuple-element.97), channel_id=1, source_target_pairs={{0,1},{1,0},{2,3},{3,2},{4,5},{5,4},{6,7},{7,6},{8,9},{9,8},{10,11... | collective-permute-start | bytes 3538952 | tf_op jit(solution)/shard_map/ppermute | solution.py:629
  235.6 6.2 %collective-permute-start.20 = (bf16[128,1536]{1,0:T(8,128)(2,1)S(1)}, bf16[128,1536]{1,0:T(8,128)(2,1)S(1)}, u32[]{:S(2)}, u32[]{:S(2)}) collective-permute-start(bf16[128,1536]{1,0:T(8,128)(2,1)S(1)} %get-tuple-element.98), channel_id=1, source_target_pairs={{0,1},{1,0},{2,3},{3,2},{4,5},{5,4},{6,7},{7,6},{8,9},{9,8},{10,11... | collective-permute-start | bytes 1179656 | tf_op jit(solution)/shard_map/ppermute | solution.py:618
  239.6 2.3 copy-start.9
  239.6 2.3 copy-start.10
  239.6 2.5 copy-start.18
  241.7 3.9 %copy-start.20 = (f32[4,96,1536]{2,1,0:T(8,128)}, f32[4,96,1536]{2,1,0:T(8,128)S(1)}, u32[]{:S(2)}) copy-start(f32[4,96,1536]{2,1,0:T(8,128)S(1)} %convert_add_fusion.1) | copy-start | bytes 7077892
  241.8 14.6 %collective-permute-start.21 = (bf16[2,96,1536]{2,1,0:T(8,128)(2,1)S(1)}, bf16[2,96,1536]{2,1,0:T(8,128)(2,1)S(1)}, u32[]{:S(2)}, u32[]{:S(2)}) collective-permute-start(bf16[2,96,1536]{2,1,0:T(8,128)(2,1)S(1)} %fusion.2), channel_id=1, source_target_pairs={{0,2},{1,3},{2,0},{3,1},{4,6},{5,7},{6,4},{7,5},{8,10},{9,11},{10,... | collective-permute-start | bytes 1769480 | tf_op jit(solution)/shard_map/ppermute | solution.py:629
  256.4 3.8 %collective-permute-start.22 = (bf16[4,96,1536]{2,1,0:T(8,128)(2,1)S(1)}, bf16[4,96,1536]{2,1,0:T(8,128)(2,1)}, u32[]{:S(2)}, u32[]{:S(2)}) collective-permute-start(bf16[4,96,1536]{2,1,0:T(8,128)(2,1)S(1)} %get-tuple-element.105), channel_id=1, source_target_pairs={{0,1},{1,0},{2,3},{3,2},{4,5},{5,4},{6,7},{7,6},{8,9},{9,8},{10,11... | collective-permute-start | bytes 3538952 | tf_op jit(solution)/shard_map/ppermute | solution.py:629
  260.2 2.0 copy-start.21
  262.1 20.9 %collective-permute-start.23 = (bf16[2,96,1536]{2,1,0:T(8,128)(2,1)S(1)}, bf16[2,96,1536]{2,1,0:T(8,128)(2,1)S(1)}, u32[]{:S(2)}, u32[]{:S(2)}) collective-permute-start(bf16[2,96,1536]{2,1,0:T(8,128)(2,1)S(1)} %fusion.3), channel_id=1, source_target_pairs={{0,2},{1,3},{2,0},{3,1},{4,6},{5,7},{6,4},{7,5},{8,10},{9,11},{10,... | collective-permute-start | bytes 1769480 | tf_op jit(solution)/shard_map/ppermute | solution.py:629
  262.5 20.8 %collective-permute-start.25 = (bf16[1,96,1536]{2,1,0:T(8,128)(2,1)S(1)}, bf16[1,96,1536]{2,1,0:T(8,128)(2,1)S(1)}, u32[]{:S(2)}, u32[]{:S(2)}) collective-permute-start(bf16[1,96,1536]{2,1,0:T(8,128)(2,1)S(1)} %dynamic-slice_convert_fusion), channel_id=1, source_target_pairs={{0,4},{1,5},{2,6},{3,7},{4,0},{5,1},{6,2},{7,3},{8,12},{9,13},{10,... | collective-permute-start | bytes 884744 | tf_op jit(solution)/shard_map/ppermute | solution.py:629
  283.2 15.2 %collective-permute-start.24 = (bf16[1,96,1536]{2,1,0:T(8,128)(2,1)S(1)}, bf16[1,96,1536]{2,1,0:T(8,128)(2,1)S(1)}, u32[]{:S(2)}, u32[]{:S(2)}) collective-permute-start(bf16[1,96,1536]{2,1,0:T(8,128)(2,1)S(1)} %dynamic-slice_convert_fusion.1), channel_id=1, source_target_pairs={{0,4},{1,5},{2,6},{3,7},{4,0},{5,1},{6,2},{7,3},{8,12},{9,13},{10,... | collective-permute-start | bytes 884744 | tf_op jit(solution)/shard_map/ppermute | solution.py:629
  283.4 17.8 %copy-start.1 = (bf16[33,768]{1,0:T(8,128)(2,1)S(1)}, bf16[33,768]{1,0:T(8,128)(2,1)}, u32[]{:S(2)}) copy-start(bf16[33,768]{1,0:T(8,128)(2,1)} %param.7) | copy-start | bytes 152068
  (5 other events, 4.5 us)

commit v9 on v8

--- a/solution.py
+++ b/solution.py
@@ -297,13 +297,13 @@
         probs = next(it)
     get_q = Weights(info, 0, own_q, stages, slice(0, 3 * width), wq, sem_q)
     get_o = Weights(info, 2, own_o, stages, slice(3 * width, 4 * width), wo, sem_o)
-    own = info[0] == 0
+    own, onward = info[0] == 0, info[8] == 1
     gain = gains[pl.ds(info[6], 1), :]
 
     @pl.when(step == 0)
     def _():
-        get_q.start()
-        get_o.start()
+        pl.when(onward)(get_q.start)
+        pl.when(onward)(get_o.start)
         if is_top:
 
             def keep(h, value):
@@ -316,20 +316,23 @@
     mix(dl, qkv, HEADS, dqkv, 0, scale, seq)
     mix(dlt, qkv, 0, dqkv, width, scale, seq)
     mix(pt, dmix, 0, dqkv, 2 * width, None, seq)
-    pl.when(step == 0)(get_q.wait)
-    d_hat = mm_nt(dqkv[...], wq[...]).astype(BF16).astype(F32) * gain
-    hat, rstd = norm_parts(x_in[...])
-    mean_d = jnp.mean(d_hat, axis=-1, keepdims=True)
-    mean_dh = jnp.mean(d_hat * hat, axis=-1, keepdims=True)
-    d_x = dy[...].astype(F32) + rstd * (d_hat - mean_d - hat * mean_dh)
-    dy_out[...] = d_x
-    pl.when(step == 0)(get_o.wait)
-    pack_rows(mm_nt(d_x.astype(BF16), wo[...]).astype(BF16), dmix_out, 0, seq)
-    scores(dmix_out, 0, v_prev, 0, score_out, 0, seq, step == 0)
-
-    @pl.when(step == steps - 1)
-    def _():
-        send_out[...] = score_out[...].astype(BF16)
+
+    @pl.when(onward)
+    def _():
+        pl.when(step == 0)(get_q.wait)
+        d_hat = mm_nt(dqkv[...], wq[...]).astype(BF16).astype(F32) * gain
+        hat, rstd = norm_parts(x_in[...])
+        mean_d = jnp.mean(d_hat, axis=-1, keepdims=True)
+        mean_dh = jnp.mean(d_hat * hat, axis=-1, keepdims=True)
+        d_x = dy[...].astype(F32) + rstd * (d_hat - mean_d - hat * mean_dh)
+        dy_out[...] = d_x
+        pl.when(step == 0)(get_o.wait)
+        pack_rows(mm_nt(d_x.astype(BF16), wo[...]).astype(BF16), dmix_out, 0, seq)
+        scores(dmix_out, 0, v_prev, 0, score_out, 0, seq, step == 0)
+
+        @pl.when(step == steps - 1)
+        def _():
+            send_out[...] = score_out[...].astype(BF16)
 
     @pl.when(own)
     def _():
@@ -401,7 +404,7 @@
     def info(self, now, other):
         picks = self.fetched.choices(now) + self.fetched.choices(other)
         picks += [self.member, self.fetched.half, self.fetched.section ^ now]
-        picks.append(self.fetched.section <= now)
+        picks += [self.fetched.section <= now, self.fetched.section < now]
         return jnp.stack(picks).astype(jnp.int32)
 
     def whole(self, rows, lanes):

time: 307 us -> 301 us (0.980)
  the two profiles are of different devices: /device:TPU:3 before, /device:TPU:0 now
where the time goes in v9:
time: 301 us; the launch traced here: 295 us
  Pallas kernels  136 us (45%)
  waiting for transfers between devices  100 us (33%)
  starting transfers between devices  27.2 us (9%)
  local copies, waits for them, and re-layouts  15.2 us (5%)
  other arithmetic  12.7 us (4%)
    pallas_call x9, Pallas kernels, call(): pl.pallas_call(functools.partial(body, layout=layout), name=name, out_sha...  136 us
    ppermute x6, waiting for transfers between devices, exchange(): return lax.ppermute(self.send.astype(BF16), 'row', perm)  45 us
    ppermute x3, waiting for transfers between devices, hop(): return lax.ppermute(value, ('section', 'row'), perm)  19.4 us
    ppermute x3, waiting for transfers between devices, local(): lax.ppermute(ln_gain, 'section', [(s, s ^ offset) for s in range(n_sectio...  11.6 us
    ppermute x7, waiting for transfers between devices, group_swap(): other = lax.ppermute(send, 'row', [(r, r ^ bit) for r in range(n_row)])  8.96 us
    ppermute x2, waiting for transfers between devices, cross(): return lax.ppermute(value[:self.block], 'row', perm)  7.94 us
    unnamed x50, local copies, waits for them, and re-layouts  7.47 us
  transfers between devices with their start and end apart: 28, of which 15 were waited for; matrix products, arithmetic and copies ran while one was open for 5% of the time, Pallas kernels for 16%

profile of v9, /device:TPU:0, one launch (start us, length us, event | category | flops | bytes accessed | tf_op | source)
XLA Modules:
  0.0 295.4 jit_solution(16566304850369088438)
XLA Ops:
  0.7 1.1 dynamic-slice_bitcast_fusion.5
  1.8 1.3 dynamic-slice_bitcast_fusion.3
  3.3 3.0 %collective-permute-start = (bf16[256,3072]{1,0:T(8,128)(2,1)S(1)}, bf16[256,3072]{1,0:T(8,128)(2,1)}, u32[]{:S(2)}, u32[]{:S(2)}) collective-permute-start(bf16[256,3072]{1,0:T(8,128)(2,1)S(1)} %maximum_maximum_fusion), channel_id=1, source_target_pairs={{0,8},{1,17},{2,10},{3,19},{4,12},{5,21},{6,14},{7,23},{8,0},{9,25... | collective-permute-start | bytes 4718600 | tf_op jit(solution)/shard_map/ppermute | solution.py:679
  6.3 1.5 collective-permute-start.3
  8.2 1.6 collective-permute-start.1
  9.8 4.9 %all-to-all-start = ((s32[4,2,128]{2,1,0:T(2,128)}), s32[4,2,128]{2,1,0:T(2,128)S(1)}, u32[]{:S(2)}, u32[]{:S(2)}) async-start(s32[4,2,128]{2,1,0:T(2,128)} %param.6), calls=%async_computation | async-start | bytes 8192 | tf_op jit(solution)/shard_map/all_to_all | solution.py:746
  14.7 11.6 %collective-permute-done.3 = f32[1,768]{1,0:T(1,128)S(1)} collective-permute-done((f32[1,768]{1,0:T(1,128)S(1)}, f32[1,768]{1,0:T(1,128)S(1)}, u32[]{:S(2)}, u32[]{:S(2)}) %collective-permute-start.3) | collective-permute-done | bytes 3104 | tf_op jit(solution)/shard_map/ppermute | solution.py:749
  26.3 2.3 fusion.4.refs_0_.refs_3_.refs_4_
  28.6 1.6 broadcast_select_fusion
  30.9 1.2 slice.22
  32.1 1.6 collective-permute-start.5
  33.8 1.6 dynamic-slice_bitcast_fusion
  35.4 15.5 %collective-permute-done.7 = bf16[256,3072]{1,0:T(8,128)(2,1)} collective-permute-done((bf16[256,3072]{1,0:T(8,128)(2,1)}, bf16[256,3072]{1,0:T(8,128)(2,1)}, u32[]{:S(2)}, u32[]{:S(2)}) %collective-permute-start.7) | collective-permute-done | bytes 1572896 | tf_op jit(solution)/shard_map/ppermute | solution.py:679
  51.0 1.2 slice.23
  52.2 1.6 collective-permute-start.9
  53.8 1.6 broadcast_select_fusion.2
  55.5 2.3 maximum_select_fusion
  58.4 2.5 collective-permute-start.6
  60.9 7.9 %collective-permute-done.9 = bf16[128,3072]{1,0:T(8,128)(2,1)S(1)} collective-permute-done((bf16[128,3072]{1,0:T(8,128)(2,1)S(1)}, bf16[128,3072]{1,0:T(8,128)(2,1)S(1)}, u32[]{:S(2)}, u32[]{:S(2)}) %collective-permute-start.9) | collective-permute-done | bytes 786464 | tf_op jit(solution)/shard_map/ppermute | solution.py:683
  68.9 2.2 collective-permute-done.10.refs_11_.refs_14_.refs_15_.refs_17_.refs_22_
  71.1 10.8 %layer_in_0.1 = (bf16[512,4608]{1,0:T(8,128)(2,1)}, f32[128,1536]{1,0:T(8,128)S(1)}) custom-call(s32[9]{0:T(128)S(1)} %stack.85.info, f32[1024,768]{1,0:T(8,128)} %fusion.4.refs_0_.refs_3_.refs_4_, f32[4,768]{1,0:T(4,128)S(1)} %pad_maximum_fusion.1.refs_1_.refs_4_.refs_5_.refs_6_, bf16[1,768,2304]{2,1,0:T(8,128)(2,1)} %refs_13_.3, ...), custom_call_target="tpu_custom_call" | custom-call | flops 6039797760 | bytes 8663040 | tf_op jit(solution)/shard_map/layer_in_0/pallas_call | solution.py:431
  83.0 3.9 %collective-permute-done.11 = bf16[384,3072]{1,0:T(8,128)(2,1)} collective-permute-done((bf16[384,3072]{1,0:T(8,128)(2,1)}, bf16[384,3072]{1,0:T(8,128)(2,1)}, u32[]{:S(2)}, u32[]{:S(2)}) %collective-permute-start.11) | collective-permute-done | bytes 2359328 | tf_op jit(solution)/shard_map/ppermute | solution.py:679
  87.4 4.6 %all-to-all-start.1 = ((bf16[4,2,128,768]{3,2,1,0:T(8,128)(2,1)}), bf16[4,2,128,768]{3,2,1,0:T(8,128)(2,1)}, u32[]{:S(2)}, u32[]{:S(2)}) async-start(bf16[4,2,128,768]{3,2,1,0:T(8,128)(2,1)} %param.11), calls=%async_computation.1 | async-start | bytes 3145728 | tf_op jit(solution)/shard_map/all_to_all | solution.py:747
  92.1 14.0 %layer_in_1.1 = (bf16[128,1536]{1,0:T(8,128)(2,1)S(1)}, f32[1024,768]{1,0:T(8,128)}, bf16[512,4608]{1,0:T(8,128)(2,1)}, f32[128,1536]{1,0:T(8,128)S(1)}) custom-call(s32[9]{0:T(128)S(1)} %stack.183.info, f32[128,1536]{1,0:T(8,128)S(1)} %copy-done.12, f32[128,1536]{1,0:T(8,128)S(1)} %collective-permute-done.12.refs_1_, ...), custom_call_target="tpu_custom_call" | custom-call | flops 6039797760 | bytes 18493440 | tf_op jit(solution)/shard_map/layer_in_1/pallas_call | solution.py:431
  107.2 2.1 collective-permute-done.14.refs_1_
  109.2 14.1 %layer_in_2.1 = (bf16[128,1536]{1,0:T(8,128)(2,1)S(1)}, f32[1024,768]{1,0:T(8,128)}, bf16[512,4608]{1,0:T(8,128)(2,1)}, f32[128,1536]{1,0:T(8,128)}) custom-call(s32[9]{0:T(128)S(1)} %stack.191.info, f32[128,1536]{1,0:T(8,128)S(1)} %get-tuple-element.62.refs_0_, f32[128,1536]{1,0:T(8,128)S(1)} %collective-permute-done.14.refs_1_, ...), custom_call_target="tpu_custom_call" | custom-call | flops 6039797760 | bytes 18493440 | tf_op jit(solution)/shard_map/layer_in_2/pallas_call | solution.py:431
  124.3 5.3 %all-to-all-done.1 = bf16[4,2,128,768]{3,2,1,0:T(8,128)(2,1)} async-done(((bf16[4,2,128,768]{3,2,1,0:T(8,128)(2,1)}), bf16[4,2,128,768]{3,2,1,0:T(8,128)(2,1)}, u32[]{:S(2)}, u32[]{:S(2)}) %all-to-all-start.1) | async-done | bytes 1572896 | tf_op jit(solution)/shard_map/all_to_all | solution.py:747
  129.6 19.0 %layer_in_3.1 = (bf16[128,1536]{1,0:T(8,128)(2,1)S(1)}, f32[1024,768]{1,0:T(8,128)}, bf16[512,4608]{1,0:T(8,128)(2,1)}, f32[256,1536]{1,0:T(8,128)}, bf16[512,1536]{1,0:T(8,128)(2,1)}) custom-call(s32[9]{0:T(128)S(1)} %stack.199.info, f32[128,1536]{1,0:T(8,128)} %get-tuple-element.65.refs_0_, f32[128,1536]{1,0:T(8,128)S(1)} %collective-permute-done.15.refs_1_, ...), custom_call_target="tpu_custom_call" | custom-call | flops 6039797760 | bytes 22425600 | tf_op jit(solution)/shard_map/layer_in_3/pallas_call | solution.py:431
  148.7 3.6 %collective-permute-done.16.refs_1_ = f32[256,1536]{1,0:T(8,128)S(1)} collective-permute-done((f32[256,1536]{1,0:T(8,128)}, f32[256,1536]{1,0:T(8,128)S(1)}, u32[]{:S(2)}, u32[]{:S(2)}) %collective-permute-start.16) | collective-permute-done | bytes 1572896 | tf_op jit(solution)/shard_map/ppermute | solution.py:621
  152.3 1.2 copy-done.22
  153.5 20.4 %layer_back_3.1 = (f32[1024,768]{1,0:T(8,128)}, bf16[512,1536]{1,0:T(8,128)(2,1)}, f32[128,1536]{1,0:T(8,128)S(1)}, bf16[128,1536]{1,0:T(8,128)(2,1)S(1)}, bf16[...) custom-call(s32[9]{0:T(128)S(1)} %stack.199.info, ...), custom_call_target="tpu_custom_call" | custom-call | flops 6039797760 | bytes 29503488 | tf_op jit(solution)/shard_map/layer_back_3/pallas_call | solution.py:431
  174.0 1.6 collective-permute-done.17.refs_1_
  175.7 19.4 %layer_back_2.1 = (f32[1024,768]{1,0:T(8,128)}, bf16[512,1536]{1,0:T(8,128)(2,1)}, f32[128,1536]{1,0:T(8,128)S(1)}, bf16[128,1536]{1,0:T(8,128)(2,1)S(1)}, bf16[...) custom-call(s32[9]{0:T(128)S(1)} %stack.191.info, ...), custom_call_target="tpu_custom_call", output_to_operand_aliasing={{4}: (10, {}), {5}: (11, {}), {6}: (12, {}), {7}: (13, {})} | custom-call | flops 6039797760 | bytes 34222080 | tf_op jit(solution)/shard_map/layer_back_2/pallas_call | solution.py:431
  195.2 1.7 collective-permute-done.18.refs_1_
  196.9 19.3 %layer_back_1.1 = (f32[1024,768]{1,0:T(8,128)}, bf16[512,1536]{1,0:T(8,128)(2,1)}, f32[128,1536]{1,0:T(8,128)S(1)}, bf16[128,1536]{1,0:T(8,128)(2,1)S(1)}, bf16[...) custom-call(s32[9]{0:T(128)S(1)} %stack.183.info, ...), custom_call_target="tpu_custom_call", output_to_operand_aliasing={{4}: (10, {}), {5}: (11, {}), {6}: (12, {}), {7}: (13, {})} | custom-call | flops 6039797760 | bytes 34222080 | tf_op jit(solution)/shard_map/layer_back_1/pallas_call | solution.py:431
  216.2 1.5 copy-done.7
  217.8 10.1 %early_back_0.1 = (bf16[4,96,1536]{2,1,0:T(8,128)(2,1)S(1)}, bf16[4,96,1536]{2,1,0:T(8,128)(2,1)}) custom-call(s32[9]{0:T(128)S(1)} %stack.85.info, bf16[128,1536]{1,0:T(8,128)(2,1)S(1)} %copy-done.16, bf16[512,4608]{1,0:T(8,128)(2,1)} %get-tuple-element.60.refs_2_.refs_8_.refs_1_.refs_3_, ...), custom_call_target="tpu_custom_call", output_to_operand_aliasing={{0}: (7, {}), {1}: (8, {})} | custom-call | flops 3623878656 | bytes 17707008 | tf_op jit(solution)/shard_map/early_back_0/pallas_call | solution.py:431
  229.5 2.5 collective-permute-done.19
  232.0 1.0 copy-done.23
  233.1 2.1 convert_add_fusion.1
  235.6 8.8 %late_back_0.1 = (bf16[4,96,1536]{2,1,0:T(8,128)(2,1)S(1)}, bf16[4,96,1536]{2,1,0:T(8,128)(2,1)S(1)}) custom-call(s32[9]{0:T(128)S(1)} %stack.85.info, f32[128,1536]{1,0:T(8,128)S(1)} %copy-done.18, bf16[128,1536]{1,0:T(8,128)(2,1)S(1)} %collective-permute-done.20.refs_1_, ...), custom_call_target="tpu_custom_call", output_to_operand_aliasing={{0}: (7, {}), {1}: (8, {})} | custom-call | flops 3623878656 | bytes 14168064 | tf_op jit(solution)/shard_map/late_back_0/pallas_call | solution.py:431
  244.4 6.5 %collective-permute-done.21 = bf16[2,96,1536]{2,1,0:T(8,128)(2,1)S(1)} collective-permute-done((bf16[2,96,1536]{2,1,0:T(8,128)(2,1)S(1)}, bf16[2,96,1536]{2,1,0:T(8,128)(2,1)S(1)}, u32[]{:S(2)}, u32[]{:S(2)}) %collective-permute-start.21) | collective-permute-done | bytes 589856 | tf_op jit(solution)/shard_map/ppermute | solution.py:632
  250.9 3.0 %collective-permute-done.22 = bf16[4,96,1536]{2,1,0:T(8,128)(2,1)} collective-permute-done((bf16[4,96,1536]{2,1,0:T(8,128)(2,1)S(1)}, bf16[4,96,1536]{2,1,0:T(8,128)(2,1)}, u32[]{:S(2)}, u32[]{:S(2)}) %collective-permute-start.22) | collective-permute-done | bytes 1179680 | tf_op jit(solution)/shard_map/ppermute | solution.py:632
  253.9 1.7 convert_add_fusion
  256.2 1.8 collective-permute-start.25
  258.0 19.4 %collective-permute-done.23 = bf16[2,96,1536]{2,1,0:T(8,128)(2,1)S(1)} collective-permute-done((bf16[2,96,1536]{2,1,0:T(8,128)(2,1)S(1)}, bf16[2,96,1536]{2,1,0:T(8,128)(2,1)S(1)}, u32[]{:S(2)}, u32[]{:S(2)}) %collective-permute-start.23) | collective-permute-done | bytes 589856 | tf_op jit(solution)/shard_map/ppermute | solution.py:632
  278.6 13.6 %collective-permute-done.24 = bf16[1,96,1536]{2,1,0:T(8,128)(2,1)S(1)} collective-permute-done((bf16[1,96,1536]{2,1,0:T(8,128)(2,1)S(1)}, bf16[1,96,1536]{2,1,0:T(8,128)(2,1)S(1)}, u32[]{:S(2)}, u32[]{:S(2)}) %collective-permute-start.24) | collective-permute-done | bytes 294944 | tf_op jit(solution)/shard_map/ppermute | solution.py:632
  292.2 2.1 fusion
  (96 shorter events, 10.4 us)
Async XLA Ops:
  0.6 25.7 %copy-start = (bf16[33,768]{1,0:T(8,128)(2,1)S(1)}, bf16[33,768]{1,0:T(8,128)(2,1)}, u32[]{:S(2)}) copy-start(bf16[33,768]{1,0:T(8,128)(2,1)} %param.7) | copy-start | bytes 152068
  3.1 3.2 %copy-start.24 = (f32[1,768]{1,0:T(1,128)S(1)}, f32[1,768]{1,0:T(1,128)}, u32[]{:S(2)}) copy-start(f32[1,768]{1,0:T(1,128)} %param.8) | copy-start | bytes 9220
  3.3 25.3 %collective-permute-start = (bf16[256,3072]{1,0:T(8,128)(2,1)S(1)}, bf16[256,3072]{1,0:T(8,128)(2,1)}, u32[]{:S(2)}, u32[]{:S(2)}) collective-permute-start(bf16[256,3072]{1,0:T(8,128)(2,1)S(1)} %maximum_maximum_fusion), channel_id=1, source_target_pairs={{0,8},{1,17},{2,10},{3,19},{4,12},{5,21},{6,14},{7,23},{8,0},{9,25... | collective-permute-start | bytes 4718600 | tf_op jit(solution)/shard_map/ppermute | solution.py:679
  6.3 20.0 %collective-permute-start.3 = (f32[1,768]{1,0:T(1,128)S(1)}, f32[1,768]{1,0:T(1,128)S(1)}, u32[]{:S(2)}, u32[]{:S(2)}) collective-permute-start(f32[1,768]{1,0:T(1,128)S(1)} %copy-done.24), channel_id=1, source_target_pairs={{0,24},{8,16},{16,8},{24,0},{1,25},{9,17},{17,9},{25,1},{2,26},{10... | collective-permute-start | bytes 9224 | tf_op jit(solution)/shard_map/ppermute | solution.py:749
  7.8 18.5 %collective-permute-start.2 = (f32[1,768]{1,0:T(1,128)S(1)}, f32[1,768]{1,0:T(1,128)S(1)}, u32[]{:S(2)}, u32[]{:S(2)}) collective-permute-start(f32[1,768]{1,0:T(1,128)S(1)} %copy-done.24), channel_id=1, source_target_pairs={{0,16},{8,24},{16,0},{24,8},{1,17},{9,25},{17,1},{25,9},{2,18},{10... | collective-permute-start | bytes 9224 | tf_op jit(solution)/shard_map/ppermute | solution.py:749
  8.2 18.1 %collective-permute-start.1 = (f32[1,768]{1,0:T(1,128)S(1)}, f32[1,768]{1,0:T(1,128)S(1)}, u32[]{:S(2)}, u32[]{:S(2)}) collective-permute-start(f32[1,768]{1,0:T(1,128)S(1)} %copy-done.24), channel_id=1, source_target_pairs={{0,8},{8,0},{16,24},{24,16},{1,9},{9,1},{17,25},{25,17},{2,10},{10... | collective-permute-start | bytes 9224 | tf_op jit(solution)/shard_map/ppermute | solution.py:749
  9.8 16.5 %all-to-all-start = ((s32[4,2,128]{2,1,0:T(2,128)}), s32[4,2,128]{2,1,0:T(2,128)S(1)}, u32[]{:S(2)}, u32[]{:S(2)}) async-start(s32[4,2,128]{2,1,0:T(2,128)} %param.6), calls=%async_computation | async-start | bytes 8192 | tf_op jit(solution)/shard_map/all_to_all | solution.py:746
  30.3 3.5 %copy-start.19 = (bf16[1,768,768]{2,1,0:T(8,128)(2,1)S(1)}, bf16[1,768,768]{2,1,0:T(8,128)(2,1)}, u32[]{:S(2)}) copy-start(bf16[1,768,768]{2,1,0:T(8,128)(2,1)} %refs_14_.3) | copy-start | bytes 3538948
  30.3 20.7 %collective-permute-start.7 = (bf16[256,3072]{1,0:T(8,128)(2,1)}, bf16[256,3072]{1,0:T(8,128)(2,1)}, u32[]{:S(2)}, u32[]{:S(2)}) collective-permute-start(bf16[256,3072]{1,0:T(8,128)(2,1)} %broadcast_select_fusion), channel_id=1, source_target_pairs={{0,16},{1,9},{2,18},{3,11},{4,20},{5,13},{6,22},{7,15},{8,24},{9,1... | collective-permute-start | bytes 4718600 | tf_op jit(solution)/shard_map/ppermute | solution.py:679
  32.1 21.8 %collective-permute-start.5 = (bf16[128,3072]{1,0:T(8,128)(2,1)S(1)}, bf16[128,3072]{1,0:T(8,128)(2,1)S(1)}, u32[]{:S(2)}, u32[]{:S(2)}) collective-permute-start(bf16[128,3072]{1,0:T(8,128)(2,1)S(1)} %slice.22), channel_id=1, source_target_pairs={{0,2},{1,3},{2,0},{3,1},{4,6},{5,7},{6,4},{7,5},{8,10},{9,11},{10,... | collective-permute-start | bytes 2359304 | tf_op jit(solution)/shard_map/ppermute | solution.py:683
  35.4 33.5 %collective-permute-start.4 = (bf16[1,256,3072]{2,1,0:T(8,128)(2,1)}, bf16[1,256,3072]{2,1,0:T(8,128)(2,1)}, u32[]{:S(2)}, u32[]{:S(2)}) collective-permute-start(bf16[1,256,3072]{2,1,0:T(8,128)(2,1)} %bitcast.27.refs_4_.refs_7_.refs_8_.refs_10_.refs_15_), channel_id=1, source_target_pairs={{0,1},{1,0},{2,3},{3,2},{4,5},{5,4},{6,7},{7,6},{8,9},{9,8},{10,11... | collective-permute-start | bytes 4718600 | tf_op jit(solution)/shard_map/ppermute | solution.py:709
  52.2 16.6 %collective-permute-start.9 = (bf16[128,3072]{1,0:T(8,128)(2,1)S(1)}, bf16[128,3072]{1,0:T(8,128)(2,1)S(1)}, u32[]{:S(2)}, u32[]{:S(2)}) collective-permute-start(bf16[128,3072]{1,0:T(8,128)(2,1)S(1)} %slice.23), channel_id=1, source_target_pairs={{0,2},{1,3},{2,0},{3,1},{4,6},{5,7},{6,4},{7,5},{8,10},{9,11},{10,... | collective-permute-start | bytes 2359304 | tf_op jit(solution)/shard_map/ppermute | solution.py:683
  53.8 17.3 %collective-permute-start.8 = (bf16[1,256,3072]{2,1,0:T(8,128)(2,1)}, bf16[1,256,3072]{2,1,0:T(8,128)(2,1)}, u32[]{:S(2)}, u32[]{:S(2)}) collective-permute-start(bf16[1,256,3072]{2,1,0:T(8,128)(2,1)} %bitcast.29.refs_8_.refs_11_.refs_12_.refs_14_.refs_19_), channel_id=1, source_target_pairs={{0,1},{1,0},{2,3},{3,2},{4,5},{5,4},{6,7},{7,6},{8,9},{9,8},{10,11... | collective-permute-start | bytes 4718600 | tf_op jit(solution)/shard_map/ppermute | solution.py:709
  57.7 29.2 %collective-permute-start.11 = (bf16[384,3072]{1,0:T(8,128)(2,1)}, bf16[384,3072]{1,0:T(8,128)(2,1)}, u32[]{:S(2)}, u32[]{:S(2)}) collective-permute-start(bf16[384,3072]{1,0:T(8,128)(2,1)} %maximum_select_fusion), channel_id=1, source_target_pairs={{0,16},{1,9},{2,18},{3,11},{4,20},{5,13},{6,22},{7,15},{8,24},{9,1... | collective-permute-start | bytes 7077896 | tf_op jit(solution)/shard_map/ppermute | solution.py:679
  58.4 10.5 %collective-permute-start.6 = (bf16[1,128,3072]{2,1,0:T(8,128)(2,1)S(1)}, bf16[1,128,3072]{2,1,0:T(8,128)(2,1)S(1)}, u32[]{:S(2)}, u32[]{:S(2)}) collective-permute-start(bf16[1,128,3072]{2,1,0:T(8,128)(2,1)S(1)} %bitcast.73), channel_id=1, source_target_pairs={{0,1},{1,0},{2,3},{3,2},{4,5},{5,4},{6,7},{7,6},{8,9},{9,8},{10,11... | collective-permute-start | bytes 2359304 | tf_op jit(solution)/shard_map/ppermute | solution.py:709
  68.8 13.1 %copy-start.2 = (bf16[128,3072]{1,0:T(8,128)(2,1)}, bf16[128,3072]{1,0:T(8,128)(2,1)S(1)}, u32[]{:S(2)}) copy-start(bf16[128,3072]{1,0:T(8,128)(2,1)S(1)} %collective-permute-done.9) | copy-start | bytes 2359300
  68.8 2.3 collective-permute-start.10
  68.9 13.0 %copy-start.4 = (bf16[1,128,3072]{2,1,0:T(8,128)(2,1)}, bf16[1,128,3072]{2,1,0:T(8,128)(2,1)S(1)}, u32[]{:S(2)}) copy-start(bf16[1,128,3072]{2,1,0:T(8,128)(2,1)S(1)} %collective-permute-done.6.refs_7_.refs_10_.refs_11_.refs_13_.refs_18_) | copy-start | bytes 2359300
  71.1 10.8 %copy-start.6 = (bf16[1,128,3072]{2,1,0:T(8,128)(2,1)}, bf16[1,128,3072]{2,1,0:T(8,128)(2,1)S(1)}, u32[]{:S(2)}) copy-start(bf16[1,128,3072]{2,1,0:T(8,128)(2,1)S(1)} %collective-permute-done.10.refs_11_.refs_14_.refs_15_.refs_17_.refs_22_) | copy-start | bytes 2359300
  81.9 5.0 %collective-permute-start.12 = (f32[128,1536]{1,0:T(8,128)S(1)}, f32[128,1536]{1,0:T(8,128)S(1)}, u32[]{:S(2)}, u32[]{:S(2)}) collective-permute-start(f32[128,1536]{1,0:T(8,128)S(1)} %get-tuple-element.58.refs_0_), channel_id=1, source_target_pairs={{0,1},{1,0},{2,3},{3,2},{4,5},{5,4},{6,7},{7,6},{8,9},{9,8},{10,11... | collective-permute-start | bytes 2359304 | tf_op jit(solution)/shard_map/ppermute | solution.py:621
  86.9 5.2 %copy-start.12 = (f32[128,1536]{1,0:T(8,128)S(1)}, f32[128,1536]{1,0:T(8,128)}, u32[]{:S(2)}) copy-start(f32[128,1536]{1,0:T(8,128)} %copy-done.11) | copy-start | bytes 2359300
  86.9 5.2 %collective-permute-start.13 = (bf16[1,384,3072]{2,1,0:T(8,128)(2,1)}, bf16[1,384,3072]{2,1,0:T(8,128)(2,1)}, u32[]{:S(2)}, u32[]{:S(2)}) collective-permute-start(bf16[1,384,3072]{2,1,0:T(8,128)(2,1)} %bitcast.33.refs_15_.refs_16_.refs_18_.refs_23_), channel_id=1, source_target_pairs={{0,1},{1,0},{2,3},{3,2},{4,5},{5,4},{6,7},{7,6},{8,9},{9,8},{10,11... | collective-permute-start | bytes 7077896 | tf_op jit(solution)/shard_map/ppermute | solution.py:709
  87.4 42.2 %all-to-all-start.1 = ((bf16[4,2,128,768]{3,2,1,0:T(8,128)(2,1)}), bf16[4,2,128,768]{3,2,1,0:T(8,128)(2,1)}, u32[]{:S(2)}, u32[]{:S(2)}) async-start(bf16[4,2,128,768]{3,2,1,0:T(8,128)(2,1)} %param.11), calls=%async_computation.1 | async-start | bytes 3145728 | tf_op jit(solution)/shard_map/all_to_all | solution.py:747
  106.9 2.3 collective-permute-start.14
  109.2 20.4 %copy-start.5 = (bf16[1,128,3072]{2,1,0:T(8,128)(2,1)S(1)}, bf16[1,128,3072]{2,1,0:T(8,128)(2,1)}, u32[]{:S(2)}) copy-start(bf16[1,128,3072]{2,1,0:T(8,128)(2,1)} %copy-done.4) | copy-start | bytes 2359300
  124.1 5.5 %collective-permute-start.15 = (f32[128,1536]{1,0:T(8,128)}, f32[128,1536]{1,0:T(8,128)S(1)}, u32[]{:S(2)}, u32[]{:S(2)}) collective-permute-start(f32[128,1536]{1,0:T(8,128)} %get-tuple-element.65.refs_0_), channel_id=1, source_target_pairs={{0,1},{1,0},{2,3},{3,2},{4,5},{5,4},{6,7},{7,6},{8,9},{9,8},{10,11... | collective-permute-start | bytes 2359304 | tf_op jit(solution)/shard_map/ppermute | solution.py:621
  129.6 23.9 %copy-start.3 = (bf16[128,3072]{1,0:T(8,128)(2,1)S(1)}, bf16[128,3072]{1,0:T(8,128)(2,1)}, u32[]{:S(2)}) copy-start(bf16[128,3072]{1,0:T(8,128)(2,1)} %copy-done.2) | copy-start | bytes 2359300
  148.6 3.7 %collective-permute-start.16 = (f32[256,1536]{1,0:T(8,128)}, f32[256,1536]{1,0:T(8,128)S(1)}, u32[]{:S(2)}, u32[]{:S(2)}) collective-permute-start(f32[256,1536]{1,0:T(8,128)} %get-tuple-element.68.refs_0_), channel_id=1, source_target_pairs={{0,1},{1,0},{2,3},{3,2},{4,5},{5,4},{6,7},{7,6},{8,9},{9,8},{10,11... | collective-permute-start | bytes 4718600 | tf_op jit(solution)/shard_map/ppermute | solution.py:621
  152.3 1.2 copy-start.22
  173.9 1.8 collective-permute-start.17
  175.7 21.2 %copy-start.14 = (bf16[128,1536]{1,0:T(8,128)(2,1)S(1)}, bf16[128,1536]{1,0:T(8,128)(2,1)}, u32[]{:S(2)}) copy-start(bf16[128,1536]{1,0:T(8,128)(2,1)} %copy-done.13) | copy-start | bytes 1179652
  195.1 1.8 collective-permute-start.18
  196.9 19.3 %copy-start.16 = (bf16[128,1536]{1,0:T(8,128)(2,1)S(1)}, bf16[128,1536]{1,0:T(8,128)(2,1)}, u32[]{:S(2)}) copy-start(bf16[128,1536]{1,0:T(8,128)(2,1)} %copy-done.15) | copy-start | bytes 1179652
  216.2 11.7 %copy-start.17 = (f32[128,1536]{1,0:T(8,128)}, f32[128,1536]{1,0:T(8,128)S(1)}, u32[]{:S(2)}) copy-start(f32[128,1536]{1,0:T(8,128)S(1)} %get-tuple-element.90.refs_0_) | copy-start | bytes 2359300
  216.2 1.6 copy-start.7
  229.0 3.1 %collective-permute-start.19 = (bf16[4,96,1536]{2,1,0:T(8,128)(2,1)}, bf16[4,96,1536]{2,1,0:T(8,128)(2,1)S(1)}, u32[]{:S(2)}, u32[]{:S(2)}) collective-permute-start(bf16[4,96,1536]{2,1,0:T(8,128)(2,1)} %get-tuple-element.97), channel_id=1, source_target_pairs={{0,1},{1,0},{2,3},{3,2},{4,5},{5,4},{6,7},{7,6},{8,9},{9,8},{10,11... | collective-permute-start | bytes 3538952 | tf_op jit(solution)/shard_map/ppermute | solution.py:632
  229.3 6.0 %collective-permute-start.20 = (bf16[128,1536]{1,0:T(8,128)(2,1)S(1)}, bf16[128,1536]{1,0:T(8,128)(2,1)S(1)}, u32[]{:S(2)}, u32[]{:S(2)}) collective-permute-start(bf16[128,1536]{1,0:T(8,128)(2,1)S(1)} %get-tuple-element.98), channel_id=1, source_target_pairs={{0,1},{1,0},{2,3},{3,2},{4,5},{5,4},{6,7},{7,6},{8,9},{9,8},{10,11... | collective-permute-start | bytes 1179656 | tf_op jit(solution)/shard_map/ppermute | solution.py:621
  233.1 2.3 copy-start.9
  233.1 2.3 copy-start.10
  233.1 2.5 copy-start.18
  235.2 9.2 %copy-start.20 = (f32[4,96,1536]{2,1,0:T(8,128)}, f32[4,96,1536]{2,1,0:T(8,128)S(1)}, u32[]{:S(2)}) copy-start(f32[4,96,1536]{2,1,0:T(8,128)S(1)} %convert_add_fusion.1) | copy-start | bytes 7077892
  235.3 15.6 %collective-permute-start.21 = (bf16[2,96,1536]{2,1,0:T(8,128)(2,1)S(1)}, bf16[2,96,1536]{2,1,0:T(8,128)(2,1)S(1)}, u32[]{:S(2)}, u32[]{:S(2)}) collective-permute-start(bf16[2,96,1536]{2,1,0:T(8,128)(2,1)S(1)} %fusion.2), channel_id=1, source_target_pairs={{0,2},{1,3},{2,0},{3,1},{4,6},{5,7},{6,4},{7,5},{8,10},{9,11},{10,... | collective-permute-start | bytes 1769480 | tf_op jit(solution)/shard_map/ppermute | solution.py:632
  250.9 3.0 %collective-permute-start.22 = (bf16[4,96,1536]{2,1,0:T(8,128)(2,1)S(1)}, bf16[4,96,1536]{2,1,0:T(8,128)(2,1)}, u32[]{:S(2)}, u32[]{:S(2)}) collective-permute-start(bf16[4,96,1536]{2,1,0:T(8,128)(2,1)S(1)} %get-tuple-element.105), channel_id=1, source_target_pairs={{0,1},{1,0},{2,3},{3,2},{4,5},{5,4},{6,7},{7,6},{8,9},{9,8},{10,11... | collective-permute-start | bytes 3538952 | tf_op jit(solution)/shard_map/ppermute | solution.py:632
  253.9 2.2 copy-start.21
  255.7 21.8 %collective-permute-start.23 = (bf16[2,96,1536]{2,1,0:T(8,128)(2,1)S(1)}, bf16[2,96,1536]{2,1,0:T(8,128)(2,1)S(1)}, u32[]{:S(2)}, u32[]{:S(2)}) collective-permute-start(bf16[2,96,1536]{2,1,0:T(8,128)(2,1)S(1)} %fusion.3), channel_id=1, source_target_pairs={{0,2},{1,3},{2,0},{3,1},{4,6},{5,7},{6,4},{7,5},{8,10},{9,11},{10,... | collective-permute-start | bytes 1769480 | tf_op jit(solution)/shard_map/ppermute | solution.py:632
  256.2 21.5 %collective-permute-start.25 = (bf16[1,96,1536]{2,1,0:T(8,128)(2,1)S(1)}, bf16[1,96,1536]{2,1,0:T(8,128)(2,1)S(1)}, u32[]{:S(2)}, u32[]{:S(2)}) collective-permute-start(bf16[1,96,1536]{2,1,0:T(8,128)(2,1)S(1)} %dynamic-slice_convert_fusion), channel_id=1, source_target_pairs={{0,4},{1,5},{2,6},{3,7},{4,0},{5,1},{6,2},{7,3},{8,12},{9,13},{10,... | collective-permute-start | bytes 884744 | tf_op jit(solution)/shard_map/ppermute | solution.py:632
  277.6 14.5 %collective-permute-start.24 = (bf16[1,96,1536]{2,1,0:T(8,128)(2,1)S(1)}, bf16[1,96,1536]{2,1,0:T(8,128)(2,1)S(1)}, u32[]{:S(2)}, u32[]{:S(2)}) collective-permute-start(bf16[1,96,1536]{2,1,0:T(8,128)(2,1)S(1)} %dynamic-slice_convert_fusion.1), channel_id=1, source_target_pairs={{0,4},{1,5},{2,6},{3,7},{4,0},{5,1},{6,2},{7,3},{8,12},{9,13},{10,... | collective-permute-start | bytes 884744 | tf_op jit(solution)/shard_map/ppermute | solution.py:632
  277.8 17.1 %copy-start.1 = (bf16[33,768]{1,0:T(8,128)(2,1)S(1)}, bf16[33,768]{1,0:T(8,128)(2,1)}, u32[]{:S(2)}) copy-start(bf16[33,768]{1,0:T(8,128)(2,1)} %param.7) | copy-start | bytes 152068
  (5 other events, 4.5 us)
